TPU v7x, 32 devices: a whole 2x2x4 slice. The times are simulated.
32 devices in a mesh: section: 2 (over core), dp: 4 (over y, x), tensor: 4 (over z).
Axes of the slice: x: 2, y: 2, z: 4, core: 2. Of those that a mesh axis runs over, the one named last changes fastest.
Arguments:
- boundary_in: float32 [2, 16, 577, 1024], P('section', 'dp', None, 'tensor'), may hold values from -6 to 6
- counts: int32 [4, 2], P('dp'), may hold values from 1 to 2, as said below
- qkv_weight: bfloat16 [2, 1024, 3, 1024], P('section', 'dp', None, 'tensor'), may hold values from -0.1875 to 0.1875
- proj_weight: bfloat16 [2, 1024, 1024], P('section', 'tensor', 'dp'), may hold values from -1 to 1
- fc1_weight: bfloat16 [2, 1024, 4096], P('section', 'dp', 'tensor'), may hold values from -0.1875 to 0.1875
- fc2_weight: bfloat16 [2, 4096, 1024], P('section', 'tensor', 'dp'), may hold values from -0.09375 to 0.09375
- vectors: bfloat16 [2, 8, 4, 256], P('section', None, 'tensor', 'dp')
- fc1_bias: bfloat16 [2, 4, 1024], P('section', 'tensor', 'dp'), may hold values from -3 to 3
Outputs:
- boundary_out: float32 [2, 16, 577, 1024], P('section', 'dp', None, 'tensor')
- grad_qkv: float32 [2, 1024, 3, 1024], P('section', 'dp', None, 'tensor')
- grad_proj: float32 [2, 1024, 1024], P('section', 'tensor', 'dp')
- grad_fc1: float32 [2, 1024, 4096], P('section', 'dp', 'tensor')
- grad_fc2: float32 [2, 4096, 1024], P('section', 'tensor', 'dp')
- grad_vectors: float32 [2, 8, 4, 256], P('section', None, 'tensor', 'dp')
- grad_fc1_bias: float32 [2, 4, 1024], P('section', 'tensor', 'dp')
Inputs may be any that keep to these rules, and one draw needn't show every extreme that they name: The first counts[s, m] slots of micro-batch m of data shard s are live; some count equals 2 and some count equals 1.
All inputs are finite; a program needn't handle non-finite values.
Results may differ from a plain program's by a relative error of at most 0.013.
Values may be sent and summed in bfloat16 or wider, within the bound.
No kernel may reach another device: no remote copies, remote signals or barrier semaphores. Data moves between devices by JAX's collectives and lax.ppermute only.
A program may use at most 256 MiB of HBM per device.

v0:
```python
import jax
import jax.numpy as jnp
from jax import lax
from jax.sharding import PartitionSpec as P

HD = 64


EPS = 1e-06


def shifted(block, axis, distance):
    devices = range(lax.axis_size(axis))
    route = [(i - distance, i) for i in devices if i - distance in devices]
    return lax.ppermute(block, axis, route)


def fetch_layer(shards):
    gathered = (
        lax.all_gather(shards[0], "dp", axis=1, tiled=True),
        lax.all_gather(shards[1], "dp", axis=2, tiled=True),
        lax.all_gather(shards[2], "dp", axis=1, tiled=True),
        lax.all_gather(shards[3], "dp", axis=2, tiled=True),
        lax.all_gather(shards[4], "dp", axis=3, tiled=True),
        lax.all_gather(shards[5], "dp", axis=2, tiled=True),
    )
    return (
        gathered[0][0],
        gathered[1][0],
        gathered[2][0],
        gathered[3][0],
        gathered[4][0, :, 0, :].astype(jnp.float32),
        gathered[5][0, 0].astype(jnp.float32),
    )


def settle_grads(grads):
    return (
        lax.psum_scatter(
            grads[0].astype(jnp.bfloat16), "dp", scatter_dimension=1, tiled=True
        ).astype(jnp.float32),
        lax.psum_scatter(
            grads[1].astype(jnp.bfloat16), "dp", scatter_dimension=2, tiled=True
        ).astype(jnp.float32),
        lax.psum_scatter(
            grads[2].astype(jnp.bfloat16), "dp", scatter_dimension=1, tiled=True
        ).astype(jnp.float32),
        lax.psum_scatter(
            grads[3].astype(jnp.bfloat16), "dp", scatter_dimension=2, tiled=True
        ).astype(jnp.float32),
        lax.psum_scatter(
            grads[4].astype(jnp.bfloat16), "dp", scatter_dimension=3, tiled=True
        ).astype(jnp.float32),
        lax.psum_scatter(
            grads[5].astype(jnp.bfloat16), "dp", scatter_dimension=2, tiled=True
        ).astype(jnp.float32),
    )


def layer_norm(value, gain, shift, width):
    totals, squares = lax.psum((jnp.sum(value, -1), jnp.sum(value * value, -1)), "tensor")
    center = (totals / width)[..., None]
    spread = (squares / width)[..., None] - center * center
    factor = lax.rsqrt(spread + EPS)
    centred = (value - center) * factor
    normed = (centred * gain + shift).astype(jnp.bfloat16)
    whole = lax.all_gather(normed, "tensor", axis=2, tiled=True)
    return (whole, centred, factor)


def norm_backward(grad_normed, centred, factor, gain, width):
    grad_centred = grad_normed * gain
    totals, inner = lax.psum(
        (jnp.sum(grad_centred, -1), jnp.sum(grad_centred * centred, -1)), "tensor"
    )
    return factor * (
        grad_centred - (totals / width)[..., None] - centred * (inner / width)[..., None]
    )


def branch_total(partial_value):
    return lax.psum_scatter(partial_value, "tensor", scatter_dimension=2, tiled=True)


def branch_spread(gradient):
    return lax.all_gather(gradient.astype(jnp.bfloat16), "tensor", axis=2, tiled=True)


def rows_total(partial_value):
    return lax.psum_scatter(
        partial_value.astype(jnp.bfloat16), "tensor", scatter_dimension=2, tiled=True
    ).astype(jnp.float32)


def gelu_slope(value):
    return (
        0.5 * (1.0 + lax.erf(value * 0.7071067811865476))
        + value * jnp.exp(-0.5 * value * value) * 0.3989422804014327
    )


def forward_layer(weights, value):
    qkv_matrix, out_matrix, up_matrix, down_matrix, vector_rows, up_bias = weights
    images, tokens, local = value.shape
    width = qkv_matrix.shape[0]
    split = (images, tokens, local // HD, HD)
    normed, centred, factor = layer_norm(value, vector_rows[0], vector_rows[1], width)
    projected = jnp.einsum("btd,dce->btce", normed, qkv_matrix, preferred_element_type=jnp.float32)
    queries = (projected[:, :, 0] + vector_rows[2]).astype(jnp.bfloat16)
    keyset = projected[:, :, 1].astype(jnp.bfloat16)
    valueset = (projected[:, :, 2] + vector_rows[3]).astype(jnp.bfloat16)
    scores = jnp.einsum(
        "bqhd,bkhd->bhqk",
        queries.reshape(split),
        keyset.reshape(split),
        preferred_element_type=jnp.float32,
    ) * HD ** (-0.5)
    highest = jnp.max(scores, -1, keepdims=True)
    exponent = jnp.exp(scores - highest)
    denominator = jnp.sum(exponent, -1, keepdims=True)
    weights_low = (exponent / denominator).astype(jnp.bfloat16)
    log_total = highest + jnp.log(denominator)
    mixed = jnp.einsum(
        "bhqk,bkhd->bqhd", weights_low, valueset.reshape(split), preferred_element_type=jnp.float32
    )
    mixed = mixed.astype(jnp.bfloat16).reshape(images, tokens, local)
    attended = branch_total(
        jnp.einsum("bte,ed->btd", mixed, out_matrix, preferred_element_type=jnp.float32)
    )
    middle = value + attended + vector_rows[4]
    normed_two, centred_two, factor_two = layer_norm(middle, vector_rows[5], vector_rows[6], width)
    before = (
        jnp.einsum("btd,df->btf", normed_two, up_matrix, preferred_element_type=jnp.float32)
        + up_bias
    )
    hidden = jax.nn.gelu(before, approximate=False).astype(jnp.bfloat16)
    output = (
        middle
        + branch_total(
            jnp.einsum("btf,fd->btd", hidden, down_matrix, preferred_element_type=jnp.float32)
        )
        + vector_rows[7]
    )
    kept = (
        normed,
        centred,
        factor,
        queries,
        keyset,
        valueset,
        log_total,
        mixed,
        normed_two,
        centred_two,
        factor_two,
        before,
        hidden,
    )
    return (output, kept)


def backward_layer(weights, kept, grad_out):
    qkv_matrix, out_matrix, up_matrix, down_matrix, vector_rows, up_bias = weights
    (
        normed,
        centred,
        factor,
        queries,
        keyset,
        valueset,
        log_total,
        mixed,
        normed_two,
        centred_two,
        factor_two,
        before,
        hidden,
    ) = kept
    images, tokens, local = grad_out.shape
    width = qkv_matrix.shape[0]
    split = (images, tokens, local // HD, HD)
    grad_down_bias = jnp.sum(grad_out, (0, 1))
    grad_branch = branch_spread(grad_out)
    grad_down = jnp.einsum("btf,btd->fd", hidden, grad_branch, preferred_element_type=jnp.float32)
    grad_hidden = jnp.einsum(
        "btd,fd->btf", grad_branch, down_matrix, preferred_element_type=jnp.float32
    )
    grad_before = grad_hidden * gelu_slope(before)
    grad_up_bias = jnp.sum(grad_before, (0, 1))
    before_low = grad_before.astype(jnp.bfloat16)
    grad_up = jnp.einsum("btd,btf->df", normed_two, before_low, preferred_element_type=jnp.float32)
    grad_normed_two = rows_total(
        jnp.einsum("btf,df->btd", before_low, up_matrix, preferred_element_type=jnp.float32)
    )
    grad_gain_two = jnp.sum(grad_normed_two * centred_two, (0, 1))
    grad_shift_two = jnp.sum(grad_normed_two, (0, 1))
    grad_middle = grad_out + norm_backward(
        grad_normed_two, centred_two, factor_two, vector_rows[5], width
    )
    grad_out_bias = jnp.sum(grad_middle, (0, 1))
    grad_attended = branch_spread(grad_middle)
    grad_outproj = jnp.einsum(
        "bte,btd->ed", mixed, grad_attended, preferred_element_type=jnp.float32
    )
    grad_mixed = jnp.einsum(
        "btd,ed->bte", grad_attended, out_matrix, preferred_element_type=jnp.float32
    )
    grad_mixed = grad_mixed.astype(jnp.bfloat16).reshape(split)
    query_heads = queries.reshape(split)
    key_heads = keyset.reshape(split)
    scores = jnp.einsum(
        "bqhd,bkhd->bhqk", query_heads, key_heads, preferred_element_type=jnp.float32
    ) * HD ** (-0.5)
    weights_full = jnp.exp(scores - log_total)
    weights_low = weights_full.astype(jnp.bfloat16)
    grad_values = jnp.einsum(
        "bhqk,bqhd->bkhd", weights_low, grad_mixed, preferred_element_type=jnp.float32
    )
    grad_weights = jnp.einsum(
        "bqhd,bkhd->bhqk", grad_mixed, valueset.reshape(split), preferred_element_type=jnp.float32
    )
    row_inner = jnp.sum(grad_weights * weights_full, -1, keepdims=True)
    grad_scores = (weights_full * (grad_weights - row_inner)).astype(jnp.bfloat16)
    grad_queries = jnp.einsum(
        "bhqk,bkhd->bqhd", grad_scores, key_heads, preferred_element_type=jnp.float32
    ) * HD ** (-0.5)
    grad_keys = jnp.einsum(
        "bhqk,bqhd->bkhd", grad_scores, query_heads, preferred_element_type=jnp.float32
    ) * HD ** (-0.5)
    grad_queries = grad_queries.reshape(images, tokens, local)
    grad_keys = grad_keys.reshape(images, tokens, local)
    grad_values = grad_values.reshape(images, tokens, local)
    grad_query_bias = jnp.sum(grad_queries, (0, 1))
    grad_value_bias = jnp.sum(grad_values, (0, 1))
    grad_stack = jnp.stack([grad_queries, grad_keys, grad_values], 2).astype(jnp.bfloat16)
    grad_qkv_local = jnp.einsum(
        "btd,btce->dce", normed, grad_stack, preferred_element_type=jnp.float32
    )
    grad_normed = rows_total(
        jnp.einsum("btce,dce->btd", grad_stack, qkv_matrix, preferred_element_type=jnp.float32)
    )
    grad_gain_one = jnp.sum(grad_normed * centred, (0, 1))
    grad_shift_one = jnp.sum(grad_normed, (0, 1))
    grad_value = grad_middle + norm_backward(grad_normed, centred, factor, vector_rows[0], width)
    grad_rows = jnp.stack(
        [
            grad_gain_one,
            grad_shift_one,
            grad_query_bias,
            grad_value_bias,
            grad_out_bias,
            grad_gain_two,
            grad_shift_two,
            grad_down_bias,
        ]
    )
    grads = (
        grad_qkv_local[None],
        grad_outproj[None],
        grad_up[None],
        grad_down[None],
        grad_rows[None, :, None, :],
        grad_up_bias[None, None, :],
    )
    return (grad_value, grads)


def body(boundary_in, counts, qkv_weight, proj_weight, fc1_weight, fc2_weight, vectors, fc1_bias):
    section_index = lax.axis_index("section")
    is_first = section_index == 0
    batches = counts.shape[1]
    images = boundary_in.shape[1] // batches
    tokens = boundary_in.shape[2]
    local = boundary_in.shape[3]
    shards = (qkv_weight, proj_weight, fc1_weight, fc2_weight, vectors, fc1_bias)
    slot_index = jnp.arange(images)
    live_masks = [
        (slot_index < counts[0, number]).astype(jnp.float32)[:, None, None]
        for number in range(batches)
    ]
    received = jnp.zeros((images, tokens, local), jnp.float32)
    stored = []
    outputs = []
    for tick in range(batches + 1):
        number = min(tick, batches - 1)
        source = boundary_in[0, number * images : (number + 1) * images]
        weights = fetch_layer(shards)
        value = jnp.where(is_first, source, received)
        output, kept = forward_layer(weights, value)
        stored.append(kept)
        if tick > 0:
            outputs.append(output * live_masks[tick - 1])
        if tick < batches:
            received = shifted(output.astype(jnp.bfloat16), "section", 1).astype(jnp.float32)
    grad_received = jnp.zeros((images, tokens, local), jnp.float32)
    grad_inputs = [None] * batches
    totals = None
    for turn in range(batches + 1):
        number = batches - 1 - turn
        if turn < batches:
            start_grad = (
                boundary_in[1, number * images : (number + 1) * images] * live_masks[number]
            )
        else:
            start_grad = jnp.zeros((images, tokens, local), jnp.float32)
        grad_out = jnp.where(is_first, grad_received, start_grad)
        weights = fetch_layer(shards)
        grad_value, grads = backward_layer(weights, stored[batches - turn], grad_out)
        part_grads = settle_grads(grads)
        if totals is None:
            totals = part_grads
        else:
            totals = jax.tree.map(lambda left, right: left + right, totals, part_grads)
        if turn > 0:
            grad_inputs[batches - turn] = grad_value
        if turn < batches:
            grad_received = shifted(grad_value.astype(jnp.bfloat16), "section", -1).astype(
                jnp.float32
            )
    pieces = [
        jnp.where(is_first, grad_inputs[number], outputs[number]) for number in range(batches)
    ]
    boundary_out = jnp.concatenate(pieces, 0)[None]
    return (boundary_out, totals[0], totals[1], totals[2], totals[3], totals[4], totals[5])


def solution(mesh):
    in_specs = (
        P("section", "dp", None, "tensor"),
        P("dp", None),
        P("section", "dp", None, "tensor"),
        P("section", "tensor", "dp"),
        P("section", "dp", "tensor"),
        P("section", "tensor", "dp"),
        P("section", None, "tensor", "dp"),
        P("section", "tensor", "dp"),
    )
    out_specs = (
        P("section", "dp", None, "tensor"),
        P("section", "dp", None, "tensor"),
        P("section", "tensor", "dp"),
        P("section", "dp", "tensor"),
        P("section", "tensor", "dp"),
        P("section", None, "tensor", "dp"),
        P("section", "tensor", "dp"),
    )
    return jax.shard_map(body, mesh=mesh, in_specs=in_specs, out_specs=out_specs, check_vma=False)
```

profile of v0, /device:TPU:1, one launch (start us, length us, event | category | flops | bytes accessed | tf_op | source)
XLA Modules:
  0.0 2559.5 jit_solution(17639357572954397036)
XLA Ops:
  55.6 43.6 %all-gather.16.cloned.1.call-done = bf16[2,577,1024]{2,1,0:T(8,128)(2,1)} async-done(((bf16[2,577,256]{2,1,0:T(8,128)(2,1)}), bf16[2,577,1024]{2,1,0:T(8,128)(2,1)}) %all-gather.16.cloned.1.call-update) | async-done | bytes 2363408 | tf_op jit(solution)/shard_map/all_gather | solution.py:67
  126.4 84.4 %reduce-scatter.43.cloned.1.call-done = f32[2,577,256]{2,1,0:T(8,128)} async-done(((f32[2,577,1024]{2,1,0:T(8,128)}), f32[2,577,256]{2,1,0:T(8,128)}) %reduce-scatter.43.cloned.1.call-update) | async-done | bytes 1181712 | tf_op jit(solution)/shard_map/reduce_scatter | solution.py:82
  248.5 52.9 %all-gather.20.cloned.1.call-done = bf16[2,577,1024]{2,1,0:T(8,128)(2,1)} async-done(((bf16[2,577,256]{2,1,0:T(8,128)(2,1)}), bf16[2,577,1024]{2,1,0:T(8,128)(2,1)}) %all-gather.20.cloned.1.call-update) | async-done | bytes 2363408 | tf_op jit(solution)/shard_map/all_gather | solution.py:67
  344.1 86.5 %reduce-scatter.45.cloned.1.call-done = f32[2,577,256]{2,1,0:T(8,128)} async-done(((f32[2,577,1024]{2,1,0:T(8,128)}), f32[2,577,256]{2,1,0:T(8,128)}) %reduce-scatter.45.cloned.1.call-update) | async-done | bytes 1181712 | tf_op jit(solution)/shard_map/reduce_scatter | solution.py:82
  454.7 52.2 %all-gather.26.cloned.1.call-done = bf16[2,577,1024]{2,1,0:T(8,128)(2,1)} async-done(((bf16[2,577,256]{2,1,0:T(8,128)(2,1)}), bf16[2,577,1024]{2,1,0:T(8,128)(2,1)}) %all-gather.26.cloned.1.call-update) | async-done | bytes 2363408 | tf_op jit(solution)/shard_map/all_gather | solution.py:67
  531.3 85.0 %reduce-scatter.47.cloned.1.call-done = f32[2,577,256]{2,1,0:T(8,128)} async-done(((f32[2,577,1024]{2,1,0:T(8,128)}), f32[2,577,256]{2,1,0:T(8,128)}) %reduce-scatter.47.cloned.1.call-update) | async-done | bytes 1181712 | tf_op jit(solution)/shard_map/reduce_scatter | solution.py:82
  634.2 52.6 %all-gather.28.cloned.1.call-done = bf16[2,577,1024]{2,1,0:T(8,128)(2,1)} async-done(((bf16[2,577,256]{2,1,0:T(8,128)(2,1)}), bf16[2,577,1024]{2,1,0:T(8,128)(2,1)}) %all-gather.28.cloned.1.call-update) | async-done | bytes 2363408 | tf_op jit(solution)/shard_map/all_gather | solution.py:67
  710.2 85.0 %reduce-scatter.49.cloned.1.call-done = f32[2,577,256]{2,1,0:T(8,128)} async-done(((f32[2,577,1024]{2,1,0:T(8,128)}), f32[2,577,256]{2,1,0:T(8,128)}) %reduce-scatter.49.cloned.1.call-update) | async-done | bytes 1181712 | tf_op jit(solution)/shard_map/reduce_scatter | solution.py:82
  819.5 51.9 %all-gather.30.cloned.1.call-done = bf16[2,577,1024]{2,1,0:T(8,128)(2,1)} async-done(((bf16[2,577,256]{2,1,0:T(8,128)(2,1)}), bf16[2,577,1024]{2,1,0:T(8,128)(2,1)}) %all-gather.30.cloned.1.call-update) | async-done | bytes 2363408 | tf_op jit(solution)/shard_map/all_gather | solution.py:67
  900.6 85.0 %reduce-scatter.51.cloned.1.call-done = f32[2,577,256]{2,1,0:T(8,128)} async-done(((f32[2,577,1024]{2,1,0:T(8,128)}), f32[2,577,256]{2,1,0:T(8,128)}) %reduce-scatter.51.cloned.1.call-update) | async-done | bytes 1181712 | tf_op jit(solution)/shard_map/reduce_scatter | solution.py:82
  1006.0 52.0 %all-gather.34.cloned.1.call-done = bf16[2,577,1024]{2,1,0:T(8,128)(2,1)} async-done(((bf16[2,577,256]{2,1,0:T(8,128)(2,1)}), bf16[2,577,1024]{2,1,0:T(8,128)(2,1)}) %all-gather.34.cloned.1.call-update) | async-done | bytes 2363408 | tf_op jit(solution)/shard_map/all_gather | solution.py:67
  1067.8 41.6 %all-gather.32.cloned.1.call-done = bf16[2,577,1024]{2,1,0:T(8,128)(2,1)} async-done(((bf16[2,577,256]{2,1,0:T(8,128)(2,1)}), bf16[2,577,1024]{2,1,0:T(8,128)(2,1)}) %all-gather.32.cloned.1.call-update) | async-done | bytes 2363408 | tf_op jit(solution)/shard_map/all_gather | solution.py:86
  1122.4 47.0 %reduce-scatter.53.cloned.1.call-done = bf16[2,577,256]{2,1,0:T(8,128)(2,1)} async-done(((bf16[2,577,1024]{2,1,0:T(8,128)(2,1)}), bf16[2,577,256]{2,1,0:T(8,128)(2,1)}) %reduce-scatter.53.cloned.1.call-update) | async-done | bytes 590864 | tf_op jit(solution)/shard_map/reduce_scatter | solution.py:90
  1189.3 52.6 %all-gather.36.cloned.1.call-done = bf16[2,577,1024]{2,1,0:T(8,128)(2,1)} async-done(((bf16[2,577,256]{2,1,0:T(8,128)(2,1)}), bf16[2,577,1024]{2,1,0:T(8,128)(2,1)}) %all-gather.36.cloned.1.call-update) | async-done | bytes 2363408 | tf_op jit(solution)/shard_map/all_gather | solution.py:86
  1285.1 47.0 %reduce-scatter.55.cloned.1.call-done = bf16[2,577,256]{2,1,0:T(8,128)(2,1)} async-done(((bf16[2,577,1024]{2,1,0:T(8,128)(2,1)}), bf16[2,577,256]{2,1,0:T(8,128)(2,1)}) %reduce-scatter.55.cloned.1.call-update) | async-done | bytes 590864 | tf_op jit(solution)/shard_map/reduce_scatter | solution.py:90
  1360.9 49.0 %all-gather.38.cloned.1.call-done = bf16[2,577,1024]{2,1,0:T(8,128)(2,1)} async-done(((bf16[2,577,256]{2,1,0:T(8,128)(2,1)}), bf16[2,577,1024]{2,1,0:T(8,128)(2,1)}) %all-gather.38.cloned.1.call-update) | async-done | bytes 2363408 | tf_op jit(solution)/shard_map/all_gather | solution.py:86
  1422.8 47.0 %reduce-scatter.57.cloned.1.call-done = bf16[2,577,256]{2,1,0:T(8,128)(2,1)} async-done(((bf16[2,577,1024]{2,1,0:T(8,128)(2,1)}), bf16[2,577,256]{2,1,0:T(8,128)(2,1)}) %reduce-scatter.57.cloned.1.call-update) | async-done | bytes 590864 | tf_op jit(solution)/shard_map/reduce_scatter | solution.py:90
  1490.6 52.6 %all-gather.40.cloned.1.call-done = bf16[2,577,1024]{2,1,0:T(8,128)(2,1)} async-done(((bf16[2,577,256]{2,1,0:T(8,128)(2,1)}), bf16[2,577,1024]{2,1,0:T(8,128)(2,1)}) %all-gather.40.cloned.1.call-update) | async-done | bytes 2363408 | tf_op jit(solution)/shard_map/all_gather | solution.py:86
  1641.5 72.6 %reduce-scatter.65.cloned.1.call-done = f32[2,577,256]{2,1,0:T(8,128)} async-done(((f32[2,577,1024]{2,1,0:T(8,128)}), f32[2,577,256]{2,1,0:T(8,128)}) %reduce-scatter.65.cloned.1.call-update) | async-done | bytes 1181712 | tf_op jit(solution)/shard_map/reduce_scatter | solution.py:82
  1723.3 50.9 %all-gather.42.cloned.1.call-done = bf16[2,577,1024]{2,1,0:T(8,128)(2,1)} async-done(((bf16[2,577,256]{2,1,0:T(8,128)(2,1)}), bf16[2,577,1024]{2,1,0:T(8,128)(2,1)}) %all-gather.42.cloned.1.call-update) | async-done | bytes 2363408 | tf_op jit(solution)/shard_map/all_gather | solution.py:86
  1788.6 47.0 %reduce-scatter.61.cloned.1.call-done = bf16[2,577,256]{2,1,0:T(8,128)(2,1)} async-done(((bf16[2,577,1024]{2,1,0:T(8,128)(2,1)}), bf16[2,577,256]{2,1,0:T(8,128)(2,1)}) %reduce-scatter.61.cloned.1.call-update) | async-done | bytes 590864 | tf_op jit(solution)/shard_map/reduce_scatter | solution.py:90
  2053.1 38.5 %reduce-scatter.81.cloned.1.call-done = bf16[1,256,1024]{2,1,0:T(8,128)(2,1)} async-done(((bf16[1,1024,1024]{2,1,0:T(8,128)(2,1)}), bf16[1,256,1024]{2,1,0:T(8,128)(2,1)}) %reduce-scatter.81.cloned.1.call-update) | async-done | bytes 524304 | tf_op jit(solution)/shard_map/reduce_scatter | solution.py:45
  2091.6 38.6 %reduce-scatter.83.cloned.1.call-done = bf16[1,256,1024]{2,1,0:T(8,128)(2,1)} async-done(((bf16[1,1024,1024]{2,1,0:T(8,128)(2,1)}), bf16[1,256,1024]{2,1,0:T(8,128)(2,1)}) %reduce-scatter.83.cloned.1.call-update) | async-done | bytes 524304 | tf_op jit(solution)/shard_map/reduce_scatter | solution.py:45
  2432.8 48.4 %reduce-scatter.63.cloned.1.call-done = bf16[2,577,256]{2,1,0:T(8,128)(2,1)} async-done(((bf16[2,577,1024]{2,1,0:T(8,128)(2,1)}), bf16[2,577,256]{2,1,0:T(8,128)(2,1)}) %reduce-scatter.63.cloned.1.call-update) | async-done | bytes 590864 | tf_op jit(solution)/shard_map/reduce_scatter | solution.py:90
  (596 shorter events, 1179.0 us)
Async XLA Ops:
  45.1 165.7 %reduce-scatter.43.cloned.1.call-start = ((), (), s32[]{:S(2)}) async-start(), calls=%async_computation.32 | async-start | bytes 5980160 | tf_op jit(solution)/shard_map/reduce_scatter | solution.py:82
  126.4 175.0 %all-gather.20.cloned.1.call-start = ((), (), s32[]{:S(2)}) async-start(), calls=%async_computation.33 | async-start | bytes 2990080 | tf_op jit(solution)/shard_map/all_gather | solution.py:67
  228.7 201.8 %reduce-scatter.45.cloned.1.call-start = ((), (), s32[]{:S(2)}) async-start(), calls=%async_computation.36 | async-start | bytes 5980160 | tf_op jit(solution)/shard_map/reduce_scatter | solution.py:82
  344.0 162.9 %all-gather.26.cloned.1.call-start = ((), (), s32[]{:S(2)}) async-start(), calls=%async_computation.37 | async-start | bytes 2990080 | tf_op jit(solution)/shard_map/all_gather | solution.py:67
  454.5 161.7 %reduce-scatter.47.cloned.1.call-start = ((), (), s32[]{:S(2)}) async-start(), calls=%async_computation.38 | async-start | bytes 5980160 | tf_op jit(solution)/shard_map/reduce_scatter | solution.py:82
  633.9 161.2 %reduce-scatter.49.cloned.1.call-start = ((), (), s32[]{:S(2)}) async-start(), calls=%async_computation.40 | async-start | bytes 5980160 | tf_op jit(solution)/shard_map/reduce_scatter | solution.py:82
  710.2 161.3 %all-gather.30.cloned.1.call-start = ((), (), s32[]{:S(2)}) async-start(), calls=%async_computation.41 | async-start | bytes 2990080 | tf_op jit(solution)/shard_map/all_gather | solution.py:67
  819.0 166.5 %reduce-scatter.51.cloned.1.call-start = ((), (), s32[]{:S(2)}) async-start(), calls=%async_computation.42 | async-start | bytes 5980160 | tf_op jit(solution)/shard_map/reduce_scatter | solution.py:82
  1005.8 163.5 %reduce-scatter.53.cloned.1.call-start = ((), (), s32[]{:S(2)}) async-start(), calls=%async_computation.45 | async-start | bytes 2990080 | tf_op jit(solution)/shard_map/reduce_scatter | solution.py:90
  1597.8 176.4 %all-gather.42.cloned.1.call-start = ((), (), s32[]{:S(2)}) async-start(), calls=%async_computation.52 | async-start | bytes 2990080 | tf_op jit(solution)/shard_map/all_gather | solution.py:86
  1871.1 182.0 %reduce-scatter.79.cloned.1.call-start = ((), (), s32[]{:S(2)}) async-start(), calls=%async_computation.63 | async-start | bytes 2621440 | tf_op jit(solution)/shard_map/reduce_scatter | solution.py:45
  1878.0 213.6 %reduce-scatter.81.cloned.1.call-start = ((), (), s32[]{:S(2)}) async-start(), calls=%async_computation.64 | async-start | bytes 2621440 | tf_op jit(solution)/shard_map/reduce_scatter | solution.py:45
  1883.9 246.2 %reduce-scatter.83.cloned.1.call-start = ((), (), s32[]{:S(2)}) async-start(), calls=%async_computation.65 | async-start | bytes 2621440 | tf_op jit(solution)/shard_map/reduce_scatter | solution.py:45
  1890.8 277.8 %reduce-scatter.85.cloned.1.call-start = ((), (), s32[]{:S(2)}) async-start(), calls=%async_computation.66 | async-start | bytes 2621440 | tf_op jit(solution)/shard_map/reduce_scatter | solution.py:48
  1896.9 309.9 %reduce-scatter.87.cloned.1.call-start = ((), (), s32[]{:S(2)}) async-start(), calls=%async_computation.67 | async-start | bytes 2621440 | tf_op jit(solution)/shard_map/reduce_scatter | solution.py:48
  1903.8 341.3 %reduce-scatter.89.cloned.1.call-start = ((), (), s32[]{:S(2)}) async-start(), calls=%async_computation.68 | async-start | bytes 2621440 | tf_op jit(solution)/shard_map/reduce_scatter | solution.py:48
  1909.8 362.7 %reduce-scatter.73.cloned.1.call-start = ((), (), s32[]{:S(2)}) async-start(), calls=%async_computation.60 | async-start | bytes 655360 | tf_op jit(solution)/shard_map/reduce_scatter | solution.py:42
  1913.3 387.1 %reduce-scatter.75.cloned.1.call-start = ((), (), s32[]{:S(2)}) async-start(), calls=%async_computation.61 | async-start | bytes 655360 | tf_op jit(solution)/shard_map/reduce_scatter | solution.py:42
  1916.8 411.1 %reduce-scatter.77.cloned.1.call-start = ((), (), s32[]{:S(2)}) async-start(), calls=%async_computation.62 | async-start | bytes 655360 | tf_op jit(solution)/shard_map/reduce_scatter | solution.py:42
  1920.4 441.8 %reduce-scatter.67.cloned.1.call-start = ((), (), s32[]{:S(2)}) async-start(), calls=%async_computation.57 | async-start | bytes 1966080 | tf_op jit(solution)/shard_map/reduce_scatter | solution.py:39
  1925.7 470.7 %reduce-scatter.69.cloned.1.call-start = ((), (), s32[]{:S(2)}) async-start(), calls=%async_computation.58 | async-start | bytes 1966080 | tf_op jit(solution)/shard_map/reduce_scatter | solution.py:39
  1931.3 499.3 %reduce-scatter.71.cloned.1.call-start = ((), (), s32[]{:S(2)}) async-start(), calls=%async_computation.59 | async-start | bytes 1966080 | tf_op jit(solution)/shard_map/reduce_scatter | solution.py:39
  1966.6 514.6 %reduce-scatter.63.cloned.1.call-start = ((), (), s32[]{:S(2)}) async-start(), calls=%async_computation.55 | async-start | bytes 2990080 | tf_op jit(solution)/shard_map/reduce_scatter | solution.py:90
  1971.9 552.7 %reduce-scatter.95.cloned.1.call-start = ((), (), s32[]{:S(2)}) async-start(), calls=%async_computation.71 | async-start | bytes 81920
  (142 other events, 15919.2 us)
Sparse Core Ops, SparseCore 0:
  45.2 54.0 all-gather.15
  125.9 84.8 reduce-scatter.42
  250.5 50.7 all-gather.19
  344.2 86.3 reduce-scatter.44
  454.6 52.2 all-gather.25
  531.4 84.8 reduce-scatter.46
  634.1 52.6 all-gather.27
  710.3 84.8 reduce-scatter.48
  819.2 52.2 all-gather.29
  900.7 84.8 reduce-scatter.50
  1005.4 52.6 all-gather.33
  1060.2 49.2 all-gather.31
  1122.5 46.8 reduce-scatter.52
  1189.2 52.7 all-gather.35
  1285.2 46.8 reduce-scatter.54
  1361.0 48.8 all-gather.37
  1422.9 46.8 reduce-scatter.56
  1490.4 52.7 all-gather.39
  1578.3 46.8 reduce-scatter.58
  1627.6 86.4 reduce-scatter.64
  1723.4 50.8 all-gather.41
  1788.7 46.8 reduce-scatter.60
  1855.9 52.6 all-gather.43
  2432.8 48.3 reduce-scatter.62
  (21 shorter events, 622.7 us)
where the time goes:
time: 2570 us; the launch traced here: 2560 us
  waiting for transfers between devices  1840 us (72%)
  matrix products  261 us (10%)
  blocking collectives  193 us (8%)
  other arithmetic  134 us (5%)
  local copies, waits for them, and re-layouts  104 us (4%)
    reduce_scatter x6, waiting for transfers between devices, branch_total(): lax.psum_scatter(partial_value, 'tensor', scatter_dimension=2, tiled=True)  498 us
    all_gather x6, waiting for transfers between devices, layer_norm(): whole = lax.all_gather(normed, 'tensor', axis=2, tiled=True)  305 us
    reduce_scatter x6, waiting for transfers between devices, rows_total(): lax.psum_scatter(partial_value.astype(jnp.bfloat16), 'tensor', scatter_di...  264 us
    all_gather x6, waiting for transfers between devices, branch_spread(): lax.all_gather(gradient.astype(jnp.bfloat16), 'tensor', axis=2, tiled=True)  247 us
    reduce_scatter x3, waiting for transfers between devices, settle_grads(): lax.psum_scatter(grads[2].astype(jnp.bfloat16), 'dp', scatter_dimension=1...  114 us
    reduce_scatter x3, waiting for transfers between devices, settle_grads(): lax.psum_scatter(grads[3].astype(jnp.bfloat16), 'dp', scatter_dimension=2...  112 us
    reduce_scatter x3, waiting for transfers between devices, settle_grads(): lax.psum_scatter(grads[0].astype(jnp.bfloat16), 'dp', scatter_dimension=1...  101 us
    psum x6, blocking collectives, layer_norm(): lax.psum((jnp.sum(value, -1), jnp.sum(value * value, -1)), 'tensor')  86.9 us
  transfers between devices with their start and end apart: 49, of which 45 were waited for; matrix products, arithmetic and copies ran while one was open for 8% of the time, Pallas kernels for 0%

commit v1 on v0

v1 whole, which is shorter than its diff:
```python
import jax
import jax.numpy as jnp
from jax import lax
from jax.sharding import PartitionSpec as P

HD = 64
EPS = 1e-06
ALL = ("dp", "tensor")


def swap(value):
    return lax.ppermute(value, "section", [(0, 1), (1, 0)])


def pair_sum(partial):
    low = partial.astype(jnp.bfloat16)
    return low.astype(jnp.float32) + swap(low).astype(jnp.float32)


def both_layers(shard, axis, is_first):
    half = shard.shape[axis] // 2
    low = lax.slice_in_dim(shard, 0, half, axis=axis)
    high = lax.slice_in_dim(shard, half, 2 * half, axis=axis)
    kept = jnp.where(is_first, low, high)
    received = swap(jnp.where(is_first, high, low))
    return (jnp.where(is_first, kept, received), jnp.where(is_first, received, kept))


def own_layer(first, second, axis, is_first):
    kept = jnp.where(is_first, first, second)
    received = swap(jnp.where(is_first, second, first))
    low = jnp.where(is_first, kept, received)
    high = jnp.where(is_first, received, kept)
    return jnp.concatenate([low, high], axis)


def gather(shard):
    n_dp, n_tensor = lax.axis_size("dp"), lax.axis_size("tensor")
    whole = lax.all_gather(shard, ALL, axis=0, tiled=False)
    return whole.reshape((n_dp, n_tensor) + shard.shape)


def scatter(pieces):
    low = pieces.astype(jnp.bfloat16)
    flat = low.reshape((-1,) + low.shape[2:])
    return lax.psum_scatter(flat, ALL, scatter_dimension=0, tiled=False).astype(jnp.float32)


def mm(form, left, right):
    return jnp.einsum(form, left, right, preferred_element_type=jnp.float32)


def layer_norm(value, gain, shift):
    center = jnp.mean(value, -1, keepdims=True)
    spread = jnp.mean(value * value, -1, keepdims=True) - center * center
    factor = lax.rsqrt(spread + EPS)
    centred = (value - center) * factor
    return ((centred * gain + shift).astype(jnp.bfloat16), centred, factor)


def norm_backward(grad_normed, centred, factor, gain):
    scaled = grad_normed * gain
    return factor * (
        scaled
        - jnp.mean(scaled, -1, keepdims=True)
        - centred * jnp.mean(scaled * centred, -1, keepdims=True)
    )


def gelu_parts(value):
    cdf = 0.5 * (1.0 + lax.erf(value * 0.7071067811865476))
    density = jnp.exp(-0.5 * value * value) * 0.3989422804014327
    return (cdf, density)


def forward_layer(weights, value):
    w_qkv, w_out, w_up, w_down, rows, q_bias, v_bias, up_bias = weights
    tokens = value.shape[0]
    heads = w_out.shape[0] // HD
    split = (tokens, heads, HD)
    normed, centred, factor = layer_norm(value, rows[0], rows[1])
    projected = mm("td,dce->tce", normed, w_qkv)
    queries = (projected[:, 0] + q_bias).astype(jnp.bfloat16)
    keyset = projected[:, 1].astype(jnp.bfloat16)
    valueset = (projected[:, 2] + v_bias).astype(jnp.bfloat16)
    scores = mm("qhd,khd->hqk", queries.reshape(split), keyset.reshape(split)) * HD ** (-0.5)
    highest = jnp.max(scores, -1, keepdims=True)
    exponent = jnp.exp(scores - highest)
    denominator = jnp.sum(exponent, -1, keepdims=True)
    soft = (exponent / denominator).astype(jnp.bfloat16)
    log_total = highest + jnp.log(denominator)
    mixed = mm("hqk,khd->qhd", soft, valueset.reshape(split)).astype(jnp.bfloat16)
    mixed = mixed.reshape(tokens, heads * HD)
    middle = value + pair_sum(mm("te,ed->td", mixed, w_out)) + rows[4]
    normed_two, centred_two, factor_two = layer_norm(middle, rows[5], rows[6])
    before = mm("td,df->tf", normed_two, w_up) + up_bias
    hidden = (before * gelu_parts(before)[0]).astype(jnp.bfloat16)
    output = middle + pair_sum(mm("tf,fd->td", hidden, w_down)) + rows[7]
    kept = (normed, centred, factor, queries, keyset, valueset, log_total, mixed)
    return (output, kept + (normed_two, centred_two, factor_two, before, hidden))


def backward_layer(weights, kept, grad_out):
    w_qkv, w_out, w_up, w_down, rows, q_bias, v_bias, up_bias = weights
    normed, centred, factor, queries, keyset, valueset, log_total, mixed = kept[:8]
    normed_two, centred_two, factor_two, before, hidden = kept[8:]
    tokens = grad_out.shape[0]
    heads = w_out.shape[0] // HD
    split = (tokens, heads, HD)
    scale = HD ** (-0.5)
    grad_branch = grad_out.astype(jnp.bfloat16)
    grad_down = mm("tf,td->fd", hidden, grad_branch)
    cdf, density = gelu_parts(before)
    grad_before = mm("td,fd->tf", grad_branch, w_down) * (cdf + before * density)
    grad_up_bias = jnp.sum(grad_before, 0)
    before_low = grad_before.astype(jnp.bfloat16)
    grad_up = mm("td,tf->df", normed_two, before_low)
    grad_normed_two = pair_sum(mm("tf,df->td", before_low, w_up))
    grad_middle = grad_out + norm_backward(grad_normed_two, centred_two, factor_two, rows[5])
    grad_attended = grad_middle.astype(jnp.bfloat16)
    grad_outproj = mm("te,td->ed", mixed, grad_attended)
    grad_mixed = mm("td,ed->te", grad_attended, w_out).astype(jnp.bfloat16).reshape(split)
    query_heads, key_heads = queries.reshape(split), keyset.reshape(split)
    soft = jnp.exp(mm("qhd,khd->hqk", query_heads, key_heads) * scale - log_total)
    soft_low = soft.astype(jnp.bfloat16)
    grad_values = mm("hqk,qhd->khd", soft_low, grad_mixed)
    grad_soft = mm("qhd,khd->hqk", grad_mixed, valueset.reshape(split))
    row_inner = jnp.sum(grad_soft * soft, -1, keepdims=True)
    grad_scores = (soft * (grad_soft - row_inner)).astype(jnp.bfloat16)
    grad_queries = mm("hqk,khd->qhd", grad_scores, key_heads) * scale
    grad_keys = mm("hqk,qhd->khd", grad_scores, query_heads) * scale
    grad_stack = jnp.stack([grad_queries, grad_keys, grad_values], 1)
    grad_stack = grad_stack.reshape(tokens, 3, heads * HD)
    grad_query_bias = jnp.sum(grad_stack[:, 0], 0)
    grad_value_bias = jnp.sum(grad_stack[:, 2], 0)
    stack_low = grad_stack.astype(jnp.bfloat16)
    grad_qkv = mm("td,tce->dce", normed, stack_low)
    grad_normed = pair_sum(mm("tce,dce->td", stack_low, w_qkv))
    grad_value = grad_middle + norm_backward(grad_normed, centred, factor, rows[0])
    full_rows = jnp.stack(
        [
            jnp.sum(grad_normed * centred, 0),
            jnp.sum(grad_normed, 0),
            jnp.sum(grad_middle, 0),
            jnp.sum(grad_normed_two * centred_two, 0),
            jnp.sum(grad_normed_two, 0),
            jnp.sum(grad_out, 0),
        ]
    )
    small = (full_rows, grad_query_bias, grad_value_bias, grad_up_bias)
    return (grad_value, (grad_qkv, grad_outproj, grad_up, grad_down), small)


def half_cols(core, whole, n_tensor):
    cut = whole.reshape(whole.shape[:-1] + (n_tensor, 2, -1))
    cut = jnp.where(core == 0, cut[..., 0, :], cut[..., 1, :])
    return cut.reshape(whole.shape[:-1] + (-1,))


def spread_cols(core, half, n_tensor):
    cut = half.reshape(half.shape[:-1] + (n_tensor, 1, -1))
    none = jnp.zeros_like(cut)
    both = jnp.concatenate(
        [jnp.where(core == 0, cut, none), jnp.where(core == 0, none, cut)], -2
    )
    return both.reshape(half.shape[:-1] + (-1,))


def body(boundary_in, counts, qkv_weight, proj_weight, fc1_weight, fc2_weight, vectors, fc1_bias):
    core = lax.axis_index("section")
    is_first = core == 0
    place = lax.axis_index("tensor")
    n_dp, n_tensor = lax.axis_size("dp"), lax.axis_size("tensor")
    slots_per_batch = boundary_in.shape[1] // counts.shape[1]
    live = (place % slots_per_batch < counts[0, place // slots_per_batch]).astype(jnp.float32)

    small_shard = jnp.concatenate([vectors.reshape(-1), fc1_bias.reshape(-1)])
    small_other = swap(small_shard)
    small_both = jnp.stack(
        [
            jnp.where(is_first, small_shard, small_other),
            jnp.where(is_first, small_other, small_shard),
        ]
    )
    small = gather(small_both).astype(jnp.float32)
    mine = lax.all_to_all(
        boundary_in[0].astype(jnp.bfloat16), "tensor", split_axis=0, concat_axis=2, tiled=True
    )[0]
    theirs = swap(mine)
    value = jnp.where(is_first, mine, theirs).astype(jnp.float32)
    cotangent = jnp.where(is_first, theirs, mine).astype(jnp.float32) * live

    shards = [
        both_layers(qkv_weight[0], 2, is_first),
        both_layers(proj_weight[0], 0, is_first),
        both_layers(fc1_weight[0], 1, is_first),
        both_layers(fc2_weight[0], 0, is_first),
    ]
    layers = []
    n_vec = vectors.size
    for layer in range(2):
        w_qkv = gather(shards[0][layer]).transpose(0, 2, 3, 1, 4)
        w_qkv = w_qkv.reshape(n_dp * w_qkv.shape[1], 3, -1)
        w_out = gather(shards[1][layer]).transpose(1, 2, 0, 3)
        w_out = w_out.reshape(n_tensor * w_out.shape[1], -1)
        w_up = gather(shards[2][layer]).transpose(0, 2, 1, 3)
        w_up = w_up.reshape(n_dp * w_up.shape[1], -1)
        w_down = gather(shards[3][layer]).transpose(1, 2, 0, 3)
        w_down = w_down.reshape(n_tensor * w_down.shape[1], -1)
        rows = small[:, :, layer, :n_vec].reshape(n_dp, n_tensor, 8, -1)
        rows = rows.transpose(2, 1, 0, 3).reshape(8, -1)
        bias = small[:, :, layer, n_vec:].transpose(1, 0, 2).reshape(-1)
        q_bias = half_cols(core, rows[2], n_tensor)
        v_bias = half_cols(core, rows[3], n_tensor)
        up_bias = half_cols(core, bias, n_tensor)
        layers.append((w_qkv, w_out, w_up, w_down, rows, q_bias, v_bias, up_bias))

    output, kept_first = forward_layer(layers[0], value)
    sent = output.astype(jnp.bfloat16).astype(jnp.float32)
    output, kept_second = forward_layer(layers[1], sent)
    output = output * live

    grads = [None, None]
    smalls = [None, None]
    grad, big, little = backward_layer(layers[1], kept_second, cotangent)
    grads[1], smalls[1] = big, little
    grad = grad.astype(jnp.bfloat16).astype(jnp.float32)
    grad, big, little = backward_layer(layers[0], kept_first, grad)
    grads[0], smalls[0] = big, little

    ends = jnp.where(is_first, grad, output).astype(jnp.bfloat16)
    ends = lax.all_to_all(ends[None], "tensor", split_axis=2, concat_axis=0, tiled=True)
    boundary_out = ends.astype(jnp.float32)[None]

    settled = [None, None]
    for layer in (1, 0):
        g_qkv, g_out, g_up, g_down = grads[layer]
        width = g_qkv.shape[0] // n_dp
        g_qkv = g_qkv.reshape(n_dp, width, 3, n_tensor, -1).transpose(0, 3, 1, 2, 4)
        g_out = g_out.reshape(n_tensor, -1, n_dp, width).transpose(2, 0, 1, 3)
        g_up = g_up.reshape(n_dp, width, n_tensor, -1).transpose(0, 2, 1, 3)
        g_down = g_down.reshape(n_tensor, -1, n_dp, width).transpose(2, 0, 1, 3)
        settled[layer] = tuple(scatter(g) for g in (g_down, g_up, g_out, g_qkv))
    axes = (0, 1, 0, 2)
    whole = [
        own_layer(settled[0][i], settled[1][i], axes[i], is_first)[None] for i in range(4)
    ]
    grad_down, grad_up, grad_out, grad_qkv = whole

    packed = []
    for layer in range(2):
        full_rows, q_row, v_row, up_row = smalls[layer]
        full_rows = jnp.where(core == layer, full_rows, 0.0)
        q_row = spread_cols(core, q_row, n_tensor)
        v_row = spread_cols(core, v_row, n_tensor)
        up_row = spread_cols(core, up_row, n_tensor)
        rows = jnp.stack(
            [full_rows[0], full_rows[1], q_row, v_row, full_rows[2], full_rows[3], full_rows[4], full_rows[5]]
        )
        rows = rows.reshape(8, n_tensor, n_dp, -1).transpose(2, 1, 0, 3).reshape(n_dp, n_tensor, -1)
        up_row = up_row.reshape(n_tensor, n_dp, -1).transpose(1, 0, 2)
        packed.append(jnp.concatenate([rows, up_row], -1))
    ours = jnp.where(is_first, packed[0], packed[1])
    other = swap(jnp.where(is_first, packed[1], packed[0]))
    small_grad = scatter(ours + other)
    grad_vectors = small_grad[:n_vec].reshape(vectors.shape)
    grad_bias = small_grad[n_vec:].reshape(fc1_bias.shape)
    return (boundary_out, grad_qkv, grad_out, grad_up, grad_down, grad_vectors, grad_bias)


def solution(mesh):
    in_specs = (
        P("section", "dp", None, "tensor"),
        P("dp", None),
        P("section", "dp", None, "tensor"),
        P("section", "tensor", "dp"),
        P("section", "dp", "tensor"),
        P("section", "tensor", "dp"),
        P("section", None, "tensor", "dp"),
        P("section", "tensor", "dp"),
    )
    out_specs = (
        P("section", "dp", None, "tensor"),
        P("section", "dp", None, "tensor"),
        P("section", "tensor", "dp"),
        P("section", "dp", "tensor"),
        P("section", "tensor", "dp"),
        P("section", None, "tensor", "dp"),
        P("section", "tensor", "dp"),
    )
    return jax.shard_map(body, mesh=mesh, in_specs=in_specs, out_specs=out_specs, check_vma=False)
```

time: 2570 us -> 1590 us (0.62)
  waiting for transfers between devices: 1840 us -> 919 us
  local copies, waits for them, and re-layouts: 104 us -> 222 us
  matrix products: 261 us -> 155 us
  blocking collectives: 193 us -> 138 us
  other arithmetic: 134 us -> 91.5 us
    reduce_scatter x24 -> x8, waiting for transfers between devices: 1170 us -> 520 us  [scatter(): lax.psum_scatter(flat, ALL, scatter_dimension=0, tiled=False)]
    all_gather x15 -> x8, waiting for transfers between devices: 580 us -> 352 us  [gather(): whole = lax.all_gather(shard, ALL, axis=0, tiled=False)]
    psum x12 -> x0, blocking collectives: 169 us -> none  [the longest x6 86.9 us: layer_norm(): lax.psum((jnp.sum(value, -1), jnp.sum(value * value, -1)), 'tensor')]
    unnamed x0 -> x1, blocking collectives: none -> 106 us
    dot_general x54 -> x36, matrix products: 261 us -> 155 us  [mm(): return jnp.einsum(form, left, right, preferred_element_type=jnp.float32)]
    unnamed x51 -> x16, waiting for transfers between devices: 79.5 us -> 1.99 us
    convert_element_type x7 -> x15, local copies, waits for them, and re-layouts: 3.77 us -> 63.6 us  [the longest x12 57.6 us: scatter(): low = pieces.astype(jnp.bfloat16)]
    convert_element_type x23 -> x6, other arithmetic: 77.8 us -> 22.7 us  [the longest x2 13.4 us: backward_layer(): grad_scores = (soft * (grad_soft - row_inner)).astype(jnp.bfloat16)]
  transfers between devices with their start and end apart: 49 -> 37, of which waited for: 45 -> 23; matrix products, arithmetic and copies ran while one was open for 8% -> 21% of each run, Pallas kernels for 0% -> 0%
where the time goes in v1:
time: 1590 us; the launch traced here: 1580 us
  waiting for transfers between devices  919 us (58%)
  local copies, waits for them, and re-layouts  222 us (14%)
  matrix products  155 us (10%)
  blocking collectives  138 us (9%)
  other arithmetic  91.5 us (6%)
  starting transfers between devices  39.2 us (2%)
  between operations  16.5 us (1%)
    reduce_scatter x8, waiting for transfers between devices, scatter(): lax.psum_scatter(flat, ALL, scatter_dimension=0, tiled=False)  520 us
    all_gather x8, waiting for transfers between devices, gather(): whole = lax.all_gather(shard, ALL, axis=0, tiled=False)  352 us
    dot_general x36, matrix products, mm(): return jnp.einsum(form, left, right, preferred_element_type=jnp.float32)  155 us
    unnamed x1, blocking collectives  106 us
    convert_element_type x12, local copies, waits for them, and re-layouts, scatter(): low = pieces.astype(jnp.bfloat16)  57.6 us
    unnamed x221, local copies, waits for them, and re-layouts  42 us
    reshape x8, local copies, waits for them, and re-layouts, gather(): return whole.reshape((n_dp, n_tensor) + shard.shape)  37.8 us
    all_gather x1, blocking collectives, gather(): whole = lax.all_gather(shard, ALL, axis=0, tiled=False)  32 us
  transfers between devices with their start and end apart: 37, of which 23 were waited for; matrix products, arithmetic and copies ran while one was open for 21% of the time, Pallas kernels for 0%

profile of v1, /device:TPU:1, one launch (start us, length us, event | category | flops | bytes accessed | tf_op | source)
XLA Modules:
  0.0 1581.7 jit_solution(17781040412107375610)
XLA Ops:
  29.8 30.8 %all-to-all-done = bf16[4,577,256]{2,1,0:T(8,128)(2,1)S(1)} async-done(((bf16[4,577,256]{2,1,0:T(8,128)(2,1)}), bf16[4,577,256]{2,1,0:T(8,128)(2,1)S(1)}, u32[]{:S(2)}, u32[]{:S(2)}) %all-to-all-start) | async-done | bytes 1181728 | tf_op jit(solution)/shard_map/all_to_all | solution.py:186
  65.6 32.0 %all-gather.9 = bf16[16,2,768]{2,1,0:T(2,128)(2,1)S(1)} all-gather(bf16[1,2,768]{2,1,0:T(2,128)(2,1)S(1)} %maximum_bitcast_fusion.6), channel_id=2, replica_groups=mesh['section'=2,'dp'=4,'tensor'=4] {'dp','tensor'}, dimensions={0}, use_global_device_ids=true | all-gather | bytes 52224 | tf_op jit(solution)/shard_map/all_gather | solution.py:39
  105.9 40.4 %all-gather.19.cloned.1.call-done = bf16[4096,3,128]{2,0,1:T(8,128)(2,1)} async-done(((bf16[256,3,128]{2,0,1:T(8,128)(2,1)}), bf16[4096,3,128]{2,0,1:T(8,128)(2,1)}) %all-gather.19.cloned.1.call-update) | async-done | bytes 3145744 | tf_op jit(solution)/shard_map/all_gather | solution.py:39
  187.7 36.2 %all-gather.25.cloned.1.call-done = bf16[8192,256]{1,0:T(8,128)(2,1)} async-done(((bf16[512,256]{1,0:T(8,128)(2,1)}), bf16[8192,256]{1,0:T(8,128)(2,1)}) %all-gather.25.cloned.1.call-update) | async-done | bytes 4194320 | tf_op jit(solution)/shard_map/all_gather | solution.py:39
  232.3 69.3 %all-gather.23.cloned.1.call-done = bf16[4096,512]{1,0:T(8,128)(2,1)} async-done(((bf16[256,512]{1,0:T(8,128)(2,1)}), bf16[4096,512]{1,0:T(8,128)(2,1)}) %all-gather.23.cloned.1.call-update) | async-done | bytes 4194320 | tf_op jit(solution)/shard_map/all_gather | solution.py:39
  320.9 37.2 %all-gather.29.cloned.1.call-done = bf16[2048,256]{1,0:T(8,128)(2,1)} async-done(((bf16[128,256]{1,0:T(8,128)(2,1)}), bf16[2048,256]{1,0:T(8,128)(2,1)}) %all-gather.29.cloned.1.call-update) | async-done | bytes 1048592 | tf_op jit(solution)/shard_map/all_gather | solution.py:39
  361.4 66.8 %all-gather.27.cloned.1.call-done = bf16[4096,3,128]{2,0,1:T(8,128)(2,1)} async-done(((bf16[256,3,128]{2,0,1:T(8,128)(2,1)}), bf16[4096,3,128]{2,0,1:T(8,128)(2,1)}) %all-gather.27.cloned.1.call-update) | async-done | bytes 3145744 | tf_op jit(solution)/shard_map/all_gather | solution.py:39
  472.5 32.7 %all-gather.31.cloned.1.call-done = bf16[8192,256]{1,0:T(8,128)(2,1)} async-done(((bf16[512,256]{1,0:T(8,128)(2,1)}), bf16[8192,256]{1,0:T(8,128)(2,1)}) %all-gather.31.cloned.1.call-update) | async-done | bytes 4194320 | tf_op jit(solution)/shard_map/all_gather | solution.py:39
  513.7 69.4 %all-gather.33.cloned.1.call-done = bf16[4096,512]{1,0:T(8,128)(2,1)} async-done(((bf16[256,512]{1,0:T(8,128)(2,1)}), bf16[4096,512]{1,0:T(8,128)(2,1)}) %all-gather.33.cloned.1.call-update) | async-done | bytes 4194320 | tf_op jit(solution)/shard_map/all_gather | solution.py:39
  618.9 8.4 fusion.159
  627.3 8.6 multiply_reduce_fusion.1
  696.4 8.6 multiply_reduce_fusion
  757.6 8.2 convolution_convert_fusion.2
  765.8 7.9 convert_element_type.410
  873.4 10.5 reduce.35
  896.1 106.4 %all-reduce = bf16[16,768]{1,0:T(8,128)(2,1)S(1)} all-reduce(bf16[16,768]{1,0:T(8,128)(2,1)S(1)} %reshape.729), channel_id=19, replica_groups=mesh['section'=2,'dp'=4,'tensor'=4] {'dp','tensor'}, use_global_device_ids=true, to_apply=%region_48.49.clone | all-reduce | flops 12288 | bytes 49152
  1008.8 8.0 copy.279
  1017.8 14.2 collective-permute-start.15
  1032.0 8.6 convert_reduce_fusion.3
  1043.2 64.1 %reduce-scatter.17.cloned.1.call-done = bf16[1,256,512]{2,1,0:T(8,128)(2,1)} async-done(((bf16[16,256,512]{2,1,0:T(8,128)(2,1)}), bf16[1,256,512]{2,1,0:T(8,128)(2,1)}) %reduce-scatter.17.cloned.1.call-update) | async-done | bytes 262160 | tf_op jit(solution)/shard_map/reduce_scatter | solution.py:46
  1110.1 94.2 %reduce-scatter.23.cloned.1.call-done = bf16[1,512,256]{2,1,0:T(8,128)(2,1)} async-done(((bf16[16,512,256]{2,1,0:T(8,128)(2,1)}), bf16[1,512,256]{2,1,0:T(8,128)(2,1)}) %reduce-scatter.23.cloned.1.call-update) | async-done | bytes 262160 | tf_op jit(solution)/shard_map/reduce_scatter | solution.py:46
  1204.3 96.8 %reduce-scatter.21.cloned.1.call-done = bf16[1,512,256]{2,1,0:T(8,128)(2,1)} async-done(((bf16[16,512,256]{2,1,0:T(8,128)(2,1)}), bf16[1,512,256]{2,1,0:T(8,128)(2,1)}) %reduce-scatter.21.cloned.1.call-update) | async-done | bytes 262160 | tf_op jit(solution)/shard_map/reduce_scatter | solution.py:46
  1303.1 130.4 %reduce-scatter.11.cloned.1.call-done = bf16[1,256,3,128]{3,1,2,0:T(8,128)(2,1)} async-done(((bf16[16,256,3,128]{3,1,2,0:T(8,128)(2,1)}), bf16[1,256,3,128]{3,1,2,0:T(8,128)(2,1)}) %reduce-scatter.11.cloned.1.call-update) | async-done | bytes 196624 | tf_op jit(solution)/shard_map/reduce_scatter | solution.py:46
  1433.4 134.7 %reduce-scatter.9.cloned.1.call-done = bf16[1,256,3,128]{3,1,2,0:T(8,128)(2,1)} async-done(((bf16[16,256,3,128]{3,1,2,0:T(8,128)(2,1)}), bf16[1,256,3,128]{3,1,2,0:T(8,128)(2,1)}) %reduce-scatter.9.cloned.1.call-update) | async-done | bytes 196624 | tf_op jit(solution)/shard_map/reduce_scatter | solution.py:46
  (539 shorter events, 440.8 us)
Async XLA Ops:
  7.2 91.3 %all-gather.21.cloned.1.call-start = ((), (), s32[]{:S(2)}) async-start(), calls=%async_computation.19 | async-start | bytes 1114112 | tf_op jit(solution)/shard_map/all_gather | solution.py:39
  11.1 135.2 %all-gather.19.cloned.1.call-start = ((), (), s32[]{:S(2)}) async-start(), calls=%async_computation.18 | async-start | bytes 3342336 | tf_op jit(solution)/shard_map/all_gather | solution.py:39
  15.6 208.3 %all-gather.25.cloned.1.call-start = ((), (), s32[]{:S(2)}) async-start(), calls=%async_computation.21 | async-start | bytes 4456448 | tf_op jit(solution)/shard_map/all_gather | solution.py:39
  18.1 283.5 %all-gather.23.cloned.1.call-start = ((), (), s32[]{:S(2)}) async-start(), calls=%async_computation.20 | async-start | bytes 4456448 | tf_op jit(solution)/shard_map/all_gather | solution.py:39
  20.7 337.4 %all-gather.29.cloned.1.call-start = ((), (), s32[]{:S(2)}) async-start(), calls=%async_computation.23 | async-start | bytes 1114112 | tf_op jit(solution)/shard_map/all_gather | solution.py:39
  21.3 406.9 %all-gather.27.cloned.1.call-start = ((), (), s32[]{:S(2)}) async-start(), calls=%async_computation.22 | async-start | bytes 3342336 | tf_op jit(solution)/shard_map/all_gather | solution.py:39
  23.2 37.3 %all-to-all-start = ((bf16[4,577,256]{2,1,0:T(8,128)(2,1)}), bf16[4,577,256]{2,1,0:T(8,128)(2,1)S(1)}, u32[]{:S(2)}, u32[]{:S(2)}) async-start(bf16[4,577,256]{2,1,0:T(8,128)(2,1)} %bitcast.316), calls=%async_computation | async-start | bytes 2392064 | tf_op jit(solution)/shard_map/all_to_all | solution.py:186
  29.0 476.2 %all-gather.31.cloned.1.call-start = ((), (), s32[]{:S(2)}) async-start(), calls=%async_computation.24 | async-start | bytes 4456448 | tf_op jit(solution)/shard_map/all_gather | solution.py:39
  29.7 553.4 %all-gather.33.cloned.1.call-start = ((), (), s32[]{:S(2)}) async-start(), calls=%async_computation.25 | async-start | bytes 4456448 | tf_op jit(solution)/shard_map/all_gather | solution.py:39
  61.8 40.0 %collective-permute-start = (bf16[577,1024]{1,0:T(8,128)(2,1)S(1)}, bf16[577,1024]{1,0:T(8,128)(2,1)}, u32[]{:S(2)}, u32[]{:S(2)}) collective-permute-start(bf16[577,1024]{1,0:T(8,128)(2,1)S(1)} %bitcast.362), channel_id=1, source_target_pairs={{0,16},{16,0},{1,17},{17,1},{2,18},{18,2},{3,19},{19,3},{4,20},{20... | collective-permute-start | bytes 3545096 | tf_op jit(solution)/shard_map/ppermute | solution.py:12
  182.6 834.2 %reduce-scatter.15.cloned.1.call-start = ((), (), s32[]{:S(2)}) async-start(), calls=%async_computation.13 | async-start | bytes 1114112 | tf_op jit(solution)/shard_map/reduce_scatter | solution.py:46
  317.7 122.6 %collective-permute-start.7 = (bf16[577,1024]{1,0:T(8,128)(2,1)}, bf16[577,1024]{1,0:T(8,128)(2,1)}, u32[]{:S(2)}, u32[]{:S(2)}) collective-permute-start(bf16[577,1024]{1,0:T(8,128)(2,1)} %convolution_convert_fusion.8), channel_id=1, source_target_pairs={{0,16},{16,0},{1,17},{17,1},{2,18},{18,2},{3,19},{19,3},{4,20},{20... | collective-permute-start | bytes 3545096 | tf_op jit(solution)/shard_map/ppermute | solution.py:12
  471.0 118.9 %collective-permute-start.8 = (bf16[577,1024]{1,0:T(8,128)(2,1)}, bf16[577,1024]{1,0:T(8,128)(2,1)}, u32[]{:S(2)}, u32[]{:S(2)}) collective-permute-start(bf16[577,1024]{1,0:T(8,128)(2,1)} %convolution_convert_fusion.7), channel_id=1, source_target_pairs={{0,16},{16,0},{1,17},{17,1},{2,18},{18,2},{3,19},{19,3},{4,20},{20... | collective-permute-start | bytes 3545096 | tf_op jit(solution)/shard_map/ppermute | solution.py:12
  737.1 279.8 %reduce-scatter.13.cloned.1.call-start = ((), (), s32[]{:S(2)}) async-start(), calls=%async_computation.12 | async-start | bytes 1114112 | tf_op jit(solution)/shard_map/reduce_scatter | solution.py:46
  757.6 285.6 %reduce-scatter.19.cloned.1.call-start = ((), (), s32[]{:S(2)}) async-start(), calls=%async_computation.15 | async-start | bytes 4456448 | tf_op jit(solution)/shard_map/reduce_scatter | solution.py:46
  778.9 328.4 %reduce-scatter.17.cloned.1.call-start = ((), (), s32[]{:S(2)}) async-start(), calls=%async_computation.14 | async-start | bytes 4456448 | tf_op jit(solution)/shard_map/reduce_scatter | solution.py:46
  799.9 404.4 %reduce-scatter.23.cloned.1.call-start = ((), (), s32[]{:S(2)}) async-start(), calls=%async_computation.17 | async-start | bytes 4456448 | tf_op jit(solution)/shard_map/reduce_scatter | solution.py:46
  820.7 480.4 %reduce-scatter.21.cloned.1.call-start = ((), (), s32[]{:S(2)}) async-start(), calls=%async_computation.16 | async-start | bytes 4456448 | tf_op jit(solution)/shard_map/reduce_scatter | solution.py:46
  841.4 592.0 %reduce-scatter.11.cloned.1.call-start = ((), (), s32[]{:S(2)}) async-start(), calls=%async_computation.11 | async-start | bytes 3342336 | tf_op jit(solution)/shard_map/reduce_scatter | solution.py:46
  853.5 714.6 %reduce-scatter.9.cloned.1.call-start = ((), (), s32[]{:S(2)}) async-start(), calls=%async_computation.10 | async-start | bytes 3342336 | tf_op jit(solution)/shard_map/reduce_scatter | solution.py:46
  889.5 114.9 %all-to-all-start.1 = ((bf16[4,2,73856]{2,1,0:T(2,128)(2,1)}), bf16[4,2,73856]{2,1,0:T(2,128)(2,1)}, u32[]{:S(2)}, u32[]{:S(2)}) async-start(bf16[4,2,73856]{2,1,0:T(2,128)(2,1)} %reshape.802), calls=%async_computation.1 | async-start | bytes 2363392 | tf_op jit(solution)/shard_map/all_to_all | solution.py:232
  1017.8 25.3 %collective-permute-start.15 = (f32[128,256]{1,0:T(8,128)S(1)}, f32[128,256]{1,0:T(8,128)S(1)}, u32[]{:S(2)}, u32[]{:S(2)}) collective-permute-start(f32[128,256]{1,0:T(8,128)S(1)} %fusion.128), channel_id=1, source_target_pairs={{0,16},{16,0},{1,17},{17,1},{2,18},{18,2},{3,19},{19,3},{4,20},{20... | collective-permute-start | bytes 393224 | tf_op jit(solution)/shard_map/ppermute | solution.py:12
  1108.4 463.1 %collective-permute-start.16 = (f32[256,512]{1,0:T(8,128)S(1)}, f32[256,512]{1,0:T(8,128)S(1)}, u32[]{:S(2)}, u32[]{:S(2)}) collective-permute-start(f32[256,512]{1,0:T(8,128)S(1)} %fusion.112), channel_id=1, source_target_pairs={{0,16},{16,0},{1,17},{17,1},{2,18},{18,2},{3,19},{19,3},{4,20},{20... | collective-permute-start | bytes 1572872 | tf_op jit(solution)/shard_map/ppermute | solution.py:12
  1302.2 270.6 %collective-permute-start.17 = (f32[512,256]{1,0:T(8,128)S(1)}, f32[512,256]{1,0:T(8,128)S(1)}, u32[]{:S(2)}, u32[]{:S(2)}) collective-permute-start(f32[512,256]{1,0:T(8,128)S(1)} %fusion.114), channel_id=1, source_target_pairs={{0,16},{16,0},{1,17},{17,1},{2,18},{18,2},{3,19},{19,3},{4,20},{20... | collective-permute-start | bytes 1572872 | tf_op jit(solution)/shard_map/ppermute | solution.py:12
  (117 other events, 2624.8 us)
Sparse Core Ops, SparseCore 0:
  11.4 64.8 all-gather.20
  79.0 67.1 all-gather.18
  149.6 74.2 all-gather.24
  227.1 74.4 all-gather.22
  304.2 53.8 all-gather.28
  360.8 67.3 all-gather.26
  430.9 74.2 all-gather.30
  508.5 74.4 all-gather.32
  737.2 66.4 reduce-scatter.14
  806.5 75.5 reduce-scatter.12
  884.4 124.5 reduce-scatter.18
  1011.1 96.1 reduce-scatter.16
  1109.6 94.6 reduce-scatter.22
  1206.4 94.6 reduce-scatter.20
  1305.9 127.4 reduce-scatter.10
  1438.3 129.7 reduce-scatter.8

commit v2 on v1

v2 whole, which is shorter than its diff:
```python
import jax
import jax.numpy as jnp
from jax import lax
from jax.sharding import PartitionSpec as P

HD = 64
EPS = 1e-06


def swap(value):
    return lax.ppermute(value, "section", [(0, 1), (1, 0)])


def pair_sum(partial):
    low = partial.astype(jnp.bfloat16)
    return low.astype(jnp.float32) + swap(low).astype(jnp.float32)


def swap_x(value):
    n = lax.axis_size("dp")
    return lax.ppermute(value, "dp", [(i, i ^ 1) for i in range(n)])


def swap_y(value):
    n = lax.axis_size("dp")
    return lax.ppermute(value, "dp", [(i, i ^ 2) for i in range(n)])


def gather_chunk(first, second):
    n_dp = lax.axis_size("dp")
    cut = first.shape[0]
    column = lax.all_gather(jnp.concatenate([first, second], 0), "tensor", axis=1, tiled=True)
    first, second = column[:cut], column[cut:]
    if n_dp != 4:
        return (
            far_gather(first, True),
            far_gather(second, False),
        )
    first = jnp.concatenate([first, swap_y(first)], 0)
    second = jnp.concatenate([second, swap_x(second)], 0)
    first = jnp.concatenate([first, swap_x(first)], 0)
    second = jnp.concatenate([second, swap_y(second)], 0)
    return (first, second)


def far_gather(block, is_first):
    return lax.all_gather(block, "dp", axis=0, tiled=True)


def add_low(left, right):
    return (left.astype(jnp.float32) + right.astype(jnp.float32)).astype(jnp.bfloat16)


def scatter_chunk(first, second):
    n_dp = lax.axis_size("dp")
    if n_dp != 4:
        first = lax.psum_scatter(first, "dp", scatter_dimension=0, tiled=True)
        second = lax.psum_scatter(second, "dp", scatter_dimension=0, tiled=True)
    else:
        for flip in range(2):
            half, rest = first.shape[0] // 2, second.shape[0] // 2
            got_first = (swap_y if flip else swap_x)(first[half:])
            got_second = (swap_x if flip else swap_y)(second[rest:])
            first = add_low(first[:half], got_first)
            second = add_low(second[:rest], got_second)
    column = jnp.concatenate([first, second], 0)
    return lax.psum_scatter(column, "tensor", scatter_dimension=1, tiled=True)


def flip_axis(value, axis, bit):
    return jnp.where(bit == 1, jnp.flip(value, axis), value)


def relative(value, spot):
    n_dp = lax.axis_size("dp")
    lead = value.shape[:-1]
    k = len(lead)
    if n_dp != 4:
        cut = value.reshape(lead + (n_dp, 2, -1))
        return jnp.swapaxes(cut, k, k + 1).reshape(value.shape)
    cut = value.reshape(lead + (2, 2, 2, -1))
    cut = flip_axis(flip_axis(cut, k, spot // 2), k + 1, spot % 2)
    first = jnp.swapaxes(cut[..., 0, :], k, k + 1)
    second = cut[..., 1, :]
    return jnp.concatenate([first.reshape(lead + (-1,)), second.reshape(lead + (-1,))], -1)


def absolute(value, spot):
    n_dp = lax.axis_size("dp")
    lead = value.shape[:-1]
    k = len(lead)
    if n_dp != 4:
        cut = value.reshape(lead + (2, n_dp, -1))
        return jnp.swapaxes(cut, k, k + 1).reshape(value.shape)
    cut = value.reshape(lead + (2, 2, 2, -1))
    first = jnp.swapaxes(cut[..., 0, :, :, :], k, k + 1)
    second = cut[..., 1, :, :, :]
    cut = jnp.stack([first, second], k + 2)
    cut = flip_axis(flip_axis(cut, k, spot // 2), k + 1, spot % 2)
    return cut.reshape(value.shape)


def by_chip(blocks, spot):
    n_dp = lax.axis_size("dp")
    if n_dp != 4:
        return blocks
    cut = blocks.reshape((2, 2) + blocks.shape[1:])
    cut = jnp.swapaxes(cut, 0, 1)
    cut = flip_axis(flip_axis(cut, 0, spot // 2), 1, spot % 2)
    return cut.reshape(blocks.shape)


def by_arrival(blocks, spot):
    n_dp = lax.axis_size("dp")
    if n_dp != 4:
        return blocks
    cut = blocks.reshape((2, 2) + blocks.shape[1:])
    cut = flip_axis(flip_axis(cut, 0, spot // 2), 1, spot % 2)
    return jnp.swapaxes(cut, 0, 1).reshape(blocks.shape)


def mm(form, left, right):
    return jnp.einsum(form, left, right, preferred_element_type=jnp.float32)


def layer_norm(value, gain, shift):
    center = jnp.mean(value, -1, keepdims=True)
    spread = jnp.mean(value * value, -1, keepdims=True) - center * center
    factor = lax.rsqrt(spread + EPS)
    centred = (value - center) * factor
    return ((centred * gain + shift).astype(jnp.bfloat16), centred, factor)


def norm_backward(grad_normed, centred, factor, gain):
    scaled = grad_normed * gain
    return factor * (
        scaled
        - jnp.mean(scaled, -1, keepdims=True)
        - centred * jnp.mean(scaled * centred, -1, keepdims=True)
    )


def gelu_parts(value):
    cdf = 0.5 * (1.0 + lax.erf(value * 0.7071067811865476))
    density = jnp.exp(-0.5 * value * value) * 0.3989422804014327
    return (cdf, density)


def forward_layer(weights, value):
    w_qkv, w_out, w_up, w_down, rows, q_bias, v_bias, up_bias = weights
    tokens = value.shape[0]
    heads = w_out.shape[1] // HD
    split = (tokens, heads, HD)
    normed, centred, factor = layer_norm(value, rows[0], rows[1])
    projected = mm("td,dgce->tgce", normed, w_qkv)
    queries = (projected[:, :, 0].reshape(tokens, -1) + q_bias).astype(jnp.bfloat16)
    keyset = projected[:, :, 1].reshape(tokens, -1).astype(jnp.bfloat16)
    valueset = (projected[:, :, 2].reshape(tokens, -1) + v_bias).astype(jnp.bfloat16)
    scores = mm("qhd,khd->hqk", queries.reshape(split), keyset.reshape(split)) * HD ** (-0.5)
    highest = jnp.max(scores, -1, keepdims=True)
    exponent = jnp.exp(scores - highest)
    denominator = jnp.sum(exponent, -1, keepdims=True)
    soft = (exponent / denominator).astype(jnp.bfloat16)
    log_total = highest + jnp.log(denominator)
    mixed = mm("hqk,khd->qhd", soft, valueset.reshape(split)).astype(jnp.bfloat16)
    mixed = mixed.reshape(tokens, heads * HD)
    middle = value + pair_sum(mm("te,de->td", mixed, w_out)) + rows[4]
    normed_two, centred_two, factor_two = layer_norm(middle, rows[5], rows[6])
    before = mm("td,df->tf", normed_two, w_up) + up_bias
    hidden = (before * gelu_parts(before)[0]).astype(jnp.bfloat16)
    output = middle + pair_sum(mm("tf,df->td", hidden, w_down)) + rows[7]
    kept = (normed, centred, factor, queries, keyset, valueset, log_total, mixed)
    return (output, kept + (normed_two, centred_two, factor_two, before, hidden))


def backward_layer(weights, kept, grad_out):
    w_qkv, w_out, w_up, w_down, rows, q_bias, v_bias, up_bias = weights
    normed, centred, factor, queries, keyset, valueset, log_total, mixed = kept[:8]
    normed_two, centred_two, factor_two, before, hidden = kept[8:]
    tokens = grad_out.shape[0]
    heads = w_out.shape[1] // HD
    split = (tokens, heads, HD)
    scale = HD ** (-0.5)
    grad_branch = grad_out.astype(jnp.bfloat16)
    grad_down = mm("td,tf->df", grad_branch, hidden).astype(jnp.bfloat16)
    grad_down, grad_branch = lax.optimization_barrier((grad_down, grad_branch))
    cdf, density = gelu_parts(before)
    grad_before = mm("td,df->tf", grad_branch, w_down) * (cdf + before * density)
    grad_up_bias = jnp.sum(grad_before, 0)
    before_low = grad_before.astype(jnp.bfloat16)
    grad_up = mm("td,tf->df", normed_two, before_low).astype(jnp.bfloat16)
    grad_up, before_low = lax.optimization_barrier((grad_up, before_low))
    grad_normed_two = pair_sum(mm("tf,df->td", before_low, w_up))
    grad_middle = grad_out + norm_backward(grad_normed_two, centred_two, factor_two, rows[5])
    grad_attended = grad_middle.astype(jnp.bfloat16)
    grad_outproj = mm("td,te->de", grad_attended, mixed).astype(jnp.bfloat16)
    grad_mixed = mm("td,de->te", grad_attended, w_out).astype(jnp.bfloat16).reshape(split)
    query_heads, key_heads = queries.reshape(split), keyset.reshape(split)
    soft = jnp.exp(mm("qhd,khd->hqk", query_heads, key_heads) * scale - log_total)
    soft_low = soft.astype(jnp.bfloat16)
    grad_values = mm("hqk,qhd->khd", soft_low, grad_mixed)
    grad_soft = mm("qhd,khd->hqk", grad_mixed, valueset.reshape(split))
    row_inner = jnp.sum(grad_soft * soft, -1, keepdims=True)
    grad_scores = (soft * (grad_soft - row_inner)).astype(jnp.bfloat16)
    grad_queries = mm("hqk,khd->qhd", grad_scores, key_heads) * scale
    grad_keys = mm("hqk,qhd->khd", grad_scores, query_heads) * scale
    groups = w_qkv.shape[1]
    grad_query_bias = jnp.sum(grad_queries, 0).reshape(-1)
    grad_value_bias = jnp.sum(grad_values, 0).reshape(-1)
    parts = [grad_queries, grad_keys, grad_values]
    parts = [part.astype(jnp.bfloat16).reshape(tokens, groups, -1) for part in parts]
    stack_low = jnp.stack(parts, 2)
    grad_qkv = mm("td,tgce->dgce", normed, stack_low).astype(jnp.bfloat16)
    grad_qkv, stack_low = lax.optimization_barrier((grad_qkv, stack_low))
    grad_normed = pair_sum(mm("tgce,dgce->td", stack_low, w_qkv))
    grad_value = grad_middle + norm_backward(grad_normed, centred, factor, rows[0])
    full_rows = jnp.stack(
        [
            jnp.sum(grad_normed * centred, 0),
            jnp.sum(grad_normed, 0),
            jnp.sum(grad_middle, 0),
            jnp.sum(grad_normed_two * centred_two, 0),
            jnp.sum(grad_normed_two, 0),
            jnp.sum(grad_out, 0),
        ]
    )
    small = (full_rows, grad_query_bias, grad_value_bias, grad_up_bias)
    return (grad_value, (grad_qkv, grad_outproj, grad_up, grad_down), small)


def half_cols(core, whole, n_tensor):
    cut = whole.reshape(whole.shape[:-1] + (n_tensor, 2, -1))
    cut = jnp.where(core == 0, cut[..., 0, :], cut[..., 1, :])
    return cut.reshape(whole.shape[:-1] + (-1,))


def spread_cols(core, half, n_tensor):
    cut = half.reshape(half.shape[:-1] + (n_tensor, 1, -1))
    none = jnp.zeros_like(cut)
    both = jnp.concatenate(
        [jnp.where(core == 0, cut, none), jnp.where(core == 0, none, cut)], -2
    )
    return both.reshape(half.shape[:-1] + (-1,))


def body(boundary_in, counts, qkv_weight, proj_weight, fc1_weight, fc2_weight, vectors, fc1_bias):
    core = lax.axis_index("section")
    is_first = core == 0
    place = lax.axis_index("tensor")
    spot = lax.axis_index("dp")
    n_dp, n_tensor = lax.axis_size("dp"), lax.axis_size("tensor")
    slots_per_batch = boundary_in.shape[1] // counts.shape[1]
    live = (place % slots_per_batch < counts[0, place // slots_per_batch]).astype(jnp.float32)
    depth = qkv_weight.shape[1]
    mid = depth // 2
    n_vec = vectors.size

    packs = []
    for part in range(2):
        cuts = [
            jnp.split(qkv_weight[0], 2, 2)[part].reshape(depth, -1),
            jnp.split(proj_weight[0], 2, 0)[part].T,
            jnp.split(fc1_weight[0], 2, 1)[part],
            jnp.split(fc2_weight[0], 2, 0)[part].T,
        ]
        packs.append(jnp.concatenate(cuts, 1))
    kept = jnp.where(is_first, packs[0], packs[1])
    received = swap(jnp.where(is_first, packs[1], packs[0]))
    shards = (jnp.where(is_first, kept, received), jnp.where(is_first, received, kept))
    small_shard = jnp.concatenate([vectors.reshape(-1), fc1_bias.reshape(-1)])
    small_other = swap(small_shard)
    small = jnp.concatenate(
        [
            jnp.where(is_first, small_shard, small_other),
            jnp.where(is_first, small_other, small_shard),
        ]
    )
    wide = shards[0].shape[1] // 3
    extra = 16
    small = jnp.concatenate([small, jnp.zeros((extra * wide - small.size,), small.dtype)])
    small = small.reshape(extra, wide)

    mine = lax.all_to_all(
        boundary_in[0].astype(jnp.bfloat16), "tensor", split_axis=0, concat_axis=2, tiled=True
    )[0]
    theirs = swap(mine)
    value = relative(jnp.where(is_first, mine, theirs), spot).astype(jnp.float32)
    cotangent = relative(jnp.where(is_first, theirs, mine), spot).astype(jnp.float32) * live

    chunks = []
    for layer in range(2):
        for number in range(3):
            cols = shards[layer][:, number * wide : (number + 1) * wide]
            first, second = cols[:mid], cols[mid:]
            if layer == 0 and number == 0:
                first = jnp.concatenate([first, small], 0)
            chunks.append(gather_chunk(first, second))
    first, second = chunks[0]
    first = first.reshape(n_dp, mid + extra, -1)
    small = by_chip(first[:, mid:], spot).astype(jnp.float32)
    chunks[0] = (first[:, :mid].reshape(n_dp * mid, -1), second)
    small = small.reshape(n_dp, extra, n_tensor, wide).transpose(0, 2, 1, 3)
    small = small.reshape(n_dp, n_tensor, -1)

    layers = []
    for layer in range(2):
        joined = [jnp.concatenate(chunk, 0) for chunk in chunks[3 * layer : 3 * layer + 3]]
        quad = joined[0].reshape(joined[0].shape[0], n_tensor, 4, -1)
        w_qkv = quad[:, :, :3]
        w_out = quad[:, :, 3].reshape(quad.shape[0], -1)
        one = small[:, :, layer * small_shard.size : (layer + 1) * small_shard.size]
        rows = one[:, :, :n_vec].reshape(n_dp, n_tensor, 8, -1)
        rows = rows.transpose(2, 1, 0, 3).reshape(8, -1)
        bias = one[:, :, n_vec:].transpose(1, 0, 2).reshape(-1)
        q_bias = half_cols(core, rows[2], n_tensor)
        v_bias = half_cols(core, rows[3], n_tensor)
        up_bias = half_cols(core, bias, n_tensor)
        rows = relative(rows, spot)
        layers.append((w_qkv, w_out, joined[1], joined[2], rows, q_bias, v_bias, up_bias))

    output, kept_first = forward_layer(layers[0], value)
    sent = output.astype(jnp.bfloat16).astype(jnp.float32)
    output, kept_second = forward_layer(layers[1], sent)
    output = output * live

    settled = [None, None]
    smalls = [None, None]
    grad = cotangent
    for layer in (1, 0):
        keeps = (kept_first, kept_second)[layer]
        grad, big, smalls[layer] = backward_layer(layers[layer], keeps, grad)
        if layer == 1:
            grad = grad.astype(jnp.bfloat16).astype(jnp.float32)
        g_qkv, g_out, g_up, g_down = big
        quad = jnp.concatenate([g_qkv, g_out.reshape(g_qkv.shape[:2] + (1, -1))], 2)
        quad = quad.reshape(quad.shape[0], -1)
        half = quad.shape[0] // 2
        done = [scatter_chunk(g[:half], g[half:]) for g in (g_down, g_up)]
        if layer == 1:
            done.append(scatter_chunk(quad[:half], quad[half:]))
        settled[layer] = done

    ends = absolute(jnp.where(is_first, grad, output).astype(jnp.bfloat16), spot)
    ends = lax.all_to_all(ends[None], "tensor", split_axis=2, concat_axis=0, tiled=True)
    boundary_out = ends.astype(jnp.float32)[None]

    packed = []
    for layer in range(2):
        full_rows, q_row, v_row, up_row = smalls[layer]
        full_rows = absolute(jnp.where(core == layer, full_rows, 0.0), spot)
        q_row = spread_cols(core, q_row, n_tensor)
        v_row = spread_cols(core, v_row, n_tensor)
        up_row = spread_cols(core, up_row, n_tensor)
        rows = jnp.stack(
            [full_rows[0], full_rows[1], q_row, v_row, full_rows[2], full_rows[3], full_rows[4], full_rows[5]]
        )
        rows = rows.reshape(8, n_tensor, n_dp, -1).transpose(2, 1, 0, 3).reshape(n_dp, n_tensor, -1)
        up_row = up_row.reshape(n_tensor, n_dp, -1).transpose(1, 0, 2)
        packed.append(jnp.concatenate([rows, up_row], -1))
    ours = jnp.where(is_first, packed[0], packed[1])
    other = swap(jnp.where(is_first, packed[1], packed[0]))
    little = (ours + other).astype(jnp.bfloat16)
    pad = jnp.zeros((n_dp, n_tensor, extra * wide - little.shape[-1]), little.dtype)
    little = jnp.concatenate([little, pad], -1).reshape(n_dp, n_tensor, extra, wide)
    little = by_arrival(little.transpose(0, 2, 1, 3).reshape(n_dp, extra, -1), spot)
    first = jnp.concatenate([quad[:half].reshape(n_dp, mid, -1), little], 1)
    last = scatter_chunk(first.reshape(n_dp * (mid + extra), -1), quad[half:])
    little = last[mid : mid + extra].reshape(-1).astype(jnp.float32)
    settled[0].append(jnp.concatenate([last[:mid], last[mid + extra :]], 0))
    grad_vectors = little[:n_vec].reshape(vectors.shape)
    grad_bias = little[n_vec : n_vec + fc1_bias.size].reshape(fc1_bias.shape)

    lows, highs = [], []
    for number in range(3):
        kept = jnp.where(is_first, settled[0][number], settled[1][number])
        received = swap(jnp.where(is_first, settled[1][number], settled[0][number]))
        lows.append(jnp.where(is_first, kept, received).astype(jnp.float32))
        highs.append(jnp.where(is_first, received, kept).astype(jnp.float32))
    grad_down = jnp.concatenate([lows[0].T, highs[0].T], 0)[None]
    grad_up = jnp.concatenate([lows[1], highs[1]], 1)[None]
    low, high = [part[2].reshape(depth, 4, -1) for part in (lows, highs)]
    grad_qkv = jnp.concatenate([low[:, :3], high[:, :3]], 2)[None]
    grad_out = jnp.concatenate([low[:, 3].T, high[:, 3].T], 0)[None]
    return (boundary_out, grad_qkv, grad_out, grad_up, grad_down, grad_vectors, grad_bias)


def solution(mesh):
    in_specs = (
        P("section", "dp", None, "tensor"),
        P("dp", None),
        P("section", "dp", None, "tensor"),
        P("section", "tensor", "dp"),
        P("section", "dp", "tensor"),
        P("section", "tensor", "dp"),
        P("section", None, "tensor", "dp"),
        P("section", "tensor", "dp"),
    )
    out_specs = (
        P("section", "dp", None, "tensor"),
        P("section", "dp", None, "tensor"),
        P("section", "tensor", "dp"),
        P("section", "dp", "tensor"),
        P("section", "tensor", "dp"),
        P("section", None, "tensor", "dp"),
        P("section", "tensor", "dp"),
    )
    return jax.shard_map(body, mesh=mesh, in_specs=in_specs, out_specs=out_specs, check_vma=False)
```

time: 1590 us -> 1020 us (0.64)
  waiting for transfers between devices: 919 us -> 391 us
  blocking collectives: 138 us -> 0 us
  other arithmetic: 91.5 us -> 160 us
  starting transfers between devices: 39.2 us -> 67.1 us
  local copies, waits for them, and re-layouts: 222 us -> 244 us
  matrix products: 155 us -> 134 us
    reduce_scatter x8 -> x6, waiting for transfers between devices: 520 us -> 0.07 us  [scatter_chunk(): return lax.psum_scatter(column, 'tensor', scatter_dimension=1, tiled=True)]
    all_gather x8 -> x6, waiting for transfers between devices: 352 us -> 123 us  [gather_chunk(): lax.all_gather(jnp.concatenate([first, second], 0), 'tensor', axis=1, til...]
    ppermute x0 -> x48, waiting for transfers between devices: none -> 187 us  [the longest x24 127 us: swap_x(): return lax.ppermute(value, 'dp', [(i, i ^ 1) for i in range(n)])]
    unnamed x1 -> x0, blocking collectives: 106 us -> none
    slice x21 -> x63, local copies, waits for them, and re-layouts: 18 us -> 74.7 us  [the longest x12 18.3 us: scatter_chunk(): got_first = (swap_y if flip else swap_x)(first[half:])]
    concatenate x0 -> x28, other arithmetic: none -> 41.8 us  [the longest x6 10.1 us: gather_chunk(): first = jnp.concatenate([first, swap_y(first)], 0)]
    convert_element_type x14 -> x8, local copies, waits for them, and re-layouts: 61.1 us -> 20.1 us  [the longest x6 19.6 us: add_low(): left.astype(jnp.float32) + right.astype(jnp.float32)]
    ppermute x0 -> x48, starting transfers between devices: none -> 35.4 us  [the longest x24 18.1 us: swap_x(): return lax.ppermute(value, 'dp', [(i, i ^ 1) for i in range(n)])]
  transfers between devices with their start and end apart: 37 -> 77, of which waited for: 23 -> 26; matrix products, arithmetic and copies ran while one was open for 21% -> 48% of each run, Pallas kernels for 0% -> 0%
where the time goes in v2:
time: 1020 us; the launch traced here: 1010 us
  waiting for transfers between devices  391 us (38%)
  local copies, waits for them, and re-layouts  244 us (24%)
  other arithmetic  160 us (16%)
  matrix products  134 us (13%)
  starting transfers between devices  67.1 us (7%)
  between operations  18.2 us (2%)
    dot_general x36, matrix products, mm(): return jnp.einsum(form, left, right, preferred_element_type=jnp.float32)  134 us
    ppermute x24, waiting for transfers between devices, swap_x(): return lax.ppermute(value, 'dp', [(i, i ^ 1) for i in range(n)])  127 us
    all_gather x6, waiting for transfers between devices, gather_chunk(): lax.all_gather(jnp.concatenate([first, second], 0), 'tensor', axis=1, til...  123 us
    ppermute x24, waiting for transfers between devices, swap_y(): return lax.ppermute(value, 'dp', [(i, i ^ 2) for i in range(n)])  59.3 us
    unnamed x369, local copies, waits for them, and re-layouts  54.5 us
    all_to_all x1, waiting for transfers between devices, body(): lax.all_to_all(boundary_in[0].astype(jnp.bfloat16), 'tensor', split_axis=...  41.3 us
    all_to_all x1, waiting for transfers between devices, body(): lax.all_to_all(ends[None], 'tensor', split_axis=2, concat_axis=0, tiled=T...  33.6 us
    convert_element_type x20, other arithmetic, add_low(): (left.astype(jnp.float32) + right.astype(jnp.float32)).astype(jnp.bfloat16)  26 us
  transfers between devices with their start and end apart: 77, of which 26 were waited for; matrix products, arithmetic and copies ran while one was open for 48% of the time, Pallas kernels for 0%

profile of v2, /device:TPU:1, one launch (start us, length us, event | category | flops | bytes accessed | tf_op | source)
XLA Modules:
  0.0 1014.2 jit_solution(9189416549444629646)
XLA Ops:
  28.9 41.3 %all-to-all-done = bf16[4,577,256]{2,1,0:T(8,128)(2,1)S(1)} async-done(((bf16[4,577,256]{2,1,0:T(8,128)(2,1)}), bf16[4,577,256]{2,1,0:T(8,128)(2,1)S(1)}, u32[]{:S(2)}, u32[]{:S(2)}) %all-to-all-start) | async-done | bytes 1181728 | tf_op jit(solution)/shard_map/all_to_all | solution.py:283
  77.0 17.5 %all-gather.11.cloned.1.call-done = bf16[256,2048]{1,0:T(8,128)(2,1)} async-done(((bf16[256,512]{1,0:T(8,128)(2,1)}), bf16[256,2048]{1,0:T(8,128)(2,1)}) %all-gather.11.cloned.1.call-update) | async-done | bytes 1048592 | tf_op jit(solution)/shard_map/all_gather | solution.py:32
  99.3 24.2 %all-gather.13.cloned.1.call-done = bf16[256,2048]{1,0:T(8,128)(2,1)} async-done(((bf16[256,512]{1,0:T(8,128)(2,1)}), bf16[256,2048]{1,0:T(8,128)(2,1)}) %all-gather.13.cloned.1.call-update) | async-done | bytes 1048592 | tf_op jit(solution)/shard_map/all_gather | solution.py:32
  126.0 26.4 %all-gather.15.cloned.1.call-done = bf16[256,2048]{1,0:T(8,128)(2,1)} async-done(((bf16[256,512]{1,0:T(8,128)(2,1)}), bf16[256,2048]{1,0:T(8,128)(2,1)}) %all-gather.15.cloned.1.call-update) | async-done | bytes 1048592 | tf_op jit(solution)/shard_map/all_gather | solution.py:32
  154.7 27.1 %all-gather.17.cloned.1.call-done = bf16[256,2048]{1,0:T(8,128)(2,1)} async-done(((bf16[256,512]{1,0:T(8,128)(2,1)}), bf16[256,2048]{1,0:T(8,128)(2,1)}) %all-gather.17.cloned.1.call-update) | async-done | bytes 1048592 | tf_op jit(solution)/shard_map/all_gather | solution.py:32
  184.2 28.1 %all-gather.7.cloned.1.call-done = bf16[272,2048]{1,0:T(8,128)(2,1)} async-done(((bf16[272,512]{1,0:T(8,128)(2,1)}), bf16[272,2048]{1,0:T(8,128)(2,1)}) %all-gather.7.cloned.1.call-update) | async-done | bytes 1114128 | tf_op jit(solution)/shard_map/all_gather | solution.py:32
  235.2 9.0 collective-permute-done.22
  245.6 9.9 collective-permute-done.26
  314.8 21.1 %collective-permute-done.18 = bf16[256,2048]{1,0:T(8,128)(2,1)S(1)} collective-permute-done((bf16[256,2048]{1,0:T(8,128)(2,1)}, bf16[256,2048]{1,0:T(8,128)(2,1)S(1)}, u32[]{:S(2)}, u32[]{:S(2)}) %collective-permute-start.18) | collective-permute-done | bytes 1048608 | tf_op jit(solution)/shard_map/ppermute | solution.py:21
  341.3 17.0 %collective-permute-done.23 = bf16[256,2048]{1,0:T(8,128)(2,1)S(1)} collective-permute-done((bf16[256,2048]{1,0:T(8,128)(2,1)S(1)}, bf16[256,2048]{1,0:T(8,128)(2,1)S(1)}, u32[]{:S(2)}, u32[]{:S(2)}) %collective-permute-start.23) | collective-permute-done | bytes 1048608 | tf_op jit(solution)/shard_map/ppermute | solution.py:21
  365.9 17.7 %collective-permute-done.4 = bf16[288,2048]{1,0:T(8,128)(2,1)} collective-permute-done((bf16[288,2048]{1,0:T(8,128)(2,1)}, bf16[288,2048]{1,0:T(8,128)(2,1)}, u32[]{:S(2)}, u32[]{:S(2)}) %collective-permute-start.4) | collective-permute-done | bytes 1179680 | tf_op jit(solution)/shard_map/ppermute | solution.py:21
  531.0 7.6 fusion.156
  538.6 8.7 multiply_reduce_fusion.1
  588.4 21.8 %collective-permute-done.61 = bf16[128,2048]{1,0:T(8,128)(2,1)S(1)} collective-permute-done((bf16[128,2048]{1,0:T(8,128)(2,1)S(1)}, bf16[128,2048]{1,0:T(8,128)(2,1)S(1)}, u32[]{:S(2)}, u32[]{:S(2)}) %collective-permute-start.61) | collective-permute-done | bytes 524320 | tf_op jit(solution)/shard_map/ppermute | solution.py:21
  613.1 19.6 %collective-permute-done.54 = bf16[256,2048]{1,0:T(8,128)(2,1)} collective-permute-done((bf16[256,2048]{1,0:T(8,128)(2,1)}, bf16[256,2048]{1,0:T(8,128)(2,1)}, u32[]{:S(2)}, u32[]{:S(2)}) %collective-permute-start.54) | collective-permute-done | bytes 1048608 | tf_op jit(solution)/shard_map/ppermute | solution.py:21
  638.8 17.6 %collective-permute-done.51 = bf16[256,2048]{1,0:T(8,128)(2,1)} collective-permute-done((bf16[256,2048]{1,0:T(8,128)(2,1)}, bf16[256,2048]{1,0:T(8,128)(2,1)}, u32[]{:S(2)}, u32[]{:S(2)}) %collective-permute-start.51) | collective-permute-done | bytes 1048608 | tf_op jit(solution)/shard_map/ppermute | solution.py:26
  766.1 8.7 multiply_reduce_fusion
  846.8 11.0 %collective-permute-done.38 = bf16[256,2048]{1,0:T(8,128)(2,1)} collective-permute-done((bf16[256,2048]{1,0:T(8,128)(2,1)}, bf16[256,2048]{1,0:T(8,128)(2,1)}, u32[]{:S(2)}, u32[]{:S(2)}) %collective-permute-start.38) | collective-permute-done | bytes 1048608 | tf_op jit(solution)/shard_map/ppermute | solution.py:26
  859.8 12.2 %collective-permute-done.36 = bf16[288,2048]{1,0:T(8,128)(2,1)} collective-permute-done((bf16[288,2048]{1,0:T(8,128)(2,1)}, bf16[288,2048]{1,0:T(8,128)(2,1)}, u32[]{:S(2)}, u32[]{:S(2)}) %collective-permute-start.36) | collective-permute-done | bytes 1179680 | tf_op jit(solution)/shard_map/ppermute | solution.py:21
  875.2 8.0 collective-permute-done.39
  907.8 10.5 %reduce.31 = bf16[1024,577]{1,0:T(8,128)(2,1)} reduce(bf16[1024,1,577]{2,1,0:T(2,128)(2,1)S(1)} %bitcast.296, bf16[]{:T(256)} %broadcast.586), dimensions={1}, to_apply=%bitcast.235.reduce_sub_computation | reduce | bytes 2363394
  938.9 33.6 %all-to-all-done.1 = bf16[4,2,73856]{2,1,0:T(2,128)(2,1)} async-done(((bf16[4,2,73856]{2,1,0:T(2,128)(2,1)}), bf16[4,2,73856]{2,1,0:T(2,128)(2,1)}, u32[]{:S(2)}, u32[]{:S(2)}) %all-to-all-start.1) | async-done | bytes 1181728 | tf_op jit(solution)/shard_map/all_to_all | solution.py:344
  977.0 8.0 copy.410
  985.0 8.6 convert_reduce_fusion.3
  (890 shorter events, 581.0 us)
Async XLA Ops:
  7.2 64.9 %all-gather.9.cloned.1.call-start = ((), (), s32[]{:S(2)}) async-start(), calls=%async_computation.9 | async-start | bytes 1310720 | tf_op jit(solution)/shard_map/all_gather | solution.py:32
  14.2 80.3 %all-gather.11.cloned.1.call-start = ((), (), s32[]{:S(2)}) async-start(), calls=%async_computation.10 | async-start | bytes 1310720 | tf_op jit(solution)/shard_map/all_gather | solution.py:32
  14.9 108.5 %all-gather.13.cloned.1.call-start = ((), (), s32[]{:S(2)}) async-start(), calls=%async_computation.11 | async-start | bytes 1310720 | tf_op jit(solution)/shard_map/all_gather | solution.py:32
  15.9 136.5 %all-gather.15.cloned.1.call-start = ((), (), s32[]{:S(2)}) async-start(), calls=%async_computation.12 | async-start | bytes 1310720 | tf_op jit(solution)/shard_map/all_gather | solution.py:32
  25.3 156.5 %all-gather.17.cloned.1.call-start = ((), (), s32[]{:S(2)}) async-start(), calls=%async_computation.13 | async-start | bytes 1310720 | tf_op jit(solution)/shard_map/all_gather | solution.py:32
  25.9 186.4 %all-gather.7.cloned.1.call-start = ((), (), s32[]{:S(2)}) async-start(), calls=%async_computation.8 | async-start | bytes 1392640 | tf_op jit(solution)/shard_map/all_gather | solution.py:32
  28.9 902.0 %reduce-scatter.17.cloned.1.call-start = ((), (), s32[]{:S(2)}) async-start(), calls=%async_computation.19 | async-start | bytes 1310720 | tf_op jit(solution)/shard_map/reduce_scatter | solution.py:67
  71.4 194.0 %collective-permute-start = (bf16[577,1024]{1,0:T(8,128)(2,1)S(1)}, bf16[577,1024]{1,0:T(8,128)(2,1)}, u32[]{:S(2)}, u32[]{:S(2)}) collective-permute-start(bf16[577,1024]{1,0:T(8,128)(2,1)S(1)} %bitcast.316), channel_id=1, source_target_pairs={{0,16},{16,0},{1,17},{17,1},{2,18},{18,2},{3,19},{19,3},{4,20},{20... | collective-permute-start | bytes 3545096 | tf_op jit(solution)/shard_map/ppermute | solution.py:11
  74.6 142.4 %collective-permute-start.10 = (bf16[128,2048]{1,0:T(8,128)(2,1)}, bf16[128,2048]{1,0:T(8,128)(2,1)}, u32[]{:S(2)}, u32[]{:S(2)}) collective-permute-start(bf16[128,2048]{1,0:T(8,128)(2,1)} %get-tuple-element.162), channel_id=1, source_target_pairs={{0,4},{4,0},{8,12},{12,8},{1,5},{5,1},{9,13},{13,9},{2,6},{6,2},{1... | collective-permute-start | bytes 1572872 | tf_op jit(solution)/shard_map/ppermute | solution.py:21
  75.8 144.7 %collective-permute-start.8 = (bf16[128,2048]{1,0:T(8,128)(2,1)}, bf16[128,2048]{1,0:T(8,128)(2,1)}, u32[]{:S(2)}, u32[]{:S(2)}) collective-permute-start(bf16[128,2048]{1,0:T(8,128)(2,1)} %get-tuple-element.164), channel_id=1, source_target_pairs={{0,8},{4,12},{8,0},{12,4},{1,9},{5,13},{9,1},{13,5},{2,10},{6,14},... | collective-permute-start | bytes 1572872 | tf_op jit(solution)/shard_map/ppermute | solution.py:26
  96.9 127.0 %collective-permute-start.14 = (bf16[128,2048]{1,0:T(8,128)(2,1)}, bf16[128,2048]{1,0:T(8,128)(2,1)}, u32[]{:S(2)}, u32[]{:S(2)}) collective-permute-start(bf16[128,2048]{1,0:T(8,128)(2,1)} %get-tuple-element.156), channel_id=1, source_target_pairs={{0,4},{4,0},{8,12},{12,8},{1,5},{5,1},{9,13},{13,9},{2,6},{6,2},{1... | collective-permute-start | bytes 1572872 | tf_op jit(solution)/shard_map/ppermute | solution.py:21
  98.1 128.4 %collective-permute-start.12 = (bf16[128,2048]{1,0:T(8,128)(2,1)}, bf16[128,2048]{1,0:T(8,128)(2,1)}, u32[]{:S(2)}, u32[]{:S(2)}) collective-permute-start(bf16[128,2048]{1,0:T(8,128)(2,1)} %get-tuple-element.158), channel_id=1, source_target_pairs={{0,8},{4,12},{8,0},{12,4},{1,9},{5,13},{9,1},{13,5},{2,10},{6,14},... | collective-permute-start | bytes 1572872 | tf_op jit(solution)/shard_map/ppermute | solution.py:26
  302.5 129.1 %collective-permute-start.20 = (bf16[256,2048]{1,0:T(8,128)(2,1)}, bf16[256,2048]{1,0:T(8,128)(2,1)}, u32[]{:S(2)}, u32[]{:S(2)}) collective-permute-start(bf16[256,2048]{1,0:T(8,128)(2,1)} %pad_maximum_fusion.19), channel_id=1, source_target_pairs={{0,8},{4,12},{8,0},{12,4},{1,9},{5,13},{9,1},{13,5},{2,10},{6,14},... | collective-permute-start | bytes 3145736 | tf_op jit(solution)/shard_map/ppermute | solution.py:26
  340.0 145.9 %collective-permute-start.25 = (bf16[256,2048]{1,0:T(8,128)(2,1)}, bf16[256,2048]{1,0:T(8,128)(2,1)}, u32[]{:S(2)}, u32[]{:S(2)}) collective-permute-start(bf16[256,2048]{1,0:T(8,128)(2,1)} %pad_maximum_fusion.21), channel_id=1, source_target_pairs={{0,8},{4,12},{8,0},{12,4},{1,9},{5,13},{9,1},{13,5},{2,10},{6,14},... | collective-permute-start | bytes 3145736 | tf_op jit(solution)/shard_map/ppermute | solution.py:26
  358.3 84.5 %collective-permute-start.27 = (bf16[256,2048]{1,0:T(8,128)(2,1)}, bf16[256,2048]{1,0:T(8,128)(2,1)}, u32[]{:S(2)}, u32[]{:S(2)}) collective-permute-start(bf16[256,2048]{1,0:T(8,128)(2,1)} %pad_maximum_fusion.22), channel_id=1, source_target_pairs={{0,4},{4,0},{8,12},{12,8},{1,5},{5,1},{9,13},{13,9},{2,6},{6,2},{1... | collective-permute-start | bytes 3145736 | tf_op jit(solution)/shard_map/ppermute | solution.py:21
  362.0 126.3 %collective-permute-start.29 = (bf16[256,2048]{1,0:T(8,128)(2,1)}, bf16[256,2048]{1,0:T(8,128)(2,1)}, u32[]{:S(2)}, u32[]{:S(2)}) collective-permute-start(bf16[256,2048]{1,0:T(8,128)(2,1)} %pad_maximum_fusion.23), channel_id=1, source_target_pairs={{0,8},{4,12},{8,0},{12,4},{1,9},{5,13},{9,1},{13,5},{2,10},{6,14},... | collective-permute-start | bytes 3145736 | tf_op jit(solution)/shard_map/ppermute | solution.py:26
  571.7 317.2 %collective-permute-start.34 = (bf16[577,1024]{1,0:T(8,128)(2,1)}, bf16[577,1024]{1,0:T(8,128)(2,1)}, u32[]{:S(2)}, u32[]{:S(2)}) collective-permute-start(bf16[577,1024]{1,0:T(8,128)(2,1)} %convolution_convert_fusion.6), channel_id=1, source_target_pairs={{0,16},{16,0},{1,17},{17,1},{2,18},{18,2},{3,19},{19,3},{4,20},{20... | collective-permute-start | bytes 3545096 | tf_op jit(solution)/shard_map/ppermute | solution.py:11
  573.9 64.9 %collective-permute-start.49 = (bf16[256,2048]{1,0:T(8,128)(2,1)}, bf16[256,2048]{1,0:T(8,128)(2,1)S(1)}, u32[]{:S(2)}, u32[]{:S(2)}) collective-permute-start(bf16[256,2048]{1,0:T(8,128)(2,1)} %get-tuple-element.117), channel_id=1, source_target_pairs={{0,4},{4,0},{8,12},{12,8},{1,5},{5,1},{9,13},{13,9},{2,6},{6,2},{1... | collective-permute-start | bytes 3145736 | tf_op jit(solution)/shard_map/ppermute | solution.py:21
  613.1 317.8 %reduce-scatter.15.cloned.1.call-start = ((), (), s32[]{:S(2)}) async-start(), calls=%async_computation.18 | async-start | bytes 1310720 | tf_op jit(solution)/shard_map/reduce_scatter | solution.py:67
  668.9 265.2 %reduce-scatter.13.cloned.1.call-start = ((), (), s32[]{:S(2)}) async-start(), calls=%async_computation.17 | async-start | bytes 1310720 | tf_op jit(solution)/shard_map/reduce_scatter | solution.py:67
  704.2 229.9 %reduce-scatter.11.cloned.1.call-start = ((), (), s32[]{:S(2)}) async-start(), calls=%async_computation.16 | async-start | bytes 1310720 | tf_op jit(solution)/shard_map/reduce_scatter | solution.py:67
  715.9 212.7 %collective-permute-start.43 = (bf16[128,2048]{1,0:T(8,128)(2,1)}, bf16[128,2048]{1,0:T(8,128)(2,1)}, u32[]{:S(2)}, u32[]{:S(2)}) collective-permute-start(bf16[128,2048]{1,0:T(8,128)(2,1)} %slice.794), channel_id=1, source_target_pairs={{0,4},{4,0},{8,12},{12,8},{1,5},{5,1},{9,13},{13,9},{2,6},{6,2},{1... | collective-permute-start | bytes 1572872 | tf_op jit(solution)/shard_map/ppermute | solution.py:21
  846.7 149.4 %reduce-scatter.7.cloned.1.call-start = ((), (), s32[]{:S(2)}) async-start(), calls=%async_computation.14 | async-start | bytes 1392640 | tf_op jit(solution)/shard_map/reduce_scatter | solution.py:67
  928.5 68.6 %reduce-scatter.9.cloned.1.call-start = ((), (), s32[]{:S(2)}) async-start(), calls=%async_computation.15 | async-start | bytes 1310720 | tf_op jit(solution)/shard_map/reduce_scatter | solution.py:67
  (205 other events, 3010.2 us)
Sparse Core Ops, SparseCore 0:
  14.3 47.0 all-gather.8
  63.5 30.8 all-gather.10
  96.0 27.4 all-gather.12
  124.9 27.4 all-gather.14
  154.4 27.4 all-gather.16
  183.8 28.4 all-gather.6
  613.2 26.9 reduce-scatter.16
  669.0 28.8 reduce-scatter.14
  704.3 29.4 reduce-scatter.12
  846.8 26.2 reduce-scatter.10
  889.0 28.2 reduce-scatter.6
  931.4 40.8 reduce-scatter.8

commit v3 on v2

v3 whole, which is shorter than its diff:
```python
import jax
import jax.numpy as jnp
from jax import lax
from jax.experimental import pallas as pl
from jax.sharding import PartitionSpec as P

HD = 64
EPS = 1e-06


def swap(value):
    return lax.ppermute(value, "section", [(0, 1), (1, 0)])


def pair_sum(partial):
    low = partial.astype(jnp.bfloat16)
    return low.astype(jnp.float32) + swap(low).astype(jnp.float32)


def swap_x(value):
    n = lax.axis_size("dp")
    return lax.ppermute(value, "dp", [(i, i ^ 1) for i in range(n)])


def swap_y(value):
    n = lax.axis_size("dp")
    return lax.ppermute(value, "dp", [(i, i ^ 2) for i in range(n)])


def tie(values, others):
    count = len(values)

    def kernel(*refs):
        pass

    anywhere = pl.BlockSpec(memory_space=pl.ANY)
    done = pl.pallas_call(
        kernel,
        out_shape=[jax.ShapeDtypeStruct(v.shape, v.dtype) for v in values],
        in_specs=[anywhere] * (count + len(others)),
        out_specs=[anywhere] * count,
        input_output_aliases={i: i for i in range(count)},
    )(*values, *others)
    return list(done)


def gather_column(shard):
    return lax.all_gather(shard, "tensor", axis=1, tiled=True)


def exchange_one(first, second):
    if lax.axis_size("dp") != 4:
        return [lax.all_gather(v, "dp", axis=0, tiled=True) for v in (first, second)]
    return [swap_y(first), swap_x(second)]


def exchange_two(first, second, near_first, near_second):
    if lax.axis_size("dp") != 4:
        return []
    return [swap_x(first), swap_x(near_first), swap_y(second), swap_y(near_second)]


def arrived(first, second, near, far):
    if lax.axis_size("dp") != 4:
        return ([near[0]], [near[1]])
    return ([first, near[0], far[0], far[1]], [second, near[1], far[2], far[3]])


def row_cuts(depth):
    half = depth // 2
    if lax.axis_size("dp") != 4:
        return [(0, half), (half, depth), None, None]
    part = half // 2
    return [(part, half), (half + part, depth), (0, part), (half, half + part)]


def add(left, right):
    return left.astype(jnp.float32) + right.astype(jnp.float32)


def scatter_one(send_first, send_second):
    if lax.axis_size("dp") != 4:
        return [
            lax.psum_scatter(v, "dp", scatter_dimension=0, tiled=True)
            for v in (send_first, send_second)
        ]
    return [swap_x(send_first), swap_y(send_second)]


def scatter_two(keep_first, keep_second, got):
    if lax.axis_size("dp") != 4:
        return (got, [])
    stay, come = [], []
    for keep, new, far in zip((keep_first, keep_second), got, (swap_y, swap_x)):
        half = keep.shape[0] // 2
        come.append(far(add(keep[half:], new[half:]).astype(jnp.bfloat16)))
        stay.append(add(keep[:half], new[:half]).astype(jnp.bfloat16))
    return (stay, come)


def scatter_column(stay, come):
    if come:
        stay = [add(s, c).astype(jnp.bfloat16) for s, c in zip(stay, come)]
    return lax.psum_scatter(
        jnp.concatenate(stay, 0), "tensor", scatter_dimension=1, tiled=True
    )


def flip_axis(value, axis, bit):
    return jnp.where(bit == 1, jnp.flip(value, axis), value)


def relative(value, spot):
    n_dp = lax.axis_size("dp")
    lead = value.shape[:-1]
    k = len(lead)
    if n_dp != 4:
        cut = value.reshape(lead + (n_dp, 2, -1))
        return jnp.swapaxes(cut, k, k + 1).reshape(value.shape)
    cut = value.reshape(lead + (2, 2, 2, -1))
    cut = flip_axis(flip_axis(cut, k, spot // 2), k + 1, spot % 2)
    first = jnp.swapaxes(cut[..., 0, :], k, k + 1)
    second = cut[..., 1, :]
    return jnp.concatenate([first.reshape(lead + (-1,)), second.reshape(lead + (-1,))], -1)


def absolute(value, spot):
    n_dp = lax.axis_size("dp")
    lead = value.shape[:-1]
    k = len(lead)
    if n_dp != 4:
        cut = value.reshape(lead + (2, n_dp, -1))
        return jnp.swapaxes(cut, k, k + 1).reshape(value.shape)
    cut = value.reshape(lead + (2, 2, 2, -1))
    first = jnp.swapaxes(cut[..., 0, :, :, :], k, k + 1)
    second = cut[..., 1, :, :, :]
    cut = jnp.stack([first, second], k + 2)
    cut = flip_axis(flip_axis(cut, k, spot // 2), k + 1, spot % 2)
    return cut.reshape(value.shape)


def by_chip(blocks, spot):
    n_dp = lax.axis_size("dp")
    if n_dp != 4:
        return blocks
    cut = blocks.reshape((2, 2) + blocks.shape[1:])
    cut = jnp.swapaxes(cut, 0, 1)
    cut = flip_axis(flip_axis(cut, 0, spot // 2), 1, spot % 2)
    return cut.reshape(blocks.shape)


def by_arrival(blocks, spot):
    n_dp = lax.axis_size("dp")
    if n_dp != 4:
        return blocks
    cut = blocks.reshape((2, 2) + blocks.shape[1:])
    cut = flip_axis(flip_axis(cut, 0, spot // 2), 1, spot % 2)
    return jnp.swapaxes(cut, 0, 1).reshape(blocks.shape)


def mm(form, left, right):
    return jnp.einsum(form, left, right, preferred_element_type=jnp.float32)


def layer_norm(value, gain, shift):
    center = jnp.mean(value, -1, keepdims=True)
    spread = jnp.mean(value * value, -1, keepdims=True) - center * center
    factor = lax.rsqrt(spread + EPS)
    centred = (value - center) * factor
    return ((centred * gain + shift).astype(jnp.bfloat16), centred, factor)


def norm_backward(grad_normed, centred, factor, gain):
    scaled = grad_normed * gain
    return factor * (
        scaled
        - jnp.mean(scaled, -1, keepdims=True)
        - centred * jnp.mean(scaled * centred, -1, keepdims=True)
    )


def gelu_parts(value):
    cdf = 0.5 * (1.0 + lax.erf(value * 0.7071067811865476))
    density = jnp.exp(-0.5 * value * value) * 0.3989422804014327
    return (cdf, density)


def forward_attention(w_qkv, w_out, rows, q_bias, v_bias, value):
    tokens = value.shape[0]
    heads = w_out.shape[1] // HD
    split = (tokens, heads, HD)
    normed, centred, factor = layer_norm(value, rows[0], rows[1])
    projected = mm("td,dgce->tgce", normed, w_qkv)
    queries = (projected[:, :, 0].reshape(tokens, -1) + q_bias).astype(jnp.bfloat16)
    keyset = projected[:, :, 1].reshape(tokens, -1).astype(jnp.bfloat16)
    valueset = (projected[:, :, 2].reshape(tokens, -1) + v_bias).astype(jnp.bfloat16)
    scores = mm("qhd,khd->hqk", queries.reshape(split), keyset.reshape(split)) * HD ** (-0.5)
    highest = jnp.max(scores, -1, keepdims=True)
    exponent = jnp.exp(scores - highest)
    denominator = jnp.sum(exponent, -1, keepdims=True)
    soft = (exponent / denominator).astype(jnp.bfloat16)
    log_total = highest + jnp.log(denominator)
    mixed = mm("hqk,khd->qhd", soft, valueset.reshape(split)).astype(jnp.bfloat16)
    mixed = mixed.reshape(tokens, heads * HD)
    middle = value + pair_sum(mm("te,de->td", mixed, w_out)) + rows[4]
    normed_two, centred_two, factor_two = layer_norm(middle, rows[5], rows[6])
    kept = (normed, centred, factor, queries, keyset, valueset, log_total, mixed)
    return (middle, kept + (normed_two, centred_two, factor_two))


def forward_up(w_up, up_bias, normed_two):
    before = mm("td,df->tf", normed_two, w_up) + up_bias
    hidden = (before * gelu_parts(before)[0]).astype(jnp.bfloat16)
    return (before, hidden)


def forward_down(w_down, rows, middle, hidden):
    return middle + pair_sum(mm("tf,df->td", hidden, w_down)) + rows[7]


def weight_grad(form, left, right, axis=1):
    cuts = row_cuts(left.shape[axis])
    return [
        None
        if cut is None
        else mm(form, lax.slice_in_dim(left, cut[0], cut[1], axis=axis), right).astype(jnp.bfloat16)
        for cut in cuts
    ]


def backward_down(w_down, kept, before, hidden, grad_out):
    grad_branch = grad_out.astype(jnp.bfloat16)
    grad_down = weight_grad("td,tf->df", grad_branch, hidden)
    cdf, density = gelu_parts(before)
    grad_before = mm("td,df->tf", grad_branch, w_down) * (cdf + before * density)
    return (grad_down, grad_before.astype(jnp.bfloat16), jnp.sum(grad_before, 0))


def backward_up(w_up, rows, kept, before_low, grad_out):
    normed_two, centred_two, factor_two = kept[8:]
    grad_up = weight_grad("td,tf->df", normed_two, before_low)
    grad_normed_two = pair_sum(mm("tf,df->td", before_low, w_up))
    grad_middle = grad_out + norm_backward(grad_normed_two, centred_two, factor_two, rows[5])
    sums = [
        jnp.sum(grad_middle, 0),
        jnp.sum(grad_normed_two * centred_two, 0),
        jnp.sum(grad_normed_two, 0),
        jnp.sum(grad_out, 0),
    ]
    return (grad_up, grad_middle, sums)


def backward_attention(w_qkv, w_out, rows, kept, grad_middle):
    normed, centred, factor, queries, keyset, valueset, log_total, mixed = kept[:8]
    tokens = grad_middle.shape[0]
    heads = w_out.shape[1] // HD
    split = (tokens, heads, HD)
    scale = HD ** (-0.5)
    groups = w_qkv.shape[1]
    grad_attended = grad_middle.astype(jnp.bfloat16)
    grad_mixed = mm("td,de->te", grad_attended, w_out).astype(jnp.bfloat16).reshape(split)
    query_heads, key_heads = queries.reshape(split), keyset.reshape(split)
    soft = jnp.exp(mm("qhd,khd->hqk", query_heads, key_heads) * scale - log_total)
    soft_low = soft.astype(jnp.bfloat16)
    grad_values = mm("hqk,qhd->khd", soft_low, grad_mixed)
    grad_soft = mm("qhd,khd->hqk", grad_mixed, valueset.reshape(split))
    row_inner = jnp.sum(grad_soft * soft, -1, keepdims=True)
    grad_scores = (soft * (grad_soft - row_inner)).astype(jnp.bfloat16)
    grad_queries = mm("hqk,khd->qhd", grad_scores, key_heads) * scale
    grad_keys = mm("hqk,qhd->khd", grad_scores, query_heads) * scale
    parts = [grad_queries, grad_keys, grad_values]
    parts = [part.astype(jnp.bfloat16).reshape(tokens, groups, -1) for part in parts]
    stack_low = jnp.stack(parts, 2)
    grad_normed = pair_sum(mm("tgce,dgce->td", stack_low, w_qkv))
    grad_value = grad_middle + norm_backward(grad_normed, centred, factor, rows[0])
    grad_qkv = weight_grad("td,tgce->dgce", normed, stack_low)
    grad_out = weight_grad("td,te->de", grad_attended, mixed)
    quads = []
    for left, right in zip(grad_qkv, grad_out):
        if left is None:
            quads.append(None)
            continue
        right = right.reshape(left.shape[:2] + (1, -1))
        quads.append(jnp.concatenate([left, right], 2).reshape(left.shape[0], -1))
    sums = [
        jnp.sum(grad_normed * centred, 0),
        jnp.sum(grad_normed, 0),
        jnp.sum(grad_queries, 0).reshape(-1),
        jnp.sum(grad_values, 0).reshape(-1),
    ]
    return (quads, grad_value, sums)


def half_cols(core, whole, n_tensor):
    cut = whole.reshape(whole.shape[:-1] + (n_tensor, 2, -1))
    cut = jnp.where(core == 0, cut[..., 0, :], cut[..., 1, :])
    return cut.reshape(whole.shape[:-1] + (-1,))


def spread_cols(core, half, n_tensor):
    cut = half.reshape(half.shape[:-1] + (n_tensor, 1, -1))
    none = jnp.zeros_like(cut)
    both = jnp.concatenate(
        [jnp.where(core == 0, cut, none), jnp.where(core == 0, none, cut)], -2
    )
    return both.reshape(half.shape[:-1] + (-1,))


def body(boundary_in, counts, qkv_weight, proj_weight, fc1_weight, fc2_weight, vectors, fc1_bias):
    core = lax.axis_index("section")
    is_first = core == 0
    place = lax.axis_index("tensor")
    spot = lax.axis_index("dp")
    n_dp, n_tensor = lax.axis_size("dp"), lax.axis_size("tensor")
    slots_per_batch = boundary_in.shape[1] // counts.shape[1]
    live = (place % slots_per_batch < counts[0, place // slots_per_batch]).astype(jnp.float32)
    depth = qkv_weight.shape[1]
    mid = depth // 2
    n_vec = vectors.size

    small_size = n_vec + fc1_bias.size
    packs = []
    for part in range(2):
        cuts = [
            jnp.split(qkv_weight[0], 2, 2)[part].reshape(depth, -1),
            jnp.split(proj_weight[0], 2, 0)[part].T,
            jnp.split(fc1_weight[0], 2, 1)[part],
            jnp.split(fc2_weight[0], 2, 0)[part].T,
        ]
        packs.append(jnp.concatenate(cuts, 1))
    wide = packs[0].shape[1] // 3
    extra = 16
    small = jnp.concatenate([vectors.reshape(-1), fc1_bias.reshape(-1)])
    small = jnp.pad(small, (0, extra * wide - small_size)).reshape(extra, wide)
    small = jnp.pad(small, ((0, 0), (0, 2 * wide)))
    kept = jnp.concatenate([jnp.where(is_first, packs[0], packs[1]), small], 0)
    received = swap(
        jnp.concatenate([jnp.where(is_first, packs[1], packs[0]), small], 0)
    )
    shards = (jnp.where(is_first, kept, received), jnp.where(is_first, received, kept))
    columns = []
    for layer in range(2):
        for number in range(3):
            cols = shards[layer][:, number * wide : (number + 1) * wide]
            if number == 0:
                cols = jnp.concatenate([cols[:mid], cols[depth:], cols[mid:depth]], 0)
            else:
                cols = cols[:depth]
            columns.append(cols)

    tokens = boundary_in.shape[2]
    pad = -tokens % 16
    reach = (tokens + pad) // 2
    ends_in = jnp.pad(boundary_in[0].astype(jnp.bfloat16), ((0, 0), (0, pad), (0, 0)))
    ends_low, ends_high = ends_in[:, :reach], ends_in[:, reach:]
    ends_got = swap(jnp.where(is_first, ends_high, ends_low))
    half_in = jnp.where(is_first, ends_low, ends_got)
    half_cot = jnp.where(is_first, ends_got, ends_high)

    def whole_image(half):
        half = lax.all_to_all(half, "tensor", split_axis=0, concat_axis=2, tiled=True)[0]
        other = swap(half)
        both = [jnp.where(is_first, half, other), jnp.where(is_first, other, half)]
        return relative(jnp.concatenate(both, 0)[:tokens], spot)

    def image_rows(image):
        image = absolute(image.astype(jnp.bfloat16), spot)
        image = jnp.pad(image, ((0, pad), (0, 0)))
        half = jnp.where(is_first, image[:reach], image[reach:])
        half = lax.all_to_all(half[None], "tensor", split_axis=2, concat_axis=0, tiled=True)
        return half

    def small_of(piece):
        extras = jnp.concatenate(piece, 0)
        one = by_chip(extras.reshape(n_dp, extra, -1), spot).astype(jnp.float32)
        one = one.reshape(n_dp, extra, n_tensor, wide).transpose(0, 2, 1, 3)
        one = one.reshape(n_dp, n_tensor, -1)
        rows = one[:, :, :n_vec].reshape(n_dp, n_tensor, 8, -1)
        rows = rows.transpose(2, 1, 0, 3).reshape(8, -1)
        bias = one[:, :, n_vec:small_size].transpose(1, 0, 2).reshape(-1)
        q_bias = half_cols(core, rows[2], n_tensor)
        v_bias = half_cols(core, rows[3], n_tensor)
        up_bias = half_cols(core, bias, n_tensor)
        return (relative(rows, spot), q_bias, v_bias, up_bias)

    value = whole_image(half_in).astype(jnp.float32)

    number = len(columns)
    cut = [mid + extra if k % 3 == 0 else mid for k in range(number)]
    halves, near, far = [None] * number, [None] * number, [None] * number
    pieces = [None] * number
    params = [dict(), dict()]
    state = value
    output = None
    for r in range(number + 4):
        tied = []
        if r < number:
            whole = gather_column(columns[r])
            tied.append(whole)
        if 0 <= r - 1 < number:
            near[r - 1] = exchange_one(*halves[r - 1])
            tied += near[r - 1]
        if 0 <= r - 2 < number:
            far[r - 2] = exchange_two(*halves[r - 2], *near[r - 2])
            tied += far[r - 2]
        k = r - 3
        if 0 <= k < number:
            layer, kind = k // 3, k % 3
            one = params[layer]
            first, second = arrived(*halves[k], near[k], far[k])
            if kind == 0:
                blocks = [p.reshape((-1, mid + extra) + p.shape[1:]) for p in first]
                one["small"] = small_of([p[:, mid:].reshape(-1, p.shape[-1]) for p in blocks])
                first = [p[:, :mid].reshape(-1, p.shape[-1]) for p in blocks]
            matrix = jnp.concatenate(first + second, 0)
            if kind == 0:
                quad = matrix.reshape(matrix.shape[0], n_tensor, 4, -1)
                one["qkv"] = quad[:, :, :3]
                one["out"] = quad[:, :, 3].reshape(quad.shape[0], -1)
                rows, q_bias, v_bias, up_bias = one["small"]
                state, one["kept"] = forward_attention(
                    one["qkv"], one["out"], rows, q_bias, v_bias, state
                )
            elif kind == 1:
                one["up"] = matrix
                one["before"], one["hidden"] = forward_up(
                    matrix, one["small"][3], one["kept"][8]
                )
            else:
                one["down"] = matrix
                state = forward_down(matrix, one["small"][0], state, one["hidden"])
                if layer == 0:
                    state = state.astype(jnp.bfloat16).astype(jnp.float32)
        if r < number + 2:
            extras = [state] if r >= 3 else []
            if r >= 3 and (r - 3) % 3 == 1:
                extras.append(params[(r - 3) // 3]["hidden"])
            if r == 5:
                extras.append(half_cot)
            if r + 1 < number:
                extras.append(columns[r + 1])
            done = tie(tied + extras, [])
            if r + 1 < number:
                columns[r + 1] = done.pop()
            if r == 5:
                half_cot = done.pop()
            if r >= 3 and (r - 3) % 3 == 1:
                params[(r - 3) // 3]["hidden"] = done.pop()
            if r >= 3:
                state = done.pop()
            at = 0
            if r < number:
                halves[r] = (done[0][: cut[r]], done[0][cut[r] :])
                at = 1
            if 0 <= r - 1 < number:
                near[r - 1] = done[at : at + 2]
                at += 2
            if 0 <= r - 2 < number:
                far[r - 2] = done[at:]
        if r == 5:
            cotangent = whole_image(half_cot).astype(jnp.float32) * live
    output = state * live
    out_rows = image_rows(output)

    grads, got, moved, settled = [None] * number, [None] * number, [None] * number, [None] * number
    sums = [dict(), dict()]
    grad = cotangent
    for r in range(number):
        layer, kind = (number - 1 - r) // 3, (number - 1 - r) % 3
        one, total = params[layer], sums[layer]
        rows = one["small"][0]
        tied = []
        if r >= 1:
            got[r - 1] = scatter_one(*grads[r - 1][:2])
            tied += got[r - 1]
        if r >= 2:
            moved[r - 2] = scatter_two(*grads[r - 2][2:], got[r - 2])
            tied += moved[r - 2][0] + moved[r - 2][1]
        if r >= 3:
            settled[r - 3] = scatter_column(*moved[r - 3])
            tied.append(settled[r - 3])
        if kind == 2:
            grads[r], low, total["up_bias"] = backward_down(
                one["down"], one["kept"], one["before"], one["hidden"], grad
            )
            carry = low
        elif kind == 1:
            grads[r], middle, total["two"] = backward_up(
                one["up"], rows, one["kept"], low, grad
            )
            carry = middle
        else:
            grads[r], grad, total["one"] = backward_attention(
                one["qkv"], one["out"], rows, one["kept"], middle
            )
            if layer == 1:
                grad = grad.astype(jnp.bfloat16).astype(jnp.float32)
            carry = grad
        if r < number - 1:
            new = [g for g in grads[r] if g is not None]
            done = tie([carry] + new + tied, [])
            if kind == 2:
                low = done[0]
            elif kind == 1:
                middle = done[0]
            else:
                grad = done[0]
            grads[r] = (done[1 : 1 + len(new)] + [None, None])[:4]
            done = done[1 + len(new) :]
            if r >= 1:
                got[r - 1], done = done[:2], done[2:]
            if r >= 2:
                count = len(moved[r - 2][1])
                moved[r - 2] = (done[:2], done[2 : 2 + count])
                done = done[2 + count :]
            if r >= 3:
                settled[r - 3] = done[0]

    grad_rows = image_rows(grad)
    packed = []
    for layer in range(2):
        total = sums[layer]
        full = [total["one"][0], total["one"][1]] + total["two"]
        full = absolute(jnp.where(core == layer, jnp.stack(full), 0.0), spot)
        q_row = spread_cols(core, total["one"][2], n_tensor)
        v_row = spread_cols(core, total["one"][3], n_tensor)
        up_row = spread_cols(core, total["up_bias"], n_tensor)
        rows = jnp.concatenate([full[:2], q_row[None], v_row[None], full[2:]], 0)
        rows = rows.reshape(8, n_tensor, n_dp, -1).transpose(2, 1, 0, 3).reshape(n_dp, n_tensor, -1)
        up_row = up_row.reshape(n_tensor, n_dp, -1).transpose(1, 0, 2)
        packed.append(jnp.concatenate([rows, up_row], -1))
    ours = jnp.where(is_first, packed[0], packed[1])
    other = swap(jnp.where(is_first, packed[1], packed[0]))
    little = (ours + other).astype(jnp.bfloat16).reshape(n_dp * n_tensor, -1)
    little = lax.psum_scatter(little, ("dp", "tensor"), scatter_dimension=0, tiled=True)[0]
    little = little.astype(jnp.float32)

    last = number - 1
    got[last] = scatter_one(*grads[last][:2])
    for k in range(number):
        if moved[k] is None:
            moved[k] = scatter_two(*grads[k][2:], got[k])
    for k in range(number):
        if settled[k] is None:
            settled[k] = scatter_column(*moved[k])
    grad_vectors = little[:n_vec].reshape(vectors.shape)
    grad_bias = little[n_vec:small_size].reshape(fc1_bias.shape)

    own = jnp.where(is_first, grad_rows, out_rows)
    other = swap(jnp.where(is_first, out_rows, grad_rows))
    ends = [jnp.where(is_first, own, other), jnp.where(is_first, other, own)]
    boundary_out = jnp.concatenate(ends, 1)[:, :tokens].astype(jnp.float32)[None]
    lows, highs = [], []
    for kind in range(3):
        first, second = settled[last - kind], settled[last - kind - 3]
        kept = jnp.where(is_first, first, second)
        received = swap(jnp.where(is_first, second, first))
        lows.append(jnp.where(is_first, kept, received).astype(jnp.float32))
        highs.append(jnp.where(is_first, received, kept).astype(jnp.float32))
    low, high = [part[0].reshape(depth, 4, -1) for part in (lows, highs)]
    grad_qkv = jnp.concatenate([low[:, :3], high[:, :3]], 2)[None]
    grad_proj = jnp.concatenate([low[:, 3].T, high[:, 3].T], 0)[None]
    grad_up = jnp.concatenate([lows[1], highs[1]], 1)[None]
    grad_down = jnp.concatenate([lows[2].T, highs[2].T], 0)[None]
    return (boundary_out, grad_qkv, grad_proj, grad_up, grad_down, grad_vectors, grad_bias)


def solution(mesh):
    in_specs = (
        P("section", "dp", None, "tensor"),
        P("dp", None),
        P("section", "dp", None, "tensor"),
        P("section", "tensor", "dp"),
        P("section", "dp", "tensor"),
        P("section", "tensor", "dp"),
        P("section", None, "tensor", "dp"),
        P("section", "tensor", "dp"),
    )
    out_specs = (
        P("section", "dp", None, "tensor"),
        P("section", "dp", None, "tensor"),
        P("section", "tensor", "dp"),
        P("section", "dp", "tensor"),
        P("section", "tensor", "dp"),
        P("section", None, "tensor", "dp"),
        P("section", "tensor", "dp"),
    )
    return jax.shard_map(body, mesh=mesh, in_specs=in_specs, out_specs=out_specs, check_vma=False)
```

time: 1020 us -> 1010 us (level)
  waiting for transfers between devices: 391 us -> 164 us
  blocking collectives: 0 us -> 62.8 us
  matrix products: 134 us -> 185 us
  starting transfers between devices: 67.1 us -> 112 us
  local copies, waits for them, and re-layouts: 244 us -> 274 us
  other arithmetic: 160 us -> 180 us
    all_gather x6, waiting for transfers between devices: 123 us -> 20.3 us  [gather_column(): return lax.all_gather(shard, 'tensor', axis=1, tiled=True)]
    unnamed x0 -> x1, blocking collectives: none -> 62.8 us
    all_to_all x2 -> x4, waiting for transfers between devices: 74.9 us -> 13.8 us  [the longest x2 11.4 us: whole_image(): lax.all_to_all(half, 'tensor', split_axis=0, concat_axis=2, tiled=True)[0]]
    dot_general x36 -> x60, matrix products: 134 us -> 185 us  [mm(): return jnp.einsum(form, left, right, preferred_element_type=jnp.float32)]
    ppermute x24 -> x30, waiting for transfers between devices: 127 us -> 82.8 us  [swap_x(): return lax.ppermute(value, 'dp', [(i, i ^ 1) for i in range(n)])]
    unnamed x369 -> x441, local copies, waits for them, and re-layouts: 54.5 us -> 96.8 us
    slice x66 -> x50, local copies, waits for them, and re-layouts: 73.1 us -> 39.1 us  [the longest x8 7.53 us: body(): first = [p[:, :mid].reshape(-1, p.shape[-1]) for p in blocks]]
    concatenate x27 -> x22, other arithmetic: 41.2 us -> 15.5 us  [the longest x6 6.56 us: scatter_column(): jnp.concatenate(stay, 0)]
  transfers between devices with their start and end apart: 77 -> 93, of which waited for: 26 -> 28; matrix products, arithmetic and copies ran while one was open for 48% -> 47% of each run, Pallas kernels for 0% -> 0%
where the time goes in v3:
time: 1010 us; the launch traced here: 997 us
  local copies, waits for them, and re-layouts  274 us (27%)
  matrix products  185 us (18%)
  other arithmetic  180 us (18%)
  waiting for transfers between devices  164 us (16%)
  starting transfers between devices  112 us (11%)
  blocking collectives  62.8 us (6%)
  between operations  18.8 us (2%)
    dot_general x60, matrix products, mm(): return jnp.einsum(form, left, right, preferred_element_type=jnp.float32)  185 us
    unnamed x441, local copies, waits for them, and re-layouts  96.8 us
    ppermute x30, waiting for transfers between devices, swap_x(): return lax.ppermute(value, 'dp', [(i, i ^ 1) for i in range(n)])  82.8 us
    unnamed x1, blocking collectives  62.8 us
    ppermute x30, waiting for transfers between devices, swap_y(): return lax.ppermute(value, 'dp', [(i, i ^ 2) for i in range(n)])  46.1 us
    ppermute x17, starting transfers between devices, swap(): return lax.ppermute(value, 'section', [(0, 1), (1, 0)])  46 us
    concatenate x22, local copies, waits for them, and re-layouts, body(): matrix = jnp.concatenate(first + second, 0)  32.7 us
    convert_element_type x12, other arithmetic, scatter_two(): come.append(far(add(keep[half:], new[half:]).astype(jnp.bfloat16)))  24.9 us
  transfers between devices with their start and end apart: 93, of which 28 were waited for; matrix products, arithmetic and copies ran while one was open for 47% of the time, Pallas kernels for 0%

profile of v3, /device:TPU:1, one launch (start us, length us, event | category | flops | bytes accessed | tf_op | source)
XLA Modules:
  0.0 997.4 jit_solution(17466702896884620294)
XLA Ops:
  30.3 11.4 %all-to-all-done = bf16[4,296,256]{2,1,0:T(8,128)(2,1)S(1)} async-done(((bf16[4,296,256]{2,1,0:T(8,128)(2,1)}), bf16[4,296,256]{2,1,0:T(8,128)(2,1)S(1)}, u32[]{:S(2)}, u32[]{:S(2)}) %all-to-all-start) | async-done | bytes 606240 | tf_op jit(solution)/shard_map/all_to_all | solution.py:361
  50.7 10.4 %all-gather.7.cloned.1.call-done.refs_0_ = bf16[272,2048]{1,0:T(8,128)(2,1)} async-done(((bf16[272,512]{1,0:T(8,128)(2,1)}), bf16[272,2048]{1,0:T(8,128)(2,1)}) %all-gather.7.cloned.1.call-update) | async-done | bytes 1114128 | tf_op jit(solution)/shard_map/all_gather | solution.py:48
  80.0 9.9 all-gather.9.cloned.1.call-done.refs_0_
  115.7 17.3 %collective-permute-done.4.refs_2_ = bf16[128,2048]{1,0:T(8,128)(2,1)S(1)} collective-permute-done((bf16[128,2048]{1,0:T(8,128)(2,1)}, bf16[128,2048]{1,0:T(8,128)(2,1)S(1)}, u32[]{:S(2)}, u32[]{:S(2)}) %collective-permute-start.4) | collective-permute-done | bytes 524320 | tf_op jit(solution)/shard_map/ppermute | solution.py:22
  198.1 9.6 collective-permute-done.9.refs_1_
  219.4 7.6 multiply_convert_fusion.3
  282.3 10.2 %collective-permute-done.25.refs_2_ = bf16[128,2048]{1,0:T(8,128)(2,1)S(1)} collective-permute-done((bf16[128,2048]{1,0:T(8,128)(2,1)}, bf16[128,2048]{1,0:T(8,128)(2,1)S(1)}, u32[]{:S(2)}, u32[]{:S(2)}) %collective-permute-start.25) | collective-permute-done | bytes 524320 | tf_op jit(solution)/shard_map/ppermute | solution.py:22
  372.0 8.1 collective-permute-done.33.refs_0_
  393.5 7.7 multiply_convert_fusion.2
  452.5 6.8 convolution_convert_fusion.18
  510.7 7.8 fusion.157
  518.5 8.6 multiply_reduce_fusion.1
  527.1 6.6 multiply_convert_fusion.1
  608.2 8.8 fusion.150
  626.4 10.6 %collective-permute-done.51.refs_5_ = bf16[256,2048]{1,0:T(8,128)(2,1)S(1)} collective-permute-done((bf16[256,2048]{1,0:T(8,128)(2,1)}, bf16[256,2048]{1,0:T(8,128)(2,1)S(1)}, u32[]{:S(2)}, u32[]{:S(2)}) %collective-permute-start.51) | collective-permute-done | bytes 1048608 | tf_op jit(solution)/shard_map/ppermute | solution.py:22
  639.6 6.8 convolution_convert_fusion.17
  675.6 20.4 %collective-permute-done.56.refs_5_ = bf16[256,2048]{1,0:T(8,128)(2,1)S(1)} collective-permute-done((bf16[256,2048]{1,0:T(8,128)(2,1)S(1)}, bf16[256,2048]{1,0:T(8,128)(2,1)S(1)}, u32[]{:S(2)}, u32[]{:S(2)}) %collective-permute-start.56) | collective-permute-done | bytes 1048608 | tf_op jit(solution)/shard_map/ppermute | solution.py:22
  706.0 6.8 fusion.155
  712.9 8.6 multiply_reduce_fusion
  721.5 6.7 multiply_convert_fusion
  785.3 14.1 %collective-permute-done.63 = bf16[256,2048]{1,0:T(8,128)(2,1)} collective-permute-done((bf16[256,2048]{1,0:T(8,128)(2,1)}, bf16[256,2048]{1,0:T(8,128)(2,1)}, u32[]{:S(2)}, u32[]{:S(2)}) %collective-permute-start.63) | collective-permute-done | bytes 1048608 | tf_op jit(solution)/shard_map/ppermute | solution.py:22
  831.5 7.5 reduce.33
  870.8 62.8 %all-reduce.5 = bf16[16,768]{1,0:T(8,128)(2,1)S(1)} all-reduce(bf16[16,768]{1,0:T(8,128)(2,1)S(1)} %reshape.821), channel_id=8, replica_groups=mesh['section'=2,'dp'=4,'tensor'=4] {'dp','tensor'}, use_global_device_ids=true, to_apply=%region_46.47.clone | all-reduce | flops 12288 | bytes 49152
  959.7 15.8 %collective-permute-start.62 = (bf16[4,296,256]{2,1,0:T(8,128)(2,1)}, bf16[4,296,256]{2,1,0:T(8,128)(2,1)S(1)}, u32[]{:S(2)}, u32[]{:S(2)}) collective-permute-start(bf16[4,296,256]{2,1,0:T(8,128)(2,1)} %bitcast.497), channel_id=1, source_target_pairs={{0,16},{16,0},{1,17},{17,1},{2,18},{18,2},{3,19},{19,3},{4,20},{20... | collective-permute-start | bytes 1818632 | tf_op jit(solution)/shard_map/ppermute | solution.py:12
  (1065 shorter events, 687.6 us)
Async XLA Ops:
  28.3 61.6 %all-gather.9.cloned.1.call-start = ((), (), s32[]{:S(2)}) async-start(), calls=%async_computation.11 | async-start | bytes 1310720 | tf_op jit(solution)/shard_map/all_gather | solution.py:48
  61.1 72.0 %all-gather.11.cloned.1.call-start = ((), (), s32[]{:S(2)}) async-start(), calls=%async_computation.12 | async-start | bytes 1310720 | tf_op jit(solution)/shard_map/all_gather | solution.py:48
  89.9 117.8 %all-gather.13.cloned.1.call-start = ((), (), s32[]{:S(2)}) async-start(), calls=%async_computation.13 | async-start | bytes 1392640 | tf_op jit(solution)/shard_map/all_gather | solution.py:48
  109.3 79.5 %collective-permute-start.13 = (bf16[128,2048]{1,0:T(8,128)(2,1)}, bf16[128,2048]{1,0:T(8,128)(2,1)}, u32[]{:S(2)}, u32[]{:S(2)}) collective-permute-start(bf16[128,2048]{1,0:T(8,128)(2,1)} %get-tuple-element.339), channel_id=1, source_target_pairs={{0,8},{4,12},{8,0},{12,4},{1,9},{5,13},{9,1},{13,5},{2,10},{6,14},... | collective-permute-start | bytes 1572872 | tf_op jit(solution)/shard_map/ppermute | solution.py:27
  114.6 75.9 %collective-permute-start.11 = (bf16[128,2048]{1,0:T(8,128)(2,1)}, bf16[128,2048]{1,0:T(8,128)(2,1)}, u32[]{:S(2)}, u32[]{:S(2)}) collective-permute-start(bf16[128,2048]{1,0:T(8,128)(2,1)} %get-tuple-element.340), channel_id=1, source_target_pairs={{0,4},{4,0},{8,12},{12,8},{1,5},{5,1},{9,13},{13,9},{2,6},{6,2},{1... | collective-permute-start | bytes 1572872 | tf_op jit(solution)/shard_map/ppermute | solution.py:22
  181.3 60.1 %all-gather.15.cloned.1.call-start = ((), (), s32[]{:S(2)}) async-start(), calls=%async_computation.14 | async-start | bytes 1310720 | tf_op jit(solution)/shard_map/all_gather | solution.py:48
  213.4 79.8 %all-gather.17.cloned.1.call-start = ((), (), s32[]{:S(2)}) async-start(), calls=%async_computation.15 | async-start | bytes 1310720 | tf_op jit(solution)/shard_map/all_gather | solution.py:48
  234.0 45.5 %collective-permute-start.26 = (bf16[144,2048]{1,0:T(8,128)(2,1)}, bf16[144,2048]{1,0:T(8,128)(2,1)}, u32[]{:S(2)}, u32[]{:S(2)}) collective-permute-start(bf16[144,2048]{1,0:T(8,128)(2,1)} %get-tuple-element.322), channel_id=1, source_target_pairs={{0,4},{4,0},{8,12},{12,8},{1,5},{5,1},{9,13},{13,9},{2,6},{6,2},{1... | collective-permute-start | bytes 1769480 | tf_op jit(solution)/shard_map/ppermute | solution.py:22
  279.5 78.9 %collective-permute-start.37 = (bf16[128,2048]{1,0:T(8,128)(2,1)}, bf16[128,2048]{1,0:T(8,128)(2,1)}, u32[]{:S(2)}, u32[]{:S(2)}) collective-permute-start(bf16[128,2048]{1,0:T(8,128)(2,1)} %get-tuple-element.333), channel_id=1, source_target_pairs={{0,8},{4,12},{8,0},{12,4},{1,9},{5,13},{9,1},{13,5},{2,10},{6,14},... | collective-permute-start | bytes 1572872 | tf_op jit(solution)/shard_map/ppermute | solution.py:27
  282.1 85.1 %collective-permute-start.35 = (bf16[128,2048]{1,0:T(8,128)(2,1)}, bf16[128,2048]{1,0:T(8,128)(2,1)}, u32[]{:S(2)}, u32[]{:S(2)}) collective-permute-start(bf16[128,2048]{1,0:T(8,128)(2,1)} %get-tuple-element.334), channel_id=1, source_target_pairs={{0,4},{4,0},{8,12},{12,8},{1,5},{5,1},{9,13},{13,9},{2,6},{6,2},{1... | collective-permute-start | bytes 1572872 | tf_op jit(solution)/shard_map/ppermute | solution.py:22
  329.7 309.8 %reduce-scatter.7.cloned.1.call-start = ((), (), s32[]{:S(2)}) async-start(), calls=%async_computation.16 | async-start | bytes 1310720 | tf_op jit(solution)/shard_map/reduce_scatter | solution.py:104
  367.2 60.2 %collective-permute-start.41 = (bf16[128,2048]{1,0:T(8,128)(2,1)}, bf16[128,2048]{1,0:T(8,128)(2,1)}, u32[]{:S(2)}, u32[]{:S(2)}) collective-permute-start(bf16[128,2048]{1,0:T(8,128)(2,1)} %get-tuple-element.330), channel_id=1, source_target_pairs={{0,8},{4,12},{8,0},{12,4},{1,9},{5,13},{9,1},{13,5},{2,10},{6,14},... | collective-permute-start | bytes 1572872 | tf_op jit(solution)/shard_map/ppermute | solution.py:27
  367.5 59.9 %collective-permute-start.39 = (bf16[128,2048]{1,0:T(8,128)(2,1)}, bf16[128,2048]{1,0:T(8,128)(2,1)}, u32[]{:S(2)}, u32[]{:S(2)}) collective-permute-start(bf16[128,2048]{1,0:T(8,128)(2,1)} %get-tuple-element.331), channel_id=1, source_target_pairs={{0,4},{4,0},{8,12},{12,8},{1,5},{5,1},{9,13},{13,9},{2,6},{6,2},{1... | collective-permute-start | bytes 1572872 | tf_op jit(solution)/shard_map/ppermute | solution.py:22
  380.1 47.2 %collective-permute-start.40 = (bf16[128,2048]{1,0:T(8,128)(2,1)}, bf16[128,2048]{1,0:T(8,128)(2,1)}, u32[]{:S(2)}, u32[]{:S(2)}) collective-permute-start(bf16[128,2048]{1,0:T(8,128)(2,1)} %get-tuple-element.151), channel_id=1, source_target_pairs={{0,4},{4,0},{8,12},{12,8},{1,5},{5,1},{9,13},{13,9},{2,6},{6,2},{1... | collective-permute-start | bytes 1572872 | tf_op jit(solution)/shard_map/ppermute | solution.py:22
  599.7 98.3 %reduce-scatter.9.cloned.1.call-start = ((), (), s32[]{:S(2)}) async-start(), calls=%async_computation.17 | async-start | bytes 1310720 | tf_op jit(solution)/shard_map/reduce_scatter | solution.py:104
  653.9 324.0 %reduce-scatter.17.cloned.1.call-start = ((), (), s32[]{:S(2)}) async-start(), calls=%async_computation.21 | async-start | bytes 1310720 | tf_op jit(solution)/shard_map/reduce_scatter | solution.py:104
  745.1 111.2 %collective-permute-start.70 = (bf16[256,2048]{1,0:T(8,128)(2,1)}, bf16[256,2048]{1,0:T(8,128)(2,1)}, u32[]{:S(2)}, u32[]{:S(2)}) collective-permute-start(bf16[256,2048]{1,0:T(8,128)(2,1)} %get-tuple-element.204), channel_id=1, source_target_pairs={{0,8},{4,12},{8,0},{12,4},{1,9},{5,13},{9,1},{13,5},{2,10},{6,14},... | collective-permute-start | bytes 3145736 | tf_op jit(solution)/shard_map/ppermute | solution.py:27
  761.2 220.4 %reduce-scatter.13.cloned.1.call-start = ((), (), s32[]{:S(2)}) async-start(), calls=%async_computation.19 | async-start | bytes 1310720 | tf_op jit(solution)/shard_map/reduce_scatter | solution.py:104
  784.5 153.3 %collective-permute-start.69 = (bf16[128,2048]{1,0:T(8,128)(2,1)}, bf16[128,2048]{1,0:T(8,128)(2,1)}, u32[]{:S(2)}, u32[]{:S(2)}) collective-permute-start(bf16[128,2048]{1,0:T(8,128)(2,1)} %add_convert_fusion.19), channel_id=1, source_target_pairs={{0,8},{4,12},{8,0},{12,4},{1,9},{5,13},{9,1},{13,5},{2,10},{6,14},... | collective-permute-start | bytes 1572872 | tf_op jit(solution)/shard_map/ppermute | solution.py:27
  801.5 46.0 %collective-permute-start.64 = (bf16[128,2048]{1,0:T(8,128)(2,1)}, bf16[128,2048]{1,0:T(8,128)(2,1)}, u32[]{:S(2)}, u32[]{:S(2)}) collective-permute-start(bf16[128,2048]{1,0:T(8,128)(2,1)} %add_convert_fusion.27), channel_id=1, source_target_pairs={{0,8},{4,12},{8,0},{12,4},{1,9},{5,13},{9,1},{13,5},{2,10},{6,14},... | collective-permute-start | bytes 1572872 | tf_op jit(solution)/shard_map/ppermute | solution.py:27
  842.7 90.9 %all-to-all-start.2 = ((bf16[4,2,37888]{2,1,0:T(2,128)(2,1)}), bf16[4,2,37888]{2,1,0:T(2,128)(2,1)}, u32[]{:S(2)}, u32[]{:S(2)}) async-start(bf16[4,2,37888]{2,1,0:T(2,128)(2,1)} %reshape.906), calls=%async_computation.4 | async-start | bytes 1212416 | tf_op jit(solution)/shard_map/all_to_all | solution.py:370
  847.5 134.2 %reduce-scatter.11.cloned.1.call-start = ((), (), s32[]{:S(2)}) async-start(), calls=%async_computation.18 | async-start | bytes 1310720 | tf_op jit(solution)/shard_map/reduce_scatter | solution.py:104
  857.5 81.8 %collective-permute-start.71 = (bf16[128,2048]{1,0:T(8,128)(2,1)S(1)}, bf16[128,2048]{1,0:T(8,128)(2,1)}, u32[]{:S(2)}, u32[]{:S(2)}) collective-permute-start(bf16[128,2048]{1,0:T(8,128)(2,1)S(1)} %add_convert_fusion.16), channel_id=1, source_target_pairs={{0,4},{4,0},{8,12},{12,8},{1,5},{5,1},{9,13},{13,9},{2,6},{6,2},{1... | collective-permute-start | bytes 1572872 | tf_op jit(solution)/shard_map/ppermute | solution.py:22
  937.8 46.9 %reduce-scatter.15.cloned.1.call-start = ((), (), s32[]{:S(2)}) async-start(), calls=%async_computation.20 | async-start | bytes 1310720 | tf_op jit(solution)/shard_map/reduce_scatter | solution.py:104
  (249 other events, 3091.7 us)
Sparse Core Ops, SparseCore 0:
  29.0 32.0 all-gather.6
  63.2 26.6 all-gather.8
  92.0 27.4 all-gather.10
  181.4 25.9 all-gather.12
  213.5 27.1 all-gather.14
  263.6 25.9 all-gather.16
  599.8 28.0 reduce-scatter.6
  654.0 29.6 reduce-scatter.8
  761.3 28.6 reduce-scatter.16
  792.8 25.7 reduce-scatter.12
  851.7 30.8 reduce-scatter.10
  942.0 41.4 reduce-scatter.14

commit v4 on v3

--- a/solution.py
+++ b/solution.py
@@ -2,6 +2,7 @@
 import jax.numpy as jnp
 from jax import lax
 from jax.experimental import pallas as pl
+from jax.experimental.pallas import tpu as pltpu
 from jax.sharding import PartitionSpec as P
 
 HD = 64
@@ -158,16 +159,50 @@
     return jnp.swapaxes(cut, 0, 1).reshape(blocks.shape)
 
 
-def mm(form, left, right):
-    return jnp.einsum(form, left, right, preferred_element_type=jnp.float32)
-
-
-def layer_norm(value, gain, shift):
+VMEM_BYTES = 50 * 2**20
+BF = jnp.bfloat16
+F32 = jnp.float32
+
+
+def shape(dims, kind=jnp.bfloat16):
+    return jax.ShapeDtypeStruct(dims, kind)
+
+
+def run(kernel, outs, ins, flops):
+    block = pl.BlockSpec(memory_space=pltpu.VMEM)
+    moved = sum(v.size * v.dtype.itemsize for v in list(ins) + list(outs))
+    done = pl.pallas_call(
+        kernel,
+        out_shape=list(outs),
+        in_specs=[block] * len(ins),
+        out_specs=[block] * len(outs),
+        cost_estimate=pl.CostEstimate(flops=flops, bytes_accessed=moved, transcendentals=0),
+        compiler_params=pltpu.CompilerParams(vmem_limit_bytes=VMEM_BYTES),
+    )(*ins)
+    return list(done)
+
+
+def nn(left, right):
+    return lax.dot_general(left, right, (((1,), (0,)), ((), ())), preferred_element_type=F32)
+
+
+def nt(left, right):
+    return lax.dot_general(left, right, (((1,), (1,)), ((), ())), preferred_element_type=F32)
+
+
+def tn(left, right):
+    return lax.dot_general(left, right, (((0,), (0,)), ((), ())), preferred_element_type=F32)
+
+
+def stack_rows(pieces, counts, cols):
+    return jnp.concatenate([p[:n, cols] for p, n in zip(pieces, counts)], 0)
+
+
+def center_scale(value):
     center = jnp.mean(value, -1, keepdims=True)
     spread = jnp.mean(value * value, -1, keepdims=True) - center * center
     factor = lax.rsqrt(spread + EPS)
-    centred = (value - center) * factor
-    return ((centred * gain + shift).astype(jnp.bfloat16), centred, factor)
+    return ((value - center) * factor, factor)
 
 
 def norm_backward(grad_normed, centred, factor, gain):
@@ -179,116 +214,251 @@
     )
 
 
-def gelu_parts(value):
-    cdf = 0.5 * (1.0 + lax.erf(value * 0.7071067811865476))
-    density = jnp.exp(-0.5 * value * value) * 0.3989422804014327
-    return (cdf, density)
-
-
-def forward_attention(w_qkv, w_out, rows, q_bias, v_bias, value):
-    tokens = value.shape[0]
-    heads = w_out.shape[1] // HD
-    split = (tokens, heads, HD)
-    normed, centred, factor = layer_norm(value, rows[0], rows[1])
-    projected = mm("td,dgce->tgce", normed, w_qkv)
-    queries = (projected[:, :, 0].reshape(tokens, -1) + q_bias).astype(jnp.bfloat16)
-    keyset = projected[:, :, 1].reshape(tokens, -1).astype(jnp.bfloat16)
-    valueset = (projected[:, :, 2].reshape(tokens, -1) + v_bias).astype(jnp.bfloat16)
-    scores = mm("qhd,khd->hqk", queries.reshape(split), keyset.reshape(split)) * HD ** (-0.5)
-    highest = jnp.max(scores, -1, keepdims=True)
-    exponent = jnp.exp(scores - highest)
-    denominator = jnp.sum(exponent, -1, keepdims=True)
-    soft = (exponent / denominator).astype(jnp.bfloat16)
-    log_total = highest + jnp.log(denominator)
-    mixed = mm("hqk,khd->qhd", soft, valueset.reshape(split)).astype(jnp.bfloat16)
-    mixed = mixed.reshape(tokens, heads * HD)
-    middle = value + pair_sum(mm("te,de->td", mixed, w_out)) + rows[4]
-    normed_two, centred_two, factor_two = layer_norm(middle, rows[5], rows[6])
-    kept = (normed, centred, factor, queries, keyset, valueset, log_total, mixed)
-    return (middle, kept + (normed_two, centred_two, factor_two))
-
-
-def forward_up(w_up, up_bias, normed_two):
-    before = mm("td,df->tf", normed_two, w_up) + up_bias
-    hidden = (before * gelu_parts(before)[0]).astype(jnp.bfloat16)
-    return (before, hidden)
-
-
-def forward_down(w_down, rows, middle, hidden):
-    return middle + pair_sum(mm("tf,df->td", hidden, w_down)) + rows[7]
-
-
-def weight_grad(form, left, right, axis=1):
-    cuts = row_cuts(left.shape[axis])
-    return [
-        None
-        if cut is None
-        else mm(form, lax.slice_in_dim(left, cut[0], cut[1], axis=axis), right).astype(jnp.bfloat16)
-        for cut in cuts
-    ]
-
-
-def backward_down(w_down, kept, before, hidden, grad_out):
-    grad_branch = grad_out.astype(jnp.bfloat16)
-    grad_down = weight_grad("td,tf->df", grad_branch, hidden)
-    cdf, density = gelu_parts(before)
-    grad_before = mm("td,df->tf", grad_branch, w_down) * (cdf + before * density)
-    return (grad_down, grad_before.astype(jnp.bfloat16), jnp.sum(grad_before, 0))
-
-
-def backward_up(w_up, rows, kept, before_low, grad_out):
-    normed_two, centred_two, factor_two = kept[8:]
-    grad_up = weight_grad("td,tf->df", normed_two, before_low)
-    grad_normed_two = pair_sum(mm("tf,df->td", before_low, w_up))
-    grad_middle = grad_out + norm_backward(grad_normed_two, centred_two, factor_two, rows[5])
-    sums = [
-        jnp.sum(grad_middle, 0),
-        jnp.sum(grad_normed_two * centred_two, 0),
-        jnp.sum(grad_normed_two, 0),
-        jnp.sum(grad_out, 0),
-    ]
-    return (grad_up, grad_middle, sums)
-
-
-def backward_attention(w_qkv, w_out, rows, kept, grad_middle):
-    normed, centred, factor, queries, keyset, valueset, log_total, mixed = kept[:8]
-    tokens = grad_middle.shape[0]
-    heads = w_out.shape[1] // HD
-    split = (tokens, heads, HD)
+def column_sum(value):
+    return jnp.sum(value, 0, keepdims=True)
+
+
+def attention_forward(tokens, terms, bias_row, low, weights, rows, q_bias, v_bias):
+    pieces, counts = weights
+    size, depth = terms[0].shape
+    wide = pieces[0].shape[1]
+    groups = wide // 512
+    half = groups * 128
+    n_terms, n_pieces = len(terms), len(pieces)
+
+    def kernel(*refs):
+        term_refs, refs = refs[:n_terms], refs[n_terms:]
+        bias_ref, rows_ref, qb_ref, vb_ref = refs[:4]
+        piece_refs, refs = refs[4 : 4 + n_pieces], refs[4 + n_pieces :]
+        u_ref, n_ref, q_ref, k_ref, v_ref, p_ref, o_ref, part_ref = refs
+        value = term_refs[0][...].astype(F32)
+        for ref in term_refs[1:]:
+            value = value + ref[...].astype(F32)
+        if n_terms > 1:
+            value = value + bias_ref[...]
+        if low:
+            value = value.astype(BF).astype(F32)
+        u_ref[...] = value
+        centred, factor = center_scale(value)
+        n_ref[...] = (centred * rows_ref[0:1] + rows_ref[1:2]).astype(BF)
+        lane = lax.broadcasted_iota(jnp.int32, (size, 128), 1)
+        key_lane = lax.broadcasted_iota(jnp.int32, (size, size), 1)
+        normed = n_ref[...]
+        for g in range(groups):
+            at = slice(g * 128, (g + 1) * 128)
+            matrix = stack_rows(piece_refs, counts, slice(g * 512, g * 512 + 384))
+            projected = nn(normed, matrix)
+            q = (projected[:, :128] + qb_ref[:, at]).astype(BF)
+            k = projected[:, 128:256].astype(BF)
+            v = (projected[:, 256:384] + vb_ref[:, at]).astype(BF)
+            q_ref[:, at] = q
+            k_ref[:, at] = k
+            v_ref[:, at] = v
+            mixed = None
+            for h in range(2):
+                mine = (lane // HD) == h
+                scores = nt(jnp.where(mine, q, jnp.zeros_like(q)), k) * HD ** (-0.5)
+                scores = jnp.where(key_lane < tokens, scores, -1e30)
+                highest = jnp.max(scores, -1, keepdims=True)
+                exponent = jnp.exp(scores - highest)
+                inverse = 1.0 / jnp.sum(exponent, -1, keepdims=True)
+                soft = (exponent * inverse).astype(BF)
+                p_ref[2 * g + h] = soft
+                out = nn(soft, v)
+                mixed = out if h == 0 else jnp.where(mine, out, mixed)
+            o_ref[:, at] = mixed.astype(BF)
+        matrix = jnp.concatenate(
+            [stack_rows(piece_refs, counts, slice(g * 512 + 384, g * 512 + 512)) for g in range(groups)], 1
+        )
+        part_ref[...] = nt(o_ref[...], matrix).astype(BF)
+
+    outs = [shape((size, depth), F32), shape((size, depth))] + [shape((size, half))] * 3
+    outs += [shape((2 * groups, size, size)), shape((size, half)), shape((size, depth))]
+    flops = 2 * size * depth * wide + 8 * size * size * half
+    return run(kernel, outs, [*terms, bias_row, rows, q_bias, v_bias, *pieces], flops)
+
+
+def up_forward(terms, weights, rows, up_bias):
+    pieces, counts = weights
+    size, depth = terms[0].shape
+    wide = pieces[0].shape[1]
+
+    def kernel(*refs):
+        u_ref, own_ref, far_ref, rows_ref, bias_ref = refs[:5]
+        piece_refs = refs[5 : 5 + len(pieces)]
+        mid_ref, n_ref, slope_ref, hidden_ref = refs[5 + len(pieces) :]
+        value = u_ref[...] + own_ref[...].astype(F32) + far_ref[...].astype(F32) + rows_ref[4:5]
+        mid_ref[...] = value
+        centred, factor = center_scale(value)
+        n_ref[...] = (centred * rows_ref[5:6] + rows_ref[6:7]).astype(BF)
+        step = 512
+        for at in range(0, wide, step):
+            cols = slice(at, at + step)
+            before = nn(n_ref[...], stack_rows(piece_refs, counts, cols)) + bias_ref[:, cols]
+            cdf = 0.5 * (1.0 + lax.erf(before * 0.7071067811865476))
+            density = jnp.exp(-0.5 * before * before) * 0.3989422804014327
+            hidden_ref[:, cols] = (before * cdf).astype(BF)
+            slope_ref[:, cols] = (cdf + before * density).astype(BF)
+
+    outs = [shape((size, depth), F32), shape((size, depth)), shape((size, wide)), shape((size, wide))]
+    return run(kernel, outs, [*terms, rows, up_bias, *pieces], 2 * size * depth * wide)
+
+
+def contract_wide(left, weights):
+    pieces, counts = weights
+    size, wide = left.shape
+    depth = sum(counts)
+
+    def kernel(*refs):
+        left_ref, piece_refs, out_ref = refs[0], refs[1:-1], refs[-1]
+        matrix = stack_rows(piece_refs, counts, slice(0, wide))
+        out_ref[...] = nt(left_ref[...], matrix).astype(BF)
+
+    return run(kernel, [shape((size, depth))], [left, *pieces], 2 * size * depth * wide)[0]
+
+
+def weight_outs(depth, wide):
+    cuts = [c for c in row_cuts(depth) if c is not None]
+    return cuts, [shape((c[1] - c[0], wide)) for c in cuts]
+
+
+def fill(grads):
+    return (list(grads) + [None, None])[:4]
+
+
+def down_backward(grad_out, hidden, slope, weights):
+    pieces, counts = weights
+    size, depth = grad_out.shape
+    wide = hidden.shape[1]
+    cuts, grad_outs = weight_outs(depth, wide)
+
+    def kernel(*refs):
+        g_ref, hidden_ref, slope_ref = refs[:3]
+        piece_refs, refs = refs[3 : 3 + len(pieces)], refs[3 + len(pieces) :]
+        low_ref, sum_ref, bias_ref = refs[:3]
+        sum_ref[...] = column_sum(g_ref[...])
+        branch = g_ref[...].astype(BF)
+        for cut, ref in zip(cuts, refs[3:]):
+            ref[...] = tn(branch[:, cut[0] : cut[1]], hidden_ref[...]).astype(BF)
+        step = 512
+        for at in range(0, wide, step):
+            cols = slice(at, at + step)
+            back = nn(branch, stack_rows(piece_refs, counts, cols)) * slope_ref[:, cols].astype(F32)
+            bias_ref[:, cols] = column_sum(back)
+            low_ref[:, cols] = back.astype(BF)
+
+    outs = [shape((size, wide)), shape((1, depth), F32), shape((1, wide), F32)] + grad_outs
+    done = run(kernel, outs, [grad_out, hidden, slope, *pieces], 4 * size * depth * wide)
+    return done[0], done[1], done[2], fill(done[3:])
+
+
+def up_grad(normed, low):
+    size, depth = normed.shape
+    wide = low.shape[1]
+    cuts, outs = weight_outs(depth, wide)
+
+    def kernel(n_ref, low_ref, *refs):
+        for cut, ref in zip(cuts, refs):
+            ref[...] = tn(n_ref[:, cut[0] : cut[1]], low_ref[...]).astype(BF)
+
+    return fill(run(kernel, outs, [normed, low], 2 * size * depth * wide))
+
+
+def attention_backward(grad_out, own, far, middle, rows, saved, weights):
+    pieces, counts = weights
+    size, depth = grad_out.shape
+    wide = pieces[0].shape[1]
+    groups = wide // 512
+    half = groups * 128
     scale = HD ** (-0.5)
-    groups = w_qkv.shape[1]
-    grad_attended = grad_middle.astype(jnp.bfloat16)
-    grad_mixed = mm("td,de->te", grad_attended, w_out).astype(jnp.bfloat16).reshape(split)
-    query_heads, key_heads = queries.reshape(split), keyset.reshape(split)
-    soft = jnp.exp(mm("qhd,khd->hqk", query_heads, key_heads) * scale - log_total)
-    soft_low = soft.astype(jnp.bfloat16)
-    grad_values = mm("hqk,qhd->khd", soft_low, grad_mixed)
-    grad_soft = mm("qhd,khd->hqk", grad_mixed, valueset.reshape(split))
-    row_inner = jnp.sum(grad_soft * soft, -1, keepdims=True)
-    grad_scores = (soft * (grad_soft - row_inner)).astype(jnp.bfloat16)
-    grad_queries = mm("hqk,khd->qhd", grad_scores, key_heads) * scale
-    grad_keys = mm("hqk,qhd->khd", grad_scores, query_heads) * scale
-    parts = [grad_queries, grad_keys, grad_values]
-    parts = [part.astype(jnp.bfloat16).reshape(tokens, groups, -1) for part in parts]
-    stack_low = jnp.stack(parts, 2)
-    grad_normed = pair_sum(mm("tgce,dgce->td", stack_low, w_qkv))
-    grad_value = grad_middle + norm_backward(grad_normed, centred, factor, rows[0])
-    grad_qkv = weight_grad("td,tgce->dgce", normed, stack_low)
-    grad_out = weight_grad("td,te->de", grad_attended, mixed)
-    quads = []
-    for left, right in zip(grad_qkv, grad_out):
-        if left is None:
-            quads.append(None)
-            continue
-        right = right.reshape(left.shape[:2] + (1, -1))
-        quads.append(jnp.concatenate([left, right], 2).reshape(left.shape[0], -1))
-    sums = [
-        jnp.sum(grad_normed * centred, 0),
-        jnp.sum(grad_normed, 0),
-        jnp.sum(grad_queries, 0).reshape(-1),
-        jnp.sum(grad_values, 0).reshape(-1),
-    ]
-    return (quads, grad_value, sums)
+
+    def kernel(*refs):
+        g_ref, own_ref, far_ref, mid_ref, rows_ref, q_ref, k_ref, v_ref, p_ref, o_ref = refs[:10]
+        piece_refs, refs = refs[10 : 10 + len(pieces)], refs[10 + len(pieces) :]
+        dmid_ref, dz_ref, dq_ref, dk_ref, dv_ref, part_ref, sum_ref, qs_ref, vs_ref = refs
+        grad_normed = own_ref[...].astype(F32) + far_ref[...].astype(F32)
+        centred, factor = center_scale(mid_ref[...])
+        sum_ref[1:2] = column_sum(grad_normed * centred)
+        sum_ref[2:3] = column_sum(grad_normed)
+        dmid = g_ref[...] + norm_backward(grad_normed, centred, factor, rows_ref[5:6])
+        dmid_ref[...] = dmid
+        sum_ref[0:1] = column_sum(dmid)
+        dz_ref[...] = dmid.astype(BF)
+        lane = lax.broadcasted_iota(jnp.int32, (size, 128), 1)
+        for g in range(groups):
+            at = slice(g * 128, (g + 1) * 128)
+            matrix = stack_rows(piece_refs, counts, slice(g * 512 + 384, g * 512 + 512))
+            grad_mixed = nn(dz_ref[...], matrix).astype(BF)
+            q, k, v = q_ref[:, at], k_ref[:, at], v_ref[:, at]
+            inner = grad_mixed.astype(F32) * o_ref[:, at].astype(F32)
+            dq, dk, dv = None, None, None
+            for h in range(2):
+                mine = (lane // HD) == h
+                soft = p_ref[2 * g + h]
+                none = jnp.zeros_like(q)
+                do = jnp.where(mine, grad_mixed, none)
+                total = jnp.sum(jnp.where(mine, inner, 0.0), -1, keepdims=True)
+                grad_soft = nt(do, v)
+                grad_scores = (soft.astype(F32) * (grad_soft - total)).astype(BF)
+                new_q = nn(grad_scores, k)
+                new_k = tn(jnp.where(mine, q, none), grad_scores)
+                new_v = tn(do, soft)
+                dq = new_q if h == 0 else jnp.where(mine, new_q, dq)
+                dk = new_k if h == 0 else dk + new_k
+                dv = new_v if h == 0 else dv + new_v
+            dq, dk, dv = dq * scale, dk.T * scale, dv.T
+            qs_ref[:, at] = column_sum(dq)
+            vs_ref[:, at] = column_sum(dv)
+            dq_ref[:, at] = dq.astype(BF)
+            dk_ref[:, at] = dk.astype(BF)
+            dv_ref[:, at] = dv.astype(BF)
+        total = None
+        for g in range(groups):
+            at = slice(g * 128, (g + 1) * 128)
+            left = jnp.concatenate([dq_ref[:, at], dk_ref[:, at], dv_ref[:, at]], 1)
+            new = nt(left, stack_rows(piece_refs, counts, slice(g * 512, g * 512 + 384)))
+            total = new if g == 0 else total + new
+        part_ref[...] = total.astype(BF)
+
+    outs = [shape((size, depth), F32), shape((size, depth))] + [shape((size, half))] * 3
+    outs += [shape((size, depth)), shape((3, depth), F32)] + [shape((1, half), F32)] * 2
+    flops = 2 * size * depth * wide + 16 * size * size * half
+    return run(kernel, outs, [grad_out, own, far, middle, rows, *saved, *pieces], flops)
+
+
+def attention_grad(normed, dz, dq, dk, dv, mixed):
+    size, depth = normed.shape
+    groups = dq.shape[1] // 128
+    cuts, outs = weight_outs(depth, groups * 512)
+
+    def kernel(n_ref, dz_ref, dq_ref, dk_ref, dv_ref, o_ref, *refs):
+        for cut, ref in zip(cuts, refs):
+            rows = slice(cut[0], cut[1])
+            for g in range(groups):
+                at = slice(g * 128, (g + 1) * 128)
+                right = jnp.concatenate([dq_ref[:, at], dk_ref[:, at], dv_ref[:, at]], 1)
+                ref[:, g * 512 : g * 512 + 384] = tn(n_ref[:, rows], right).astype(BF)
+                ref[:, g * 512 + 384 : g * 512 + 512] = tn(dz_ref[:, rows], o_ref[:, at]).astype(BF)
+
+    flops = 2 * size * depth * groups * 512
+    return fill(run(kernel, outs, [normed, dz, dq, dk, dv, mixed], flops))
+
+
+def value_backward(dmid, own, far, value, rows, low):
+    size, depth = dmid.shape
+
+    def kernel(dmid_ref, own_ref, far_ref, u_ref, rows_ref, out_ref, sum_ref):
+        grad_normed = own_ref[...].astype(F32) + far_ref[...].astype(F32)
+        centred, factor = center_scale(u_ref[...])
+        sum_ref[0:1] = column_sum(grad_normed * centred)
+        sum_ref[1:2] = column_sum(grad_normed)
+        out = dmid_ref[...] + norm_backward(grad_normed, centred, factor, rows_ref[0:1])
+        if low:
+            out = out.astype(BF).astype(F32)
+        out_ref[...] = out
+
+    outs = [shape((size, depth), F32), shape((2, depth), F32)]
+    return run(kernel, outs, [dmid, own, far, value, rows], 20 * size * depth)
 
 
 def half_cols(core, whole, n_tensor):
@@ -361,11 +531,10 @@
         half = lax.all_to_all(half, "tensor", split_axis=0, concat_axis=2, tiled=True)[0]
         other = swap(half)
         both = [jnp.where(is_first, half, other), jnp.where(is_first, other, half)]
-        return relative(jnp.concatenate(both, 0)[:tokens], spot)
+        return relative(jnp.concatenate(both, 0), spot)
 
     def image_rows(image):
         image = absolute(image.astype(jnp.bfloat16), spot)
-        image = jnp.pad(image, ((0, pad), (0, 0)))
         half = jnp.where(is_first, image[:reach], image[reach:])
         half = lax.all_to_all(half[None], "tensor", split_axis=2, concat_axis=0, tiled=True)
         return half
@@ -381,18 +550,16 @@
         q_bias = half_cols(core, rows[2], n_tensor)
         v_bias = half_cols(core, rows[3], n_tensor)
         up_bias = half_cols(core, bias, n_tensor)
-        return (relative(rows, spot), q_bias, v_bias, up_bias)
+        return (relative(rows, spot), q_bias[None], v_bias[None], up_bias[None])
 
     value = whole_image(half_in).astype(jnp.float32)
 
     number = len(columns)
     cut = [mid + extra if k % 3 == 0 else mid for k in range(number)]
     halves, near, far = [None] * number, [None] * number, [None] * number
-    pieces = [None] * number
     params = [dict(), dict()]
-    state = value
     output = None
-    for r in range(number + 4):
+    for r in range(number + 3):
         tied = []
         if r < number:
             whole = gather_column(columns[r])
@@ -404,6 +571,7 @@
             far[r - 2] = exchange_two(*halves[r - 2], *near[r - 2])
             tied += far[r - 2]
         k = r - 3
+        ready = None
         if 0 <= k < number:
             layer, kind = k // 3, k % 3
             one = params[layer]
@@ -411,30 +579,37 @@
             if kind == 0:
                 blocks = [p.reshape((-1, mid + extra) + p.shape[1:]) for p in first]
                 one["small"] = small_of([p[:, mid:].reshape(-1, p.shape[-1]) for p in blocks])
-                first = [p[:, :mid].reshape(-1, p.shape[-1]) for p in blocks]
-            matrix = jnp.concatenate(first + second, 0)
+                if n_dp != 4:
+                    first = [p[:, :mid].reshape(-1, p.shape[-1]) for p in blocks]
+            pieces = first + second
+            counts = [mid if n_dp == 4 else p.shape[0] for p in pieces]
+            weights = (pieces, counts)
+            rows, q_bias, v_bias, up_bias = one["small"]
             if kind == 0:
-                quad = matrix.reshape(matrix.shape[0], n_tensor, 4, -1)
-                one["qkv"] = quad[:, :, :3]
-                one["out"] = quad[:, :, 3].reshape(quad.shape[0], -1)
-                rows, q_bias, v_bias, up_bias = one["small"]
-                state, one["kept"] = forward_attention(
-                    one["qkv"], one["out"], rows, q_bias, v_bias, state
+                one["qkvo"] = weights
+                terms = [value] if layer == 0 else [state, *pair]
+                bias_row = (rows if layer == 0 else params[0]["small"][0])[7:8]
+                done = attention_forward(
+                    tokens, terms, bias_row, layer == 1, weights, rows, q_bias, v_bias
                 )
+                one["u"], one["n1"], one["saved"], part = done[0], done[1], done[2:7], done[7]
+                pair = [part, swap(part)]
+                ready = pair
             elif kind == 1:
-                one["up"] = matrix
-                one["before"], one["hidden"] = forward_up(
-                    matrix, one["small"][3], one["kept"][8]
+                one["up"] = weights
+                one["mid"], one["n2"], one["slope"], one["hidden"] = up_forward(
+                    [one["u"], *pair], weights, rows, up_bias
                 )
+                ready = [one["hidden"]]
             else:
-                one["down"] = matrix
-                state = forward_down(matrix, one["small"][0], state, one["hidden"])
-                if layer == 0:
-                    state = state.astype(jnp.bfloat16).astype(jnp.float32)
+                one["down"] = weights
+                part = contract_wide(one["hidden"], weights)
+                state = one["mid"]
+                pair = [part, swap(part)]
+                ready = pair
         if r < number + 2:
-            extras = [state] if r >= 3 else []
-            if r >= 3 and (r - 3) % 3 == 1:
-                extras.append(params[(r - 3) // 3]["hidden"])
+            extras = list(ready) if ready else []
+            count = len(extras)
             if r == 5:
                 extras.append(half_cot)
             if r + 1 < number:
@@ -444,10 +619,10 @@
                 columns[r + 1] = done.pop()
             if r == 5:
                 half_cot = done.pop()
-            if r >= 3 and (r - 3) % 3 == 1:
-                params[(r - 3) // 3]["hidden"] = done.pop()
-            if r >= 3:
-                state = done.pop()
+            if count == 2:
+                pair = done[-2:]
+            elif count == 1:
+                one["hidden"] = done[-1]
             at = 0
             if r < number:
                 halves[r] = (done[0][: cut[r]], done[0][cut[r] :])
@@ -456,11 +631,12 @@
                 near[r - 1] = done[at : at + 2]
                 at += 2
             if 0 <= r - 2 < number:
-                far[r - 2] = done[at:]
+                far[r - 2] = done[at : at + len(far[r - 2])]
         if r == 5:
             cotangent = whole_image(half_cot).astype(jnp.float32) * live
-    output = state * live
-    out_rows = image_rows(output)
+    last_rows = params[1]["small"][0]
+    output = state + pair[0].astype(jnp.float32) + pair[1].astype(jnp.float32) + last_rows[7:8]
+    out_rows = image_rows(output * live)
 
     grads, got, moved, settled = [None] * number, [None] * number, [None] * number, [None] * number
     sums = [dict(), dict()]
@@ -480,21 +656,23 @@
             settled[r - 3] = scatter_column(*moved[r - 3])
             tied.append(settled[r - 3])
         if kind == 2:
-            grads[r], low, total["up_bias"] = backward_down(
-                one["down"], one["kept"], one["before"], one["hidden"], grad
+            low, total["out"], total["up_bias"], grads[r] = down_backward(
+                grad, one["hidden"], one["slope"], one["down"]
             )
             carry = low
         elif kind == 1:
-            grads[r], middle, total["two"] = backward_up(
-                one["up"], rows, one["kept"], low, grad
+            part = contract_wide(low, one["up"])
+            grads[r] = up_grad(one["n2"], low)
+            pair = [part, swap(part)]
+            done = attention_backward(
+                grad, *pair, one["mid"], rows, one["saved"], one["qkvo"]
             )
-            carry = middle
+            dmid, dz, dq, dk, dv, part, total["mid"], total["q"], total["v"] = done
+            carry = part
         else:
-            grads[r], grad, total["one"] = backward_attention(
-                one["qkv"], one["out"], rows, one["kept"], middle
-            )
-            if layer == 1:
-                grad = grad.astype(jnp.bfloat16).astype(jnp.float32)
+            pair = [part, swap(part)]
+            grads[r] = attention_grad(one["n1"], dz, dq, dk, dv, one["saved"][4])
+            grad, total["one"] = value_backward(dmid, *pair, one["u"], rows, layer == 1)
             carry = grad
         if r < number - 1:
             new = [g for g in grads[r] if g is not None]
@@ -502,10 +680,10 @@
             if kind == 2:
                 low = done[0]
             elif kind == 1:
-                middle = done[0]
+                part = done[0]
             else:
                 grad = done[0]
-            grads[r] = (done[1 : 1 + len(new)] + [None, None])[:4]
+            grads[r] = fill(done[1 : 1 + len(new)])
             done = done[1 + len(new) :]
             if r >= 1:
                 got[r - 1], done = done[:2], done[2:]
@@ -520,20 +698,26 @@
     packed = []
     for layer in range(2):
         total = sums[layer]
-        full = [total["one"][0], total["one"][1]] + total["two"]
-        full = absolute(jnp.where(core == layer, jnp.stack(full), 0.0), spot)
-        q_row = spread_cols(core, total["one"][2], n_tensor)
-        v_row = spread_cols(core, total["one"][3], n_tensor)
-        up_row = spread_cols(core, total["up_bias"], n_tensor)
+        full = jnp.concatenate([total["one"], total["mid"], total["out"]], 0)
+        full = absolute(jnp.where(core == layer, full, 0.0), spot)
+        q_row = spread_cols(core, total["q"][0], n_tensor)
+        v_row = spread_cols(core, total["v"][0], n_tensor)
+        up_row = spread_cols(core, total["up_bias"][0], n_tensor)
         rows = jnp.concatenate([full[:2], q_row[None], v_row[None], full[2:]], 0)
         rows = rows.reshape(8, n_tensor, n_dp, -1).transpose(2, 1, 0, 3).reshape(n_dp, n_tensor, -1)
         up_row = up_row.reshape(n_tensor, n_dp, -1).transpose(1, 0, 2)
         packed.append(jnp.concatenate([rows, up_row], -1))
     ours = jnp.where(is_first, packed[0], packed[1])
     other = swap(jnp.where(is_first, packed[1], packed[0]))
-    little = (ours + other).astype(jnp.bfloat16).reshape(n_dp * n_tensor, -1)
-    little = lax.psum_scatter(little, ("dp", "tensor"), scatter_dimension=0, tiled=True)[0]
-    little = little.astype(jnp.float32)
+    little = (ours + other).astype(jnp.bfloat16)
+    room = jnp.zeros((n_dp, n_tensor, extra * wide - small_size), little.dtype)
+    little = jnp.concatenate([little, room], -1).reshape(n_dp, n_tensor, extra, wide)
+    little = by_arrival(little.transpose(0, 2, 1, 3).reshape(n_dp, extra, -1), spot)
+    if n_dp != 4:
+        little = lax.psum_scatter(little, "dp", scatter_dimension=0, tiled=True)[0]
+    else:
+        little = add(little[:2], swap_x(little[2:])).astype(jnp.bfloat16)
+        little = add(little[0], swap_y(little[1])).astype(jnp.bfloat16)
 
     last = number - 1
     got[last] = scatter_one(*grads[last][:2])
@@ -542,7 +726,13 @@
             moved[k] = scatter_two(*grads[k][2:], got[k])
     for k in range(number):
         if settled[k] is None:
-            settled[k] = scatter_column(*moved[k])
+            stay, come = moved[k]
+            if k == last:
+                stay = [add(s, c).astype(jnp.bfloat16) for s, c in zip(stay, come)] if come else stay
+                stay, come = [*stay, little], []
+            settled[k] = scatter_column(stay, come)
+    little = settled[last][depth:].reshape(-1).astype(jnp.float32)
+    settled[last] = settled[last][:depth]
     grad_vectors = little[:n_vec].reshape(vectors.shape)
     grad_bias = little[n_vec:small_size].reshape(fc1_bias.shape)
 

time: 1010 us -> 824 us (0.82)
  Pallas kernels: 0.02 us -> 187 us
  matrix products: 185 us -> 0 us
  local copies, waits for them, and re-layouts: 274 us -> 135 us
  other arithmetic: 180 us -> 112 us
  waiting for transfers between devices: 164 us -> 232 us
  blocking collectives: 62.8 us -> 31.6 us
  starting transfers between devices: 112 us -> 99.6 us
    pallas_call x0 -> x18, Pallas kernels: none -> 187 us  [run(): pl.pallas_call(kernel, out_shape=list(outs), in_specs=[block] * len(ins),...]
    dot_general x60 -> x0, matrix products: 185 us -> none  [mm(): return jnp.einsum(form, left, right, preferred_element_type=jnp.float32)]
    ppermute x30 -> x31, waiting for transfers between devices: 46.1 us -> 114 us  [swap_y(): return lax.ppermute(value, 'dp', [(i, i ^ 2) for i in range(n)])]
    unnamed x1 -> x0, blocking collectives: 62.8 us -> none
    unnamed x441 -> x298, local copies, waits for them, and re-layouts: 96.8 us -> 48.5 us
    slice x26 -> x4, local copies, waits for them, and re-layouts: 34.6 us -> 1.52 us  [the longest x2 1.44 us: small_of(): bias = one[:, :, n_vec:small_size].transpose(1, 0, 2).reshape(-1)]
    concatenate x22 -> x5, local copies, waits for them, and re-layouts: 32.7 us -> 0.15 us  [the longest x4 0.08 us: body(): full = jnp.concatenate([total['one'], total['mid'], total['out']], 0)]
    all_to_all x0 -> x1, blocking collectives: none -> 31.6 us  [whole_image(): lax.all_to_all(half, 'tensor', split_axis=0, concat_axis=2, tiled=True)[0]]
  transfers between devices with their start and end apart: 93 -> 94, of which waited for: 28 -> 36; matrix products, arithmetic and copies ran while one was open for 47% -> 24% of each run, Pallas kernels for 0% -> 22%
where the time goes in v4:
time: 824 us; the launch traced here: 815 us
  waiting for transfers between devices  232 us (28%)
  Pallas kernels  187 us (23%)
  local copies, waits for them, and re-layouts  135 us (16%)
  other arithmetic  112 us (14%)
  starting transfers between devices  99.6 us (12%)
  blocking collectives  31.6 us (4%)
  between operations  17.2 us (2%)
    pallas_call x18, Pallas kernels, run(): pl.pallas_call(kernel, out_shape=list(outs), in_specs=[block] * len(ins),...  187 us
    ppermute x31, waiting for transfers between devices, swap_y(): return lax.ppermute(value, 'dp', [(i, i ^ 2) for i in range(n)])  114 us
    ppermute x31, waiting for transfers between devices, swap_x(): return lax.ppermute(value, 'dp', [(i, i ^ 1) for i in range(n)])  78.8 us
    unnamed x298, local copies, waits for them, and re-layouts  48.5 us
    ppermute x17, starting transfers between devices, swap(): return lax.ppermute(value, 'section', [(0, 1), (1, 0)])  37.3 us
    all_to_all x1, blocking collectives, whole_image(): lax.all_to_all(half, 'tensor', split_axis=0, concat_axis=2, tiled=True)[0]  31.6 us
    convert_element_type x12, other arithmetic, scatter_two(): come.append(far(add(keep[half:], new[half:]).astype(jnp.bfloat16)))  26.1 us
    ppermute x31, starting transfers between devices, swap_x(): return lax.ppermute(value, 'dp', [(i, i ^ 1) for i in range(n)])  24 us
  transfers between devices with their start and end apart: 94, of which 36 were waited for; matrix products, arithmetic and copies ran while one was open for 24% of the time, Pallas kernels for 22%

profile of v4, /device:TPU:1, one launch (start us, length us, event | category | flops | bytes accessed | tf_op | source)
XLA Modules:
  0.0 814.8 jit_solution(14538823435938473970)
XLA Ops:
  18.3 31.6 %all_to_all.48 = bf16[4,296,256]{2,1,0:T(8,128)(2,1)S(1)} all-to-all(bf16[4,296,256]{2,1,0:T(8,128)(2,1)S(1)} %get-tuple-element.412), channel_id=1, replica_groups=mesh['section'=2,'dp'=4,'tensor'=4] {'tensor'}, dimensions={0} | all-to-all | bytes 1212416 | tf_op jit(solution)/shard_map/all_to_all | solution.py:531
  69.8 9.3 %collective-permute-done.2.refs_2_ = bf16[128,2048]{1,0:T(8,128)(2,1)S(1)} collective-permute-done((bf16[128,2048]{1,0:T(8,128)(2,1)}, bf16[128,2048]{1,0:T(8,128)(2,1)S(1)}, u32[]{:S(2)}, u32[]{:S(2)}) %collective-permute-start.2) | collective-permute-done | bytes 524320 | tf_op jit(solution)/shard_map/ppermute | solution.py:23
  144.9 15.6 %shard_map.138 = (f32[592,1024]{1,0:T(8,128)}, bf16[592,1024]{1,0:T(8,128)(2,1)}, bf16[592,512]{1,0:T(8,128)(2,1)}, bf16[592,512]{1,0:T(8,128)(2,1)}, bf16[592,5...) custom-call(f32[592,1024]{1,0:T(8,128)} %maximum_convert_fusion.refs_0_, ...), custom_call_target="tpu_custom_call" | custom-call | flops 3918528512 | bytes 19804160 | tf_op jit(solution)/shard_map/pallas_call | solution.py:174
  166.4 9.7 %collective-permute-done.11.refs_3_ = bf16[128,2048]{1,0:T(8,128)(2,1)S(1)} collective-permute-done((bf16[128,2048]{1,0:T(8,128)(2,1)S(1)}, bf16[128,2048]{1,0:T(8,128)(2,1)S(1)}, u32[]{:S(2)}, u32[]{:S(2)}) %collective-permute-start.11) | collective-permute-done | bytes 524320 | tf_op jit(solution)/shard_map/ppermute | solution.py:23
  178.5 9.8 %collective-permute-done.9.refs_1_ = bf16[128,2048]{1,0:T(8,128)(2,1)} collective-permute-done((bf16[128,2048]{1,0:T(8,128)(2,1)}, bf16[128,2048]{1,0:T(8,128)(2,1)}, u32[]{:S(2)}, u32[]{:S(2)}) %collective-permute-start.9) | collective-permute-done | bytes 524320 | tf_op jit(solution)/shard_map/ppermute | solution.py:28
  188.3 10.3 %collective-permute-done.12.refs_4_ = bf16[128,2048]{1,0:T(8,128)(2,1)S(1)} collective-permute-done((bf16[128,2048]{1,0:T(8,128)(2,1)S(1)}, bf16[128,2048]{1,0:T(8,128)(2,1)S(1)}, u32[]{:S(2)}, u32[]{:S(2)}) %collective-permute-start.12) | collective-permute-done | bytes 524320 | tf_op jit(solution)/shard_map/ppermute | solution.py:23
  215.2 10.0 %shard_map.140 = (f32[592,1024]{1,0:T(8,128)}, bf16[592,1024]{1,0:T(8,128)(2,1)}, bf16[592,2048]{1,0:T(8,128)(2,1)}, bf16[592,2048]{1,0:T(8,128)(2,1)}) custom-call(f32[592,1024]{1,0:T(8,128)} %get-tuple-element.205.refs_0_.u_ref, bf16[592,1024]{1,0:T(8,128)(2,1)} %get-tuple-element.206.refs_1_, bf16[592,1024]{1,0:T(8,128)(2,1)} %get-tuple-element.207.refs_2_, ...), custom_call_target="tpu_custom_call" | custom-call | flops 2483027968 | bytes 17571840 | tf_op jit(solution)/shard_map/pallas_call | solution.py:174
  261.1 10.0 %collective-permute-done.24.refs_1_ = bf16[128,2048]{1,0:T(8,128)(2,1)} collective-permute-done((bf16[128,2048]{1,0:T(8,128)(2,1)}, bf16[128,2048]{1,0:T(8,128)(2,1)}, u32[]{:S(2)}, u32[]{:S(2)}) %collective-permute-start.24) | collective-permute-done | bytes 524320 | tf_op jit(solution)/shard_map/ppermute | solution.py:28
  272.3 10.0 %collective-permute-done.29.refs_6_ = bf16[128,2048]{1,0:T(8,128)(2,1)S(1)} collective-permute-done((bf16[128,2048]{1,0:T(8,128)(2,1)S(1)}, bf16[128,2048]{1,0:T(8,128)(2,1)S(1)}, u32[]{:S(2)}, u32[]{:S(2)}) %collective-permute-start.29) | collective-permute-done | bytes 524320 | tf_op jit(solution)/shard_map/ppermute | solution.py:28
  292.8 17.3 %shard_map.144 = (f32[592,1024]{1,0:T(8,128)}, bf16[592,1024]{1,0:T(8,128)(2,1)}, bf16[592,512]{1,0:T(8,128)(2,1)}, bf16[592,512]{1,0:T(8,128)(2,1)}, bf16[592,5...) custom-call(f32[592,1024]{1,0:T(8,128)} %get-tuple-element.226.refs_0_.refs, ...), custom_call_target="tpu_custom_call" | custom-call | flops 3918528512 | bytes 22228992 | tf_op jit(solution)/shard_map/pallas_call | solution.py:174
  321.3 11.2 %all-to-all-done.1 = bf16[4,296,256]{2,1,0:T(8,128)(2,1)} async-done(((bf16[4,296,256]{2,1,0:T(8,128)(2,1)}), bf16[4,296,256]{2,1,0:T(8,128)(2,1)}, u32[]{:S(2)}, u32[]{:S(2)}) %all-to-all-start.1) | async-done | bytes 606240 | tf_op jit(solution)/shard_map/all_to_all | solution.py:531
  346.5 10.8 %shard_map.146 = (f32[592,1024]{1,0:T(8,128)}, bf16[592,1024]{1,0:T(8,128)(2,1)}, bf16[592,2048]{1,0:T(8,128)(2,1)}, bf16[592,2048]{1,0:T(8,128)(2,1)}) custom-call(f32[592,1024]{1,0:T(8,128)} %get-tuple-element.236.refs_0_.u_ref, bf16[592,1024]{1,0:T(8,128)(2,1)} %get-tuple-element.237.refs_1_, bf16[592,1024]{1,0:T(8,128)(2,1)} %get-tuple-element.238.refs_2_, ...), custom_call_target="tpu_custom_call" | custom-call | flops 2483027968 | bytes 17571840 | tf_op jit(solution)/shard_map/pallas_call | solution.py:174
  394.8 11.9 %shard_map.148 = (bf16[592,2048]{1,0:T(8,128)(2,1)}, f32[1,1024]{1,0:T(1,128)S(1)}, f32[1,2048]{1,0:T(1,128)S(1)}, bf16[256,2048]{1,0:T(8,128)(2,1)}, bf16[256,2...) custom-call(f32[592,1024]{1,0:T(8,128)} %convert_multiply_fusion.refs_0_, ...), custom_call_target="tpu_custom_call" | custom-call | flops 4966055936 | bytes 18100224 | tf_op jit(solution)/shard_map/pallas_call | solution.py:174
  437.6 21.5 %shard_map.151 = (f32[592,1024]{1,0:T(8,128)}, bf16[592,1024]{1,0:T(8,128)(2,1)}, bf16[592,512]{1,0:T(8,128)(2,1)}, bf16[592,512]{1,0:T(8,128)(2,1)}, bf16[592,5...) custom-call(f32[592,1024]{1,0:T(8,128)} %convert_multiply_fusion.ref, ...), custom_call_target="tpu_custom_call" | custom-call | flops 5354029056 | bytes 26480640 | tf_op jit(solution)/shard_map/pallas_call | solution.py:174
  475.9 7.8 shard_map.155
  510.2 11.8 %shard_map.157 = (bf16[592,2048]{1,0:T(8,128)(2,1)}, f32[1,1024]{1,0:T(1,128)S(1)}, f32[1,2048]{1,0:T(1,128)S(1)}, bf16[256,2048]{1,0:T(8,128)(2,1)}, bf16[256,2...) custom-call(f32[592,1024]{1,0:T(8,128)} %get-tuple-element.288.refs_0_, ...), custom_call_target="tpu_custom_call" | custom-call | flops 4966055936 | bytes 18100224 | tf_op jit(solution)/shard_map/pallas_call | solution.py:174
  522.0 14.2 %collective-permute-done.53.refs_9_ = bf16[128,2048]{1,0:T(8,128)(2,1)} collective-permute-done((bf16[128,2048]{1,0:T(8,128)(2,1)}, bf16[128,2048]{1,0:T(8,128)(2,1)}, u32[]{:S(2)}, u32[]{:S(2)}) %collective-permute-start.53) | collective-permute-done | bytes 524320 | tf_op jit(solution)/shard_map/ppermute | solution.py:28
  569.4 21.6 %shard_map.160 = (f32[592,1024]{1,0:T(8,128)}, bf16[592,1024]{1,0:T(8,128)(2,1)}, bf16[592,512]{1,0:T(8,128)(2,1)}, bf16[592,512]{1,0:T(8,128)(2,1)}, bf16[592,5...) custom-call(f32[592,1024]{1,0:T(8,128)} %get-tuple-element.288.refs_, ...), custom_call_target="tpu_custom_call" | custom-call | flops 5354029056 | bytes 26480640 | tf_op jit(solution)/shard_map/pallas_call | solution.py:174
  598.8 8.0 collective-permute-done.77
  609.9 21.2 %collective-permute-done.73 = bf16[256,2048]{1,0:T(8,128)(2,1)} collective-permute-done((bf16[256,2048]{1,0:T(8,128)(2,1)S(1)}, bf16[256,2048]{1,0:T(8,128)(2,1)}, u32[]{:S(2)}, u32[]{:S(2)}) %collective-permute-start.73) | collective-permute-done | bytes 1048608 | tf_op jit(solution)/shard_map/ppermute | solution.py:28
  636.8 7.8 collective-permute-done.74
  651.1 7.8 shard_map.165
  667.2 13.2 %collective-permute-done.65 = bf16[256,2048]{1,0:T(8,128)(2,1)} collective-permute-done((bf16[256,2048]{1,0:T(8,128)(2,1)}, bf16[256,2048]{1,0:T(8,128)(2,1)}, u32[]{:S(2)}, u32[]{:S(2)}) %collective-permute-start.65) | collective-permute-done | bytes 1048608 | tf_op jit(solution)/shard_map/ppermute | solution.py:28
  762.2 13.9 %all-to-all-done.3 = bf16[4,2,37888]{2,1,0:T(2,128)(2,1)S(1)} async-done(((bf16[4,2,37888]{2,1,0:T(2,128)(2,1)}), bf16[4,2,37888]{2,1,0:T(2,128)(2,1)S(1)}, u32[]{:S(2)}, u32[]{:S(2)}) %all-to-all-start.3) | async-done | bytes 606240 | tf_op jit(solution)/shard_map/all_to_all | solution.py:539
  (757 shorter events, 481.3 us)
Async XLA Ops:
  7.2 51.7 %all-gather.7.cloned.1.call-start = ((), (), s32[]{:S(2)}) async-start(), calls=%async_computation.10 | async-start | bytes 1392640 | tf_op jit(solution)/shard_map/all_gather | solution.py:49
  15.7 71.4 %all-gather.9.cloned.1.call-start = ((), (), s32[]{:S(2)}) async-start(), calls=%async_computation.11 | async-start | bytes 1310720 | tf_op jit(solution)/shard_map/all_gather | solution.py:49
  58.9 78.0 %all-gather.11.cloned.1.call-start = ((), (), s32[]{:S(2)}) async-start(), calls=%async_computation.12 | async-start | bytes 1310720 | tf_op jit(solution)/shard_map/all_gather | solution.py:49
  87.2 113.0 %all-gather.13.cloned.1.call-start = ((), (), s32[]{:S(2)}) async-start(), calls=%async_computation.13 | async-start | bytes 1392640 | tf_op jit(solution)/shard_map/all_gather | solution.py:49
  142.8 98.4 %all-gather.15.cloned.1.call-start = ((), (), s32[]{:S(2)}) async-start(), calls=%async_computation.14 | async-start | bytes 1310720 | tf_op jit(solution)/shard_map/all_gather | solution.py:49
  160.5 39.7 %collective-permute-start.17 = (bf16[592,1024]{1,0:T(8,128)(2,1)}, bf16[592,1024]{1,0:T(8,128)(2,1)}, u32[]{:S(2)}, u32[]{:S(2)}) collective-permute-start(bf16[592,1024]{1,0:T(8,128)(2,1)} %get-tuple-element.200.refs_7_), channel_id=1, source_target_pairs={{0,16},{16,0},{1,17},{17,1},{2,18},{18,2},{3,19},{19,3},{4,20},{20... | collective-permute-start | bytes 3637256 | tf_op jit(solution)/shard_map/ppermute | solution.py:13
  200.2 84.2 %all-gather.17.cloned.1.call-start = ((), (), s32[]{:S(2)}) async-start(), calls=%async_computation.15 | async-start | bytes 1310720 | tf_op jit(solution)/shard_map/all_gather | solution.py:49
  271.1 49.1 %collective-permute-start.35 = (bf16[128,2048]{1,0:T(8,128)(2,1)}, bf16[128,2048]{1,0:T(8,128)(2,1)}, u32[]{:S(2)}, u32[]{:S(2)}) collective-permute-start(bf16[128,2048]{1,0:T(8,128)(2,1)} %get-tuple-element.438.refs_5_.refs_1_), channel_id=1, source_target_pairs={{0,4},{4,0},{8,12},{12,8},{1,5},{5,1},{9,13},{13,9},{2,6},{6,2},{1... | collective-permute-start | bytes 1572872 | tf_op jit(solution)/shard_map/ppermute | solution.py:23
  271.8 49.3 %collective-permute-start.37 = (bf16[128,2048]{1,0:T(8,128)(2,1)}, bf16[128,2048]{1,0:T(8,128)(2,1)}, u32[]{:S(2)}, u32[]{:S(2)}) collective-permute-start(bf16[128,2048]{1,0:T(8,128)(2,1)} %get-tuple-element.437.refs_9_.refs_5_), channel_id=1, source_target_pairs={{0,8},{4,12},{8,0},{12,4},{1,9},{5,13},{9,1},{13,5},{2,10},{6,14},... | collective-permute-start | bytes 1572872 | tf_op jit(solution)/shard_map/ppermute | solution.py:28
  316.0 220.2 %reduce-scatter.7.cloned.1.call-start = ((), (), s32[]{:S(2)}) async-start(), calls=%async_computation.16 | async-start | bytes 1310720 | tf_op jit(solution)/shard_map/reduce_scatter | solution.py:105
  337.5 47.9 %collective-permute-start.32 = (bf16[128,2048]{1,0:T(8,128)(2,1)}, bf16[128,2048]{1,0:T(8,128)(2,1)}, u32[]{:S(2)}, u32[]{:S(2)}) collective-permute-start(bf16[128,2048]{1,0:T(8,128)(2,1)} %get-tuple-element.436.refs_3_.refs_1_), channel_id=1, source_target_pairs={{0,4},{4,0},{8,12},{12,8},{1,5},{5,1},{9,13},{13,9},{2,6},{6,2},{1... | collective-permute-start | bytes 1572872 | tf_op jit(solution)/shard_map/ppermute | solution.py:23
  344.4 41.0 %collective-permute-start.41 = (bf16[128,2048]{1,0:T(8,128)(2,1)}, bf16[128,2048]{1,0:T(8,128)(2,1)}, u32[]{:S(2)}, u32[]{:S(2)}) collective-permute-start(bf16[128,2048]{1,0:T(8,128)(2,1)} %get-tuple-element.435.refs_7_.refs_5_), channel_id=1, source_target_pairs={{0,8},{4,12},{8,0},{12,4},{1,9},{5,13},{9,1},{13,5},{2,10},{6,14},... | collective-permute-start | bytes 1572872 | tf_op jit(solution)/shard_map/ppermute | solution.py:28
  344.6 40.9 %collective-permute-start.40 = (bf16[128,2048]{1,0:T(8,128)(2,1)}, bf16[128,2048]{1,0:T(8,128)(2,1)}, u32[]{:S(2)}, u32[]{:S(2)}) collective-permute-start(bf16[128,2048]{1,0:T(8,128)(2,1)} %get-tuple-element.234.refs_4_.refs_2_), channel_id=1, source_target_pairs={{0,4},{4,0},{8,12},{12,8},{1,5},{5,1},{9,13},{13,9},{2,6},{6,2},{1... | collective-permute-start | bytes 1572872 | tf_op jit(solution)/shard_map/ppermute | solution.py:23
  345.2 40.2 %collective-permute-start.42 = (bf16[128,2048]{1,0:T(8,128)(2,1)}, bf16[128,2048]{1,0:T(8,128)(2,1)}, u32[]{:S(2)}, u32[]{:S(2)}) collective-permute-start(bf16[128,2048]{1,0:T(8,128)(2,1)} %get-tuple-element.235.refs_8_.refs_6_), channel_id=1, source_target_pairs={{0,8},{4,12},{8,0},{12,4},{1,9},{5,13},{9,1},{13,5},{2,10},{6,14},... | collective-permute-start | bytes 1572872 | tf_op jit(solution)/shard_map/ppermute | solution.py:28
  413.3 45.8 %collective-permute-start.44 = (bf16[256,2048]{1,0:T(8,128)(2,1)}, bf16[256,2048]{1,0:T(8,128)(2,1)}, u32[]{:S(2)}, u32[]{:S(2)}) collective-permute-start(bf16[256,2048]{1,0:T(8,128)(2,1)} %get-tuple-element.269), channel_id=1, source_target_pairs={{0,4},{4,0},{8,12},{12,8},{1,5},{5,1},{9,13},{13,9},{2,6},{6,2},{1... | collective-permute-start | bytes 3145736 | tf_op jit(solution)/shard_map/ppermute | solution.py:23
  414.2 44.9 %collective-permute-start.45 = (bf16[256,2048]{1,0:T(8,128)(2,1)}, bf16[256,2048]{1,0:T(8,128)(2,1)}, u32[]{:S(2)}, u32[]{:S(2)}) collective-permute-start(bf16[256,2048]{1,0:T(8,128)(2,1)} %get-tuple-element.270), channel_id=1, source_target_pairs={{0,8},{4,12},{8,0},{12,4},{1,9},{5,13},{9,1},{13,5},{2,10},{6,14},... | collective-permute-start | bytes 3145736 | tf_op jit(solution)/shard_map/ppermute | solution.py:28
  500.5 91.5 %reduce-scatter.9.cloned.1.call-start = ((), (), s32[]{:S(2)}) async-start(), calls=%async_computation.17 | async-start | bytes 1310720 | tf_op jit(solution)/shard_map/reduce_scatter | solution.py:105
  540.0 252.7 %reduce-scatter.17.cloned.1.call-start = ((), (), s32[]{:S(2)}) async-start(), calls=%async_computation.21 | async-start | bytes 1310720 | tf_op jit(solution)/shard_map/reduce_scatter | solution.py:105
  552.8 38.3 %collective-permute-start.56 = (bf16[256,2048]{1,0:T(8,128)(2,1)S(1)}, bf16[256,2048]{1,0:T(8,128)(2,1)S(1)}, u32[]{:S(2)}, u32[]{:S(2)}) collective-permute-start(bf16[256,2048]{1,0:T(8,128)(2,1)S(1)} %copy-done.126), channel_id=1, source_target_pairs={{0,4},{4,0},{8,12},{12,8},{1,5},{5,1},{9,13},{13,9},{2,6},{6,2},{1... | collective-permute-start | bytes 3145736 | tf_op jit(solution)/shard_map/ppermute | solution.py:23
  553.4 38.6 %collective-permute-start.57 = (bf16[256,2048]{1,0:T(8,128)(2,1)S(1)}, bf16[256,2048]{1,0:T(8,128)(2,1)}, u32[]{:S(2)}, u32[]{:S(2)}) collective-permute-start(bf16[256,2048]{1,0:T(8,128)(2,1)S(1)} %copy-done.127), channel_id=1, source_target_pairs={{0,8},{4,12},{8,0},{12,4},{1,9},{5,13},{9,1},{13,5},{2,10},{6,14},... | collective-permute-start | bytes 3145736 | tf_op jit(solution)/shard_map/ppermute | solution.py:28
  609.8 188.6 %reduce-scatter.15.cloned.1.call-start = ((), (), s32[]{:S(2)}) async-start(), calls=%async_computation.20 | async-start | bytes 1310720 | tf_op jit(solution)/shard_map/reduce_scatter | solution.py:105
  648.8 150.8 %reduce-scatter.13.cloned.1.call-start = ((), (), s32[]{:S(2)}) async-start(), calls=%async_computation.19 | async-start | bytes 1310720 | tf_op jit(solution)/shard_map/reduce_scatter | solution.py:105
  686.5 70.6 %collective-permute-start.64 = (bf16[128,2048]{1,0:T(8,128)(2,1)}, bf16[128,2048]{1,0:T(8,128)(2,1)}, u32[]{:S(2)}, u32[]{:S(2)}) collective-permute-start(bf16[128,2048]{1,0:T(8,128)(2,1)} %add_convert_fusion.18), channel_id=1, source_target_pairs={{0,8},{4,12},{8,0},{12,4},{1,9},{5,13},{9,1},{13,5},{2,10},{6,14},... | collective-permute-start | bytes 1572872 | tf_op jit(solution)/shard_map/ppermute | solution.py:28
  757.0 42.6 %reduce-scatter.11.cloned.1.call-start = ((), (), s32[]{:S(2)}) async-start(), calls=%async_computation.18 | async-start | bytes 1392640 | tf_op jit(solution)/shard_map/reduce_scatter | solution.py:105
  (206 other events, 2753.0 us)
Sparse Core Ops, SparseCore 0:
  15.8 42.9 all-gather.6
  60.4 26.6 all-gather.8
  89.3 27.4 all-gather.10
  142.9 29.0 all-gather.12
  200.4 26.7 all-gather.14
  242.1 29.2 all-gather.16
  500.6 28.5 reduce-scatter.6
  540.1 29.5 reduce-scatter.8
  609.9 31.6 reduce-scatter.16
  648.9 30.6 reduce-scatter.14
  684.3 31.9 reduce-scatter.12
  760.0 31.2 reduce-scatter.10

commit v5 on v4

--- a/solution.py
+++ b/solution.py
@@ -168,15 +168,14 @@
     return jax.ShapeDtypeStruct(dims, kind)
 
 
-def run(kernel, outs, ins, flops):
+def run(kernel, outs, ins):
     block = pl.BlockSpec(memory_space=pltpu.VMEM)
-    moved = sum(v.size * v.dtype.itemsize for v in list(ins) + list(outs))
     done = pl.pallas_call(
         kernel,
         out_shape=list(outs),
         in_specs=[block] * len(ins),
         out_specs=[block] * len(outs),
-        cost_estimate=pl.CostEstimate(flops=flops, bytes_accessed=moved, transcendentals=0),
+        cost_estimate=pl.CostEstimate(flops=1, bytes_accessed=1, transcendentals=0),
         compiler_params=pltpu.CompilerParams(vmem_limit_bytes=VMEM_BYTES),
     )(*ins)
     return list(done)
@@ -274,8 +273,7 @@
 
     outs = [shape((size, depth), F32), shape((size, depth))] + [shape((size, half))] * 3
     outs += [shape((2 * groups, size, size)), shape((size, half)), shape((size, depth))]
-    flops = 2 * size * depth * wide + 8 * size * size * half
-    return run(kernel, outs, [*terms, bias_row, rows, q_bias, v_bias, *pieces], flops)
+    return run(kernel, outs, [*terms, bias_row, rows, q_bias, v_bias, *pieces])
 
 
 def up_forward(terms, weights, rows, up_bias):
@@ -301,7 +299,7 @@
             slope_ref[:, cols] = (cdf + before * density).astype(BF)
 
     outs = [shape((size, depth), F32), shape((size, depth)), shape((size, wide)), shape((size, wide))]
-    return run(kernel, outs, [*terms, rows, up_bias, *pieces], 2 * size * depth * wide)
+    return run(kernel, outs, [*terms, rows, up_bias, *pieces])
 
 
 def contract_wide(left, weights):
@@ -314,7 +312,7 @@
         matrix = stack_rows(piece_refs, counts, slice(0, wide))
         out_ref[...] = nt(left_ref[...], matrix).astype(BF)
 
-    return run(kernel, [shape((size, depth))], [left, *pieces], 2 * size * depth * wide)[0]
+    return run(kernel, [shape((size, depth))], [left, *pieces])[0]
 
 
 def weight_outs(depth, wide):
@@ -348,7 +346,7 @@
             low_ref[:, cols] = back.astype(BF)
 
     outs = [shape((size, wide)), shape((1, depth), F32), shape((1, wide), F32)] + grad_outs
-    done = run(kernel, outs, [grad_out, hidden, slope, *pieces], 4 * size * depth * wide)
+    done = run(kernel, outs, [grad_out, hidden, slope, *pieces])
     return done[0], done[1], done[2], fill(done[3:])
 
 
@@ -361,7 +359,7 @@
         for cut, ref in zip(cuts, refs):
             ref[...] = tn(n_ref[:, cut[0] : cut[1]], low_ref[...]).astype(BF)
 
-    return fill(run(kernel, outs, [normed, low], 2 * size * depth * wide))
+    return fill(run(kernel, outs, [normed, low]))
 
 
 def attention_backward(grad_out, own, far, middle, rows, saved, weights):
@@ -422,8 +420,7 @@
 
     outs = [shape((size, depth), F32), shape((size, depth))] + [shape((size, half))] * 3
     outs += [shape((size, depth)), shape((3, depth), F32)] + [shape((1, half), F32)] * 2
-    flops = 2 * size * depth * wide + 16 * size * size * half
-    return run(kernel, outs, [grad_out, own, far, middle, rows, *saved, *pieces], flops)
+    return run(kernel, outs, [grad_out, own, far, middle, rows, *saved, *pieces])
 
 
 def attention_grad(normed, dz, dq, dk, dv, mixed):
@@ -440,8 +437,7 @@
                 ref[:, g * 512 : g * 512 + 384] = tn(n_ref[:, rows], right).astype(BF)
                 ref[:, g * 512 + 384 : g * 512 + 512] = tn(dz_ref[:, rows], o_ref[:, at]).astype(BF)
 
-    flops = 2 * size * depth * groups * 512
-    return fill(run(kernel, outs, [normed, dz, dq, dk, dv, mixed], flops))
+    return fill(run(kernel, outs, [normed, dz, dq, dk, dv, mixed]))
 
 
 def value_backward(dmid, own, far, value, rows, low):
@@ -458,7 +454,70 @@
         out_ref[...] = out
 
     outs = [shape((size, depth), F32), shape((2, depth), F32)]
-    return run(kernel, outs, [dmid, own, far, value, rows], 20 * size * depth)
+    return run(kernel, outs, [dmid, own, far, value, rows])
+
+
+def block_lanes(spot, chunk):
+    ry, rx = chunk // 2 ^ spot // 2, chunk % 2 ^ spot % 2
+    return [(rx * 2 + ry) * 128, 512 + (ry * 2 + rx) * 128]
+
+
+def place_in(lanes, blocks):
+    size, width = blocks[0].shape
+    half = width // 2
+
+    def kernel(lanes_ref, *refs):
+        out_ref = refs[-1]
+        for d, ref in enumerate(refs[:-1]):
+            for h in range(2):
+                at = pl.multiple_of(lanes_ref[2 * d + h], 128)
+                out_ref[:, pl.ds(at, half)] = ref[:, h * half : (h + 1) * half]
+
+    block = pl.BlockSpec(memory_space=pltpu.VMEM)
+    return pl.pallas_call(
+        kernel,
+        out_shape=shape((size, width * len(blocks))),
+        in_specs=[pl.BlockSpec(memory_space=pltpu.SMEM)] + [block] * len(blocks),
+        out_specs=block,
+        compiler_params=pltpu.CompilerParams(vmem_limit_bytes=VMEM_BYTES),
+    )(lanes, *blocks)
+
+
+def place_out(numbers, scale, terms, bias_row, count):
+    size, depth = terms[0].shape
+    width = depth // count
+    half = width // 2
+
+    def kernel(numbers_ref, scale_ref, *refs):
+        term_refs, bias_ref, out_ref = refs[: len(terms)], refs[-2], refs[-1]
+        start = pl.multiple_of(numbers_ref[2 * count], 8)
+        rows = pl.ds(start, size // 2)
+        for d in range(count):
+            for h in range(2):
+                lanes = pl.ds(pl.multiple_of(numbers_ref[2 * d + h], 128), half)
+                value = term_refs[0][rows, lanes]
+                for ref in term_refs[1:]:
+                    value = value + ref[rows, lanes]
+                value = (value + bias_ref[:, lanes]) * scale_ref[0]
+                out_ref[d, :, h * half : (h + 1) * half] = value.astype(BF)
+
+    block = pl.BlockSpec(memory_space=pltpu.VMEM)
+    scalar = pl.BlockSpec(memory_space=pltpu.SMEM)
+    return pl.pallas_call(
+        kernel,
+        out_shape=shape((count, size // 2, width)),
+        in_specs=[scalar, scalar] + [block] * (len(terms) + 1),
+        out_specs=block,
+        compiler_params=pltpu.CompilerParams(vmem_limit_bytes=VMEM_BYTES),
+    )(numbers, scale, *terms, bias_row)
+
+
+def shifts(blocks):
+    n = lax.axis_size("tensor")
+    out = [blocks[0]]
+    for d in range(1, n):
+        out.append(lax.ppermute(blocks[d], "tensor", [(i, (i + d) % n) for i in range(n)]))
+    return out
 
 
 def half_cols(core, whole, n_tensor):
@@ -527,17 +586,41 @@
     half_in = jnp.where(is_first, ends_low, ends_got)
     half_cot = jnp.where(is_first, ends_got, ends_high)
 
+    below = [(place - d) % n_tensor for d in range(n_tensor)]
+    above = [(place + d) % n_tensor for d in range(n_tensor)]
+
+    def to_send(half):
+        return [lax.dynamic_index_in_dim(half, j, 0, False) for j in above]
+
+    def image_half(blocks):
+        if n_dp == 4:
+            lanes = [lane for t in below for lane in block_lanes(spot, t)]
+            return place_in(jnp.stack(lanes).astype(jnp.int32), blocks)
+        blocks = jnp.stack(blocks)
+        blocks = [lax.dynamic_index_in_dim(blocks, (place - i) % n_tensor, 0, False) for i in range(n_tensor)]
+        return relative(jnp.concatenate(blocks, 1), spot)
+
     def whole_image(half):
-        half = lax.all_to_all(half, "tensor", split_axis=0, concat_axis=2, tiled=True)[0]
         other = swap(half)
         both = [jnp.where(is_first, half, other), jnp.where(is_first, other, half)]
-        return relative(jnp.concatenate(both, 0), spot)
-
-    def image_rows(image):
-        image = absolute(image.astype(jnp.bfloat16), spot)
+        return jnp.concatenate(both, 0)
+
+    def image_rows(scale, terms, bias_row):
+        if n_dp == 4:
+            numbers = [lane for t in above for lane in block_lanes(spot, t)]
+            numbers.append(jnp.where(is_first, 0, reach))
+            numbers = jnp.stack(numbers).astype(jnp.int32)
+            blocks = place_out(numbers, scale.reshape(1), terms, bias_row, n_tensor)
+            return [blocks[d] for d in range(n_tensor)]
+        image = absolute((sum(terms[1:], terms[0]) + bias_row) * scale, spot).astype(jnp.bfloat16)
         half = jnp.where(is_first, image[:reach], image[reach:])
-        half = lax.all_to_all(half[None], "tensor", split_axis=2, concat_axis=0, tiled=True)
-        return half
+        half = half.reshape(reach, n_tensor, -1).transpose(1, 0, 2)
+        return to_send(half)
+
+    def by_image(blocks):
+        blocks = jnp.stack(blocks)
+        blocks = [lax.dynamic_index_in_dim(blocks, (place - i) % n_tensor, 0, False) for i in range(n_tensor)]
+        return jnp.stack(blocks)
 
     def small_of(piece):
         extras = jnp.concatenate(piece, 0)
@@ -552,27 +635,27 @@
         up_bias = half_cols(core, bias, n_tensor)
         return (relative(rows, spot), q_bias[None], v_bias[None], up_bias[None])
 
-    value = whole_image(half_in).astype(jnp.float32)
-
     number = len(columns)
     cut = [mid + extra if k % 3 == 0 else mid for k in range(number)]
     halves, near, far = [None] * number, [None] * number, [None] * number
     params = [dict(), dict()]
-    output = None
-    for r in range(number + 3):
+    blocks_in, blocks_cot = to_send(half_in), to_send(half_cot)
+    pair, state = None, None
+    for r in range(number + 2):
         tied = []
         if r < number:
-            whole = gather_column(columns[r])
-            tied.append(whole)
+            tied.append(gather_column(columns[r]))
         if 0 <= r - 1 < number:
             near[r - 1] = exchange_one(*halves[r - 1])
-            tied += near[r - 1]
-        if 0 <= r - 2 < number:
-            far[r - 2] = exchange_two(*halves[r - 2], *near[r - 2])
-            tied += far[r - 2]
-        k = r - 3
-        ready = None
-        if 0 <= k < number:
+            far[r - 1] = exchange_two(*halves[r - 1], *near[r - 1])
+            tied += near[r - 1] + far[r - 1]
+        if r == 1:
+            blocks_in = shifts(blocks_in)
+        if r == number:
+            blocks_cot = shifts(blocks_cot)
+        ready = []
+        k = r - 2
+        if k >= 0:
             layer, kind = k // 3, k % 3
             one = params[layer]
             first, second = arrived(*halves[k], near[k], far[k])
@@ -585,116 +668,139 @@
             counts = [mid if n_dp == 4 else p.shape[0] for p in pieces]
             weights = (pieces, counts)
             rows, q_bias, v_bias, up_bias = one["small"]
+            if pair is not None:
+                pair = [pair[0], swap(pair[0])]
             if kind == 0:
                 one["qkvo"] = weights
-                terms = [value] if layer == 0 else [state, *pair]
-                bias_row = (rows if layer == 0 else params[0]["small"][0])[7:8]
+                if layer == 0:
+                    terms = [whole_image(image_half(blocks_in)).astype(jnp.float32)]
+                else:
+                    terms = [state, *pair]
+                bias_row = params[0]["small"][0][7:8]
                 done = attention_forward(
                     tokens, terms, bias_row, layer == 1, weights, rows, q_bias, v_bias
                 )
                 one["u"], one["n1"], one["saved"], part = done[0], done[1], done[2:7], done[7]
-                pair = [part, swap(part)]
-                ready = pair
+                pair, ready = [part], [part]
             elif kind == 1:
                 one["up"] = weights
                 one["mid"], one["n2"], one["slope"], one["hidden"] = up_forward(
                     [one["u"], *pair], weights, rows, up_bias
                 )
-                ready = [one["hidden"]]
+                pair, ready = None, [one["hidden"]]
             else:
                 one["down"] = weights
+                state = one["mid"]
                 part = contract_wide(one["hidden"], weights)
-                state = one["mid"]
-                pair = [part, swap(part)]
-                ready = pair
-        if r < number + 2:
-            extras = list(ready) if ready else []
-            count = len(extras)
-            if r == 5:
-                extras.append(half_cot)
+                pair, ready = [part], [part]
+        if r <= number:
+            count = len(ready)
+            extras = list(ready)
+            if r <= 1:
+                extras += blocks_in
+            if r == number - 1:
+                extras += blocks_cot
             if r + 1 < number:
                 extras.append(columns[r + 1])
             done = tie(tied + extras, [])
             if r + 1 < number:
                 columns[r + 1] = done.pop()
-            if r == 5:
-                half_cot = done.pop()
-            if count == 2:
-                pair = done[-2:]
-            elif count == 1:
+            if r <= 1:
+                done, blocks_in = done[:-n_tensor], done[-n_tensor:]
+            if r == number - 1:
+                done, blocks_cot = done[:-n_tensor], done[-n_tensor:]
+            if count and kind == 1:
                 one["hidden"] = done[-1]
+            elif count:
+                pair = [done[-1]]
             at = 0
             if r < number:
                 halves[r] = (done[0][: cut[r]], done[0][cut[r] :])
                 at = 1
             if 0 <= r - 1 < number:
                 near[r - 1] = done[at : at + 2]
-                at += 2
-            if 0 <= r - 2 < number:
-                far[r - 2] = done[at : at + len(far[r - 2])]
-        if r == 5:
-            cotangent = whole_image(half_cot).astype(jnp.float32) * live
+                far[r - 1] = done[at + 2 : at + 2 + len(far[r - 1])]
+    cotangent = whole_image(image_half(blocks_cot)).astype(jnp.float32) * live
+    pair = [pair[0], swap(pair[0])]
     last_rows = params[1]["small"][0]
-    output = state + pair[0].astype(jnp.float32) + pair[1].astype(jnp.float32) + last_rows[7:8]
-    out_rows = image_rows(output * live)
+    out_blocks = image_rows(live, [state, *pair], last_rows[7:8])
 
     grads, got, moved, settled = [None] * number, [None] * number, [None] * number, [None] * number
+    made = [0, 1, 3, 4, 5, 7]
     sums = [dict(), dict()]
     grad = cotangent
-    for r in range(number):
-        layer, kind = (number - 1 - r) // 3, (number - 1 - r) % 3
+    for r in range(8):
+        layer, stage = 1 - r // 4, r % 4
         one, total = params[layer], sums[layer]
         rows = one["small"][0]
-        tied = []
-        if r >= 1:
-            got[r - 1] = scatter_one(*grads[r - 1][:2])
-            tied += got[r - 1]
-        if r >= 2:
-            moved[r - 2] = scatter_two(*grads[r - 2][2:], got[r - 2])
-            tied += moved[r - 2][0] + moved[r - 2][1]
-        if r >= 3:
-            settled[r - 3] = scatter_column(*moved[r - 3])
-            tied.append(settled[r - 3])
-        if kind == 2:
-            low, total["out"], total["up_bias"], grads[r] = down_backward(
+        tied, slots = [], []
+        for c in range(number):
+            if r == made[c] + 1:
+                got[c] = scatter_one(*grads[c][:2])
+                slots.append((got, c, len(got[c])))
+                tied += got[c]
+            elif r == made[c] + 2:
+                stay, come = scatter_two(*grads[c][2:], got[c])
+                moved[c] = [*stay, *come]
+                slots.append((moved, c, len(moved[c])))
+                tied += moved[c]
+            elif r == made[c] + 3:
+                settled[c] = scatter_column(moved[c][:2], moved[c][2:])
+                slots.append((settled, c, 0))
+                tied.append(settled[c])
+        new = None
+        if stage == 0:
+            low, total["out"], total["up_bias"], new = down_backward(
                 grad, one["hidden"], one["slope"], one["down"]
             )
-            carry = low
-        elif kind == 1:
+            carry = [low]
+        elif stage == 1:
             part = contract_wide(low, one["up"])
-            grads[r] = up_grad(one["n2"], low)
-            pair = [part, swap(part)]
+            new = up_grad(one["n2"], low)
+            carry = [part]
+        elif stage == 2:
             done = attention_backward(
-                grad, *pair, one["mid"], rows, one["saved"], one["qkvo"]
+                grad, part, swap(part), one["mid"], rows, one["saved"], one["qkvo"]
             )
             dmid, dz, dq, dk, dv, part, total["mid"], total["q"], total["v"] = done
-            carry = part
+            carry = [part, dz]
         else:
-            pair = [part, swap(part)]
-            grads[r] = attention_grad(one["n1"], dz, dq, dk, dv, one["saved"][4])
-            grad, total["one"] = value_backward(dmid, *pair, one["u"], rows, layer == 1)
-            carry = grad
-        if r < number - 1:
-            new = [g for g in grads[r] if g is not None]
-            done = tie([carry] + new + tied, [])
-            if kind == 2:
+            far_part = swap(part)
+            new = attention_grad(one["n1"], dz, dq, dk, dv, one["saved"][4])
+            grad, total["one"] = value_backward(dmid, part, far_part, one["u"], rows, layer == 1)
+            carry = [grad]
+        if new is not None:
+            c = made.index(r)
+            grads[c] = new
+            fresh = [g for g in new if g is not None]
+        else:
+            fresh = []
+        if r == 1:
+            out_blocks = shifts(out_blocks)
+            carry += out_blocks
+        if r < 7:
+            done = tie(carry + fresh + tied, [])
+            if stage == 0:
                 low = done[0]
-            elif kind == 1:
+            elif stage == 1:
                 part = done[0]
+            elif stage == 2:
+                part, dz = done[:2]
             else:
                 grad = done[0]
-            grads[r] = fill(done[1 : 1 + len(new)])
-            done = done[1 + len(new) :]
-            if r >= 1:
-                got[r - 1], done = done[:2], done[2:]
-            if r >= 2:
-                count = len(moved[r - 2][1])
-                moved[r - 2] = (done[:2], done[2 : 2 + count])
-                done = done[2 + count :]
-            if r >= 3:
-                settled[r - 3] = done[0]
-
-    grad_rows = image_rows(grad)
+            if r == 1:
+                out_blocks = done[1 : 1 + n_tensor]
+            done = done[len(carry) :]
+            if fresh:
+                grads[c] = fill(done[: len(fresh)])
+                done = done[len(fresh) :]
+            for store, at, count in slots:
+                store[at] = done[:count] if count else done[0]
+                done = done[max(count, 1) :]
+
+    one_scale = jnp.ones((), jnp.float32)
+    grad_blocks = shifts(image_rows(one_scale, [grad], jnp.zeros((1, grad.shape[1]), jnp.float32)))
+    grad_rows, out_rows = by_image(grad_blocks), by_image(out_blocks)
     packed = []
     for layer in range(2):
         total = sums[layer]
@@ -721,16 +827,11 @@
 
     last = number - 1
     got[last] = scatter_one(*grads[last][:2])
-    for k in range(number):
-        if moved[k] is None:
-            moved[k] = scatter_two(*grads[k][2:], got[k])
-    for k in range(number):
-        if settled[k] is None:
-            stay, come = moved[k]
-            if k == last:
-                stay = [add(s, c).astype(jnp.bfloat16) for s, c in zip(stay, come)] if come else stay
-                stay, come = [*stay, little], []
-            settled[k] = scatter_column(stay, come)
+    settled[last - 1] = scatter_column(moved[last - 1][:2], moved[last - 1][2:])
+    stay, come = scatter_two(*grads[last][2:], got[last])
+    if come:
+        stay = [add(s, c).astype(jnp.bfloat16) for s, c in zip(stay, come)]
+    settled[last] = scatter_column([*stay, little], [])
     little = settled[last][depth:].reshape(-1).astype(jnp.float32)
     settled[last] = settled[last][:depth]
     grad_vectors = little[:n_vec].reshape(vectors.shape)

time: 824 us -> 707 us (0.86)
  other arithmetic: 112 us -> 80 us
  blocking collectives: 31.6 us -> 0 us
  local copies, waits for them, and re-layouts: 135 us -> 105 us
  waiting for transfers between devices: 232 us -> 207 us
    ppermute x31, waiting for transfers between devices: 78.8 us -> 39.4 us  [swap_x(): return lax.ppermute(value, 'dp', [(i, i ^ 1) for i in range(n)])]
    ppermute x0 -> x12, waiting for transfers between devices: none -> 39.3 us  [shifts(): lax.ppermute(blocks[d], 'tensor', [(i, (i + d) % n) for i in range(n)])]
    ppermute x31, waiting for transfers between devices: 114 us -> 79.2 us  [swap_y(): return lax.ppermute(value, 'dp', [(i, i ^ 2) for i in range(n)])]
    all_to_all x1 -> x0, blocking collectives: 31.6 us -> none  [whole_image(): lax.all_to_all(half, 'tensor', split_axis=0, concat_axis=2, tiled=True)[0]]
    all_to_all x3 -> x0, waiting for transfers between devices: 29.5 us -> none  [the longest x2 18.3 us: image_rows(): lax.all_to_all(half[None], 'tensor', split_axis=2, concat_axis=0, tiled=T...]
    reduce_scatter x6, waiting for transfers between devices: 0.08 us -> 22.4 us  [scatter_column(): lax.psum_scatter(jnp.concatenate(stay, 0), 'tensor', scatter_dimension=1,...]
    reshape x6 -> x0, local copies, waits for them, and re-layouts: 14.6 us -> none  [the longest x2 5.98 us: relative(): cut = value.reshape(lead + (2, 2, 2, -1))]
    all_to_all x3 -> x0, starting transfers between devices: 12.9 us -> none  [the longest x2 8.74 us: image_rows(): lax.all_to_all(half[None], 'tensor', split_axis=2, concat_axis=0, tiled=T...]
  transfers between devices with their start and end apart: 94 -> 103, of which waited for: 36 -> 32; matrix products, arithmetic and copies ran while one was open for 24% -> 16% of each run, Pallas kernels for 22% -> 27%
where the time goes in v5:
time: 707 us; the launch traced here: 699 us
  waiting for transfers between devices  207 us (29%)
  Pallas kernels  191 us (27%)
  local copies, waits for them, and re-layouts  105 us (15%)
  starting transfers between devices  98.2 us (14%)
  other arithmetic  80 us (11%)
  between operations  17.4 us (2%)
    pallas_call x18, Pallas kernels, run(): pl.pallas_call(kernel, out_shape=list(outs), in_specs=[block] * len(ins),...  186 us
    ppermute x31, waiting for transfers between devices, swap_y(): return lax.ppermute(value, 'dp', [(i, i ^ 2) for i in range(n)])  79.2 us
    unnamed x369, local copies, waits for them, and re-layouts  52.8 us
    ppermute x31, waiting for transfers between devices, swap_x(): return lax.ppermute(value, 'dp', [(i, i ^ 1) for i in range(n)])  39.4 us
    ppermute x12, waiting for transfers between devices, shifts(): lax.ppermute(blocks[d], 'tensor', [(i, (i + d) % n) for i in range(n)])  39.3 us
    ppermute x17, starting transfers between devices, swap(): return lax.ppermute(value, 'section', [(0, 1), (1, 0)])  35.3 us
    convert_element_type x12, other arithmetic, scatter_two(): come.append(far(add(keep[half:], new[half:]).astype(jnp.bfloat16)))  27.6 us
    ppermute x31, starting transfers between devices, swap_x(): return lax.ppermute(value, 'dp', [(i, i ^ 1) for i in range(n)])  25.9 us
  transfers between devices with their start and end apart: 103, of which 32 were waited for; matrix products, arithmetic and copies ran while one was open for 16% of the time, Pallas kernels for 27%

profile of v5, /device:TPU:1, one launch (start us, length us, event | category | flops | bytes accessed | tf_op | source)
XLA Modules:
  0.0 699.1 jit_solution(581668721845302370)
XLA Ops:
  26.0 21.8 %all-gather.7.cloned.1.call-done.refs_0_ = bf16[272,2048]{1,0:T(8,128)(2,1)} async-done(((bf16[272,512]{1,0:T(8,128)(2,1)}), bf16[272,2048]{1,0:T(8,128)(2,1)}) %all-gather.7.cloned.1.call-update) | async-done | bytes 1114128 | tf_op jit(solution)/shard_map/all_gather | solution.py:49
  56.7 7.2 %collective-permute-done.2.refs_1_ = bf16[144,2048]{1,0:T(8,128)(2,1)S(1)} collective-permute-done((bf16[144,2048]{1,0:T(8,128)(2,1)S(1)}, bf16[144,2048]{1,0:T(8,128)(2,1)S(1)}, u32[]{:S(2)}, u32[]{:S(2)}) %collective-permute-start.2) | collective-permute-done | bytes 589856 | tf_op jit(solution)/shard_map/ppermute | solution.py:28
  67.5 10.6 %collective-permute-done.9.refs_9_ = bf16[296,256]{1,0:T(8,128)(2,1)S(1)} collective-permute-done((bf16[296,256]{1,0:T(8,128)(2,1)}, bf16[296,256]{1,0:T(8,128)(2,1)S(1)}, u32[]{:S(2)}, u32[]{:S(2)}) %collective-permute-start.9) | collective-permute-done | bytes 151584 | tf_op jit(solution)/shard_map/ppermute | solution.py:519
  109.3 10.0 %collective-permute-done.11.refs_1_ = bf16[128,2048]{1,0:T(8,128)(2,1)} collective-permute-done((bf16[128,2048]{1,0:T(8,128)(2,1)S(1)}, bf16[128,2048]{1,0:T(8,128)(2,1)}, u32[]{:S(2)}, u32[]{:S(2)}) %collective-permute-start.11) | collective-permute-done | bytes 524320 | tf_op jit(solution)/shard_map/ppermute | solution.py:28
  124.3 15.5 %shard_map.138 = (f32[592,1024]{1,0:T(8,128)}, bf16[592,1024]{1,0:T(8,128)(2,1)}, bf16[592,512]{1,0:T(8,128)(2,1)}, bf16[592,512]{1,0:T(8,128)(2,1)}, bf16[592,5...) custom-call(f32[592,1024]{1,0:T(8,128)} %maximum_convert_fusion.refs_0_, ...), custom_call_target="tpu_custom_call" | custom-call | flops 1 | bytes 1 | tf_op jit(solution)/shard_map/pallas_call | solution.py:173
  151.5 10.6 %collective-permute-done.19.refs_2_ = bf16[128,2048]{1,0:T(8,128)(2,1)S(1)} collective-permute-done((bf16[128,2048]{1,0:T(8,128)(2,1)S(1)}, bf16[128,2048]{1,0:T(8,128)(2,1)S(1)}, u32[]{:S(2)}, u32[]{:S(2)}) %collective-permute-start.19) | collective-permute-done | bytes 524320 | tf_op jit(solution)/shard_map/ppermute | solution.py:23
  167.0 10.3 %shard_map.140 = (f32[592,1024]{1,0:T(8,128)}, bf16[592,1024]{1,0:T(8,128)(2,1)}, bf16[592,2048]{1,0:T(8,128)(2,1)}, bf16[592,2048]{1,0:T(8,128)(2,1)}) custom-call(f32[592,1024]{1,0:T(8,128)} %get-tuple-element.230.refs_0_.u_ref, bf16[592,1024]{1,0:T(8,128)(2,1)} %get-tuple-element.231.refs_1_, bf16[592,1024]{1,0:T(8,128)(2,1)} %copy-done.161, ...), custom_call_target="tpu_custom_call" | custom-call | flops 1 | bytes 1 | tf_op jit(solution)/shard_map/pallas_call | solution.py:173
  177.3 7.2 %collective-permute-done.23.refs_6_ = bf16[128,2048]{1,0:T(8,128)(2,1)S(1)} collective-permute-done((bf16[128,2048]{1,0:T(8,128)(2,1)S(1)}, bf16[128,2048]{1,0:T(8,128)(2,1)S(1)}, u32[]{:S(2)}, u32[]{:S(2)}) %collective-permute-start.23) | collective-permute-done | bytes 524320 | tf_op jit(solution)/shard_map/ppermute | solution.py:28
  189.8 10.9 %collective-permute-done.25.refs_1_ = bf16[144,2048]{1,0:T(8,128)(2,1)S(1)} collective-permute-done((bf16[144,2048]{1,0:T(8,128)(2,1)S(1)}, bf16[144,2048]{1,0:T(8,128)(2,1)S(1)}, u32[]{:S(2)}, u32[]{:S(2)}) %collective-permute-start.25) | collective-permute-done | bytes 589856 | tf_op jit(solution)/shard_map/ppermute | solution.py:28
  213.0 11.1 %collective-permute-done.30.refs_6_ = bf16[128,2048]{1,0:T(8,128)(2,1)S(1)} collective-permute-done((bf16[128,2048]{1,0:T(8,128)(2,1)S(1)}, bf16[128,2048]{1,0:T(8,128)(2,1)S(1)}, u32[]{:S(2)}, u32[]{:S(2)}) %collective-permute-start.30) | collective-permute-done | bytes 524320 | tf_op jit(solution)/shard_map/ppermute | solution.py:28
  264.8 17.0 %shard_map.144 = (f32[592,1024]{1,0:T(8,128)}, bf16[592,1024]{1,0:T(8,128)(2,1)}, bf16[592,512]{1,0:T(8,128)(2,1)}, bf16[592,512]{1,0:T(8,128)(2,1)}, bf16[592,5...) custom-call(f32[592,1024]{1,0:T(8,128)} %get-tuple-element.250.refs_0_.refs, ...), custom_call_target="tpu_custom_call" | custom-call | flops 1 | bytes 1 | tf_op jit(solution)/shard_map/pallas_call | solution.py:173
  291.9 7.4 %collective-permute-done.39.refs_2_ = bf16[296,256]{1,0:T(8,128)(2,1)S(1)} collective-permute-done((bf16[296,256]{1,0:T(8,128)(2,1)S(1)}, bf16[296,256]{1,0:T(8,128)(2,1)S(1)}, u32[]{:S(2)}, u32[]{:S(2)}) %collective-permute-start.39) | collective-permute-done | bytes 151584 | tf_op jit(solution)/shard_map/ppermute | solution.py:519
  308.1 10.8 %shard_map.147 = (f32[592,1024]{1,0:T(8,128)}, bf16[592,1024]{1,0:T(8,128)(2,1)}, bf16[592,2048]{1,0:T(8,128)(2,1)}, bf16[592,2048]{1,0:T(8,128)(2,1)}) custom-call(f32[592,1024]{1,0:T(8,128)} %get-tuple-element.264.refs_0_.u_ref, bf16[592,1024]{1,0:T(8,128)(2,1)} %get-tuple-element.265.refs_1_, bf16[592,1024]{1,0:T(8,128)(2,1)} %copy-done.160, ...), custom_call_target="tpu_custom_call" | custom-call | flops 1 | bytes 1 | tf_op jit(solution)/shard_map/pallas_call | solution.py:173
  344.9 11.2 %shard_map.149 = (bf16[592,2048]{1,0:T(8,128)(2,1)}, f32[1,1024]{1,0:T(1,128)S(1)}, f32[1,2048]{1,0:T(1,128)S(1)}, bf16[256,2048]{1,0:T(8,128)(2,1)}, bf16[256,2...) custom-call(f32[592,1024]{1,0:T(8,128)} %convert_multiply_fusion.refs_0_, ...), custom_call_target="tpu_custom_call" | custom-call | flops 1 | bytes 1 | tf_op jit(solution)/shard_map/pallas_call | solution.py:173
  394.3 21.1 %shard_map.156 = (f32[592,1024]{1,0:T(8,128)}, bf16[592,1024]{1,0:T(8,128)(2,1)}, bf16[592,512]{1,0:T(8,128)(2,1)}, bf16[592,512]{1,0:T(8,128)(2,1)}, bf16[592,5...) custom-call(f32[592,1024]{1,0:T(8,128)} %convert_multiply_fusion.ref, ...), custom_call_target="tpu_custom_call" | custom-call | flops 1 | bytes 1 | tf_op jit(solution)/shard_map/pallas_call | solution.py:173
  432.2 7.8 %shard_map.159 = (bf16[256,2048]{1,0:T(8,128)(2,1)S(1)}, bf16[256,2048]{1,0:T(8,128)(2,1)}, bf16[256,2048]{1,0:T(8,128)(2,1)}, bf16[256,2048]{1,0:T(8,128)(2,1)}) custom-call(bf16[592,1024]{1,0:T(8,128)(2,1)} %get-tuple-element.312.n_ref, bf16[592,1024]{1,0:T(8,128)(2,1)} %get-tuple-element.313.dz_ref, bf16[592,512]{1,0:T(8,128)(2,1)S(1)} %copy-done.113, ...), custom_call_target="tpu_custom_call" | custom-call | flops 1 | bytes 1 | tf_op jit(solution)/shard_map/pallas_call | solution.py:173
  465.5 12.1 %shard_map.161 = (bf16[592,2048]{1,0:T(8,128)(2,1)}, f32[1,1024]{1,0:T(1,128)S(1)}, f32[1,2048]{1,0:T(1,128)S(1)}, bf16[256,2048]{1,0:T(8,128)(2,1)}, bf16[256,2...) custom-call(f32[592,1024]{1,0:T(8,128)} %get-tuple-element.329.refs_0_, ...), custom_call_target="tpu_custom_call" | custom-call | flops 1 | bytes 1 | tf_op jit(solution)/shard_map/pallas_call | solution.py:173
  507.5 13.7 %collective-permute-done.65.refs_7_ = bf16[128,2048]{1,0:T(8,128)(2,1)S(1)} collective-permute-done((bf16[128,2048]{1,0:T(8,128)(2,1)S(1)}, bf16[128,2048]{1,0:T(8,128)(2,1)S(1)}, u32[]{:S(2)}, u32[]{:S(2)}) %collective-permute-start.65) | collective-permute-done | bytes 524320 | tf_op jit(solution)/shard_map/ppermute | solution.py:28
  538.9 22.0 %shard_map.166 = (f32[592,1024]{1,0:T(8,128)}, bf16[592,1024]{1,0:T(8,128)(2,1)}, bf16[592,512]{1,0:T(8,128)(2,1)}, bf16[592,512]{1,0:T(8,128)(2,1)}, bf16[592,5...) custom-call(f32[592,1024]{1,0:T(8,128)} %get-tuple-element.329.refs_, ...), custom_call_target="tpu_custom_call" | custom-call | flops 1 | bytes 1 | tf_op jit(solution)/shard_map/pallas_call | solution.py:173
  560.9 9.3 %collective-permute-done.70.refs_5_ = bf16[128,2048]{1,0:T(8,128)(2,1)S(1)} collective-permute-done((bf16[128,2048]{1,0:T(8,128)(2,1)S(1)}, bf16[128,2048]{1,0:T(8,128)(2,1)S(1)}, u32[]{:S(2)}, u32[]{:S(2)}) %collective-permute-start.70) | collective-permute-done | bytes 524320 | tf_op jit(solution)/shard_map/ppermute | solution.py:28
  583.6 8.1 %shard_map.170 = (bf16[256,2048]{1,0:T(8,128)(2,1)}, bf16[256,2048]{1,0:T(8,128)(2,1)}, bf16[256,2048]{1,0:T(8,128)(2,1)}, bf16[256,2048]{1,0:T(8,128)(2,1)}) custom-call(bf16[592,1024]{1,0:T(8,128)(2,1)} %get-tuple-element.379.n_ref, bf16[592,1024]{1,0:T(8,128)(2,1)} %get-tuple-element.380.dz_ref, bf16[592,512]{1,0:T(8,128)(2,1)S(1)} %copy-done.110, ...), custom_call_target="tpu_custom_call" | custom-call | flops 1 | bytes 1 | tf_op jit(solution)/shard_map/pallas_call | solution.py:173
  599.7 14.9 %collective-permute-done.79 = bf16[256,2048]{1,0:T(8,128)(2,1)} collective-permute-done((bf16[256,2048]{1,0:T(8,128)(2,1)}, bf16[256,2048]{1,0:T(8,128)(2,1)}, u32[]{:S(2)}, u32[]{:S(2)}) %collective-permute-start.79) | collective-permute-done | bytes 1048608 | tf_op jit(solution)/shard_map/ppermute | solution.py:23
  639.0 9.5 %collective-permute-done.76 = bf16[296,256]{1,0:T(8,128)(2,1)S(1)} collective-permute-done((bf16[296,256]{1,0:T(8,128)(2,1)S(1)}, bf16[296,256]{1,0:T(8,128)(2,1)S(1)}, u32[]{:S(2)}, u32[]{:S(2)}) %collective-permute-start.76) | collective-permute-done | bytes 151584 | tf_op jit(solution)/shard_map/ppermute | solution.py:519
  665.6 18.2 %reduce-scatter.13.cloned.1.call-done = bf16[272,512]{1,0:T(8,128)(2,1)} async-done(((bf16[272,2048]{1,0:T(8,128)(2,1)}), bf16[272,512]{1,0:T(8,128)(2,1)}) %reduce-scatter.13.cloned.1.call-update) | async-done | bytes 278544 | tf_op jit(solution)/shard_map/reduce_scatter | solution.py:105
  (816 shorter events, 383.2 us)
Async XLA Ops:
  7.2 40.5 %all-gather.7.cloned.1.call-start = ((), (), s32[]{:S(2)}) async-start(), calls=%async_computation.6 | async-start | bytes 1392640 | tf_op jit(solution)/shard_map/all_gather | solution.py:49
  16.7 74.1 %all-gather.9.cloned.1.call-start = ((), (), s32[]{:S(2)}) async-start(), calls=%async_computation.7 | async-start | bytes 1310720 | tf_op jit(solution)/shard_map/all_gather | solution.py:49
  47.8 92.1 %all-gather.11.cloned.1.call-start = ((), (), s32[]{:S(2)}) async-start(), calls=%async_computation.8 | async-start | bytes 1310720 | tf_op jit(solution)/shard_map/all_gather | solution.py:49
  96.6 43.2 %collective-permute-start.15 = (bf16[128,2048]{1,0:T(8,128)(2,1)S(1)}, bf16[128,2048]{1,0:T(8,128)(2,1)S(1)}, u32[]{:S(2)}, u32[]{:S(2)}) collective-permute-start(bf16[128,2048]{1,0:T(8,128)(2,1)S(1)} %get-tuple-element.474.refs_9_.refs_5_), channel_id=1, source_target_pairs={{0,8},{4,12},{8,0},{12,4},{1,9},{5,13},{9,1},{13,5},{2,10},{6,14},... | collective-permute-start | bytes 1572872 | tf_op jit(solution)/shard_map/ppermute | solution.py:28
  98.1 41.7 %collective-permute-start.13 = (bf16[128,2048]{1,0:T(8,128)(2,1)S(1)}, bf16[128,2048]{1,0:T(8,128)(2,1)}, u32[]{:S(2)}, u32[]{:S(2)}) collective-permute-start(bf16[128,2048]{1,0:T(8,128)(2,1)S(1)} %get-tuple-element.475.refs_5_.refs_1_), channel_id=1, source_target_pairs={{0,4},{4,0},{8,12},{12,8},{1,5},{5,1},{9,13},{13,9},{2,6},{6,2},{1... | collective-permute-start | bytes 1572872 | tf_op jit(solution)/shard_map/ppermute | solution.py:23
  99.6 85.0 %all-gather.13.cloned.1.call-start = ((), (), s32[]{:S(2)}) async-start(), calls=%async_computation.9 | async-start | bytes 1392640 | tf_op jit(solution)/shard_map/all_gather | solution.py:49
  140.6 85.0 %all-gather.15.cloned.1.call-start = ((), (), s32[]{:S(2)}) async-start(), calls=%async_computation.10 | async-start | bytes 1310720 | tf_op jit(solution)/shard_map/all_gather | solution.py:49
  185.4 96.5 %all-gather.17.cloned.1.call-start = ((), (), s32[]{:S(2)}) async-start(), calls=%async_computation.11 | async-start | bytes 1310720 | tf_op jit(solution)/shard_map/all_gather | solution.py:49
  228.9 52.9 %collective-permute-start.35 = (bf16[128,2048]{1,0:T(8,128)(2,1)}, bf16[128,2048]{1,0:T(8,128)(2,1)}, u32[]{:S(2)}, u32[]{:S(2)}) collective-permute-start(bf16[128,2048]{1,0:T(8,128)(2,1)} %get-tuple-element.470.refs_9_.refs_5_), channel_id=1, source_target_pairs={{0,8},{4,12},{8,0},{12,4},{1,9},{5,13},{9,1},{13,5},{2,10},{6,14},... | collective-permute-start | bytes 1572872 | tf_op jit(solution)/shard_map/ppermute | solution.py:28
  231.1 50.7 %collective-permute-start.33 = (bf16[128,2048]{1,0:T(8,128)(2,1)}, bf16[128,2048]{1,0:T(8,128)(2,1)}, u32[]{:S(2)}, u32[]{:S(2)}) collective-permute-start(bf16[128,2048]{1,0:T(8,128)(2,1)} %get-tuple-element.471.refs_5_.refs_1_), channel_id=1, source_target_pairs={{0,4},{4,0},{8,12},{12,8},{1,5},{5,1},{9,13},{13,9},{2,6},{6,2},{1... | collective-permute-start | bytes 1572872 | tf_op jit(solution)/shard_map/ppermute | solution.py:23
  231.8 219.5 %reduce-scatter.7.cloned.1.call-start = ((), (), s32[]{:S(2)}) async-start(), calls=%async_computation.12 | async-start | bytes 1310720 | tf_op jit(solution)/shard_map/reduce_scatter | solution.py:105
  303.8 37.0 %collective-permute-start.41 = (bf16[296,1024]{1,0:T(8,128)(2,1)}, bf16[296,1024]{1,0:T(8,128)(2,1)}, u32[]{:S(2)}, u32[]{:S(2)}) collective-permute-start(bf16[296,1024]{1,0:T(8,128)(2,1)} %shard_map.146), channel_id=1, source_target_pairs={{0,16},{16,0},{1,17},{17,1},{2,18},{18,2},{3,19},{19,3},{4,20},{20... | collective-permute-start | bytes 1818632 | tf_op jit(solution)/shard_map/ppermute | solution.py:13
  383.4 35.3 %collective-permute-start.58 = (bf16[256,2048]{1,0:T(8,128)(2,1)}, bf16[256,2048]{1,0:T(8,128)(2,1)}, u32[]{:S(2)}, u32[]{:S(2)}) collective-permute-start(bf16[256,2048]{1,0:T(8,128)(2,1)} %get-tuple-element.308), channel_id=1, source_target_pairs={{0,4},{4,0},{8,12},{12,8},{1,5},{5,1},{9,13},{13,9},{2,6},{6,2},{1... | collective-permute-start | bytes 3145736 | tf_op jit(solution)/shard_map/ppermute | solution.py:23
  383.8 34.8 %collective-permute-start.59 = (bf16[256,2048]{1,0:T(8,128)(2,1)}, bf16[256,2048]{1,0:T(8,128)(2,1)}, u32[]{:S(2)}, u32[]{:S(2)}) collective-permute-start(bf16[256,2048]{1,0:T(8,128)(2,1)} %get-tuple-element.309), channel_id=1, source_target_pairs={{0,8},{4,12},{8,0},{12,4},{1,9},{5,13},{9,1},{13,5},{2,10},{6,14},... | collective-permute-start | bytes 3145736 | tf_op jit(solution)/shard_map/ppermute | solution.py:28
  422.4 60.3 %reduce-scatter.9.cloned.1.call-start = ((), (), s32[]{:S(2)}) async-start(), calls=%async_computation.13 | async-start | bytes 1310720 | tf_op jit(solution)/shard_map/reduce_scatter | solution.py:105
  454.2 117.8 %reduce-scatter.11.cloned.1.call-start = ((), (), s32[]{:S(2)}) async-start(), calls=%async_computation.14 | async-start | bytes 1310720 | tf_op jit(solution)/shard_map/reduce_scatter | solution.py:105
  486.7 34.4 %collective-permute-start.67 = (bf16[256,2048]{1,0:T(8,128)(2,1)S(1)}, bf16[256,2048]{1,0:T(8,128)(2,1)S(1)}, u32[]{:S(2)}, u32[]{:S(2)}) collective-permute-start(bf16[256,2048]{1,0:T(8,128)(2,1)S(1)} %copy-done.162), channel_id=1, source_target_pairs={{0,4},{4,0},{8,12},{12,8},{1,5},{5,1},{9,13},{13,9},{2,6},{6,2},{1... | collective-permute-start | bytes 3145736 | tf_op jit(solution)/shard_map/ppermute | solution.py:23
  525.7 131.7 %reduce-scatter.17.cloned.1.call-start = ((), (), s32[]{:S(2)}) async-start(), calls=%async_computation.17 | async-start | bytes 1310720 | tf_op jit(solution)/shard_map/reduce_scatter | solution.py:105
  533.8 36.5 %collective-permute-start.72 = (bf16[256,2048]{1,0:T(8,128)(2,1)S(1)}, bf16[256,2048]{1,0:T(8,128)(2,1)S(1)}, u32[]{:S(2)}, u32[]{:S(2)}) collective-permute-start(bf16[256,2048]{1,0:T(8,128)(2,1)S(1)} %copy-done.93), channel_id=1, source_target_pairs={{0,4},{4,0},{8,12},{12,8},{1,5},{5,1},{9,13},{13,9},{2,6},{6,2},{1... | collective-permute-start | bytes 3145736 | tf_op jit(solution)/shard_map/ppermute | solution.py:23
  534.9 37.1 %collective-permute-start.73 = (bf16[256,2048]{1,0:T(8,128)(2,1)S(1)}, bf16[256,2048]{1,0:T(8,128)(2,1)}, u32[]{:S(2)}, u32[]{:S(2)}) collective-permute-start(bf16[256,2048]{1,0:T(8,128)(2,1)S(1)} %copy-done.95), channel_id=1, source_target_pairs={{0,8},{4,12},{8,0},{12,4},{1,9},{5,13},{9,1},{13,5},{2,10},{6,14},... | collective-permute-start | bytes 3145736 | tf_op jit(solution)/shard_map/ppermute | solution.py:28
  574.9 86.9 %reduce-scatter.15.cloned.1.call-start = ((), (), s32[]{:S(2)}) async-start(), calls=%async_computation.16 | async-start | bytes 1310720 | tf_op jit(solution)/shard_map/reduce_scatter | solution.py:105
  599.7 84.1 %reduce-scatter.13.cloned.1.call-start = ((), (), s32[]{:S(2)}) async-start(), calls=%async_computation.15 | async-start | bytes 1392640 | tf_op jit(solution)/shard_map/reduce_scatter | solution.py:105
  616.8 35.1 %collective-permute-start.80 = (bf16[128,2048]{1,0:T(8,128)(2,1)}, bf16[128,2048]{1,0:T(8,128)(2,1)}, u32[]{:S(2)}, u32[]{:S(2)}) collective-permute-start(bf16[128,2048]{1,0:T(8,128)(2,1)} %add_convert_fusion.12), channel_id=1, source_target_pairs={{0,8},{4,12},{8,0},{12,4},{1,9},{5,13},{9,1},{13,5},{2,10},{6,14},... | collective-permute-start | bytes 1572872 | tf_op jit(solution)/shard_map/ppermute | solution.py:28
  619.1 34.3 %collective-permute-start.82 = (bf16[128,2048]{1,0:T(8,128)(2,1)}, bf16[128,2048]{1,0:T(8,128)(2,1)}, u32[]{:S(2)}, u32[]{:S(2)}) collective-permute-start(bf16[128,2048]{1,0:T(8,128)(2,1)} %add_convert_fusion.9), channel_id=1, source_target_pairs={{0,4},{4,0},{8,12},{12,8},{1,5},{5,1},{9,13},{13,9},{2,6},{6,2},{1... | collective-permute-start | bytes 1572872 | tf_op jit(solution)/shard_map/ppermute | solution.py:23
  (255 other events, 3133.4 us)
Sparse Core Ops, SparseCore 0:
  16.8 30.8 all-gather.6
  49.3 39.8 all-gather.8
  99.7 29.1 all-gather.10
  140.8 32.2 all-gather.12
  185.5 27.0 all-gather.14
  232.0 30.2 all-gather.16
  422.5 28.8 reduce-scatter.6
  454.3 25.7 reduce-scatter.8
  525.8 28.0 reduce-scatter.10
  575.0 26.0 reduce-scatter.16
  603.9 25.7 reduce-scatter.14
  656.1 27.6 reduce-scatter.12

commit v6 on v5

--- a/solution.py
+++ b/solution.py
@@ -571,8 +571,10 @@
     for layer in range(2):
         for number in range(3):
             cols = shards[layer][:, number * wide : (number + 1) * wide]
-            if number == 0:
-                cols = jnp.concatenate([cols[:mid], cols[depth:], cols[mid:depth]], 0)
+            if layer == 0 and number == 0:
+                room = extra // 2
+                both = [shard[depth : depth + room, :wide] for shard in shards]
+                cols = jnp.concatenate([cols[:mid], *both, cols[mid:depth]], 0)
             else:
                 cols = cols[:depth]
             columns.append(cols)
@@ -624,19 +626,20 @@
 
     def small_of(piece):
         extras = jnp.concatenate(piece, 0)
-        one = by_chip(extras.reshape(n_dp, extra, -1), spot).astype(jnp.float32)
-        one = one.reshape(n_dp, extra, n_tensor, wide).transpose(0, 2, 1, 3)
-        one = one.reshape(n_dp, n_tensor, -1)
-        rows = one[:, :, :n_vec].reshape(n_dp, n_tensor, 8, -1)
-        rows = rows.transpose(2, 1, 0, 3).reshape(8, -1)
-        bias = one[:, :, n_vec:small_size].transpose(1, 0, 2).reshape(-1)
-        q_bias = half_cols(core, rows[2], n_tensor)
-        v_bias = half_cols(core, rows[3], n_tensor)
-        up_bias = half_cols(core, bias, n_tensor)
-        return (relative(rows, spot), q_bias[None], v_bias[None], up_bias[None])
+        both = by_chip(extras.reshape(n_dp, extra, -1), spot).astype(jnp.float32)
+        both = both.reshape(n_dp, 2, extra // 2, n_tensor, wide).transpose(1, 0, 3, 2, 4)
+        both = both.reshape(2, n_dp, n_tensor, -1)
+        rows = both[..., :n_vec].reshape(2, n_dp, n_tensor, 8, -1)
+        rows = relative(rows.transpose(0, 3, 2, 1, 4).reshape(2, 8, -1), spot)
+        bias = both[..., n_vec:small_size].transpose(0, 2, 1, 3).reshape(2, -1)
+        plain = both[..., :n_vec].reshape(2, n_dp, n_tensor, 8, -1)[..., 2:4, :]
+        plain = plain.transpose(0, 3, 2, 1, 4).reshape(2, 2, -1)
+        parts = [half_cols(core, plain[:, 0], n_tensor), half_cols(core, plain[:, 1], n_tensor)]
+        parts.append(half_cols(core, bias, n_tensor))
+        return [(rows[i], parts[0][i : i + 1], parts[1][i : i + 1], parts[2][i : i + 1]) for i in range(2)]
 
     number = len(columns)
-    cut = [mid + extra if k % 3 == 0 else mid for k in range(number)]
+    cut = [mid + extra if k == 0 else mid for k in range(number)]
     halves, near, far = [None] * number, [None] * number, [None] * number
     params = [dict(), dict()]
     blocks_in, blocks_cot = to_send(half_in), to_send(half_cot)
@@ -647,8 +650,6 @@
             tied.append(gather_column(columns[r]))
         if 0 <= r - 1 < number:
             near[r - 1] = exchange_one(*halves[r - 1])
-            far[r - 1] = exchange_two(*halves[r - 1], *near[r - 1])
-            tied += near[r - 1] + far[r - 1]
         if r == 1:
             blocks_in = shifts(blocks_in)
         if r == number:
@@ -659,9 +660,10 @@
             layer, kind = k // 3, k % 3
             one = params[layer]
             first, second = arrived(*halves[k], near[k], far[k])
-            if kind == 0:
+            if k == 0:
                 blocks = [p.reshape((-1, mid + extra) + p.shape[1:]) for p in first]
-                one["small"] = small_of([p[:, mid:].reshape(-1, p.shape[-1]) for p in blocks])
+                smalls = small_of([p[:, mid:].reshape(-1, p.shape[-1]) for p in blocks])
+                params[0]["small"], params[1]["small"] = smalls
                 if n_dp != 4:
                     first = [p[:, :mid].reshape(-1, p.shape[-1]) for p in blocks]
             pieces = first + second
@@ -696,9 +698,15 @@
         if r <= number:
             count = len(ready)
             extras = list(ready)
+            if 0 <= r - 1 < number:
+                if ready:
+                    done = tie(near[r - 1] + extras, [])
+                    near[r - 1], extras = done[: len(near[r - 1])], done[len(near[r - 1]) :]
+                far[r - 1] = exchange_two(*halves[r - 1], *near[r - 1])
+                tied += near[r - 1] + far[r - 1]
             if r <= 1:
                 extras += blocks_in
-            if r == number - 1:
+            if r >= number - 1:
                 extras += blocks_cot
             if r + 1 < number:
                 extras.append(columns[r + 1])
@@ -707,7 +715,7 @@
                 columns[r + 1] = done.pop()
             if r <= 1:
                 done, blocks_in = done[:-n_tensor], done[-n_tensor:]
-            if r == number - 1:
+            if r >= number - 1:
                 done, blocks_cot = done[:-n_tensor], done[-n_tensor:]
             if count and kind == 1:
                 one["hidden"] = done[-1]
@@ -726,7 +734,7 @@
     out_blocks = image_rows(live, [state, *pair], last_rows[7:8])
 
     grads, got, moved, settled = [None] * number, [None] * number, [None] * number, [None] * number
-    made = [0, 1, 3, 4, 5, 7]
+    made = [0, 1, 2, 4, 5, 6]
     sums = [dict(), dict()]
     grad = cotangent
     for r in range(8):
@@ -763,12 +771,15 @@
                 grad, part, swap(part), one["mid"], rows, one["saved"], one["qkvo"]
             )
             dmid, dz, dq, dk, dv, part, total["mid"], total["q"], total["v"] = done
-            carry = [part, dz]
+            new = attention_grad(one["n1"], dz, dq, dk, dv, one["saved"][4])
+            carry = [part]
         else:
-            far_part = swap(part)
-            new = attention_grad(one["n1"], dz, dq, dk, dv, one["saved"][4])
-            grad, total["one"] = value_backward(dmid, part, far_part, one["u"], rows, layer == 1)
+            grad, total["one"] = value_backward(dmid, part, swap(part), one["u"], rows, layer == 1)
             carry = [grad]
+            if r == 7:
+                one_scale = jnp.ones((), jnp.float32)
+                no_bias = jnp.zeros((1, grad.shape[1]), jnp.float32)
+                carry = shifts(image_rows(one_scale, [grad], no_bias))
         if new is not None:
             c = made.index(r)
             grads[c] = new
@@ -778,16 +789,18 @@
         if r == 1:
             out_blocks = shifts(out_blocks)
             carry += out_blocks
-        if r < 7:
+        if r < 8:
             done = tie(carry + fresh + tied, [])
             if stage == 0:
                 low = done[0]
             elif stage == 1:
                 part = done[0]
             elif stage == 2:
-                part, dz = done[:2]
+                part = done[0]
+            elif r < 7:
+                grad = done[0]
             else:
-                grad = done[0]
+                grad_blocks = done[:n_tensor]
             if r == 1:
                 out_blocks = done[1 : 1 + n_tensor]
             done = done[len(carry) :]
@@ -798,8 +811,6 @@
                 store[at] = done[:count] if count else done[0]
                 done = done[max(count, 1) :]
 
-    one_scale = jnp.ones((), jnp.float32)
-    grad_blocks = shifts(image_rows(one_scale, [grad], jnp.zeros((1, grad.shape[1]), jnp.float32)))
     grad_rows, out_rows = by_image(grad_blocks), by_image(out_blocks)
     packed = []
     for layer in range(2):
@@ -826,7 +837,6 @@
         little = add(little[0], swap_y(little[1])).astype(jnp.bfloat16)
 
     last = number - 1
-    got[last] = scatter_one(*grads[last][:2])
     settled[last - 1] = scatter_column(moved[last - 1][:2], moved[last - 1][2:])
     stay, come = scatter_two(*grads[last][2:], got[last])
     if come:

time: 707 us -> 718 us (1.016)
  waiting for transfers between devices: 207 us -> 253 us
  starting transfers between devices: 98.2 us -> 79 us
  other arithmetic: 80 us -> 69.5 us
    ppermute x31, waiting for transfers between devices: 39.4 us -> 110 us  [swap_x(): return lax.ppermute(value, 'dp', [(i, i ^ 1) for i in range(n)])]
    ppermute x31, waiting for transfers between devices: 79.2 us -> 38.8 us  [swap_y(): return lax.ppermute(value, 'dp', [(i, i ^ 2) for i in range(n)])]
    reduce_scatter x6, waiting for transfers between devices: 22.4 us -> 35.9 us  [scatter_column(): lax.psum_scatter(jnp.concatenate(stay, 0), 'tensor', scatter_dimension=1,...]
    ppermute x17, starting transfers between devices: 35.3 us -> 23.4 us  [swap(): return lax.ppermute(value, 'section', [(0, 1), (1, 0)])]
    unnamed x369 -> x350, local copies, waits for them, and re-layouts: 52.8 us -> 51.5 us
  transfers between devices with their start and end apart: 103 -> 103, of which waited for: 32 -> 39; matrix products, arithmetic and copies ran while one was open for 16% -> 15% of each run, Pallas kernels for 27% -> 27%
where the time goes in v6:
time: 718 us; the launch traced here: 711 us
  waiting for transfers between devices  253 us (35%)
  Pallas kernels  190 us (26%)
  local copies, waits for them, and re-layouts  102 us (14%)
  starting transfers between devices  79 us (11%)
  other arithmetic  69.5 us (10%)
  between operations  17.2 us (2%)
    pallas_call x18, Pallas kernels, run(): pl.pallas_call(kernel, out_shape=list(outs), in_specs=[block] * len(ins),...  185 us
    ppermute x31, waiting for transfers between devices, swap_x(): return lax.ppermute(value, 'dp', [(i, i ^ 1) for i in range(n)])  110 us
    unnamed x350, local copies, waits for them, and re-layouts  51.5 us
    ppermute x12, waiting for transfers between devices, shifts(): lax.ppermute(blocks[d], 'tensor', [(i, (i + d) % n) for i in range(n)])  39.9 us
    ppermute x31, waiting for transfers between devices, swap_y(): return lax.ppermute(value, 'dp', [(i, i ^ 2) for i in range(n)])  38.8 us
    reduce_scatter x6, waiting for transfers between devices, scatter_column(): lax.psum_scatter(jnp.concatenate(stay, 0), 'tensor', scatter_dimension=1,...  35.9 us
    convert_element_type x12, other arithmetic, scatter_two(): come.append(far(add(keep[half:], new[half:]).astype(jnp.bfloat16)))  26.4 us
    all_gather x6, waiting for transfers between devices, gather_column(): return lax.all_gather(shard, 'tensor', axis=1, tiled=True)  23.9 us
  transfers between devices with their start and end apart: 103, of which 39 were waited for; matrix products, arithmetic and copies ran while one was open for 15% of the time, Pallas kernels for 27%

profile of v6, /device:TPU:1, one launch (start us, length us, event | category | flops | bytes accessed | tf_op | source)
XLA Modules:
  0.0 710.9 jit_solution(17113653087861756417)
XLA Ops:
  23.8 23.9 %all-gather.7.cloned.1.call-done.refs_0_ = bf16[272,2048]{1,0:T(8,128)(2,1)} async-done(((bf16[272,512]{1,0:T(8,128)(2,1)}), bf16[272,2048]{1,0:T(8,128)(2,1)}) %all-gather.7.cloned.1.call-update) | async-done | bytes 1114128 | tf_op jit(solution)/shard_map/all_gather | solution.py:49
  66.7 10.7 %collective-permute-done.9.refs_9_ = bf16[296,256]{1,0:T(8,128)(2,1)} collective-permute-done((bf16[296,256]{1,0:T(8,128)(2,1)}, bf16[296,256]{1,0:T(8,128)(2,1)}, u32[]{:S(2)}, u32[]{:S(2)}) %collective-permute-start.9) | collective-permute-done | bytes 151584 | tf_op jit(solution)/shard_map/ppermute | solution.py:519
  125.3 15.9 %shard_map.138 = (f32[592,1024]{1,0:T(8,128)}, bf16[592,1024]{1,0:T(8,128)(2,1)}, bf16[592,512]{1,0:T(8,128)(2,1)}, bf16[592,512]{1,0:T(8,128)(2,1)}, bf16[592,5...) custom-call(f32[592,1024]{1,0:T(8,128)} %maximum_convert_fusion.refs_0_, ...), custom_call_target="tpu_custom_call" | custom-call | flops 1 | bytes 1 | tf_op jit(solution)/shard_map/pallas_call | solution.py:173
  145.8 9.9 %collective-permute-done.15.refs_4_ = bf16[128,2048]{1,0:T(8,128)(2,1)S(1)} collective-permute-done((bf16[128,2048]{1,0:T(8,128)(2,1)}, bf16[128,2048]{1,0:T(8,128)(2,1)S(1)}, u32[]{:S(2)}, u32[]{:S(2)}) %collective-permute-start.15) | collective-permute-done | bytes 524320 | tf_op jit(solution)/shard_map/ppermute | solution.py:23
  164.4 10.4 %shard_map.141 = (f32[592,1024]{1,0:T(8,128)}, bf16[592,1024]{1,0:T(8,128)(2,1)}, bf16[592,2048]{1,0:T(8,128)(2,1)}, bf16[592,2048]{1,0:T(8,128)(2,1)}) custom-call(f32[592,1024]{1,0:T(8,128)} %get-tuple-element.265.refs_0_.u_ref, bf16[592,1024]{1,0:T(8,128)(2,1)} %get-tuple-element.266.refs_1_, bf16[592,1024]{1,0:T(8,128)(2,1)} %collective-permute-done.20.refs_2_, ...), custom_call_target="tpu_custom_call" | custom-call | flops 1 | bytes 1 | tf_op jit(solution)/shard_map/pallas_call | solution.py:173
  176.5 8.6 %collective-permute-done.23.refs_5_ = bf16[128,2048]{1,0:T(8,128)(2,1)} collective-permute-done((bf16[128,2048]{1,0:T(8,128)(2,1)S(1)}, bf16[128,2048]{1,0:T(8,128)(2,1)}, u32[]{:S(2)}, u32[]{:S(2)}) %collective-permute-start.23) | collective-permute-done | bytes 524320 | tf_op jit(solution)/shard_map/ppermute | solution.py:28
  185.1 11.1 %collective-permute-done.22.refs_4_ = bf16[128,2048]{1,0:T(8,128)(2,1)S(1)} collective-permute-done((bf16[128,2048]{1,0:T(8,128)(2,1)}, bf16[128,2048]{1,0:T(8,128)(2,1)S(1)}, u32[]{:S(2)}, u32[]{:S(2)}) %collective-permute-start.22) | collective-permute-done | bytes 524320 | tf_op jit(solution)/shard_map/ppermute | solution.py:23
  215.2 9.1 %collective-permute-done.29.refs_5_ = bf16[128,2048]{1,0:T(8,128)(2,1)} collective-permute-done((bf16[128,2048]{1,0:T(8,128)(2,1)}, bf16[128,2048]{1,0:T(8,128)(2,1)}, u32[]{:S(2)}, u32[]{:S(2)}) %collective-permute-start.29) | collective-permute-done | bytes 524320 | tf_op jit(solution)/shard_map/ppermute | solution.py:28
  224.2 10.7 %collective-permute-done.28.refs_4_ = bf16[128,2048]{1,0:T(8,128)(2,1)S(1)} collective-permute-done((bf16[128,2048]{1,0:T(8,128)(2,1)}, bf16[128,2048]{1,0:T(8,128)(2,1)S(1)}, u32[]{:S(2)}, u32[]{:S(2)}) %collective-permute-start.28) | collective-permute-done | bytes 524320 | tf_op jit(solution)/shard_map/ppermute | solution.py:23
  244.1 16.8 %shard_map.147 = (f32[592,1024]{1,0:T(8,128)}, bf16[592,1024]{1,0:T(8,128)(2,1)}, bf16[592,512]{1,0:T(8,128)(2,1)}, bf16[592,512]{1,0:T(8,128)(2,1)}, bf16[592,5...) custom-call(f32[592,1024]{1,0:T(8,128)} %get-tuple-element.291.refs_0_.refs, ...), custom_call_target="tpu_custom_call" | custom-call | flops 1 | bytes 1 | tf_op jit(solution)/shard_map/pallas_call | solution.py:173
  266.4 11.0 %collective-permute-done.35.refs_4_ = bf16[128,2048]{1,0:T(8,128)(2,1)S(1)} collective-permute-done((bf16[128,2048]{1,0:T(8,128)(2,1)}, bf16[128,2048]{1,0:T(8,128)(2,1)S(1)}, u32[]{:S(2)}, u32[]{:S(2)}) %collective-permute-start.35) | collective-permute-done | bytes 524320 | tf_op jit(solution)/shard_map/ppermute | solution.py:23
  285.8 10.7 %shard_map.150 = (f32[592,1024]{1,0:T(8,128)}, bf16[592,1024]{1,0:T(8,128)(2,1)}, bf16[592,2048]{1,0:T(8,128)(2,1)}, bf16[592,2048]{1,0:T(8,128)(2,1)}) custom-call(f32[592,1024]{1,0:T(8,128)} %get-tuple-element.304.refs_0_.u_ref, bf16[592,1024]{1,0:T(8,128)(2,1)} %get-tuple-element.305.refs_1_, bf16[592,1024]{1,0:T(8,128)(2,1)} %copy-done.142, ...), custom_call_target="tpu_custom_call" | custom-call | flops 1 | bytes 1 | tf_op jit(solution)/shard_map/pallas_call | solution.py:173
  305.2 7.7 %collective-permute-done.46.refs_9_ = bf16[296,256]{1,0:T(8,128)(2,1)S(1)} collective-permute-done((bf16[296,256]{1,0:T(8,128)(2,1)}, bf16[296,256]{1,0:T(8,128)(2,1)S(1)}, u32[]{:S(2)}, u32[]{:S(2)}) %collective-permute-start.46) | collective-permute-done | bytes 151584 | tf_op jit(solution)/shard_map/ppermute | solution.py:519
  340.4 11.4 %shard_map.154 = (bf16[592,2048]{1,0:T(8,128)(2,1)}, f32[1,1024]{1,0:T(1,128)S(1)}, f32[1,2048]{1,0:T(1,128)S(1)}, bf16[256,2048]{1,0:T(8,128)(2,1)}, bf16[256,2...) custom-call(f32[592,1024]{1,0:T(8,128)} %convert_multiply_fusion.refs_0_, ...), custom_call_target="tpu_custom_call" | custom-call | flops 1 | bytes 1 | tf_op jit(solution)/shard_map/pallas_call | solution.py:173
  388.1 22.3 %shard_map.161 = (f32[592,1024]{1,0:T(8,128)}, bf16[592,1024]{1,0:T(8,128)(2,1)}, bf16[592,512]{1,0:T(8,128)(2,1)}, bf16[592,512]{1,0:T(8,128)(2,1)}, bf16[592,5...) custom-call(f32[592,1024]{1,0:T(8,128)} %convert_multiply_fusion.ref, ...), custom_call_target="tpu_custom_call" | custom-call | flops 1 | bytes 1 | tf_op jit(solution)/shard_map/pallas_call | solution.py:173
  413.6 7.9 %shard_map.162 = (bf16[256,2048]{1,0:T(8,128)(2,1)S(1)}, bf16[256,2048]{1,0:T(8,128)(2,1)}, bf16[256,2048]{1,0:T(8,128)(2,1)}, bf16[256,2048]{1,0:T(8,128)(2,1)}) custom-call(bf16[592,1024]{1,0:T(8,128)(2,1)} %get-tuple-element.354.n_ref, bf16[592,1024]{1,0:T(8,128)(2,1)} %get-tuple-element.355.dz_ref, bf16[592,512]{1,0:T(8,128)(2,1)S(1)} %copy-done.95, ...), custom_call_target="tpu_custom_call" | custom-call | flops 1 | bytes 1 | tf_op jit(solution)/shard_map/pallas_call | solution.py:173
  441.5 21.8 %collective-permute-done.62.refs_5_ = bf16[128,2048]{1,0:T(8,128)(2,1)} collective-permute-done((bf16[128,2048]{1,0:T(8,128)(2,1)S(1)}, bf16[128,2048]{1,0:T(8,128)(2,1)}, u32[]{:S(2)}, u32[]{:S(2)}) %collective-permute-start.62) | collective-permute-done | bytes 524320 | tf_op jit(solution)/shard_map/ppermute | solution.py:23
  475.9 11.2 %shard_map.166 = (bf16[592,2048]{1,0:T(8,128)(2,1)}, f32[1,1024]{1,0:T(1,128)S(1)}, f32[1,2048]{1,0:T(1,128)S(1)}, bf16[256,2048]{1,0:T(8,128)(2,1)}, bf16[256,2...) custom-call(f32[592,1024]{1,0:T(8,128)} %get-tuple-element.381.refs_0_, ...), custom_call_target="tpu_custom_call" | custom-call | flops 1 | bytes 1 | tf_op jit(solution)/shard_map/pallas_call | solution.py:173
  487.1 8.1 %reduce-scatter.9.cloned.1.call-done.refs_5_ = bf16[256,512]{1,0:T(8,128)(2,1)} async-done(((bf16[256,2048]{1,0:T(8,128)(2,1)}), bf16[256,512]{1,0:T(8,128)(2,1)}) %reduce-scatter.9.cloned.1.call-update) | async-done | bytes 262160 | tf_op jit(solution)/shard_map/reduce_scatter | solution.py:105
  536.2 21.5 %shard_map.171 = (f32[592,1024]{1,0:T(8,128)}, bf16[592,1024]{1,0:T(8,128)(2,1)}, bf16[592,512]{1,0:T(8,128)(2,1)}, bf16[592,512]{1,0:T(8,128)(2,1)}, bf16[592,5...) custom-call(f32[592,1024]{1,0:T(8,128)} %get-tuple-element.381.refs_, ...), custom_call_target="tpu_custom_call" | custom-call | flops 1 | bytes 1 | tf_op jit(solution)/shard_map/pallas_call | solution.py:173
  561.0 7.9 %shard_map.172 = (bf16[256,2048]{1,0:T(8,128)(2,1)S(1)}, bf16[256,2048]{1,0:T(8,128)(2,1)}, bf16[256,2048]{1,0:T(8,128)(2,1)}, bf16[256,2048]{1,0:T(8,128)(2,1)}) custom-call(bf16[592,1024]{1,0:T(8,128)(2,1)} %get-tuple-element.416.n_ref, bf16[592,1024]{1,0:T(8,128)(2,1)} %get-tuple-element.417.dz_ref, bf16[592,512]{1,0:T(8,128)(2,1)S(1)} %copy-done.92, ...), custom_call_target="tpu_custom_call" | custom-call | flops 1 | bytes 1 | tf_op jit(solution)/shard_map/pallas_call | solution.py:173
  599.5 21.9 %collective-permute-done.86 = bf16[2,16,2048]{2,1,0:T(8,128)(2,1)S(1)} collective-permute-done((bf16[2,16,2048]{2,1,0:T(8,128)(2,1)S(1)}, bf16[2,16,2048]{2,1,0:T(8,128)(2,1)S(1)}, u32[]{:S(2)}, u32[]{:S(2)}) %collective-permute-start.86) | collective-permute-done | bytes 131104 | tf_op jit(solution)/shard_map/ppermute | solution.py:23
  643.8 9.9 %collective-permute-done.84 = bf16[128,2048]{1,0:T(8,128)(2,1)S(1)} collective-permute-done((bf16[128,2048]{1,0:T(8,128)(2,1)S(1)}, bf16[128,2048]{1,0:T(8,128)(2,1)S(1)}, u32[]{:S(2)}, u32[]{:S(2)}) %collective-permute-start.84) | collective-permute-done | bytes 524320 | tf_op jit(solution)/shard_map/ppermute | solution.py:23
  671.2 24.1 %reduce-scatter.15.cloned.1.call-done = bf16[272,512]{1,0:T(8,128)(2,1)} async-done(((bf16[272,2048]{1,0:T(8,128)(2,1)}), bf16[272,512]{1,0:T(8,128)(2,1)}) %reduce-scatter.15.cloned.1.call-update) | async-done | bytes 278544 | tf_op jit(solution)/shard_map/reduce_scatter | solution.py:105
  (774 shorter events, 369.1 us)
Async XLA Ops:
  7.2 40.5 %all-gather.7.cloned.1.call-start = ((), (), s32[]{:S(2)}) async-start(), calls=%async_computation.6 | async-start | bytes 1392640 | tf_op jit(solution)/shard_map/all_gather | solution.py:49
  16.7 74.1 %all-gather.9.cloned.1.call-start = ((), (), s32[]{:S(2)}) async-start(), calls=%async_computation.7 | async-start | bytes 1310720 | tf_op jit(solution)/shard_map/all_gather | solution.py:49
  47.7 108.7 %all-gather.11.cloned.1.call-start = ((), (), s32[]{:S(2)}) async-start(), calls=%async_computation.8 | async-start | bytes 1310720 | tf_op jit(solution)/shard_map/all_gather | solution.py:49
  93.0 52.7 %collective-permute-start.16 = (bf16[128,2048]{1,0:T(8,128)(2,1)S(1)}, bf16[128,2048]{1,0:T(8,128)(2,1)}, u32[]{:S(2)}, u32[]{:S(2)}) collective-permute-start(bf16[128,2048]{1,0:T(8,128)(2,1)S(1)} %get-tuple-element.542.refs_9_.refs_5_), channel_id=1, source_target_pairs={{0,8},{4,12},{8,0},{12,4},{1,9},{5,13},{9,1},{13,5},{2,10},{6,14},... | collective-permute-start | bytes 1572872 | tf_op jit(solution)/shard_map/ppermute | solution.py:28
  93.3 48.0 %collective-permute-start.12 = (bf16[128,2048]{1,0:T(8,128)(2,1)S(1)}, bf16[128,2048]{1,0:T(8,128)(2,1)S(1)}, u32[]{:S(2)}, u32[]{:S(2)}) collective-permute-start(bf16[128,2048]{1,0:T(8,128)(2,1)S(1)} %get-tuple-element.542.refs_9_.refs_5_), channel_id=1, source_target_pairs={{0,4},{4,0},{8,12},{12,8},{1,5},{5,1},{9,13},{13,9},{2,6},{6,2},{1... | collective-permute-start | bytes 1572872 | tf_op jit(solution)/shard_map/ppermute | solution.py:23
  94.5 51.2 %collective-permute-start.14 = (bf16[128,2048]{1,0:T(8,128)(2,1)}, bf16[128,2048]{1,0:T(8,128)(2,1)}, u32[]{:S(2)}, u32[]{:S(2)}) collective-permute-start(bf16[128,2048]{1,0:T(8,128)(2,1)} %get-tuple-element.543.refs_5_.refs_1_), channel_id=1, source_target_pairs={{0,4},{4,0},{8,12},{12,8},{1,5},{5,1},{9,13},{13,9},{2,6},{6,2},{1... | collective-permute-start | bytes 1572872 | tf_op jit(solution)/shard_map/ppermute | solution.py:23
  94.8 46.5 %collective-permute-start.11 = (bf16[128,2048]{1,0:T(8,128)(2,1)}, bf16[128,2048]{1,0:T(8,128)(2,1)S(1)}, u32[]{:S(2)}, u32[]{:S(2)}) collective-permute-start(bf16[128,2048]{1,0:T(8,128)(2,1)} %get-tuple-element.543.refs_5_.refs_1_), channel_id=1, source_target_pairs={{0,8},{4,12},{8,0},{12,4},{1,9},{5,13},{9,1},{13,5},{2,10},{6,14},... | collective-permute-start | bytes 1572872 | tf_op jit(solution)/shard_map/ppermute | solution.py:28
  96.0 89.1 %all-gather.13.cloned.1.call-start = ((), (), s32[]{:S(2)}) async-start(), calls=%async_computation.9 | async-start | bytes 1310720 | tf_op jit(solution)/shard_map/all_gather | solution.py:49
  158.8 76.6 %all-gather.15.cloned.1.call-start = ((), (), s32[]{:S(2)}) async-start(), calls=%async_computation.10 | async-start | bytes 1310720 | tf_op jit(solution)/shard_map/all_gather | solution.py:49
  197.3 69.1 %all-gather.17.cloned.1.call-start = ((), (), s32[]{:S(2)}) async-start(), calls=%async_computation.11 | async-start | bytes 1310720 | tf_op jit(solution)/shard_map/all_gather | solution.py:49
  238.6 225.4 %reduce-scatter.7.cloned.1.call-start = ((), (), s32[]{:S(2)}) async-start(), calls=%async_computation.12 | async-start | bytes 1310720 | tf_op jit(solution)/shard_map/reduce_scatter | solution.py:105
  376.7 45.9 %collective-permute-start.58 = (bf16[256,2048]{1,0:T(8,128)(2,1)}, bf16[256,2048]{1,0:T(8,128)(2,1)S(1)}, u32[]{:S(2)}, u32[]{:S(2)}) collective-permute-start(bf16[256,2048]{1,0:T(8,128)(2,1)} %get-tuple-element.367), channel_id=1, source_target_pairs={{0,4},{4,0},{8,12},{12,8},{1,5},{5,1},{9,13},{13,9},{2,6},{6,2},{1... | collective-permute-start | bytes 3145736 | tf_op jit(solution)/shard_map/ppermute | solution.py:23
  377.7 45.7 %collective-permute-start.59 = (bf16[256,2048]{1,0:T(8,128)(2,1)}, bf16[256,2048]{1,0:T(8,128)(2,1)}, u32[]{:S(2)}, u32[]{:S(2)}) collective-permute-start(bf16[256,2048]{1,0:T(8,128)(2,1)} %get-tuple-element.368), channel_id=1, source_target_pairs={{0,8},{4,12},{8,0},{12,4},{1,9},{5,13},{9,1},{13,5},{2,10},{6,14},... | collective-permute-start | bytes 3145736 | tf_op jit(solution)/shard_map/ppermute | solution.py:28
  383.8 38.7 %collective-permute-start.57 = (bf16[128,2048]{1,0:T(8,128)(2,1)S(1)}, bf16[128,2048]{1,0:T(8,128)(2,1)S(1)}, u32[]{:S(2)}, u32[]{:S(2)}) collective-permute-start(bf16[128,2048]{1,0:T(8,128)(2,1)S(1)} %get-tuple-element.516), channel_id=1, source_target_pairs={{0,4},{4,0},{8,12},{12,8},{1,5},{5,1},{9,13},{13,9},{2,6},{6,2},{1... | collective-permute-start | bytes 1572872 | tf_op jit(solution)/shard_map/ppermute | solution.py:23
  427.1 68.2 %reduce-scatter.9.cloned.1.call-start = ((), (), s32[]{:S(2)}) async-start(), calls=%async_computation.13 | async-start | bytes 1310720 | tf_op jit(solution)/shard_map/reduce_scatter | solution.py:105
  427.6 36.4 %collective-permute-start.63 = (bf16[256,2048]{1,0:T(8,128)(2,1)}, bf16[256,2048]{1,0:T(8,128)(2,1)}, u32[]{:S(2)}, u32[]{:S(2)}) collective-permute-start(bf16[256,2048]{1,0:T(8,128)(2,1)} %get-tuple-element.379), channel_id=1, source_target_pairs={{0,4},{4,0},{8,12},{12,8},{1,5},{5,1},{9,13},{13,9},{2,6},{6,2},{1... | collective-permute-start | bytes 3145736 | tf_op jit(solution)/shard_map/ppermute | solution.py:23
  468.4 56.3 %reduce-scatter.11.cloned.1.call-start = ((), (), s32[]{:S(2)}) async-start(), calls=%async_computation.14 | async-start | bytes 1310720 | tf_op jit(solution)/shard_map/reduce_scatter | solution.py:105
  498.1 137.3 %reduce-scatter.13.cloned.1.call-start = ((), (), s32[]{:S(2)}) async-start(), calls=%async_computation.15 | async-start | bytes 1310720 | tf_op jit(solution)/shard_map/reduce_scatter | solution.py:105
  530.2 41.1 %collective-permute-start.71 = (bf16[128,2048]{1,0:T(8,128)(2,1)}, bf16[128,2048]{1,0:T(8,128)(2,1)}, u32[]{:S(2)}, u32[]{:S(2)}) collective-permute-start(bf16[128,2048]{1,0:T(8,128)(2,1)} %get-tuple-element.504), channel_id=1, source_target_pairs={{0,4},{4,0},{8,12},{12,8},{1,5},{5,1},{9,13},{13,9},{2,6},{6,2},{1... | collective-permute-start | bytes 1572872 | tf_op jit(solution)/shard_map/ppermute | solution.py:23
  531.0 40.2 %collective-permute-start.72 = (bf16[256,2048]{1,0:T(8,128)(2,1)S(1)}, bf16[256,2048]{1,0:T(8,128)(2,1)S(1)}, u32[]{:S(2)}, u32[]{:S(2)}) collective-permute-start(bf16[256,2048]{1,0:T(8,128)(2,1)S(1)} %copy-done.85), channel_id=1, source_target_pairs={{0,4},{4,0},{8,12},{12,8},{1,5},{5,1},{9,13},{13,9},{2,6},{6,2},{1... | collective-permute-start | bytes 3145736 | tf_op jit(solution)/shard_map/ppermute | solution.py:23
  531.7 39.6 %collective-permute-start.73 = (bf16[256,2048]{1,0:T(8,128)(2,1)S(1)}, bf16[256,2048]{1,0:T(8,128)(2,1)}, u32[]{:S(2)}, u32[]{:S(2)}) collective-permute-start(bf16[256,2048]{1,0:T(8,128)(2,1)S(1)} %copy-done.87), channel_id=1, source_target_pairs={{0,8},{4,12},{8,0},{12,4},{1,9},{5,13},{9,1},{13,5},{2,10},{6,14},... | collective-permute-start | bytes 3145736 | tf_op jit(solution)/shard_map/ppermute | solution.py:28
  577.8 88.5 %reduce-scatter.17.cloned.1.call-start = ((), (), s32[]{:S(2)}) async-start(), calls=%async_computation.17 | async-start | bytes 1310720 | tf_op jit(solution)/shard_map/reduce_scatter | solution.py:105
  580.9 41.0 %collective-permute-start.79 = (bf16[128,2048]{1,0:T(8,128)(2,1)}, bf16[128,2048]{1,0:T(8,128)(2,1)}, u32[]{:S(2)}, u32[]{:S(2)}) collective-permute-start(bf16[128,2048]{1,0:T(8,128)(2,1)} %get-tuple-element.500), channel_id=1, source_target_pairs={{0,4},{4,0},{8,12},{12,8},{1,5},{5,1},{9,13},{13,9},{2,6},{6,2},{1... | collective-permute-start | bytes 1572872 | tf_op jit(solution)/shard_map/ppermute | solution.py:23
  639.9 55.4 %reduce-scatter.15.cloned.1.call-start = ((), (), s32[]{:S(2)}) async-start(), calls=%async_computation.16 | async-start | bytes 1392640 | tf_op jit(solution)/shard_map/reduce_scatter | solution.py:105
  (246 other events, 2514.1 us)
Sparse Core Ops, SparseCore 0:
  16.8 30.8 all-gather.6
  49.9 38.8 all-gather.8
  96.1 29.1 all-gather.10
  158.9 25.3 all-gather.12
  197.4 26.9 all-gather.14
  238.7 25.4 all-gather.16
  427.2 25.9 reduce-scatter.6
  468.5 26.6 reduce-scatter.8
  498.2 25.7 reduce-scatter.10
  577.9 24.9 reduce-scatter.12
  640.0 26.1 reduce-scatter.16
  668.5 26.8 reduce-scatter.14

commit v7 on v6

--- a/solution.py
+++ b/solution.py
@@ -574,7 +574,7 @@
             if layer == 0 and number == 0:
                 room = extra // 2
                 both = [shard[depth : depth + room, :wide] for shard in shards]
-                cols = jnp.concatenate([cols[:mid], *both, cols[mid:depth]], 0)
+                cols = jnp.concatenate([cols[:depth], *both], 0)
             else:
                 cols = cols[:depth]
             columns.append(cols)
@@ -624,8 +624,12 @@
         blocks = [lax.dynamic_index_in_dim(blocks, (place - i) % n_tensor, 0, False) for i in range(n_tensor)]
         return jnp.stack(blocks)
 
-    def small_of(piece):
-        extras = jnp.concatenate(piece, 0)
+    def small_of(extras):
+        if n_dp != 4:
+            extras = lax.all_gather(extras, "dp", axis=0, tiled=True)
+        else:
+            extras = jnp.concatenate([extras, swap_y(extras)], 0)
+            extras = jnp.concatenate([extras, swap_x(extras)], 0)
         both = by_chip(extras.reshape(n_dp, extra, -1), spot).astype(jnp.float32)
         both = both.reshape(n_dp, 2, extra // 2, n_tensor, wide).transpose(1, 0, 3, 2, 4)
         both = both.reshape(2, n_dp, n_tensor, -1)
@@ -639,7 +643,6 @@
         return [(rows[i], parts[0][i : i + 1], parts[1][i : i + 1], parts[2][i : i + 1]) for i in range(2)]
 
     number = len(columns)
-    cut = [mid + extra if k == 0 else mid for k in range(number)]
     halves, near, far = [None] * number, [None] * number, [None] * number
     params = [dict(), dict()]
     blocks_in, blocks_cot = to_send(half_in), to_send(half_cot)
@@ -651,6 +654,7 @@
         if 0 <= r - 1 < number:
             near[r - 1] = exchange_one(*halves[r - 1])
         if r == 1:
+            smalls = small_of(extra_rows)
             blocks_in = shifts(blocks_in)
         if r == number:
             blocks_cot = shifts(blocks_cot)
@@ -660,14 +664,8 @@
             layer, kind = k // 3, k % 3
             one = params[layer]
             first, second = arrived(*halves[k], near[k], far[k])
-            if k == 0:
-                blocks = [p.reshape((-1, mid + extra) + p.shape[1:]) for p in first]
-                smalls = small_of([p[:, mid:].reshape(-1, p.shape[-1]) for p in blocks])
-                params[0]["small"], params[1]["small"] = smalls
-                if n_dp != 4:
-                    first = [p[:, :mid].reshape(-1, p.shape[-1]) for p in blocks]
             pieces = first + second
-            counts = [mid if n_dp == 4 else p.shape[0] for p in pieces]
+            counts = [p.shape[0] for p in pieces]
             weights = (pieces, counts)
             rows, q_bias, v_bias, up_bias = one["small"]
             if pair is not None:
@@ -706,6 +704,8 @@
                 tied += near[r - 1] + far[r - 1]
             if r <= 1:
                 extras += blocks_in
+            if r == 1:
+                extras += [v for layer in range(2) for v in smalls[layer]]
             if r >= number - 1:
                 extras += blocks_cot
             if r + 1 < number:
@@ -713,6 +713,9 @@
             done = tie(tied + extras, [])
             if r + 1 < number:
                 columns[r + 1] = done.pop()
+            if r == 1:
+                done, smalls = done[:-8], done[-8:]
+                params[0]["small"], params[1]["small"] = smalls[:4], smalls[4:]
             if r <= 1:
                 done, blocks_in = done[:-n_tensor], done[-n_tensor:]
             if r >= number - 1:
@@ -723,7 +726,9 @@
                 pair = [done[-1]]
             at = 0
             if r < number:
-                halves[r] = (done[0][: cut[r]], done[0][cut[r] :])
+                halves[r] = (done[0][:mid], done[0][mid:depth])
+                if r == 0:
+                    extra_rows = done[0][depth:]
                 at = 1
             if 0 <= r - 1 < number:
                 near[r - 1] = done[at : at + 2]
@@ -733,9 +738,28 @@
     last_rows = params[1]["small"][0]
     out_blocks = image_rows(live, [state, *pair], last_rows[7:8])
 
+    sums = [dict(), dict()]
+
+    def small_grads():
+        packed = []
+        for layer in range(2):
+            total = sums[layer]
+            full = jnp.concatenate([total["one"], total["mid"], total["out"]], 0)
+            full = absolute(jnp.where(core == layer, full, 0.0), spot)
+            q_row = spread_cols(core, total["q"][0], n_tensor)
+            v_row = spread_cols(core, total["v"][0], n_tensor)
+            up_row = spread_cols(core, total["up_bias"][0], n_tensor)
+            rows = jnp.concatenate([full[:2], q_row[None], v_row[None], full[2:]], 0)
+            rows = rows.reshape(8, n_tensor, n_dp, -1).transpose(2, 1, 0, 3).reshape(n_dp, n_tensor, -1)
+            up_row = up_row.reshape(n_tensor, n_dp, -1).transpose(1, 0, 2)
+            packed.append(jnp.concatenate([rows, up_row], -1))
+        ours = jnp.where(is_first, packed[0], packed[1])
+        other = swap(jnp.where(is_first, packed[1], packed[0]))
+        little = (ours + other).astype(jnp.bfloat16)
+        return little
+
     grads, got, moved, settled = [None] * number, [None] * number, [None] * number, [None] * number
     made = [0, 1, 2, 4, 5, 6]
-    sums = [dict(), dict()]
     grad = cotangent
     for r in range(8):
         layer, stage = 1 - r // 4, r % 4
@@ -750,8 +774,9 @@
             elif r == made[c] + 2:
                 stay, come = scatter_two(*grads[c][2:], got[c])
                 moved[c] = [*stay, *come]
-                slots.append((moved, c, len(moved[c])))
-                tied += moved[c]
+                if r < 7:
+                    slots.append((moved, c, len(moved[c])))
+                    tied += moved[c]
             elif r == made[c] + 3:
                 settled[c] = scatter_column(moved[c][:2], moved[c][2:])
                 slots.append((settled, c, 0))
@@ -779,7 +804,7 @@
             if r == 7:
                 one_scale = jnp.ones((), jnp.float32)
                 no_bias = jnp.zeros((1, grad.shape[1]), jnp.float32)
-                carry = shifts(image_rows(one_scale, [grad], no_bias))
+                carry = [small_grads(), *shifts(image_rows(one_scale, [grad], no_bias))]
         if new is not None:
             c = made.index(r)
             grads[c] = new
@@ -800,7 +825,7 @@
             elif r < 7:
                 grad = done[0]
             else:
-                grad_blocks = done[:n_tensor]
+                little, grad_blocks = done[0], done[1 : 1 + n_tensor]
             if r == 1:
                 out_blocks = done[1 : 1 + n_tensor]
             done = done[len(carry) :]
@@ -812,21 +837,6 @@
                 done = done[max(count, 1) :]
 
     grad_rows, out_rows = by_image(grad_blocks), by_image(out_blocks)
-    packed = []
-    for layer in range(2):
-        total = sums[layer]
-        full = jnp.concatenate([total["one"], total["mid"], total["out"]], 0)
-        full = absolute(jnp.where(core == layer, full, 0.0), spot)
-        q_row = spread_cols(core, total["q"][0], n_tensor)
-        v_row = spread_cols(core, total["v"][0], n_tensor)
-        up_row = spread_cols(core, total["up_bias"][0], n_tensor)
-        rows = jnp.concatenate([full[:2], q_row[None], v_row[None], full[2:]], 0)
-        rows = rows.reshape(8, n_tensor, n_dp, -1).transpose(2, 1, 0, 3).reshape(n_dp, n_tensor, -1)
-        up_row = up_row.reshape(n_tensor, n_dp, -1).transpose(1, 0, 2)
-        packed.append(jnp.concatenate([rows, up_row], -1))
-    ours = jnp.where(is_first, packed[0], packed[1])
-    other = swap(jnp.where(is_first, packed[1], packed[0]))
-    little = (ours + other).astype(jnp.bfloat16)
     room = jnp.zeros((n_dp, n_tensor, extra * wide - small_size), little.dtype)
     little = jnp.concatenate([little, room], -1).reshape(n_dp, n_tensor, extra, wide)
     little = by_arrival(little.transpose(0, 2, 1, 3).reshape(n_dp, extra, -1), spot)

time: 718 us -> 698 us (0.972)
  waiting for transfers between devices: 253 us -> 229 us
  starting transfers between devices: 79 us -> 99.8 us
  local copies, waits for them, and re-layouts: 102 us -> 86.5 us
    ppermute x31 -> x32, waiting for transfers between devices: 110 us -> 89.4 us  [swap_x(): return lax.ppermute(value, 'dp', [(i, i ^ 1) for i in range(n)])]
    reduce_scatter x6, waiting for transfers between devices: 35.9 us -> 26.5 us  [scatter_column(): lax.psum_scatter(jnp.concatenate(stay, 0), 'tensor', scatter_dimension=1,...]
    ppermute x12, starting transfers between devices: 8.25 us -> 16 us  [shifts(): lax.ppermute(blocks[d], 'tensor', [(i, (i + d) % n) for i in range(n)])]
    ppermute x12, waiting for transfers between devices: 39.9 us -> 47.6 us  [shifts(): lax.ppermute(blocks[d], 'tensor', [(i, (i + d) % n) for i in range(n)])]
    ppermute x17, starting transfers between devices: 23.4 us -> 31.1 us  [swap(): return lax.ppermute(value, 'section', [(0, 1), (1, 0)])]
    ppermute x31 -> x32, waiting for transfers between devices: 38.8 us -> 33.9 us  [swap_y(): return lax.ppermute(value, 'dp', [(i, i ^ 2) for i in range(n)])]
    ppermute x31 -> x32, starting transfers between devices: 21.9 us -> 26 us  [swap_y(): return lax.ppermute(value, 'dp', [(i, i ^ 2) for i in range(n)])]
    unnamed x350 -> x354, local copies, waits for them, and re-layouts: 51.5 us -> 54.9 us
  transfers between devices with their start and end apart: 103 -> 105, of which waited for: 39 -> 44; matrix products, arithmetic and copies ran while one was open for 15% -> 12% of each run, Pallas kernels for 27% -> 27%
where the time goes in v7:
time: 698 us; the launch traced here: 690 us
  waiting for transfers between devices  229 us (33%)
  Pallas kernels  191 us (27%)
  starting transfers between devices  99.8 us (14%)
  local copies, waits for them, and re-layouts  86.5 us (12%)
  other arithmetic  67.5 us (10%)
  between operations  17.4 us (2%)
    pallas_call x18, Pallas kernels, run(): pl.pallas_call(kernel, out_shape=list(outs), in_specs=[block] * len(ins),...  184 us
    ppermute x32, waiting for transfers between devices, swap_x(): return lax.ppermute(value, 'dp', [(i, i ^ 1) for i in range(n)])  89.4 us
    unnamed x354, local copies, waits for them, and re-layouts  54.9 us
    ppermute x12, waiting for transfers between devices, shifts(): lax.ppermute(blocks[d], 'tensor', [(i, (i + d) % n) for i in range(n)])  47.6 us
    ppermute x32, waiting for transfers between devices, swap_y(): return lax.ppermute(value, 'dp', [(i, i ^ 2) for i in range(n)])  33.9 us
    ppermute x17, starting transfers between devices, swap(): return lax.ppermute(value, 'section', [(0, 1), (1, 0)])  31.1 us
    all_gather x6, waiting for transfers between devices, gather_column(): return lax.all_gather(shard, 'tensor', axis=1, tiled=True)  26.8 us
    reduce_scatter x6, waiting for transfers between devices, scatter_column(): lax.psum_scatter(jnp.concatenate(stay, 0), 'tensor', scatter_dimension=1,...  26.5 us
  transfers between devices with their start and end apart: 105, of which 44 were waited for; matrix products, arithmetic and copies ran while one was open for 12% of the time, Pallas kernels for 27%

profile of v7, /device:TPU:1, one launch (start us, length us, event | category | flops | bytes accessed | tf_op | source)
XLA Modules:
  0.0 690.2 jit_solution(12097632269206373537)
XLA Ops:
  23.8 24.0 %all-gather.7.cloned.1.call-done.refs_0_ = bf16[272,2048]{1,0:T(8,128)(2,1)} async-done(((bf16[272,512]{1,0:T(8,128)(2,1)}), bf16[272,2048]{1,0:T(8,128)(2,1)}) %all-gather.7.cloned.1.call-update) | async-done | bytes 1114128 | tf_op jit(solution)/shard_map/all_gather | solution.py:49
  68.0 9.6 %collective-permute-done.2.refs_1_ = bf16[128,2048]{1,0:T(8,128)(2,1)S(1)} collective-permute-done((bf16[128,2048]{1,0:T(8,128)(2,1)}, bf16[128,2048]{1,0:T(8,128)(2,1)S(1)}, u32[]{:S(2)}, u32[]{:S(2)}) %collective-permute-start.2) | collective-permute-done | bytes 524320 | tf_op jit(solution)/shard_map/ppermute | solution.py:28
  107.7 15.5 %shard_map.138 = (f32[592,1024]{1,0:T(8,128)}, bf16[592,1024]{1,0:T(8,128)(2,1)}, bf16[592,512]{1,0:T(8,128)(2,1)}, bf16[592,512]{1,0:T(8,128)(2,1)}, bf16[592,5...) custom-call(f32[592,1024]{1,0:T(8,128)} %maximum_convert_fusion.refs_0_, ...), custom_call_target="tpu_custom_call" | custom-call | flops 1 | bytes 1 | tf_op jit(solution)/shard_map/pallas_call | solution.py:173
  128.1 8.6 %collective-permute-done.17.refs_4_ = bf16[128,2048]{1,0:T(8,128)(2,1)S(1)} collective-permute-done((bf16[128,2048]{1,0:T(8,128)(2,1)}, bf16[128,2048]{1,0:T(8,128)(2,1)S(1)}, u32[]{:S(2)}, u32[]{:S(2)}) %collective-permute-start.17) | collective-permute-done | bytes 524320 | tf_op jit(solution)/shard_map/ppermute | solution.py:23
  148.4 10.0 %shard_map.141 = (f32[592,1024]{1,0:T(8,128)}, bf16[592,1024]{1,0:T(8,128)(2,1)}, bf16[592,2048]{1,0:T(8,128)(2,1)}, bf16[592,2048]{1,0:T(8,128)(2,1)}) custom-call(f32[592,1024]{1,0:T(8,128)} %get-tuple-element.273.refs_0_.u_ref, bf16[592,1024]{1,0:T(8,128)(2,1)} %get-tuple-element.274.refs_1_, bf16[592,1024]{1,0:T(8,128)(2,1)} %collective-permute-done.22.refs_2_, ...), custom_call_target="tpu_custom_call" | custom-call | flops 1 | bytes 1 | tf_op jit(solution)/shard_map/pallas_call | solution.py:173
  167.9 10.3 %collective-permute-done.24.refs_4_ = bf16[128,2048]{1,0:T(8,128)(2,1)S(1)} collective-permute-done((bf16[128,2048]{1,0:T(8,128)(2,1)}, bf16[128,2048]{1,0:T(8,128)(2,1)S(1)}, u32[]{:S(2)}, u32[]{:S(2)}) %collective-permute-start.24) | collective-permute-done | bytes 524320 | tf_op jit(solution)/shard_map/ppermute | solution.py:23
  198.1 8.2 %collective-permute-done.31.refs_5_ = bf16[128,2048]{1,0:T(8,128)(2,1)} collective-permute-done((bf16[128,2048]{1,0:T(8,128)(2,1)}, bf16[128,2048]{1,0:T(8,128)(2,1)}, u32[]{:S(2)}, u32[]{:S(2)}) %collective-permute-start.31) | collective-permute-done | bytes 524320 | tf_op jit(solution)/shard_map/ppermute | solution.py:28
  206.3 10.7 %collective-permute-done.30.refs_4_ = bf16[128,2048]{1,0:T(8,128)(2,1)S(1)} collective-permute-done((bf16[128,2048]{1,0:T(8,128)(2,1)}, bf16[128,2048]{1,0:T(8,128)(2,1)S(1)}, u32[]{:S(2)}, u32[]{:S(2)}) %collective-permute-start.30) | collective-permute-done | bytes 524320 | tf_op jit(solution)/shard_map/ppermute | solution.py:23
  226.2 17.0 %shard_map.147 = (f32[592,1024]{1,0:T(8,128)}, bf16[592,1024]{1,0:T(8,128)(2,1)}, bf16[592,512]{1,0:T(8,128)(2,1)}, bf16[592,512]{1,0:T(8,128)(2,1)}, bf16[592,5...) custom-call(f32[592,1024]{1,0:T(8,128)} %get-tuple-element.300.refs_0_.refs, ...), custom_call_target="tpu_custom_call" | custom-call | flops 1 | bytes 1 | tf_op jit(solution)/shard_map/pallas_call | solution.py:173
  248.8 10.7 %collective-permute-done.37.refs_4_ = bf16[128,2048]{1,0:T(8,128)(2,1)S(1)} collective-permute-done((bf16[128,2048]{1,0:T(8,128)(2,1)}, bf16[128,2048]{1,0:T(8,128)(2,1)S(1)}, u32[]{:S(2)}, u32[]{:S(2)}) %collective-permute-start.37) | collective-permute-done | bytes 524320 | tf_op jit(solution)/shard_map/ppermute | solution.py:23
  268.2 10.7 %shard_map.150 = (f32[592,1024]{1,0:T(8,128)}, bf16[592,1024]{1,0:T(8,128)(2,1)}, bf16[592,2048]{1,0:T(8,128)(2,1)}, bf16[592,2048]{1,0:T(8,128)(2,1)}) custom-call(f32[592,1024]{1,0:T(8,128)} %get-tuple-element.316.refs_0_.u_ref, bf16[592,1024]{1,0:T(8,128)(2,1)} %get-tuple-element.317.refs_1_, bf16[592,1024]{1,0:T(8,128)(2,1)} %copy-done.152, ...), custom_call_target="tpu_custom_call" | custom-call | flops 1 | bytes 1 | tf_op jit(solution)/shard_map/pallas_call | solution.py:173
  323.0 11.4 %shard_map.154 = (bf16[592,2048]{1,0:T(8,128)(2,1)}, f32[1,1024]{1,0:T(1,128)S(1)}, f32[1,2048]{1,0:T(1,128)S(1)}, bf16[256,2048]{1,0:T(8,128)(2,1)}, bf16[256,2...) custom-call(f32[592,1024]{1,0:T(8,128)} %convert_multiply_fusion.refs_0_, ...), custom_call_target="tpu_custom_call" | custom-call | flops 1 | bytes 1 | tf_op jit(solution)/shard_map/pallas_call | solution.py:173
  371.1 22.4 %shard_map.161 = (f32[592,1024]{1,0:T(8,128)}, bf16[592,1024]{1,0:T(8,128)(2,1)}, bf16[592,512]{1,0:T(8,128)(2,1)}, bf16[592,512]{1,0:T(8,128)(2,1)}, bf16[592,5...) custom-call(f32[592,1024]{1,0:T(8,128)} %convert_multiply_fusion.ref, ...), custom_call_target="tpu_custom_call" | custom-call | flops 1 | bytes 1 | tf_op jit(solution)/shard_map/pallas_call | solution.py:173
  396.7 7.9 %shard_map.162 = (bf16[256,2048]{1,0:T(8,128)(2,1)S(1)}, bf16[256,2048]{1,0:T(8,128)(2,1)}, bf16[256,2048]{1,0:T(8,128)(2,1)}, bf16[256,2048]{1,0:T(8,128)(2,1)}) custom-call(bf16[592,1024]{1,0:T(8,128)(2,1)} %get-tuple-element.367.n_ref, bf16[592,1024]{1,0:T(8,128)(2,1)} %get-tuple-element.368.dz_ref, bf16[592,512]{1,0:T(8,128)(2,1)S(1)} %copy-done.100, ...), custom_call_target="tpu_custom_call" | custom-call | flops 1 | bytes 1 | tf_op jit(solution)/shard_map/pallas_call | solution.py:173
  424.6 21.8 %collective-permute-done.64.refs_5_ = bf16[128,2048]{1,0:T(8,128)(2,1)} collective-permute-done((bf16[128,2048]{1,0:T(8,128)(2,1)S(1)}, bf16[128,2048]{1,0:T(8,128)(2,1)}, u32[]{:S(2)}, u32[]{:S(2)}) %collective-permute-start.64) | collective-permute-done | bytes 524320 | tf_op jit(solution)/shard_map/ppermute | solution.py:23
  457.5 11.2 %shard_map.166 = (bf16[592,2048]{1,0:T(8,128)(2,1)}, f32[1,1024]{1,0:T(1,128)S(1)}, f32[1,2048]{1,0:T(1,128)S(1)}, bf16[256,2048]{1,0:T(8,128)(2,1)}, bf16[256,2...) custom-call(f32[592,1024]{1,0:T(8,128)} %get-tuple-element.394.refs_0_, ...), custom_call_target="tpu_custom_call" | custom-call | flops 1 | bytes 1 | tf_op jit(solution)/shard_map/pallas_call | solution.py:173
  469.0 8.7 %reduce-scatter.9.cloned.1.call-done.refs_5_ = bf16[256,512]{1,0:T(8,128)(2,1)} async-done(((bf16[256,2048]{1,0:T(8,128)(2,1)}), bf16[256,512]{1,0:T(8,128)(2,1)}) %reduce-scatter.9.cloned.1.call-update) | async-done | bytes 262160 | tf_op jit(solution)/shard_map/reduce_scatter | solution.py:105
  499.8 7.4 %collective-permute-done.69.refs_6_ = bf16[256,2048]{1,0:T(8,128)(2,1)} collective-permute-done((bf16[256,2048]{1,0:T(8,128)(2,1)}, bf16[256,2048]{1,0:T(8,128)(2,1)}, u32[]{:S(2)}, u32[]{:S(2)}) %collective-permute-start.69) | collective-permute-done | bytes 1048608 | tf_op jit(solution)/shard_map/ppermute | solution.py:23
  519.0 21.6 %shard_map.171 = (f32[592,1024]{1,0:T(8,128)}, bf16[592,1024]{1,0:T(8,128)(2,1)}, bf16[592,512]{1,0:T(8,128)(2,1)}, bf16[592,512]{1,0:T(8,128)(2,1)}, bf16[592,5...) custom-call(f32[592,1024]{1,0:T(8,128)} %get-tuple-element.394.refs_, ...), custom_call_target="tpu_custom_call" | custom-call | flops 1 | bytes 1 | tf_op jit(solution)/shard_map/pallas_call | solution.py:173
  543.8 7.9 %shard_map.172 = (bf16[256,2048]{1,0:T(8,128)(2,1)S(1)}, bf16[256,2048]{1,0:T(8,128)(2,1)}, bf16[256,2048]{1,0:T(8,128)(2,1)}, bf16[256,2048]{1,0:T(8,128)(2,1)}) custom-call(bf16[592,1024]{1,0:T(8,128)(2,1)} %get-tuple-element.429.n_ref, bf16[592,1024]{1,0:T(8,128)(2,1)} %get-tuple-element.430.dz_ref, bf16[592,512]{1,0:T(8,128)(2,1)S(1)} %copy-done.103, ...), custom_call_target="tpu_custom_call" | custom-call | flops 1 | bytes 1 | tf_op jit(solution)/shard_map/pallas_call | solution.py:173
  595.0 7.9 %collective-permute-done.80.refs_4_ = bf16[296,256]{1,0:T(8,128)(2,1)S(1)} collective-permute-done((bf16[296,256]{1,0:T(8,128)(2,1)S(1)}, bf16[296,256]{1,0:T(8,128)(2,1)S(1)}, u32[]{:S(2)}, u32[]{:S(2)}) %collective-permute-start.80) | collective-permute-done | bytes 151584 | tf_op jit(solution)/shard_map/ppermute | solution.py:519
  602.9 19.1 %collective-permute-done.79.refs_3_ = bf16[296,256]{1,0:T(8,128)(2,1)S(1)} collective-permute-done((bf16[296,256]{1,0:T(8,128)(2,1)S(1)}, bf16[296,256]{1,0:T(8,128)(2,1)S(1)}, u32[]{:S(2)}, u32[]{:S(2)}) %collective-permute-start.79) | collective-permute-done | bytes 151584 | tf_op jit(solution)/shard_map/ppermute | solution.py:519
  632.2 7.7 %collective-permute-done.85 = bf16[128,2048]{1,0:T(8,128)(2,1)S(1)} collective-permute-done((bf16[128,2048]{1,0:T(8,128)(2,1)S(1)}, bf16[128,2048]{1,0:T(8,128)(2,1)S(1)}, u32[]{:S(2)}, u32[]{:S(2)}) %collective-permute-start.85) | collective-permute-done | bytes 524320 | tf_op jit(solution)/shard_map/ppermute | solution.py:23
  657.0 17.8 %reduce-scatter.15.cloned.1.call-done = bf16[272,512]{1,0:T(8,128)(2,1)} async-done(((bf16[272,2048]{1,0:T(8,128)(2,1)}), bf16[272,512]{1,0:T(8,128)(2,1)}) %reduce-scatter.15.cloned.1.call-update) | async-done | bytes 278544 | tf_op jit(solution)/shard_map/reduce_scatter | solution.py:105
  (778 shorter events, 364.9 us)
Async XLA Ops:
  7.2 40.5 %all-gather.7.cloned.1.call-start = ((), (), s32[]{:S(2)}) async-start(), calls=%async_computation.6 | async-start | bytes 1392640 | tf_op jit(solution)/shard_map/all_gather | solution.py:49
  16.7 78.1 %all-gather.9.cloned.1.call-start = ((), (), s32[]{:S(2)}) async-start(), calls=%async_computation.7 | async-start | bytes 1310720 | tf_op jit(solution)/shard_map/all_gather | solution.py:49
  55.1 37.2 %collective-permute-start.6 = (bf16[128,2048]{1,0:T(8,128)(2,1)S(1)}, bf16[128,2048]{1,0:T(8,128)(2,1)S(1)}, u32[]{:S(2)}, u32[]{:S(2)}) collective-permute-start(bf16[128,2048]{1,0:T(8,128)(2,1)S(1)} %get-tuple-element.531.refs_9_.refs_14_), channel_id=1, source_target_pairs={{0,8},{4,12},{8,0},{12,4},{1,9},{5,13},{9,1},{13,5},{2,10},{6,14},... | collective-permute-start | bytes 1572872 | tf_op jit(solution)/shard_map/ppermute | solution.py:28
  56.6 35.8 %collective-permute-start.4 = (bf16[128,2048]{1,0:T(8,128)(2,1)}, bf16[128,2048]{1,0:T(8,128)(2,1)S(1)}, u32[]{:S(2)}, u32[]{:S(2)}) collective-permute-start(bf16[128,2048]{1,0:T(8,128)(2,1)} %get-tuple-element.532.refs_5_.refs_10_), channel_id=1, source_target_pairs={{0,4},{4,0},{8,12},{12,8},{1,5},{5,1},{9,13},{13,9},{2,6},{6,2},{1... | collective-permute-start | bytes 1572872 | tf_op jit(solution)/shard_map/ppermute | solution.py:23
  58.1 79.2 %all-gather.11.cloned.1.call-start = ((), (), s32[]{:S(2)}) async-start(), calls=%async_computation.8 | async-start | bytes 1310720 | tf_op jit(solution)/shard_map/all_gather | solution.py:49
  100.2 67.7 %all-gather.13.cloned.1.call-start = ((), (), s32[]{:S(2)}) async-start(), calls=%async_computation.9 | async-start | bytes 1310720 | tf_op jit(solution)/shard_map/all_gather | solution.py:49
  140.3 77.2 %all-gather.15.cloned.1.call-start = ((), (), s32[]{:S(2)}) async-start(), calls=%async_computation.10 | async-start | bytes 1310720 | tf_op jit(solution)/shard_map/all_gather | solution.py:49
  179.5 69.3 %all-gather.17.cloned.1.call-start = ((), (), s32[]{:S(2)}) async-start(), calls=%async_computation.11 | async-start | bytes 1310720 | tf_op jit(solution)/shard_map/all_gather | solution.py:49
  220.7 225.9 %reduce-scatter.7.cloned.1.call-start = ((), (), s32[]{:S(2)}) async-start(), calls=%async_computation.12 | async-start | bytes 1310720 | tf_op jit(solution)/shard_map/reduce_scatter | solution.py:105
  359.7 45.9 %collective-permute-start.60 = (bf16[256,2048]{1,0:T(8,128)(2,1)}, bf16[256,2048]{1,0:T(8,128)(2,1)S(1)}, u32[]{:S(2)}, u32[]{:S(2)}) collective-permute-start(bf16[256,2048]{1,0:T(8,128)(2,1)} %get-tuple-element.380), channel_id=1, source_target_pairs={{0,4},{4,0},{8,12},{12,8},{1,5},{5,1},{9,13},{13,9},{2,6},{6,2},{1... | collective-permute-start | bytes 3145736 | tf_op jit(solution)/shard_map/ppermute | solution.py:23
  360.3 46.2 %collective-permute-start.61 = (bf16[256,2048]{1,0:T(8,128)(2,1)}, bf16[256,2048]{1,0:T(8,128)(2,1)}, u32[]{:S(2)}, u32[]{:S(2)}) collective-permute-start(bf16[256,2048]{1,0:T(8,128)(2,1)} %get-tuple-element.381), channel_id=1, source_target_pairs={{0,8},{4,12},{8,0},{12,4},{1,9},{5,13},{9,1},{13,5},{2,10},{6,14},... | collective-permute-start | bytes 3145736 | tf_op jit(solution)/shard_map/ppermute | solution.py:28
  365.5 40.2 %collective-permute-start.59 = (bf16[128,2048]{1,0:T(8,128)(2,1)S(1)}, bf16[128,2048]{1,0:T(8,128)(2,1)S(1)}, u32[]{:S(2)}, u32[]{:S(2)}) collective-permute-start(bf16[128,2048]{1,0:T(8,128)(2,1)S(1)} %get-tuple-element.515), channel_id=1, source_target_pairs={{0,4},{4,0},{8,12},{12,8},{1,5},{5,1},{9,13},{13,9},{2,6},{6,2},{1... | collective-permute-start | bytes 1572872 | tf_op jit(solution)/shard_map/ppermute | solution.py:23
  368.7 36.9 %collective-permute-start.58 = (bf16[128,2048]{1,0:T(8,128)(2,1)S(1)}, bf16[128,2048]{1,0:T(8,128)(2,1)S(1)}, u32[]{:S(2)}, u32[]{:S(2)}) collective-permute-start(bf16[128,2048]{1,0:T(8,128)(2,1)S(1)} %get-tuple-element.517), channel_id=1, source_target_pairs={{0,8},{4,12},{8,0},{12,4},{1,9},{5,13},{9,1},{13,5},{2,10},{6,14},... | collective-permute-start | bytes 1572872 | tf_op jit(solution)/shard_map/ppermute | solution.py:28
  410.2 67.5 %reduce-scatter.9.cloned.1.call-start = ((), (), s32[]{:S(2)}) async-start(), calls=%async_computation.13 | async-start | bytes 1310720 | tf_op jit(solution)/shard_map/reduce_scatter | solution.py:105
  410.6 35.9 %collective-permute-start.65 = (bf16[256,2048]{1,0:T(8,128)(2,1)}, bf16[256,2048]{1,0:T(8,128)(2,1)}, u32[]{:S(2)}, u32[]{:S(2)}) collective-permute-start(bf16[256,2048]{1,0:T(8,128)(2,1)} %get-tuple-element.392), channel_id=1, source_target_pairs={{0,4},{4,0},{8,12},{12,8},{1,5},{5,1},{9,13},{13,9},{2,6},{6,2},{1... | collective-permute-start | bytes 3145736 | tf_op jit(solution)/shard_map/ppermute | solution.py:23
  411.2 35.4 %collective-permute-start.66 = (bf16[256,2048]{1,0:T(8,128)(2,1)}, bf16[256,2048]{1,0:T(8,128)(2,1)}, u32[]{:S(2)}, u32[]{:S(2)}) collective-permute-start(bf16[256,2048]{1,0:T(8,128)(2,1)} %get-tuple-element.393), channel_id=1, source_target_pairs={{0,8},{4,12},{8,0},{12,4},{1,9},{5,13},{9,1},{13,5},{2,10},{6,14},... | collective-permute-start | bytes 3145736 | tf_op jit(solution)/shard_map/ppermute | solution.py:28
  451.2 56.9 %reduce-scatter.11.cloned.1.call-start = ((), (), s32[]{:S(2)}) async-start(), calls=%async_computation.14 | async-start | bytes 1310720 | tf_op jit(solution)/shard_map/reduce_scatter | solution.py:105
  480.4 141.5 %reduce-scatter.13.cloned.1.call-start = ((), (), s32[]{:S(2)}) async-start(), calls=%async_computation.15 | async-start | bytes 1310720 | tf_op jit(solution)/shard_map/reduce_scatter | solution.py:105
  512.8 39.9 %collective-permute-start.73 = (bf16[128,2048]{1,0:T(8,128)(2,1)}, bf16[128,2048]{1,0:T(8,128)(2,1)}, u32[]{:S(2)}, u32[]{:S(2)}) collective-permute-start(bf16[128,2048]{1,0:T(8,128)(2,1)} %get-tuple-element.503), channel_id=1, source_target_pairs={{0,4},{4,0},{8,12},{12,8},{1,5},{5,1},{9,13},{13,9},{2,6},{6,2},{1... | collective-permute-start | bytes 1572872 | tf_op jit(solution)/shard_map/ppermute | solution.py:23
  513.0 39.7 %collective-permute-start.74 = (bf16[256,2048]{1,0:T(8,128)(2,1)}, bf16[256,2048]{1,0:T(8,128)(2,1)}, u32[]{:S(2)}, u32[]{:S(2)}) collective-permute-start(bf16[256,2048]{1,0:T(8,128)(2,1)} %get-tuple-element.442), channel_id=1, source_target_pairs={{0,4},{4,0},{8,12},{12,8},{1,5},{5,1},{9,13},{13,9},{2,6},{6,2},{1... | collective-permute-start | bytes 3145736 | tf_op jit(solution)/shard_map/ppermute | solution.py:23
  514.2 38.5 %collective-permute-start.75 = (bf16[256,2048]{1,0:T(8,128)(2,1)}, bf16[256,2048]{1,0:T(8,128)(2,1)}, u32[]{:S(2)}, u32[]{:S(2)}) collective-permute-start(bf16[256,2048]{1,0:T(8,128)(2,1)} %get-tuple-element.443), channel_id=1, source_target_pairs={{0,8},{4,12},{8,0},{12,4},{1,9},{5,13},{9,1},{13,5},{2,10},{6,14},... | collective-permute-start | bytes 3145736 | tf_op jit(solution)/shard_map/ppermute | solution.py:28
  518.2 34.5 %collective-permute-start.72 = (bf16[128,2048]{1,0:T(8,128)(2,1)}, bf16[128,2048]{1,0:T(8,128)(2,1)}, u32[]{:S(2)}, u32[]{:S(2)}) collective-permute-start(bf16[128,2048]{1,0:T(8,128)(2,1)} %get-tuple-element.505), channel_id=1, source_target_pairs={{0,8},{4,12},{8,0},{12,4},{1,9},{5,13},{9,1},{13,5},{2,10},{6,14},... | collective-permute-start | bytes 1572872 | tf_op jit(solution)/shard_map/ppermute | solution.py:28
  556.5 95.5 %reduce-scatter.17.cloned.1.call-start = ((), (), s32[]{:S(2)}) async-start(), calls=%async_computation.17 | async-start | bytes 1310720 | tf_op jit(solution)/shard_map/reduce_scatter | solution.py:105
  575.1 99.7 %reduce-scatter.15.cloned.1.call-start = ((), (), s32[]{:S(2)}) async-start(), calls=%async_computation.16 | async-start | bytes 1392640 | tf_op jit(solution)/shard_map/reduce_scatter | solution.py:105
  (249 other events, 2418.0 us)
Sparse Core Ops, SparseCore 0:
  16.8 30.8 all-gather.6
  58.2 36.5 all-gather.8
  100.3 26.8 all-gather.10
  140.4 27.4 all-gather.12
  179.7 27.9 all-gather.14
  220.8 27.4 all-gather.16
  410.3 24.7 reduce-scatter.6
  451.3 26.3 reduce-scatter.8
  480.6 25.7 reduce-scatter.10
  556.6 26.5 reduce-scatter.12
  586.1 37.0 reduce-scatter.16
  645.6 29.0 reduce-scatter.14

commit v8 on v7

--- a/solution.py
+++ b/solution.py
@@ -647,7 +647,12 @@
     params = [dict(), dict()]
     blocks_in, blocks_cot = to_send(half_in), to_send(half_cot)
     pair, state = None, None
-    for r in range(number + 2):
+
+    def weights_of(k):
+        first, second = arrived(*halves[k], near[k], far[k])
+        return (first + second, [p.shape[0] for p in first + second])
+
+    for r in range(number + 1):
         tied = []
         if r < number:
             tied.append(gather_column(columns[r]))
@@ -656,17 +661,18 @@
         if r == 1:
             smalls = small_of(extra_rows)
             blocks_in = shifts(blocks_in)
+        if r == number - 2:
+            blocks_cot = shifts(blocks_cot)
+        if r == number - 1:
+            cot_half = image_half(blocks_cot)
         if r == number:
-            blocks_cot = shifts(blocks_cot)
+            cotangent = whole_image(cot_half).astype(jnp.float32) * live
         ready = []
         k = r - 2
         if k >= 0:
             layer, kind = k // 3, k % 3
             one = params[layer]
-            first, second = arrived(*halves[k], near[k], far[k])
-            pieces = first + second
-            counts = [p.shape[0] for p in pieces]
-            weights = (pieces, counts)
+            weights = weights_of(k)
             rows, q_bias, v_bias, up_bias = one["small"]
             if pair is not None:
                 pair = [pair[0], swap(pair[0])]
@@ -706,8 +712,12 @@
                 extras += blocks_in
             if r == 1:
                 extras += [v for layer in range(2) for v in smalls[layer]]
-            if r >= number - 1:
+            if r in (number - 3, number - 2):
                 extras += blocks_cot
+            elif r == number - 1:
+                extras.append(cot_half)
+            elif r == number:
+                extras.append(cotangent)
             if r + 1 < number:
                 extras.append(columns[r + 1])
             done = tie(tied + extras, [])
@@ -718,8 +728,12 @@
                 params[0]["small"], params[1]["small"] = smalls[:4], smalls[4:]
             if r <= 1:
                 done, blocks_in = done[:-n_tensor], done[-n_tensor:]
-            if r >= number - 1:
+            if r in (number - 3, number - 2):
                 done, blocks_cot = done[:-n_tensor], done[-n_tensor:]
+            elif r == number - 1:
+                cot_half = done.pop()
+            elif r == number:
+                cotangent = done.pop()
             if count and kind == 1:
                 one["hidden"] = done[-1]
             elif count:
@@ -733,10 +747,6 @@
             if 0 <= r - 1 < number:
                 near[r - 1] = done[at : at + 2]
                 far[r - 1] = done[at + 2 : at + 2 + len(far[r - 1])]
-    cotangent = whole_image(image_half(blocks_cot)).astype(jnp.float32) * live
-    pair = [pair[0], swap(pair[0])]
-    last_rows = params[1]["small"][0]
-    out_blocks = image_rows(live, [state, *pair], last_rows[7:8])
 
     sums = [dict(), dict()]
 
@@ -761,13 +771,16 @@
     grads, got, moved, settled = [None] * number, [None] * number, [None] * number, [None] * number
     made = [0, 1, 2, 4, 5, 6]
     grad = cotangent
+    last_down = weights_of(number - 1)
+    params[1]["down"] = last_down
+    last_bias = params[1]["small"][0][7:8]
     for r in range(8):
         layer, stage = 1 - r // 4, r % 4
         one, total = params[layer], sums[layer]
         rows = one["small"][0]
         tied, slots = [], []
         for c in range(number):
-            if r == made[c] + 1:
+            if r == made[c] + 1 and c != 2:
                 got[c] = scatter_one(*grads[c][:2])
                 slots.append((got, c, len(got[c])))
                 tied += got[c]
@@ -781,7 +794,7 @@
                 settled[c] = scatter_column(moved[c][:2], moved[c][2:])
                 slots.append((settled, c, 0))
                 tied.append(settled[c])
-        new = None
+        new, made_now = None, None
         if stage == 0:
             low, total["out"], total["up_bias"], new = down_backward(
                 grad, one["hidden"], one["slope"], one["down"]
@@ -796,23 +809,38 @@
                 grad, part, swap(part), one["mid"], rows, one["saved"], one["qkvo"]
             )
             dmid, dz, dq, dk, dv, part, total["mid"], total["q"], total["v"] = done
-            new = attention_grad(one["n1"], dz, dq, dk, dv, one["saved"][4])
+            if layer == 0:
+                new = attention_grad(one["n1"], dz, dq, dk, dv, one["saved"][4])
             carry = [part]
         else:
+            if layer == 1:
+                made_now = attention_grad(one["n1"], dz, dq, dk, dv, one["saved"][4])
+                got[2] = scatter_one(*made_now[:2])
+                slots.append((got, 2, len(got[2])))
+                tied += got[2]
             grad, total["one"] = value_backward(dmid, part, swap(part), one["u"], rows, layer == 1)
             carry = [grad]
             if r == 7:
                 one_scale = jnp.ones((), jnp.float32)
                 no_bias = jnp.zeros((1, grad.shape[1]), jnp.float32)
-                carry = [small_grads(), *shifts(image_rows(one_scale, [grad], no_bias))]
-        if new is not None:
+                carry = [small_grads()]
+                grad_blocks = shifts(image_rows(one_scale, [grad], no_bias))
+        if made_now is not None:
+            c, grads[2] = 2, made_now
+            fresh = [g for g in made_now[2:] if g is not None]
+        elif new is not None:
             c = made.index(r)
             grads[c] = new
             fresh = [g for g in new if g is not None]
         else:
             fresh = []
-        if r == 1:
-            out_blocks = shifts(out_blocks)
+        if r == 3:
+            last_part = contract_wide(params[1]["hidden"], last_down)
+            carry.append(last_part)
+        elif r == 4:
+            out_blocks = shifts(image_rows(
+                live, [params[1]["mid"], last_part, swap(last_part)], last_bias
+            ))
             carry += out_blocks
         if r < 8:
             done = tie(carry + fresh + tied, [])
@@ -825,18 +853,22 @@
             elif r < 7:
                 grad = done[0]
             else:
-                little, grad_blocks = done[0], done[1 : 1 + n_tensor]
-            if r == 1:
+                little = done[0]
+            if r == 3:
+                last_part = done[1]
+            elif r == 4:
                 out_blocks = done[1 : 1 + n_tensor]
             done = done[len(carry) :]
-            if fresh:
+            if made_now is not None:
+                grads[c][2 : 2 + len(fresh)] = done[: len(fresh)]
+                done = done[len(fresh) :]
+            elif fresh:
                 grads[c] = fill(done[: len(fresh)])
                 done = done[len(fresh) :]
             for store, at, count in slots:
                 store[at] = done[:count] if count else done[0]
                 done = done[max(count, 1) :]
 
-    grad_rows, out_rows = by_image(grad_blocks), by_image(out_blocks)
     room = jnp.zeros((n_dp, n_tensor, extra * wide - small_size), little.dtype)
     little = jnp.concatenate([little, room], -1).reshape(n_dp, n_tensor, extra, wide)
     little = by_arrival(little.transpose(0, 2, 1, 3).reshape(n_dp, extra, -1), spot)
@@ -849,6 +881,10 @@
     last = number - 1
     settled[last - 1] = scatter_column(moved[last - 1][:2], moved[last - 1][2:])
     stay, come = scatter_two(*grads[last][2:], got[last])
+    done = tie([*grad_blocks, *stay, *come], [])
+    grad_blocks, done = done[:n_tensor], done[n_tensor:]
+    grad_rows, out_rows = by_image(grad_blocks), by_image(out_blocks)
+    stay, come = done[:2], done[2:]
     if come:
         stay = [add(s, c).astype(jnp.bfloat16) for s, c in zip(stay, come)]
     settled[last] = scatter_column([*stay, little], [])

time: 698 us -> 684 us (0.980)
  waiting for transfers between devices: 229 us -> 202 us
  other arithmetic: 67.5 us -> 74.5 us
    ppermute x32, waiting for transfers between devices: 89.4 us -> 72.2 us  [swap_x(): return lax.ppermute(value, 'dp', [(i, i ^ 1) for i in range(n)])]
    reduce_scatter x6, waiting for transfers between devices: 26.5 us -> 14.8 us  [scatter_column(): lax.psum_scatter(jnp.concatenate(stay, 0), 'tensor', scatter_dimension=1,...]
    ppermute x12, starting transfers between devices: 16 us -> 23.4 us  [shifts(): lax.ppermute(blocks[d], 'tensor', [(i, (i + d) % n) for i in range(n)])]
    unnamed x354 -> x374, local copies, waits for them, and re-layouts: 54.9 us -> 52.9 us
  transfers between devices with their start and end apart: 105 -> 105, of which waited for: 44 -> 37; matrix products, arithmetic and copies ran while one was open for 12% -> 14% of each run, Pallas kernels for 27% -> 26%
where the time goes in v8:
time: 684 us; the launch traced here: 677 us
  waiting for transfers between devices  202 us (30%)
  Pallas kernels  192 us (28%)
  starting transfers between devices  104 us (15%)
  local copies, waits for them, and re-layouts  86.7 us (13%)
  other arithmetic  74.5 us (11%)
  between operations  17.3 us (3%)
    pallas_call x18, Pallas kernels, run(): pl.pallas_call(kernel, out_shape=list(outs), in_specs=[block] * len(ins),...  186 us
    ppermute x32, waiting for transfers between devices, swap_x(): return lax.ppermute(value, 'dp', [(i, i ^ 1) for i in range(n)])  72.2 us
    unnamed x374, local copies, waits for them, and re-layouts  52.9 us
    ppermute x12, waiting for transfers between devices, shifts(): lax.ppermute(blocks[d], 'tensor', [(i, (i + d) % n) for i in range(n)])  48.5 us
    ppermute x32, waiting for transfers between devices, swap_y(): return lax.ppermute(value, 'dp', [(i, i ^ 2) for i in range(n)])  35.1 us
    convert_element_type x12, other arithmetic, scatter_two(): come.append(far(add(keep[half:], new[half:]).astype(jnp.bfloat16)))  28.6 us
    all_gather x6, waiting for transfers between devices, gather_column(): return lax.all_gather(shard, 'tensor', axis=1, tiled=True)  27.4 us
    ppermute x17, starting transfers between devices, swap(): return lax.ppermute(value, 'section', [(0, 1), (1, 0)])  26.9 us
  transfers between devices with their start and end apart: 105, of which 37 were waited for; matrix products, arithmetic and copies ran while one was open for 14% of the time, Pallas kernels for 26%

profile of v8, /device:TPU:1, one launch (start us, length us, event | category | flops | bytes accessed | tf_op | source)
XLA Modules:
  0.0 676.9 jit_solution(6199763965313023245)
XLA Ops:
  23.7 24.0 %all-gather.7.cloned.1.call-done.refs_0_ = bf16[272,2048]{1,0:T(8,128)(2,1)} async-done(((bf16[272,512]{1,0:T(8,128)(2,1)}), bf16[272,2048]{1,0:T(8,128)(2,1)}) %all-gather.7.cloned.1.call-update) | async-done | bytes 1114128 | tf_op jit(solution)/shard_map/all_gather | solution.py:49
  68.1 9.5 %collective-permute-done.2.refs_1_ = bf16[128,2048]{1,0:T(8,128)(2,1)S(1)} collective-permute-done((bf16[128,2048]{1,0:T(8,128)(2,1)}, bf16[128,2048]{1,0:T(8,128)(2,1)S(1)}, u32[]{:S(2)}, u32[]{:S(2)}) %collective-permute-start.2) | collective-permute-done | bytes 524320 | tf_op jit(solution)/shard_map/ppermute | solution.py:28
  108.5 15.5 %shard_map.138 = (f32[592,1024]{1,0:T(8,128)}, bf16[592,1024]{1,0:T(8,128)(2,1)}, bf16[592,512]{1,0:T(8,128)(2,1)}, bf16[592,512]{1,0:T(8,128)(2,1)}, bf16[592,5...) custom-call(f32[592,1024]{1,0:T(8,128)} %maximum_convert_fusion.refs_0_, ...), custom_call_target="tpu_custom_call" | custom-call | flops 1 | bytes 1 | tf_op jit(solution)/shard_map/pallas_call | solution.py:173
  128.4 9.0 %collective-permute-done.17.refs_4_ = bf16[128,2048]{1,0:T(8,128)(2,1)S(1)} collective-permute-done((bf16[128,2048]{1,0:T(8,128)(2,1)}, bf16[128,2048]{1,0:T(8,128)(2,1)S(1)}, u32[]{:S(2)}, u32[]{:S(2)}) %collective-permute-start.17) | collective-permute-done | bytes 524320 | tf_op jit(solution)/shard_map/ppermute | solution.py:23
  149.4 10.1 %shard_map.141 = (f32[592,1024]{1,0:T(8,128)}, bf16[592,1024]{1,0:T(8,128)(2,1)}, bf16[592,2048]{1,0:T(8,128)(2,1)}, bf16[592,2048]{1,0:T(8,128)(2,1)}) custom-call(f32[592,1024]{1,0:T(8,128)} %get-tuple-element.278.refs_0_.u_ref, bf16[592,1024]{1,0:T(8,128)(2,1)} %get-tuple-element.279.refs_1_, bf16[592,1024]{1,0:T(8,128)(2,1)} %collective-permute-done.22.refs_2_, ...), custom_call_target="tpu_custom_call" | custom-call | flops 1 | bytes 1 | tf_op jit(solution)/shard_map/pallas_call | solution.py:173
  169.3 10.2 %collective-permute-done.24.refs_4_ = bf16[128,2048]{1,0:T(8,128)(2,1)S(1)} collective-permute-done((bf16[128,2048]{1,0:T(8,128)(2,1)}, bf16[128,2048]{1,0:T(8,128)(2,1)S(1)}, u32[]{:S(2)}, u32[]{:S(2)}) %collective-permute-start.24) | collective-permute-done | bytes 524320 | tf_op jit(solution)/shard_map/ppermute | solution.py:23
  201.2 8.4 %collective-permute-done.33.refs_9_ = bf16[296,256]{1,0:T(8,128)(2,1)S(1)} collective-permute-done((bf16[296,256]{1,0:T(8,128)(2,1)S(1)}, bf16[296,256]{1,0:T(8,128)(2,1)S(1)}, u32[]{:S(2)}, u32[]{:S(2)}) %collective-permute-start.33) | collective-permute-done | bytes 151584 | tf_op jit(solution)/shard_map/ppermute | solution.py:519
  233.7 16.9 %shard_map.147 = (f32[592,1024]{1,0:T(8,128)}, bf16[592,1024]{1,0:T(8,128)(2,1)}, bf16[592,512]{1,0:T(8,128)(2,1)}, bf16[592,512]{1,0:T(8,128)(2,1)}, bf16[592,5...) custom-call(f32[592,1024]{1,0:T(8,128)} %get-tuple-element.309.refs_0_.refs, ...), custom_call_target="tpu_custom_call" | custom-call | flops 1 | bytes 1 | tf_op jit(solution)/shard_map/pallas_call | solution.py:173
  257.3 10.0 %collective-permute-done.40.refs_4_ = bf16[128,2048]{1,0:T(8,128)(2,1)S(1)} collective-permute-done((bf16[128,2048]{1,0:T(8,128)(2,1)}, bf16[128,2048]{1,0:T(8,128)(2,1)S(1)}, u32[]{:S(2)}, u32[]{:S(2)}) %collective-permute-start.40) | collective-permute-done | bytes 524320 | tf_op jit(solution)/shard_map/ppermute | solution.py:23
  275.0 10.5 %shard_map.151 = (f32[592,1024]{1,0:T(8,128)}, bf16[592,1024]{1,0:T(8,128)(2,1)}, bf16[592,2048]{1,0:T(8,128)(2,1)}, bf16[592,2048]{1,0:T(8,128)(2,1)}) custom-call(f32[592,1024]{1,0:T(8,128)} %get-tuple-element.329.refs_0_.u_ref, bf16[592,1024]{1,0:T(8,128)(2,1)} %get-tuple-element.330.refs_1_, bf16[592,1024]{1,0:T(8,128)(2,1)} %copy-done.159, ...), custom_call_target="tpu_custom_call" | custom-call | flops 1 | bytes 1 | tf_op jit(solution)/shard_map/pallas_call | solution.py:173
  296.8 10.9 %collective-permute-done.47.refs_3_ = bf16[128,2048]{1,0:T(8,128)(2,1)} collective-permute-done((bf16[128,2048]{1,0:T(8,128)(2,1)}, bf16[128,2048]{1,0:T(8,128)(2,1)}, u32[]{:S(2)}, u32[]{:S(2)}) %collective-permute-start.47) | collective-permute-done | bytes 524320 | tf_op jit(solution)/shard_map/ppermute | solution.py:23
  308.0 11.7 %shard_map.154 = (bf16[592,2048]{1,0:T(8,128)(2,1)}, f32[1,1024]{1,0:T(1,128)S(1)}, f32[1,2048]{1,0:T(1,128)S(1)}, bf16[256,2048]{1,0:T(8,128)(2,1)}, bf16[256,2...) custom-call(f32[592,1024]{1,0:T(8,128)} %get-tuple-element.343.refs_0_, ...), custom_call_target="tpu_custom_call" | custom-call | flops 1 | bytes 1 | tf_op jit(solution)/shard_map/pallas_call | solution.py:173
  328.6 6.9 %shard_map.157 = (bf16[256,2048]{1,0:T(8,128)(2,1)S(1)}, bf16[256,2048]{1,0:T(8,128)(2,1)S(1)}, bf16[256,2048]{1,0:T(8,128)(2,1)S(1)}, bf16[256,2048]{1,0:T(8,128)(2,1)}) custom-call(bf16[592,1024]{1,0:T(8,128)(2,1)} %get-tuple-element.358.n_ref, bf16[592,2048]{1,0:T(8,128)(2,1)} %get-tuple-element.357.refs_0_.low_ref), custom_call_target="tpu_custom_call" | custom-call | flops 1 | bytes 1 | tf_op jit(solution)/shard_map/pallas_call | solution.py:173
  355.7 22.1 %shard_map.159 = (f32[592,1024]{1,0:T(8,128)}, bf16[592,1024]{1,0:T(8,128)(2,1)}, bf16[592,512]{1,0:T(8,128)(2,1)}, bf16[592,512]{1,0:T(8,128)(2,1)}, bf16[592,5...) custom-call(f32[592,1024]{1,0:T(8,128)} %get-tuple-element.343.refs_, ...), custom_call_target="tpu_custom_call" | custom-call | flops 1 | bytes 1 | tf_op jit(solution)/shard_map/pallas_call | solution.py:173
  388.6 7.9 %shard_map.163 = (bf16[256,2048]{1,0:T(8,128)(2,1)S(1)}, bf16[256,2048]{1,0:T(8,128)(2,1)}, bf16[256,2048]{1,0:T(8,128)(2,1)}, bf16[256,2048]{1,0:T(8,128)(2,1)}) custom-call(bf16[592,1024]{1,0:T(8,128)(2,1)} %get-tuple-element.382.n_ref, bf16[592,1024]{1,0:T(8,128)(2,1)} %get-tuple-element.383.dz_ref, bf16[592,512]{1,0:T(8,128)(2,1)S(1)} %copy-done.99, ...), custom_call_target="tpu_custom_call" | custom-call | flops 1 | bytes 1 | tf_op jit(solution)/shard_map/pallas_call | solution.py:173
  404.3 6.6 shard_map.162.refs_1_
  416.9 15.5 %collective-permute-done.60.refs_8_ = bf16[128,2048]{1,0:T(8,128)(2,1)S(1)} collective-permute-done((bf16[128,2048]{1,0:T(8,128)(2,1)S(1)}, bf16[128,2048]{1,0:T(8,128)(2,1)S(1)}, u32[]{:S(2)}, u32[]{:S(2)}) %collective-permute-start.60) | collective-permute-done | bytes 524320 | tf_op jit(solution)/shard_map/ppermute | solution.py:23
  454.7 11.9 %shard_map.165 = (bf16[592,2048]{1,0:T(8,128)(2,1)}, f32[1,1024]{1,0:T(1,128)S(1)}, f32[1,2048]{1,0:T(1,128)S(1)}, bf16[256,2048]{1,0:T(8,128)(2,1)}, bf16[256,2...) custom-call(f32[592,1024]{1,0:T(8,128)} %get-tuple-element.399.refs_0_, ...), custom_call_target="tpu_custom_call" | custom-call | flops 1 | bytes 1 | tf_op jit(solution)/shard_map/pallas_call | solution.py:173
  466.6 11.6 %collective-permute-done.65.refs_3_ = bf16[296,256]{1,0:T(8,128)(2,1)} collective-permute-done((bf16[296,256]{1,0:T(8,128)(2,1)}, bf16[296,256]{1,0:T(8,128)(2,1)}, u32[]{:S(2)}, u32[]{:S(2)}) %collective-permute-start.65) | collective-permute-done | bytes 151584 | tf_op jit(solution)/shard_map/ppermute | solution.py:519
  521.8 21.4 %shard_map.171 = (f32[592,1024]{1,0:T(8,128)}, bf16[592,1024]{1,0:T(8,128)(2,1)}, bf16[592,512]{1,0:T(8,128)(2,1)}, bf16[592,512]{1,0:T(8,128)(2,1)}, bf16[592,5...) custom-call(f32[592,1024]{1,0:T(8,128)} %get-tuple-element.399.refs_, ...), custom_call_target="tpu_custom_call" | custom-call | flops 1 | bytes 1 | tf_op jit(solution)/shard_map/pallas_call | solution.py:173
  546.4 8.0 %shard_map.172 = (bf16[256,2048]{1,0:T(8,128)(2,1)}, bf16[256,2048]{1,0:T(8,128)(2,1)}, bf16[256,2048]{1,0:T(8,128)(2,1)}, bf16[256,2048]{1,0:T(8,128)(2,1)}) custom-call(bf16[592,1024]{1,0:T(8,128)(2,1)} %get-tuple-element.435.n_ref, bf16[592,1024]{1,0:T(8,128)(2,1)} %get-tuple-element.436.dz_ref, bf16[592,512]{1,0:T(8,128)(2,1)S(1)} %copy-done.102, ...), custom_call_target="tpu_custom_call" | custom-call | flops 1 | bytes 1 | tf_op jit(solution)/shard_map/pallas_call | solution.py:173
  607.2 7.2 %collective-permute-done.87 = bf16[16,2048]{1,0:T(8,128)(2,1)S(1)} collective-permute-done((bf16[16,2048]{1,0:T(8,128)(2,1)S(1)}, bf16[16,2048]{1,0:T(8,128)(2,1)S(1)}, u32[]{:S(2)}, u32[]{:S(2)}) %collective-permute-start.87) | collective-permute-done | bytes 65568 | tf_op jit(solution)/shard_map/ppermute | solution.py:28
  615.6 15.0 %collective-permute-done.78.refs_2_ = bf16[296,256]{1,0:T(8,128)(2,1)S(1)} collective-permute-done((bf16[296,256]{1,0:T(8,128)(2,1)S(1)}, bf16[296,256]{1,0:T(8,128)(2,1)S(1)}, u32[]{:S(2)}, u32[]{:S(2)}) %collective-permute-start.78) | collective-permute-done | bytes 151584 | tf_op jit(solution)/shard_map/ppermute | solution.py:519
  646.7 14.8 %reduce-scatter.15.cloned.1.call-done = bf16[272,512]{1,0:T(8,128)(2,1)} async-done(((bf16[272,2048]{1,0:T(8,128)(2,1)}), bf16[272,512]{1,0:T(8,128)(2,1)}) %reduce-scatter.15.cloned.1.call-update) | async-done | bytes 278544 | tf_op jit(solution)/shard_map/reduce_scatter | solution.py:105
  (799 shorter events, 363.7 us)
Async XLA Ops:
  7.2 40.5 %all-gather.7.cloned.1.call-start = ((), (), s32[]{:S(2)}) async-start(), calls=%async_computation.6 | async-start | bytes 1392640 | tf_op jit(solution)/shard_map/all_gather | solution.py:49
  16.7 79.1 %all-gather.9.cloned.1.call-start = ((), (), s32[]{:S(2)}) async-start(), calls=%async_computation.7 | async-start | bytes 1310720 | tf_op jit(solution)/shard_map/all_gather | solution.py:49
  55.1 37.3 %collective-permute-start.6 = (bf16[128,2048]{1,0:T(8,128)(2,1)S(1)}, bf16[128,2048]{1,0:T(8,128)(2,1)S(1)}, u32[]{:S(2)}, u32[]{:S(2)}) collective-permute-start(bf16[128,2048]{1,0:T(8,128)(2,1)S(1)} %get-tuple-element.545.refs_9_.refs_14_), channel_id=1, source_target_pairs={{0,8},{4,12},{8,0},{12,4},{1,9},{5,13},{9,1},{13,5},{2,10},{6,14},... | collective-permute-start | bytes 1572872 | tf_op jit(solution)/shard_map/ppermute | solution.py:28
  56.6 35.8 %collective-permute-start.4 = (bf16[128,2048]{1,0:T(8,128)(2,1)}, bf16[128,2048]{1,0:T(8,128)(2,1)S(1)}, u32[]{:S(2)}, u32[]{:S(2)}) collective-permute-start(bf16[128,2048]{1,0:T(8,128)(2,1)} %get-tuple-element.546.refs_5_.refs_10_), channel_id=1, source_target_pairs={{0,4},{4,0},{8,12},{12,8},{1,5},{5,1},{9,13},{13,9},{2,6},{6,2},{1... | collective-permute-start | bytes 1572872 | tf_op jit(solution)/shard_map/ppermute | solution.py:23
  58.1 79.4 %all-gather.11.cloned.1.call-start = ((), (), s32[]{:S(2)}) async-start(), calls=%async_computation.8 | async-start | bytes 1310720 | tf_op jit(solution)/shard_map/all_gather | solution.py:49
  101.0 68.2 %all-gather.13.cloned.1.call-start = ((), (), s32[]{:S(2)}) async-start(), calls=%async_computation.9 | async-start | bytes 1310720 | tf_op jit(solution)/shard_map/all_gather | solution.py:49
  140.6 83.8 %all-gather.15.cloned.1.call-start = ((), (), s32[]{:S(2)}) async-start(), calls=%async_computation.10 | async-start | bytes 1310720 | tf_op jit(solution)/shard_map/all_gather | solution.py:49
  181.3 76.0 %all-gather.17.cloned.1.call-start = ((), (), s32[]{:S(2)}) async-start(), calls=%async_computation.11 | async-start | bytes 1310720 | tf_op jit(solution)/shard_map/all_gather | solution.py:49
  185.6 38.8 %collective-permute-start.31 = (bf16[128,2048]{1,0:T(8,128)(2,1)}, bf16[128,2048]{1,0:T(8,128)(2,1)}, u32[]{:S(2)}, u32[]{:S(2)}) collective-permute-start(bf16[128,2048]{1,0:T(8,128)(2,1)} %get-tuple-element.551.refs_11_.refs_14_), channel_id=1, source_target_pairs={{0,8},{4,12},{8,0},{12,4},{1,9},{5,13},{9,1},{13,5},{2,10},{6,14},... | collective-permute-start | bytes 1572872 | tf_op jit(solution)/shard_map/ppermute | solution.py:28
  185.8 38.6 %collective-permute-start.29 = (bf16[128,2048]{1,0:T(8,128)(2,1)}, bf16[128,2048]{1,0:T(8,128)(2,1)}, u32[]{:S(2)}, u32[]{:S(2)}) collective-permute-start(bf16[128,2048]{1,0:T(8,128)(2,1)} %get-tuple-element.552.refs_7_.refs_10_), channel_id=1, source_target_pairs={{0,4},{4,0},{8,12},{12,8},{1,5},{5,1},{9,13},{13,9},{2,6},{6,2},{1... | collective-permute-start | bytes 1572872 | tf_op jit(solution)/shard_map/ppermute | solution.py:23
  227.5 206.4 %reduce-scatter.7.cloned.1.call-start = ((), (), s32[]{:S(2)}) async-start(), calls=%async_computation.12 | async-start | bytes 1310720 | tf_op jit(solution)/shard_map/reduce_scatter | solution.py:105
  343.6 34.2 %collective-permute-start.56 = (bf16[256,2048]{1,0:T(8,128)(2,1)}, bf16[256,2048]{1,0:T(8,128)(2,1)}, u32[]{:S(2)}, u32[]{:S(2)}) collective-permute-start(bf16[256,2048]{1,0:T(8,128)(2,1)} %get-tuple-element.378), channel_id=1, source_target_pairs={{0,4},{4,0},{8,12},{12,8},{1,5},{5,1},{9,13},{13,9},{2,6},{6,2},{1... | collective-permute-start | bytes 3145736 | tf_op jit(solution)/shard_map/ppermute | solution.py:23
  344.3 33.5 %collective-permute-start.57 = (bf16[256,2048]{1,0:T(8,128)(2,1)}, bf16[256,2048]{1,0:T(8,128)(2,1)}, u32[]{:S(2)}, u32[]{:S(2)}) collective-permute-start(bf16[256,2048]{1,0:T(8,128)(2,1)} %get-tuple-element.379), channel_id=1, source_target_pairs={{0,8},{4,12},{8,0},{12,4},{1,9},{5,13},{9,1},{13,5},{2,10},{6,14},... | collective-permute-start | bytes 3145736 | tf_op jit(solution)/shard_map/ppermute | solution.py:28
  381.6 96.6 %reduce-scatter.9.cloned.1.call-start = ((), (), s32[]{:S(2)}) async-start(), calls=%async_computation.13 | async-start | bytes 1310720 | tf_op jit(solution)/shard_map/reduce_scatter | solution.py:105
  396.5 36.6 %collective-permute-start.61 = (bf16[256,2048]{1,0:T(8,128)(2,1)S(1)}, bf16[256,2048]{1,0:T(8,128)(2,1)S(1)}, u32[]{:S(2)}, u32[]{:S(2)}) collective-permute-start(bf16[256,2048]{1,0:T(8,128)(2,1)S(1)} %get-tuple-element.397), channel_id=1, source_target_pairs={{0,4},{4,0},{8,12},{12,8},{1,5},{5,1},{9,13},{13,9},{2,6},{6,2},{1... | collective-permute-start | bytes 3145736 | tf_op jit(solution)/shard_map/ppermute | solution.py:23
  397.4 36.5 %collective-permute-start.62 = (bf16[256,2048]{1,0:T(8,128)(2,1)}, bf16[256,2048]{1,0:T(8,128)(2,1)}, u32[]{:S(2)}, u32[]{:S(2)}) collective-permute-start(bf16[256,2048]{1,0:T(8,128)(2,1)} %get-tuple-element.398), channel_id=1, source_target_pairs={{0,8},{4,12},{8,0},{12,4},{1,9},{5,13},{9,1},{13,5},{2,10},{6,14},... | collective-permute-start | bytes 3145736 | tf_op jit(solution)/shard_map/ppermute | solution.py:28
  437.7 70.3 %reduce-scatter.11.cloned.1.call-start = ((), (), s32[]{:S(2)}) async-start(), calls=%async_computation.14 | async-start | bytes 1310720 | tf_op jit(solution)/shard_map/reduce_scatter | solution.py:105
  482.1 113.5 %reduce-scatter.13.cloned.1.call-start = ((), (), s32[]{:S(2)}) async-start(), calls=%async_computation.15 | async-start | bytes 1310720 | tf_op jit(solution)/shard_map/reduce_scatter | solution.py:105
  513.2 41.2 %collective-permute-start.73 = (bf16[128,2048]{1,0:T(8,128)(2,1)S(1)}, bf16[128,2048]{1,0:T(8,128)(2,1)S(1)}, u32[]{:S(2)}, u32[]{:S(2)}) collective-permute-start(bf16[128,2048]{1,0:T(8,128)(2,1)S(1)} %get-tuple-element.517), channel_id=1, source_target_pairs={{0,4},{4,0},{8,12},{12,8},{1,5},{5,1},{9,13},{13,9},{2,6},{6,2},{1... | collective-permute-start | bytes 1572872 | tf_op jit(solution)/shard_map/ppermute | solution.py:23
  514.0 40.5 %collective-permute-start.74 = (bf16[256,2048]{1,0:T(8,128)(2,1)S(1)}, bf16[256,2048]{1,0:T(8,128)(2,1)S(1)}, u32[]{:S(2)}, u32[]{:S(2)}) collective-permute-start(bf16[256,2048]{1,0:T(8,128)(2,1)S(1)} %copy-done.86), channel_id=1, source_target_pairs={{0,4},{4,0},{8,12},{12,8},{1,5},{5,1},{9,13},{13,9},{2,6},{6,2},{1... | collective-permute-start | bytes 3145736 | tf_op jit(solution)/shard_map/ppermute | solution.py:23
  514.7 39.7 %collective-permute-start.75 = (bf16[256,2048]{1,0:T(8,128)(2,1)S(1)}, bf16[256,2048]{1,0:T(8,128)(2,1)S(1)}, u32[]{:S(2)}, u32[]{:S(2)}) collective-permute-start(bf16[256,2048]{1,0:T(8,128)(2,1)S(1)} %copy-done.88), channel_id=1, source_target_pairs={{0,8},{4,12},{8,0},{12,4},{1,9},{5,13},{9,1},{13,5},{2,10},{6,14},... | collective-permute-start | bytes 3145736 | tf_op jit(solution)/shard_map/ppermute | solution.py:28
  518.5 35.9 %collective-permute-start.72 = (bf16[128,2048]{1,0:T(8,128)(2,1)S(1)}, bf16[128,2048]{1,0:T(8,128)(2,1)S(1)}, u32[]{:S(2)}, u32[]{:S(2)}) collective-permute-start(bf16[128,2048]{1,0:T(8,128)(2,1)S(1)} %get-tuple-element.519), channel_id=1, source_target_pairs={{0,8},{4,12},{8,0},{12,4},{1,9},{5,13},{9,1},{13,5},{2,10},{6,14},... | collective-permute-start | bytes 1572872 | tf_op jit(solution)/shard_map/ppermute | solution.py:28
  566.3 70.8 %reduce-scatter.17.cloned.1.call-start = ((), (), s32[]{:S(2)}) async-start(), calls=%async_computation.17 | async-start | bytes 1310720 | tf_op jit(solution)/shard_map/reduce_scatter | solution.py:105
  590.1 71.5 %reduce-scatter.15.cloned.1.call-start = ((), (), s32[]{:S(2)}) async-start(), calls=%async_computation.16 | async-start | bytes 1392640 | tf_op jit(solution)/shard_map/reduce_scatter | solution.py:105
  (259 other events, 2460.5 us)
Sparse Core Ops, SparseCore 0:
  16.8 30.8 all-gather.6
  58.2 37.5 all-gather.8
  101.2 26.9 all-gather.10
  140.7 27.9 all-gather.12
  181.4 30.2 all-gather.14
  227.6 28.8 all-gather.16
  381.7 30.2 reduce-scatter.6
  437.8 38.0 reduce-scatter.8
  482.2 25.7 reduce-scatter.10
  566.4 24.4 reduce-scatter.12
  593.8 34.3 reduce-scatter.16
  634.7 26.8 reduce-scatter.14

commit v9 on v8

--- a/solution.py
+++ b/solution.py
@@ -91,12 +91,12 @@
 def scatter_two(keep_first, keep_second, got):
     if lax.axis_size("dp") != 4:
         return (got, [])
-    stay, come = [], []
-    for keep, new, far in zip((keep_first, keep_second), got, (swap_y, swap_x)):
+    stay, send = [], []
+    for keep, new in zip((keep_first, keep_second), got):
         half = keep.shape[0] // 2
-        come.append(far(add(keep[half:], new[half:]).astype(jnp.bfloat16)))
+        send.append(add(keep[half:], new[half:]).astype(jnp.bfloat16))
         stay.append(add(keep[:half], new[:half]).astype(jnp.bfloat16))
-    return (stay, come)
+    return (stay, [swap_y(send[0]), swap_x(send[1])])
 
 
 def scatter_column(stay, come):
@@ -512,12 +512,13 @@
     )(numbers, scale, *terms, bias_row)
 
 
+def shift(block, d):
+    n = lax.axis_size("tensor")
+    return lax.ppermute(block, "tensor", [(i, (i + d) % n) for i in range(n)])
+
+
 def shifts(blocks):
-    n = lax.axis_size("tensor")
-    out = [blocks[0]]
-    for d in range(1, n):
-        out.append(lax.ppermute(blocks[d], "tensor", [(i, (i + d) % n) for i in range(n)]))
-    return out
+    return [blocks[0]] + [shift(block, d) for d, block in enumerate(blocks) if d > 0]
 
 
 def half_cols(core, whole, n_tensor):
@@ -628,8 +629,8 @@
         if n_dp != 4:
             extras = lax.all_gather(extras, "dp", axis=0, tiled=True)
         else:
-            extras = jnp.concatenate([extras, swap_y(extras)], 0)
-            extras = jnp.concatenate([extras, swap_x(extras)], 0)
+            over = lax.ppermute(extras, "dp", [(i, i ^ 3) for i in range(n_dp)])
+            extras = jnp.concatenate([extras, swap_y(extras), swap_x(extras), over], 0)
         both = by_chip(extras.reshape(n_dp, extra, -1), spot).astype(jnp.float32)
         both = both.reshape(n_dp, 2, extra // 2, n_tensor, wide).transpose(1, 0, 3, 2, 4)
         both = both.reshape(2, n_dp, n_tensor, -1)
@@ -661,8 +662,8 @@
         if r == 1:
             smalls = small_of(extra_rows)
             blocks_in = shifts(blocks_in)
-        if r == number - 2:
-            blocks_cot = shifts(blocks_cot)
+        if 2 <= r <= 1 + n_tensor - 1:
+            blocks_cot[r - 1] = shift(blocks_cot[r - 1], r - 1)
         if r == number - 1:
             cot_half = image_half(blocks_cot)
         if r == number:
@@ -712,7 +713,7 @@
                 extras += blocks_in
             if r == 1:
                 extras += [v for layer in range(2) for v in smalls[layer]]
-            if r in (number - 3, number - 2):
+            if 1 <= r <= number - 2:
                 extras += blocks_cot
             elif r == number - 1:
                 extras.append(cot_half)
@@ -723,17 +724,17 @@
             done = tie(tied + extras, [])
             if r + 1 < number:
                 columns[r + 1] = done.pop()
+            if 1 <= r <= number - 2:
+                done, blocks_cot = done[:-n_tensor], done[-n_tensor:]
+            elif r == number - 1:
+                cot_half = done.pop()
+            elif r == number:
+                cotangent = done.pop()
             if r == 1:
                 done, smalls = done[:-8], done[-8:]
                 params[0]["small"], params[1]["small"] = smalls[:4], smalls[4:]
             if r <= 1:
                 done, blocks_in = done[:-n_tensor], done[-n_tensor:]
-            if r in (number - 3, number - 2):
-                done, blocks_cot = done[:-n_tensor], done[-n_tensor:]
-            elif r == number - 1:
-                cot_half = done.pop()
-            elif r == number:
-                cotangent = done.pop()
             if count and kind == 1:
                 one["hidden"] = done[-1]
             elif count:
@@ -769,7 +770,7 @@
         return little
 
     grads, got, moved, settled = [None] * number, [None] * number, [None] * number, [None] * number
-    made = [0, 1, 2, 4, 5, 6]
+    made = [0, 1, 3, 4, 5, 6]
     grad = cotangent
     last_down = weights_of(number - 1)
     params[1]["down"] = last_down
@@ -780,7 +781,7 @@
         rows = one["small"][0]
         tied, slots = [], []
         for c in range(number):
-            if r == made[c] + 1 and c != 2:
+            if r == made[c] + 1:
                 got[c] = scatter_one(*grads[c][:2])
                 slots.append((got, c, len(got[c])))
                 tied += got[c]
@@ -794,7 +795,7 @@
                 settled[c] = scatter_column(moved[c][:2], moved[c][2:])
                 slots.append((settled, c, 0))
                 tied.append(settled[c])
-        new, made_now = None, None
+        new = None
         if stage == 0:
             low, total["out"], total["up_bias"], new = down_backward(
                 grad, one["hidden"], one["slope"], one["down"]
@@ -814,10 +815,7 @@
             carry = [part]
         else:
             if layer == 1:
-                made_now = attention_grad(one["n1"], dz, dq, dk, dv, one["saved"][4])
-                got[2] = scatter_one(*made_now[:2])
-                slots.append((got, 2, len(got[2])))
-                tied += got[2]
+                new = attention_grad(one["n1"], dz, dq, dk, dv, one["saved"][4])
             grad, total["one"] = value_backward(dmid, part, swap(part), one["u"], rows, layer == 1)
             carry = [grad]
             if r == 7:
@@ -825,10 +823,7 @@
                 no_bias = jnp.zeros((1, grad.shape[1]), jnp.float32)
                 carry = [small_grads()]
                 grad_blocks = shifts(image_rows(one_scale, [grad], no_bias))
-        if made_now is not None:
-            c, grads[2] = 2, made_now
-            fresh = [g for g in made_now[2:] if g is not None]
-        elif new is not None:
+        if new is not None:
             c = made.index(r)
             grads[c] = new
             fresh = [g for g in new if g is not None]
@@ -838,9 +833,11 @@
             last_part = contract_wide(params[1]["hidden"], last_down)
             carry.append(last_part)
         elif r == 4:
-            out_blocks = shifts(image_rows(
+            out_blocks = image_rows(
                 live, [params[1]["mid"], last_part, swap(last_part)], last_bias
-            ))
+            )
+        if 4 <= r < 4 + n_tensor - 1:
+            out_blocks[r - 3] = shift(out_blocks[r - 3], r - 3)
             carry += out_blocks
         if r < 8:
             done = tie(carry + fresh + tied, [])
@@ -856,13 +853,10 @@
                 little = done[0]
             if r == 3:
                 last_part = done[1]
-            elif r == 4:
+            elif 4 <= r < 4 + n_tensor - 1:
                 out_blocks = done[1 : 1 + n_tensor]
             done = done[len(carry) :]
-            if made_now is not None:
-                grads[c][2 : 2 + len(fresh)] = done[: len(fresh)]
-                done = done[len(fresh) :]
-            elif fresh:
+            if fresh:
                 grads[c] = fill(done[: len(fresh)])
                 done = done[len(fresh) :]
             for store, at, count in slots:

time: 684 us -> 658 us (0.962)
  starting transfers between devices: 104 us -> 90.8 us
  waiting for transfers between devices: 202 us -> 192 us
    ppermute x32, waiting for transfers between devices: 72.2 us -> 61.9 us  [swap_x(): return lax.ppermute(value, 'dp', [(i, i ^ 1) for i in range(n)])]
    ppermute x12 -> x13, starting transfers between devices: 23.4 us -> 13.6 us  [the longest x12 11.5 us: shift(): return lax.ppermute(block, 'tensor', [(i, (i + d) % n) for i in range(n)])]
    unnamed x374 -> x318, local copies, waits for them, and re-layouts: 52.9 us -> 44.1 us
    ppermute x32, waiting for transfers between devices: 35.1 us -> 43 us  [swap_y(): return lax.ppermute(value, 'dp', [(i, i ^ 2) for i in range(n)])]
    ppermute x12 -> x13, waiting for transfers between devices: 48.5 us -> 41.9 us  [the longest x12 41.9 us: shift(): return lax.ppermute(block, 'tensor', [(i, (i + d) % n) for i in range(n)])]
  transfers between devices with their start and end apart: 105 -> 106, of which waited for: 37 -> 35; matrix products, arithmetic and copies ran while one was open for 14% -> 15% of each run, Pallas kernels for 26% -> 28%
where the time goes in v9:
time: 658 us; the launch traced here: 650 us
  Pallas kernels  193 us (29%)
  waiting for transfers between devices  192 us (29%)
  starting transfers between devices  90.8 us (14%)
  local copies, waits for them, and re-layouts  82.2 us (12%)
  other arithmetic  75 us (11%)
  between operations  17.3 us (3%)
    pallas_call x18, Pallas kernels, run(): pl.pallas_call(kernel, out_shape=list(outs), in_specs=[block] * len(ins),...  187 us
    ppermute x32, waiting for transfers between devices, swap_x(): return lax.ppermute(value, 'dp', [(i, i ^ 1) for i in range(n)])  61.9 us
    unnamed x318, local copies, waits for them, and re-layouts  44.1 us
    ppermute x32, waiting for transfers between devices, swap_y(): return lax.ppermute(value, 'dp', [(i, i ^ 2) for i in range(n)])  43 us
    ppermute x12, waiting for transfers between devices, shift(): return lax.ppermute(block, 'tensor', [(i, (i + d) % n) for i in range(n)])  41.9 us
    convert_element_type x12, other arithmetic, scatter_two(): send.append(add(keep[half:], new[half:]).astype(jnp.bfloat16))  27.7 us
    ppermute x32, starting transfers between devices, swap_y(): return lax.ppermute(value, 'dp', [(i, i ^ 2) for i in range(n)])  27 us
    ppermute x17, starting transfers between devices, swap(): return lax.ppermute(value, 'section', [(0, 1), (1, 0)])  24.9 us
  transfers between devices with their start and end apart: 106, of which 35 were waited for; matrix products, arithmetic and copies ran while one was open for 15% of the time, Pallas kernels for 28%

profile of v9, /device:TPU:1, one launch (start us, length us, event | category | flops | bytes accessed | tf_op | source)
XLA Modules:
  0.0 650.1 jit_solution(4581116353004525384)
XLA Ops:
  25.0 22.7 %all-gather.7.cloned.1.call-done.refs_0_ = bf16[272,2048]{1,0:T(8,128)(2,1)} async-done(((bf16[272,512]{1,0:T(8,128)(2,1)}), bf16[272,2048]{1,0:T(8,128)(2,1)}) %all-gather.7.cloned.1.call-update) | async-done | bytes 1114128 | tf_op jit(solution)/shard_map/all_gather | solution.py:49
  78.8 9.8 %collective-permute-done.9.refs_9_ = bf16[296,256]{1,0:T(8,128)(2,1)S(1)} collective-permute-done((bf16[296,256]{1,0:T(8,128)(2,1)}, bf16[296,256]{1,0:T(8,128)(2,1)S(1)}, u32[]{:S(2)}, u32[]{:S(2)}) %collective-permute-start.9) | collective-permute-done | bytes 151584 | tf_op jit(solution)/shard_map/ppermute | solution.py:517
  108.7 15.6 %shard_map.138 = (f32[592,1024]{1,0:T(8,128)}, bf16[592,1024]{1,0:T(8,128)(2,1)}, bf16[592,512]{1,0:T(8,128)(2,1)}, bf16[592,512]{1,0:T(8,128)(2,1)}, bf16[592,5...) custom-call(f32[592,1024]{1,0:T(8,128)} %maximum_convert_fusion.refs_0_, ...), custom_call_target="tpu_custom_call" | custom-call | flops 1 | bytes 1 | tf_op jit(solution)/shard_map/pallas_call | solution.py:173
  148.6 10.3 %shard_map.141 = (f32[592,1024]{1,0:T(8,128)}, bf16[592,1024]{1,0:T(8,128)(2,1)}, bf16[592,2048]{1,0:T(8,128)(2,1)}, bf16[592,2048]{1,0:T(8,128)(2,1)}) custom-call(f32[592,1024]{1,0:T(8,128)} %get-tuple-element.300.refs_0_.u_ref, bf16[592,1024]{1,0:T(8,128)(2,1)} %get-tuple-element.301.refs_1_, bf16[592,1024]{1,0:T(8,128)(2,1)} %collective-permute-done.24.refs_2_, ...), custom_call_target="tpu_custom_call" | custom-call | flops 1 | bytes 1 | tf_op jit(solution)/shard_map/pallas_call | solution.py:173
  161.5 14.4 %collective-permute-done.29.refs_10_ = bf16[296,256]{1,0:T(8,128)(2,1)S(1)} collective-permute-done((bf16[296,256]{1,0:T(8,128)(2,1)S(1)}, bf16[296,256]{1,0:T(8,128)(2,1)S(1)}, u32[]{:S(2)}, u32[]{:S(2)}) %collective-permute-start.29) | collective-permute-done | bytes 151584 | tf_op jit(solution)/shard_map/ppermute | solution.py:517
  203.3 8.0 %collective-permute-done.36.refs_11_ = bf16[296,256]{1,0:T(8,128)(2,1)S(1)} collective-permute-done((bf16[296,256]{1,0:T(8,128)(2,1)S(1)}, bf16[296,256]{1,0:T(8,128)(2,1)S(1)}, u32[]{:S(2)}, u32[]{:S(2)}) %collective-permute-start.36) | collective-permute-done | bytes 151584 | tf_op jit(solution)/shard_map/ppermute | solution.py:517
  211.4 8.4 %collective-permute-done.33.refs_4_ = bf16[128,2048]{1,0:T(8,128)(2,1)S(1)} collective-permute-done((bf16[128,2048]{1,0:T(8,128)(2,1)}, bf16[128,2048]{1,0:T(8,128)(2,1)S(1)}, u32[]{:S(2)}, u32[]{:S(2)}) %collective-permute-start.33) | collective-permute-done | bytes 524320 | tf_op jit(solution)/shard_map/ppermute | solution.py:23
  228.0 17.1 %shard_map.147 = (f32[592,1024]{1,0:T(8,128)}, bf16[592,1024]{1,0:T(8,128)(2,1)}, bf16[592,512]{1,0:T(8,128)(2,1)}, bf16[592,512]{1,0:T(8,128)(2,1)}, bf16[592,5...) custom-call(f32[592,1024]{1,0:T(8,128)} %get-tuple-element.335.refs_0_.refs, ...), custom_call_target="tpu_custom_call" | custom-call | flops 1 | bytes 1 | tf_op jit(solution)/shard_map/pallas_call | solution.py:173
  250.6 10.7 %collective-permute-done.41.refs_4_ = bf16[128,2048]{1,0:T(8,128)(2,1)} collective-permute-done((bf16[128,2048]{1,0:T(8,128)(2,1)}, bf16[128,2048]{1,0:T(8,128)(2,1)}, u32[]{:S(2)}, u32[]{:S(2)}) %collective-permute-start.41) | collective-permute-done | bytes 524320 | tf_op jit(solution)/shard_map/ppermute | solution.py:23
  268.5 11.0 %shard_map.151 = (f32[592,1024]{1,0:T(8,128)}, bf16[592,1024]{1,0:T(8,128)(2,1)}, bf16[592,2048]{1,0:T(8,128)(2,1)}, bf16[592,2048]{1,0:T(8,128)(2,1)}) custom-call(f32[592,1024]{1,0:T(8,128)} %get-tuple-element.355.refs_0_.u_ref, bf16[592,1024]{1,0:T(8,128)(2,1)} %get-tuple-element.356.refs_1_, bf16[592,1024]{1,0:T(8,128)(2,1)} %copy-done.135, ...), custom_call_target="tpu_custom_call" | custom-call | flops 1 | bytes 1 | tf_op jit(solution)/shard_map/pallas_call | solution.py:173
  290.2 10.9 %collective-permute-done.48.refs_3_ = bf16[128,2048]{1,0:T(8,128)(2,1)} collective-permute-done((bf16[128,2048]{1,0:T(8,128)(2,1)}, bf16[128,2048]{1,0:T(8,128)(2,1)}, u32[]{:S(2)}, u32[]{:S(2)}) %collective-permute-start.48) | collective-permute-done | bytes 524320 | tf_op jit(solution)/shard_map/ppermute | solution.py:23
  301.4 11.7 %shard_map.154 = (bf16[592,2048]{1,0:T(8,128)(2,1)}, f32[1,1024]{1,0:T(1,128)S(1)}, f32[1,2048]{1,0:T(1,128)S(1)}, bf16[256,2048]{1,0:T(8,128)(2,1)}, bf16[256,2...) custom-call(f32[592,1024]{1,0:T(8,128)} %get-tuple-element.369.refs_0_, ...), custom_call_target="tpu_custom_call" | custom-call | flops 1 | bytes 1 | tf_op jit(solution)/shard_map/pallas_call | solution.py:173
  315.1 6.6 %shard_map.156.refs_0_ = bf16[592,1024]{1,0:T(8,128)(2,1)} custom-call(bf16[592,2048]{1,0:T(8,128)(2,1)} %get-tuple-element.383.refs_0_.low_ref, bf16[128,2048]{1,0:T(8,128)(2,1)} %get-tuple-element.586.refs_5_.refs_1_, bf16[128,2048]{1,0:T(8,128)(2,1)} %get-tuple-element.358.refs_6_.refs_2_, bf16[128,2048]{1,0:T(8,128)(2,1)} %get-tuple-element.359.refs_7_.refs_3_, ...), custom_call_target="tpu_custom_call" | custom-call | flops 1 | bytes 1 | tf_op jit(solution)/shard_map/pallas_call | solution.py:173
  321.7 6.9 %shard_map.157 = (bf16[256,2048]{1,0:T(8,128)(2,1)S(1)}, bf16[256,2048]{1,0:T(8,128)(2,1)S(1)}, bf16[256,2048]{1,0:T(8,128)(2,1)S(1)}, bf16[256,2048]{1,0:T(8,128)(2,1)}) custom-call(bf16[592,1024]{1,0:T(8,128)(2,1)} %get-tuple-element.384.n_ref, bf16[592,2048]{1,0:T(8,128)(2,1)} %get-tuple-element.383.refs_0_.low_ref), custom_call_target="tpu_custom_call" | custom-call | flops 1 | bytes 1 | tf_op jit(solution)/shard_map/pallas_call | solution.py:173
  349.5 22.0 %shard_map.159 = (f32[592,1024]{1,0:T(8,128)}, bf16[592,1024]{1,0:T(8,128)(2,1)}, bf16[592,512]{1,0:T(8,128)(2,1)}, bf16[592,512]{1,0:T(8,128)(2,1)}, bf16[592,5...) custom-call(f32[592,1024]{1,0:T(8,128)} %get-tuple-element.369.refs_, ...), custom_call_target="tpu_custom_call" | custom-call | flops 1 | bytes 1 | tf_op jit(solution)/shard_map/pallas_call | solution.py:173
  386.2 6.6 %shard_map.162.refs_1_ = bf16[592,1024]{1,0:T(8,128)(2,1)} custom-call(bf16[592,2048]{1,0:T(8,128)(2,1)} %get-tuple-element.370.refs_1_.refs_0_, bf16[128,2048]{1,0:T(8,128)(2,1)} %get-tuple-element.584.refs_3_.refs_1_, bf16[128,2048]{1,0:T(8,128)(2,1)} %get-tuple-element.372.refs_4_.refs_2_, bf16[128,2048]{1,0:T(8,128)(2,1)} %get-tuple-element.373.refs_5_.refs_3_, ...), custom_call_target="tpu_custom_call" | custom-call | flops 1 | bytes 1 | tf_op jit(solution)/shard_map/pallas_call | solution.py:173
  392.8 7.8 %shard_map.163 = (bf16[256,2048]{1,0:T(8,128)(2,1)S(1)}, bf16[256,2048]{1,0:T(8,128)(2,1)}, bf16[256,2048]{1,0:T(8,128)(2,1)}, bf16[256,2048]{1,0:T(8,128)(2,1)}) custom-call(bf16[592,1024]{1,0:T(8,128)(2,1)} %get-tuple-element.408.n_ref, bf16[592,1024]{1,0:T(8,128)(2,1)} %get-tuple-element.409.dz_ref, bf16[592,512]{1,0:T(8,128)(2,1)S(1)} %copy-done.79, ...), custom_call_target="tpu_custom_call" | custom-call | flops 1 | bytes 1 | tf_op jit(solution)/shard_map/pallas_call | solution.py:173
  418.3 11.7 %shard_map.165 = (bf16[592,2048]{1,0:T(8,128)(2,1)}, f32[1,1024]{1,0:T(1,128)S(1)}, f32[1,2048]{1,0:T(1,128)S(1)}, bf16[256,2048]{1,0:T(8,128)(2,1)}, bf16[256,2...) custom-call(f32[592,1024]{1,0:T(8,128)} %get-tuple-element.425.refs_0_, ...), custom_call_target="tpu_custom_call" | custom-call | flops 1 | bytes 1 | tf_op jit(solution)/shard_map/pallas_call | solution.py:173
  430.0 7.1 %collective-permute-done.64.refs_10_ = bf16[256,2048]{1,0:T(8,128)(2,1)} collective-permute-done((bf16[256,2048]{1,0:T(8,128)(2,1)}, bf16[256,2048]{1,0:T(8,128)(2,1)}, u32[]{:S(2)}, u32[]{:S(2)}) %collective-permute-start.64) | collective-permute-done | bytes 1048608 | tf_op jit(solution)/shard_map/ppermute | solution.py:23
  466.0 14.2 %collective-permute-done.67.refs_11_ = bf16[128,2048]{1,0:T(8,128)(2,1)S(1)} collective-permute-done((bf16[128,2048]{1,0:T(8,128)(2,1)S(1)}, bf16[128,2048]{1,0:T(8,128)(2,1)S(1)}, u32[]{:S(2)}, u32[]{:S(2)}) %collective-permute-start.67) | collective-permute-done | bytes 524320 | tf_op jit(solution)/shard_map/ppermute | solution.py:28
  497.1 21.1 %shard_map.171 = (f32[592,1024]{1,0:T(8,128)}, bf16[592,1024]{1,0:T(8,128)(2,1)}, bf16[592,512]{1,0:T(8,128)(2,1)}, bf16[592,512]{1,0:T(8,128)(2,1)}, bf16[592,5...) custom-call(f32[592,1024]{1,0:T(8,128)} %get-tuple-element.425.refs_, ...), custom_call_target="tpu_custom_call" | custom-call | flops 1 | bytes 1 | tf_op jit(solution)/shard_map/pallas_call | solution.py:173
  521.4 7.9 %shard_map.172 = (bf16[256,2048]{1,0:T(8,128)(2,1)}, bf16[256,2048]{1,0:T(8,128)(2,1)}, bf16[256,2048]{1,0:T(8,128)(2,1)}, bf16[256,2048]{1,0:T(8,128)(2,1)}) custom-call(bf16[592,1024]{1,0:T(8,128)(2,1)} %get-tuple-element.467.n_ref, bf16[592,1024]{1,0:T(8,128)(2,1)} %get-tuple-element.468.dz_ref, bf16[592,512]{1,0:T(8,128)(2,1)S(1)} %copy-done.82, ...), custom_call_target="tpu_custom_call" | custom-call | flops 1 | bytes 1 | tf_op jit(solution)/shard_map/pallas_call | solution.py:173
  587.8 9.2 %collective-permute-done.88 = bf16[16,2048]{1,0:T(8,128)(2,1)S(1)} collective-permute-done((bf16[16,2048]{1,0:T(8,128)(2,1)S(1)}, bf16[16,2048]{1,0:T(8,128)(2,1)S(1)}, u32[]{:S(2)}, u32[]{:S(2)}) %collective-permute-start.88) | collective-permute-done | bytes 65568 | tf_op jit(solution)/shard_map/ppermute | solution.py:28
  620.9 13.9 %reduce-scatter.15.cloned.1.call-done = bf16[272,512]{1,0:T(8,128)(2,1)} async-done(((bf16[272,2048]{1,0:T(8,128)(2,1)}), bf16[272,512]{1,0:T(8,128)(2,1)}) %reduce-scatter.15.cloned.1.call-update) | async-done | bytes 278544 | tf_op jit(solution)/shard_map/reduce_scatter | solution.py:105
  (744 shorter events, 347.0 us)
Async XLA Ops:
  7.2 40.5 %all-gather.7.cloned.1.call-start = ((), (), s32[]{:S(2)}) async-start(), calls=%async_computation.6 | async-start | bytes 1392640 | tf_op jit(solution)/shard_map/all_gather | solution.py:49
  16.7 76.3 %all-gather.9.cloned.1.call-start = ((), (), s32[]{:S(2)}) async-start(), calls=%async_computation.7 | async-start | bytes 1310720 | tf_op jit(solution)/shard_map/all_gather | solution.py:49
  52.5 40.4 %collective-permute-start.6 = (bf16[128,2048]{1,0:T(8,128)(2,1)S(1)}, bf16[128,2048]{1,0:T(8,128)(2,1)S(1)}, u32[]{:S(2)}, u32[]{:S(2)}) collective-permute-start(bf16[128,2048]{1,0:T(8,128)(2,1)S(1)} %get-tuple-element.581.refs_9_.refs_14_), channel_id=1, source_target_pairs={{0,8},{4,12},{8,0},{12,4},{1,9},{5,13},{9,1},{13,5},{2,10},{6,14},... | collective-permute-start | bytes 1572872 | tf_op jit(solution)/shard_map/ppermute | solution.py:28
  55.0 83.7 %all-gather.11.cloned.1.call-start = ((), (), s32[]{:S(2)}) async-start(), calls=%async_computation.8 | async-start | bytes 1310720 | tf_op jit(solution)/shard_map/all_gather | solution.py:49
  55.1 37.9 %collective-permute-start.4 = (bf16[128,2048]{1,0:T(8,128)(2,1)S(1)}, bf16[128,2048]{1,0:T(8,128)(2,1)S(1)}, u32[]{:S(2)}, u32[]{:S(2)}) collective-permute-start(bf16[128,2048]{1,0:T(8,128)(2,1)S(1)} %get-tuple-element.582.refs_5_.refs_10_), channel_id=1, source_target_pairs={{0,4},{4,0},{8,12},{12,8},{1,5},{5,1},{9,13},{13,9},{2,6},{6,2},{1... | collective-permute-start | bytes 1572872 | tf_op jit(solution)/shard_map/ppermute | solution.py:23
  101.0 75.0 %all-gather.13.cloned.1.call-start = ((), (), s32[]{:S(2)}) async-start(), calls=%async_computation.9 | async-start | bytes 1310720 | tf_op jit(solution)/shard_map/all_gather | solution.py:49
  141.9 77.9 %all-gather.15.cloned.1.call-start = ((), (), s32[]{:S(2)}) async-start(), calls=%async_computation.10 | async-start | bytes 1310720 | tf_op jit(solution)/shard_map/all_gather | solution.py:49
  181.7 68.9 %all-gather.17.cloned.1.call-start = ((), (), s32[]{:S(2)}) async-start(), calls=%async_computation.11 | async-start | bytes 1310720 | tf_op jit(solution)/shard_map/all_gather | solution.py:49
  222.1 185.7 %reduce-scatter.7.cloned.1.call-start = ((), (), s32[]{:S(2)}) async-start(), calls=%async_computation.12 | async-start | bytes 1310720 | tf_op jit(solution)/shard_map/reduce_scatter | solution.py:105
  336.9 34.6 %collective-permute-start.57 = (bf16[256,2048]{1,0:T(8,128)(2,1)}, bf16[256,2048]{1,0:T(8,128)(2,1)}, u32[]{:S(2)}, u32[]{:S(2)}) collective-permute-start(bf16[256,2048]{1,0:T(8,128)(2,1)} %get-tuple-element.404), channel_id=1, source_target_pairs={{0,4},{4,0},{8,12},{12,8},{1,5},{5,1},{9,13},{13,9},{2,6},{6,2},{1... | collective-permute-start | bytes 3145736 | tf_op jit(solution)/shard_map/ppermute | solution.py:23
  337.6 33.9 %collective-permute-start.58 = (bf16[256,2048]{1,0:T(8,128)(2,1)}, bf16[256,2048]{1,0:T(8,128)(2,1)}, u32[]{:S(2)}, u32[]{:S(2)}) collective-permute-start(bf16[256,2048]{1,0:T(8,128)(2,1)} %get-tuple-element.405), channel_id=1, source_target_pairs={{0,8},{4,12},{8,0},{12,4},{1,9},{5,13},{9,1},{13,5},{2,10},{6,14},... | collective-permute-start | bytes 3145736 | tf_op jit(solution)/shard_map/ppermute | solution.py:28
  375.3 65.2 %reduce-scatter.9.cloned.1.call-start = ((), (), s32[]{:S(2)}) async-start(), calls=%async_computation.13 | async-start | bytes 1310720 | tf_op jit(solution)/shard_map/reduce_scatter | solution.py:105
  410.6 119.0 %reduce-scatter.11.cloned.1.call-start = ((), (), s32[]{:S(2)}) async-start(), calls=%async_computation.14 | async-start | bytes 1310720 | tf_op jit(solution)/shard_map/reduce_scatter | solution.py:105
  445.4 34.8 %collective-permute-start.69 = (bf16[256,2048]{1,0:T(8,128)(2,1)S(1)}, bf16[256,2048]{1,0:T(8,128)(2,1)S(1)}, u32[]{:S(2)}, u32[]{:S(2)}) collective-permute-start(bf16[256,2048]{1,0:T(8,128)(2,1)S(1)} %copy-done.136), channel_id=1, source_target_pairs={{0,4},{4,0},{8,12},{12,8},{1,5},{5,1},{9,13},{13,9},{2,6},{6,2},{1... | collective-permute-start | bytes 3145736 | tf_op jit(solution)/shard_map/ppermute | solution.py:23
  445.7 34.5 %collective-permute-start.70 = (bf16[256,2048]{1,0:T(8,128)(2,1)S(1)}, bf16[256,2048]{1,0:T(8,128)(2,1)S(1)}, u32[]{:S(2)}, u32[]{:S(2)}) collective-permute-start(bf16[256,2048]{1,0:T(8,128)(2,1)S(1)} %copy-done.137), channel_id=1, source_target_pairs={{0,8},{4,12},{8,0},{12,4},{1,9},{5,13},{9,1},{13,5},{2,10},{6,14},... | collective-permute-start | bytes 3145736 | tf_op jit(solution)/shard_map/ppermute | solution.py:28
  484.5 91.6 %reduce-scatter.13.cloned.1.call-start = ((), (), s32[]{:S(2)}) async-start(), calls=%async_computation.15 | async-start | bytes 1310720 | tf_op jit(solution)/shard_map/reduce_scatter | solution.py:105
  487.4 42.1 %collective-permute-start.72 = (bf16[296,256]{1,0:T(8,128)(2,1)}, bf16[296,256]{1,0:T(8,128)(2,1)}, u32[]{:S(2)}, u32[]{:S(2)}) collective-permute-start(bf16[296,256]{1,0:T(8,128)(2,1)} %get-tuple-element.466), channel_id=1, source_target_pairs={{0,3},{1,0},{2,1},{3,2},{4,7},{5,4},{6,5},{7,6},{8,11},{9,8},{10,9... | collective-permute-start | bytes 454664 | tf_op jit(solution)/shard_map/ppermute | solution.py:517
  491.6 38.0 %collective-permute-start.74 = (bf16[128,2048]{1,0:T(8,128)(2,1)}, bf16[128,2048]{1,0:T(8,128)(2,1)}, u32[]{:S(2)}, u32[]{:S(2)}) collective-permute-start(bf16[128,2048]{1,0:T(8,128)(2,1)} %get-tuple-element.553), channel_id=1, source_target_pairs={{0,4},{4,0},{8,12},{12,8},{1,5},{5,1},{9,13},{13,9},{2,6},{6,2},{1... | collective-permute-start | bytes 1572872 | tf_op jit(solution)/shard_map/ppermute | solution.py:23
  492.6 37.1 %collective-permute-start.75 = (bf16[256,2048]{1,0:T(8,128)(2,1)S(1)}, bf16[256,2048]{1,0:T(8,128)(2,1)}, u32[]{:S(2)}, u32[]{:S(2)}) collective-permute-start(bf16[256,2048]{1,0:T(8,128)(2,1)S(1)} %copy-done.71), channel_id=1, source_target_pairs={{0,4},{4,0},{8,12},{12,8},{1,5},{5,1},{9,13},{13,9},{2,6},{6,2},{1... | collective-permute-start | bytes 3145736 | tf_op jit(solution)/shard_map/ppermute | solution.py:23
  493.1 36.5 %collective-permute-start.76 = (bf16[256,2048]{1,0:T(8,128)(2,1)S(1)}, bf16[256,2048]{1,0:T(8,128)(2,1)}, u32[]{:S(2)}, u32[]{:S(2)}) collective-permute-start(bf16[256,2048]{1,0:T(8,128)(2,1)S(1)} %copy-done.73), channel_id=1, source_target_pairs={{0,8},{4,12},{8,0},{12,4},{1,9},{5,13},{9,1},{13,5},{2,10},{6,14},... | collective-permute-start | bytes 3145736 | tf_op jit(solution)/shard_map/ppermute | solution.py:28
  496.4 33.2 %collective-permute-start.73 = (bf16[128,2048]{1,0:T(8,128)(2,1)}, bf16[128,2048]{1,0:T(8,128)(2,1)S(1)}, u32[]{:S(2)}, u32[]{:S(2)}) collective-permute-start(bf16[128,2048]{1,0:T(8,128)(2,1)} %get-tuple-element.555), channel_id=1, source_target_pairs={{0,8},{4,12},{8,0},{12,4},{1,9},{5,13},{9,1},{13,5},{2,10},{6,14},... | collective-permute-start | bytes 1572872 | tf_op jit(solution)/shard_map/ppermute | solution.py:28
  534.1 77.1 %reduce-scatter.17.cloned.1.call-start = ((), (), s32[]{:S(2)}) async-start(), calls=%async_computation.17 | async-start | bytes 1310720 | tf_op jit(solution)/shard_map/reduce_scatter | solution.py:105
  541.3 34.8 %collective-permute-start.83 = (bf16[256,2048]{1,0:T(8,128)(2,1)}, bf16[256,2048]{1,0:T(8,128)(2,1)}, u32[]{:S(2)}, u32[]{:S(2)}) collective-permute-start(bf16[256,2048]{1,0:T(8,128)(2,1)} %get-tuple-element.506), channel_id=1, source_target_pairs={{0,8},{4,12},{8,0},{12,4},{1,9},{5,13},{9,1},{13,5},{2,10},{6,14},... | collective-permute-start | bytes 3145736 | tf_op jit(solution)/shard_map/ppermute | solution.py:28
  565.7 69.1 %reduce-scatter.15.cloned.1.call-start = ((), (), s32[]{:S(2)}) async-start(), calls=%async_computation.16 | async-start | bytes 1392640 | tf_op jit(solution)/shard_map/reduce_scatter | solution.py:105
  (232 other events, 2359.9 us)
Sparse Core Ops, SparseCore 0:
  16.8 30.8 all-gather.6
  55.1 33.9 all-gather.8
  101.1 28.0 all-gather.10
  142.0 32.6 all-gather.12
  181.9 30.8 all-gather.14
  222.3 27.6 all-gather.16
  375.4 29.8 reduce-scatter.6
  410.7 29.6 reduce-scatter.8
  484.6 27.4 reduce-scatter.10
  534.2 26.7 reduce-scatter.12
  565.8 25.8 reduce-scatter.16
  606.8 27.9 reduce-scatter.14

commit v10 on v9

--- a/solution.py
+++ b/solution.py
@@ -67,12 +67,29 @@
     return ([first, near[0], far[0], far[1]], [second, near[1], far[2], far[3]])
 
 
-def row_cuts(depth):
-    half = depth // 2
-    if lax.axis_size("dp") != 4:
-        return [(0, half), (half, depth), None, None]
-    part = half // 2
-    return [(part, half), (half + part, depth), (0, part), (half, half + part)]
+def row_plan(depth):
+    late = depth // 8 if lax.axis_size("dp") == 4 else 0
+    return (depth - late) // 2, late
+
+
+def row_cuts(features):
+    n_dp = lax.axis_size("dp")
+    half, late = row_plan(features // n_dp)
+    if n_dp != 4:
+        return [[(0, features // 2)], [(features // 2, features)], None, None]
+    part = late // 2
+    base = 8 * half
+
+    def ranges(second, outer):
+        out = []
+        for inner in range(2):
+            start = (4 * second + 2 * outer + inner) * half
+            chip = 2 * inner + outer if second else 2 * outer + inner
+            extra = base + chip * late + second * part
+            out += [(start, start + half), (extra, extra + part)]
+        return out
+
+    return [ranges(0, 1), ranges(1, 1), ranges(0, 0), ranges(1, 0)]
 
 
 def add(left, right):
@@ -111,33 +128,25 @@
     return jnp.where(bit == 1, jnp.flip(value, axis), value)
 
 
-def relative(value, spot):
+def feature_order(features, spot):
     n_dp = lax.axis_size("dp")
-    lead = value.shape[:-1]
-    k = len(lead)
-    if n_dp != 4:
-        cut = value.reshape(lead + (n_dp, 2, -1))
-        return jnp.swapaxes(cut, k, k + 1).reshape(value.shape)
-    cut = value.reshape(lead + (2, 2, 2, -1))
-    cut = flip_axis(flip_axis(cut, k, spot // 2), k + 1, spot % 2)
-    first = jnp.swapaxes(cut[..., 0, :], k, k + 1)
-    second = cut[..., 1, :]
-    return jnp.concatenate([first.reshape(lead + (-1,)), second.reshape(lead + (-1,))], -1)
-
-
-def absolute(value, spot):
-    n_dp = lax.axis_size("dp")
-    lead = value.shape[:-1]
-    k = len(lead)
-    if n_dp != 4:
-        cut = value.reshape(lead + (2, n_dp, -1))
-        return jnp.swapaxes(cut, k, k + 1).reshape(value.shape)
-    cut = value.reshape(lead + (2, 2, 2, -1))
-    first = jnp.swapaxes(cut[..., 0, :, :, :], k, k + 1)
-    second = cut[..., 1, :, :, :]
-    cut = jnp.stack([first, second], k + 2)
-    cut = flip_axis(flip_axis(cut, k, spot // 2), k + 1, spot % 2)
-    return cut.reshape(value.shape)
+    depth = features // n_dp
+    half, late = row_plan(depth)
+    if n_dp == 4:
+        chip = [[(ry ^ spot // 2) * 2 + (rx ^ spot % 2) for ry in range(2)] for rx in range(2)]
+        first = [chip[rx][ry] for rx in range(2) for ry in range(2)]
+        second = [chip[rx][ry] for ry in range(2) for rx in range(2)]
+    else:
+        first = second = range(n_dp)
+    parts = [p * depth + jnp.arange(half) for p in first]
+    parts += [p * depth + half + jnp.arange(half) for p in second]
+    if late:
+        parts += [p * depth + 2 * half + jnp.arange(late) for p in first]
+    return jnp.concatenate(parts).astype(jnp.int32)
+
+
+def chooser(order):
+    return (jnp.arange(order.size)[:, None] == order[None, :]).astype(jnp.bfloat16)
 
 
 def by_chip(blocks, spot):
@@ -157,6 +166,10 @@
     cut = blocks.reshape((2, 2) + blocks.shape[1:])
     cut = flip_axis(flip_axis(cut, 0, spot // 2), 1, spot % 2)
     return jnp.swapaxes(cut, 0, 1).reshape(blocks.shape)
+
+
+def mm(form, left, right):
+    return jnp.einsum(form, left, right, preferred_element_type=jnp.float32)
 
 
 VMEM_BYTES = 50 * 2**20
@@ -194,7 +207,15 @@
 
 
 def stack_rows(pieces, counts, cols):
-    return jnp.concatenate([p[:n, cols] for p, n in zip(pieces, counts)], 0)
+    return jnp.concatenate([pieces[i][a : a + n, cols] for i, a, n in counts], 0)
+
+
+def write_rows(refs, cuts, cols, full):
+    for ref, ranges in zip(refs, cuts):
+        at = 0
+        for a, b in ranges:
+            ref[at : at + b - a, cols] = full[a:b].astype(BF)
+            at += b - a
 
 
 def center_scale(value):
@@ -305,7 +326,7 @@
 def contract_wide(left, weights):
     pieces, counts = weights
     size, wide = left.shape
-    depth = sum(counts)
+    depth = sum(n for _, _, n in counts)
 
     def kernel(*refs):
         left_ref, piece_refs, out_ref = refs[0], refs[1:-1], refs[-1]
@@ -317,7 +338,7 @@
 
 def weight_outs(depth, wide):
     cuts = [c for c in row_cuts(depth) if c is not None]
-    return cuts, [shape((c[1] - c[0], wide)) for c in cuts]
+    return cuts, [shape((sum(b - a for a, b in c), wide)) for c in cuts]
 
 
 def fill(grads):
@@ -336,11 +357,10 @@
         low_ref, sum_ref, bias_ref = refs[:3]
         sum_ref[...] = column_sum(g_ref[...])
         branch = g_ref[...].astype(BF)
-        for cut, ref in zip(cuts, refs[3:]):
-            ref[...] = tn(branch[:, cut[0] : cut[1]], hidden_ref[...]).astype(BF)
         step = 512
         for at in range(0, wide, step):
             cols = slice(at, at + step)
+            write_rows(refs[3:], cuts, cols, tn(branch, hidden_ref[:, cols]))
             back = nn(branch, stack_rows(piece_refs, counts, cols)) * slope_ref[:, cols].astype(F32)
             bias_ref[:, cols] = column_sum(back)
             low_ref[:, cols] = back.astype(BF)
@@ -356,8 +376,10 @@
     cuts, outs = weight_outs(depth, wide)
 
     def kernel(n_ref, low_ref, *refs):
-        for cut, ref in zip(cuts, refs):
-            ref[...] = tn(n_ref[:, cut[0] : cut[1]], low_ref[...]).astype(BF)
+        step = 512
+        for at in range(0, wide, step):
+            cols = slice(at, at + step)
+            write_rows(refs, cuts, cols, tn(n_ref[...], low_ref[:, cols]))
 
     return fill(run(kernel, outs, [normed, low]))
 
@@ -429,13 +451,13 @@
     cuts, outs = weight_outs(depth, groups * 512)
 
     def kernel(n_ref, dz_ref, dq_ref, dk_ref, dv_ref, o_ref, *refs):
-        for cut, ref in zip(cuts, refs):
-            rows = slice(cut[0], cut[1])
-            for g in range(groups):
-                at = slice(g * 128, (g + 1) * 128)
-                right = jnp.concatenate([dq_ref[:, at], dk_ref[:, at], dv_ref[:, at]], 1)
-                ref[:, g * 512 : g * 512 + 384] = tn(n_ref[:, rows], right).astype(BF)
-                ref[:, g * 512 + 384 : g * 512 + 512] = tn(dz_ref[:, rows], o_ref[:, at]).astype(BF)
+        for g in range(groups):
+            at = slice(g * 128, (g + 1) * 128)
+            right = jnp.concatenate([dq_ref[:, at], dk_ref[:, at], dv_ref[:, at]], 1)
+            cols = slice(g * 512, g * 512 + 384)
+            write_rows(refs, cuts, cols, tn(n_ref[...], right))
+            cols = slice(g * 512 + 384, g * 512 + 512)
+            write_rows(refs, cuts, cols, tn(dz_ref[...], o_ref[:, at]))
 
     return fill(run(kernel, outs, [normed, dz, dq, dk, dv, mixed]))
 
@@ -457,59 +479,45 @@
     return run(kernel, outs, [dmid, own, far, value, rows])
 
 
-def block_lanes(spot, chunk):
-    ry, rx = chunk // 2 ^ spot // 2, chunk % 2 ^ spot % 2
-    return [(rx * 2 + ry) * 128, 512 + (ry * 2 + rx) * 128]
-
-
 def place_in(lanes, blocks):
     size, width = blocks[0].shape
-    half = width // 2
+    features = width * len(blocks)
 
     def kernel(lanes_ref, *refs):
-        out_ref = refs[-1]
-        for d, ref in enumerate(refs[:-1]):
-            for h in range(2):
-                at = pl.multiple_of(lanes_ref[2 * d + h], 128)
-                out_ref[:, pl.ds(at, half)] = ref[:, h * half : (h + 1) * half]
-
-    block = pl.BlockSpec(memory_space=pltpu.VMEM)
-    return pl.pallas_call(
-        kernel,
-        out_shape=shape((size, width * len(blocks))),
-        in_specs=[pl.BlockSpec(memory_space=pltpu.SMEM)] + [block] * len(blocks),
-        out_specs=block,
-        compiler_params=pltpu.CompilerParams(vmem_limit_bytes=VMEM_BYTES),
-    )(lanes, *blocks)
-
-
-def place_out(numbers, scale, terms, bias_row, count):
-    size, depth = terms[0].shape
-    width = depth // count
-    half = width // 2
-
-    def kernel(numbers_ref, scale_ref, *refs):
+        value = jnp.concatenate([ref[...] for ref in refs[:-1]], 1)
+        place = lax.broadcasted_iota(jnp.int32, (features, features), 0)
+        pick = (place == lanes_ref[...]).astype(F32).astype(BF)
+        refs[-1][...] = nn(value, pick).astype(BF)
+
+    return run(kernel, [shape((size, features))], [lanes, *blocks])[0]
+
+
+def place_out(lanes, start, scale, terms, bias_row, count):
+    size, features = terms[0].shape
+    width = features // count
+
+    def kernel(start_ref, scale_ref, lanes_ref, *refs):
         term_refs, bias_ref, out_ref = refs[: len(terms)], refs[-2], refs[-1]
-        start = pl.multiple_of(numbers_ref[2 * count], 8)
-        rows = pl.ds(start, size // 2)
+        rows = pl.ds(pl.multiple_of(start_ref[0], 8), size // 2)
+        value = term_refs[0][rows, :]
+        for ref in term_refs[1:]:
+            value = value + ref[rows, :]
+        value = ((value + bias_ref[...]) * scale_ref[0]).astype(BF)
+        place = lax.broadcasted_iota(jnp.int32, (features, features), 0)
+        pick = (place == lanes_ref[...]).astype(F32).astype(BF)
+        value = nt(value, pick).astype(BF)
         for d in range(count):
-            for h in range(2):
-                lanes = pl.ds(pl.multiple_of(numbers_ref[2 * d + h], 128), half)
-                value = term_refs[0][rows, lanes]
-                for ref in term_refs[1:]:
-                    value = value + ref[rows, lanes]
-                value = (value + bias_ref[:, lanes]) * scale_ref[0]
-                out_ref[d, :, h * half : (h + 1) * half] = value.astype(BF)
+            out_ref[d] = value[:, d * width : (d + 1) * width]
 
     block = pl.BlockSpec(memory_space=pltpu.VMEM)
     scalar = pl.BlockSpec(memory_space=pltpu.SMEM)
     return pl.pallas_call(
         kernel,
         out_shape=shape((count, size // 2, width)),
-        in_specs=[scalar, scalar] + [block] * (len(terms) + 1),
+        in_specs=[scalar, scalar] + [block] * (len(terms) + 2),
         out_specs=block,
         compiler_params=pltpu.CompilerParams(vmem_limit_bytes=VMEM_BYTES),
-    )(numbers, scale, *terms, bias_row)
+    )(start, scale, lanes, *terms, bias_row)
 
 
 def shift(block, d):
@@ -545,7 +553,11 @@
     slots_per_batch = boundary_in.shape[1] // counts.shape[1]
     live = (place % slots_per_batch < counts[0, place // slots_per_batch]).astype(jnp.float32)
     depth = qkv_weight.shape[1]
-    mid = depth // 2
+    half_rows, late = row_plan(depth)
+    early = 2 * half_rows
+    features = n_dp * depth
+    order = feature_order(features, spot)
+    pick = chooser(order)
     n_vec = vectors.size
 
     small_size = n_vec + fc1_bias.size
@@ -568,17 +580,27 @@
         jnp.concatenate([jnp.where(is_first, packs[1], packs[0]), small], 0)
     )
     shards = (jnp.where(is_first, kept, received), jnp.where(is_first, received, kept))
-    columns = []
+    room = extra // 2
+    both = [shard[depth : depth + room, :wide] for shard in shards]
+    if late:
+        last = jnp.concatenate([shard[early:depth] for shard in shards], 0)
+        over = lax.ppermute(last, "dp", [(i, i ^ 3) for i in range(n_dp)])
+        last = jnp.stack([last, swap_y(last), swap_x(last), over])
+        last = last.reshape(n_dp, 2, late, -1)
+    columns, late_rows = [], []
     for layer in range(2):
         for number in range(3):
-            cols = shards[layer][:, number * wide : (number + 1) * wide]
-            if layer == 0 and number == 0:
-                room = extra // 2
-                both = [shard[depth : depth + room, :wide] for shard in shards]
-                cols = jnp.concatenate([cols[:depth], *both], 0)
-            else:
-                cols = cols[:depth]
-            columns.append(cols)
+            cols = slice(number * wide, (number + 1) * wide)
+            columns.append(shards[layer][:early, cols])
+            if late:
+                late_rows.append(last[:, layer, :, cols].reshape(n_dp * late, -1))
+    columns[0] = jnp.concatenate([columns[0], *both], 0)
+    late_at = [(k, early) for k in range(len(columns))]
+    if late:
+        for k in range(1, len(columns)):
+            more = late_rows[:2] if k == 1 else [late_rows[k]]
+            columns[k] = jnp.concatenate([columns[k], *more], 0)
+        late_at[:2] = [(1, early), (1, early + n_dp * late)]
 
     tokens = boundary_in.shape[2]
     pad = -tokens % 16
@@ -595,13 +617,12 @@
     def to_send(half):
         return [lax.dynamic_index_in_dim(half, j, 0, False) for j in above]
 
+    width = features // n_tensor
+    lanes_in = ((place - order // width) % n_tensor * width + order % width)[None]
+    lanes_out = ((order // width - place) % n_tensor * width + order % width)[None]
+
     def image_half(blocks):
-        if n_dp == 4:
-            lanes = [lane for t in below for lane in block_lanes(spot, t)]
-            return place_in(jnp.stack(lanes).astype(jnp.int32), blocks)
-        blocks = jnp.stack(blocks)
-        blocks = [lax.dynamic_index_in_dim(blocks, (place - i) % n_tensor, 0, False) for i in range(n_tensor)]
-        return relative(jnp.concatenate(blocks, 1), spot)
+        return place_in(lanes_in, blocks)
 
     def whole_image(half):
         other = swap(half)
@@ -609,16 +630,9 @@
         return jnp.concatenate(both, 0)
 
     def image_rows(scale, terms, bias_row):
-        if n_dp == 4:
-            numbers = [lane for t in above for lane in block_lanes(spot, t)]
-            numbers.append(jnp.where(is_first, 0, reach))
-            numbers = jnp.stack(numbers).astype(jnp.int32)
-            blocks = place_out(numbers, scale.reshape(1), terms, bias_row, n_tensor)
-            return [blocks[d] for d in range(n_tensor)]
-        image = absolute((sum(terms[1:], terms[0]) + bias_row) * scale, spot).astype(jnp.bfloat16)
-        half = jnp.where(is_first, image[:reach], image[reach:])
-        half = half.reshape(reach, n_tensor, -1).transpose(1, 0, 2)
-        return to_send(half)
+        start = jnp.where(is_first, 0, reach).astype(jnp.int32).reshape(1)
+        blocks = place_out(lanes_out, start, scale.reshape(1), terms, bias_row, n_tensor)
+        return [blocks[d] for d in range(n_tensor)]
 
     def by_image(blocks):
         blocks = jnp.stack(blocks)
@@ -635,7 +649,8 @@
         both = both.reshape(n_dp, 2, extra // 2, n_tensor, wide).transpose(1, 0, 3, 2, 4)
         both = both.reshape(2, n_dp, n_tensor, -1)
         rows = both[..., :n_vec].reshape(2, n_dp, n_tensor, 8, -1)
-        rows = relative(rows.transpose(0, 3, 2, 1, 4).reshape(2, 8, -1), spot)
+        rows = rows.transpose(0, 3, 2, 1, 4).reshape(16, -1).astype(jnp.bfloat16)
+        rows = mm("kd,dr->kr", rows, pick).reshape(2, 8, -1)
         bias = both[..., n_vec:small_size].transpose(0, 2, 1, 3).reshape(2, -1)
         plain = both[..., :n_vec].reshape(2, n_dp, n_tensor, 8, -1)[..., 2:4, :]
         plain = plain.transpose(0, 3, 2, 1, 4).reshape(2, 2, -1)
@@ -649,9 +664,17 @@
     blocks_in, blocks_cot = to_send(half_in), to_send(half_cot)
     pair, state = None, None
 
+    wholes = [None] * number
+
     def weights_of(k):
         first, second = arrived(*halves[k], near[k], far[k])
-        return (first + second, [p.shape[0] for p in first + second])
+        arrays = first + second
+        counts = [(i, 0, p.shape[0]) for i, p in enumerate(arrays)]
+        if late:
+            source, start = late_at[k]
+            counts.append((len(arrays), start, n_dp * late))
+            arrays = [*arrays, wholes[source]]
+        return (arrays, counts)
 
     for r in range(number + 1):
         tied = []
@@ -741,9 +764,10 @@
                 pair = [done[-1]]
             at = 0
             if r < number:
-                halves[r] = (done[0][:mid], done[0][mid:depth])
+                wholes[r] = done[0]
+                halves[r] = (done[0][:half_rows], done[0][half_rows:early])
                 if r == 0:
-                    extra_rows = done[0][depth:]
+                    extra_rows = done[0][early:]
                 at = 1
             if 0 <= r - 1 < number:
                 near[r - 1] = done[at : at + 2]
@@ -756,7 +780,8 @@
         for layer in range(2):
             total = sums[layer]
             full = jnp.concatenate([total["one"], total["mid"], total["out"]], 0)
-            full = absolute(jnp.where(core == layer, full, 0.0), spot)
+            full = jnp.where(core == layer, full, 0.0).astype(jnp.bfloat16)
+            full = mm("kr,dr->kd", full, pick)
             q_row = spread_cols(core, total["q"][0], n_tensor)
             v_row = spread_cols(core, total["v"][0], n_tensor)
             up_row = spread_cols(core, total["up_bias"][0], n_tensor)
@@ -891,6 +916,13 @@
     other = swap(jnp.where(is_first, out_rows, grad_rows))
     ends = [jnp.where(is_first, own, other), jnp.where(is_first, other, own)]
     boundary_out = jnp.concatenate(ends, 1)[:, :tokens].astype(jnp.float32)[None]
+    if late:
+        part, cut = late // 2, depth // 2
+        for k in range(number):
+            rows = settled[k]
+            parts = [rows[:half_rows], rows[cut : cut + half_rows]]
+            parts += [rows[half_rows:cut], rows[cut + half_rows :]]
+            settled[k] = jnp.concatenate(parts, 0)
     lows, highs = [], []
     for kind in range(3):
         first, second = settled[last - kind], settled[last - kind - 3]

time: 658 us -> 671 us (1.020)
  waiting for transfers between devices: 192 us -> 144 us
  local copies, waits for them, and re-layouts: 82.2 us -> 103 us
  blocking collectives: 0 us -> 19.6 us
  starting transfers between devices: 90.8 us -> 103 us
    ppermute x32 -> x33, waiting for transfers between devices: 61.9 us -> 31.1 us  [swap_x(): return lax.ppermute(value, 'dp', [(i, i ^ 1) for i in range(n)])]
    all_gather x0 -> x1, blocking collectives: none -> 19.6 us  [gather_column(): return lax.all_gather(shard, 'tensor', axis=1, tiled=True)]
    unnamed x318 -> x481, local copies, waits for them, and re-layouts: 44.1 us -> 60.6 us
    all_gather x6 -> x5, waiting for transfers between devices: 22.8 us -> 10.8 us  [gather_column(): return lax.all_gather(shard, 'tensor', axis=1, tiled=True)]
    ppermute x12, waiting for transfers between devices: 41.9 us -> 50.3 us  [shift(): return lax.ppermute(block, 'tensor', [(i, (i + d) % n) for i in range(n)])]
    slice x12 -> x24, local copies, waits for them, and re-layouts: 15.7 us -> 23.9 us  [the longest x6 12.2 us: body(): halves[r] = (done[0][:half_rows], done[0][half_rows:early])]
    concatenate x1 -> x13, other arithmetic: 0.73 us -> 7.97 us  [the longest x5 5.72 us: body(): columns[k] = jnp.concatenate([columns[k], *more], 0)]
    ppermute x32 -> x33, waiting for transfers between devices: 43 us -> 37.3 us  [swap_y(): return lax.ppermute(value, 'dp', [(i, i ^ 2) for i in range(n)])]
  transfers between devices with their start and end apart: 106 -> 108, of which waited for: 35 -> 32; matrix products, arithmetic and copies ran while one was open for 15% -> 15% of each run, Pallas kernels for 28% -> 28%
where the time goes in v10:
time: 671 us; the launch traced here: 662 us
  Pallas kernels  195 us (29%)
  waiting for transfers between devices  144 us (21%)
  local copies, waits for them, and re-layouts  103 us (15%)
  starting transfers between devices  103 us (15%)
  other arithmetic  76.8 us (11%)
  blocking collectives  19.6 us (3%)
  between operations  17.6 us (3%)
    pallas_call x20, Pallas kernels, run(): pl.pallas_call(kernel, out_shape=list(outs), in_specs=[block] * len(ins),...  192 us
    unnamed x481, local copies, waits for them, and re-layouts  60.6 us
    ppermute x12, waiting for transfers between devices, shift(): return lax.ppermute(block, 'tensor', [(i, (i + d) % n) for i in range(n)])  50.3 us
    ppermute x33, waiting for transfers between devices, swap_y(): return lax.ppermute(value, 'dp', [(i, i ^ 2) for i in range(n)])  37.3 us
    ppermute x33, waiting for transfers between devices, swap_x(): return lax.ppermute(value, 'dp', [(i, i ^ 1) for i in range(n)])  31.1 us
    ppermute x17, starting transfers between devices, swap(): return lax.ppermute(value, 'section', [(0, 1), (1, 0)])  30.4 us
    convert_element_type x12, other arithmetic, scatter_two(): send.append(add(keep[half:], new[half:]).astype(jnp.bfloat16))  28.7 us
    ppermute x33, starting transfers between devices, swap_y(): return lax.ppermute(value, 'dp', [(i, i ^ 2) for i in range(n)])  26 us
  transfers between devices with their start and end apart: 108, of which 32 were waited for; matrix products, arithmetic and copies ran while one was open for 15% of the time, Pallas kernels for 28%

profile of v10, /device:TPU:1, one launch (start us, length us, event | category | flops | bytes accessed | tf_op | source)
XLA Modules:
  0.0 661.9 jit_solution(13260855815373127752)
XLA Ops:
  24.5 19.6 %all_gather.18.refs_0_ = bf16[240,2048]{1,0:T(8,128)(2,1)} all-gather(bf16[240,512]{1,0:T(8,128)(2,1)S(1)} %pad_maximum_fusion.26), channel_id=1, replica_groups=mesh['section'=2,'dp'=4,'tensor'=4] {'tensor'}, dimensions={1}, use_global_device_ids=true | all-gather | bytes 1228800 | tf_op jit(solution)/shard_map/all_gather | solution.py:49
  64.1 7.3 %collective-permute-done.5.refs_1_ = bf16[112,2048]{1,0:T(8,128)(2,1)S(1)} collective-permute-done((bf16[112,2048]{1,0:T(8,128)(2,1)}, bf16[112,2048]{1,0:T(8,128)(2,1)S(1)}, u32[]{:S(2)}, u32[]{:S(2)}) %collective-permute-start.5) | collective-permute-done | bytes 458784 | tf_op jit(solution)/shard_map/ppermute | solution.py:28
  75.7 15.8 %collective-permute-done.12.refs_9_ = bf16[296,256]{1,0:T(8,128)(2,1)S(1)} collective-permute-done((bf16[296,256]{1,0:T(8,128)(2,1)}, bf16[296,256]{1,0:T(8,128)(2,1)S(1)}, u32[]{:S(2)}, u32[]{:S(2)}) %collective-permute-start.12) | collective-permute-done | bytes 151584 | tf_op jit(solution)/shard_map/ppermute | solution.py:525
  101.2 8.6 %all-gather.6.cloned.1.call-done.refs_0_ = bf16[480,2048]{1,0:T(8,128)(2,1)} async-done(((bf16[480,512]{1,0:T(8,128)(2,1)}), bf16[480,2048]{1,0:T(8,128)(2,1)}) %all-gather.6.cloned.1.call-update) | async-done | bytes 1966096 | tf_op jit(solution)/shard_map/all_gather | solution.py:49
  123.6 16.0 %shard_map.138 = (f32[592,1024]{1,0:T(8,128)}, bf16[592,1024]{1,0:T(8,128)(2,1)}, bf16[592,512]{1,0:T(8,128)(2,1)}, bf16[592,512]{1,0:T(8,128)(2,1)}, bf16[592,5...) custom-call(f32[592,1024]{1,0:T(8,128)} %maximum_convert_fusion.refs_0_, ...), custom_call_target="tpu_custom_call" | custom-call | flops 1 | bytes 1 | tf_op jit(solution)/shard_map/pallas_call | solution.py:186
  165.8 10.3 %shard_map.141 = (f32[592,1024]{1,0:T(8,128)}, bf16[592,1024]{1,0:T(8,128)(2,1)}, bf16[592,2048]{1,0:T(8,128)(2,1)}, bf16[592,2048]{1,0:T(8,128)(2,1)}) custom-call(f32[592,1024]{1,0:T(8,128)} %get-tuple-element.300.refs_0_.u_ref, bf16[592,1024]{1,0:T(8,128)(2,1)} %get-tuple-element.301.refs_1_, bf16[592,1024]{1,0:T(8,128)(2,1)} %copy-done.179, ...), custom_call_target="tpu_custom_call" | custom-call | flops 1 | bytes 1 | tf_op jit(solution)/shard_map/pallas_call | solution.py:186
  180.3 13.9 %collective-permute-done.32.refs_10_ = bf16[296,256]{1,0:T(8,128)(2,1)S(1)} collective-permute-done((bf16[296,256]{1,0:T(8,128)(2,1)S(1)}, bf16[296,256]{1,0:T(8,128)(2,1)S(1)}, u32[]{:S(2)}, u32[]{:S(2)}) %collective-permute-start.32) | collective-permute-done | bytes 151584 | tf_op jit(solution)/shard_map/ppermute | solution.py:525
  201.6 6.6 shard_map.144.refs_2_
  215.4 10.3 %collective-permute-done.39.refs_11_ = bf16[296,256]{1,0:T(8,128)(2,1)S(1)} collective-permute-done((bf16[296,256]{1,0:T(8,128)(2,1)S(1)}, bf16[296,256]{1,0:T(8,128)(2,1)S(1)}, u32[]{:S(2)}, u32[]{:S(2)}) %collective-permute-start.39) | collective-permute-done | bytes 151584 | tf_op jit(solution)/shard_map/ppermute | solution.py:525
  241.3 17.7 %shard_map.147 = (f32[592,1024]{1,0:T(8,128)}, bf16[592,1024]{1,0:T(8,128)(2,1)}, bf16[592,512]{1,0:T(8,128)(2,1)}, bf16[592,512]{1,0:T(8,128)(2,1)}, bf16[592,5...) custom-call(f32[592,1024]{1,0:T(8,128)} %get-tuple-element.335.refs_0_.refs, ...), custom_call_target="tpu_custom_call" | custom-call | flops 1 | bytes 1 | tf_op jit(solution)/shard_map/pallas_call | solution.py:186
  284.8 10.7 %shard_map.151 = (f32[592,1024]{1,0:T(8,128)}, bf16[592,1024]{1,0:T(8,128)(2,1)}, bf16[592,2048]{1,0:T(8,128)(2,1)}, bf16[592,2048]{1,0:T(8,128)(2,1)}) custom-call(f32[592,1024]{1,0:T(8,128)} %get-tuple-element.355.refs_0_.u_ref, bf16[592,1024]{1,0:T(8,128)(2,1)} %get-tuple-element.356.refs_1_, bf16[592,1024]{1,0:T(8,128)(2,1)} %collective-permute-done.49.refs_2_, ...), custom_call_target="tpu_custom_call" | custom-call | flops 1 | bytes 1 | tf_op jit(solution)/shard_map/pallas_call | solution.py:186
  300.9 7.9 %collective-permute-done.51.refs_3_ = bf16[112,2048]{1,0:T(8,128)(2,1)S(1)} collective-permute-done((bf16[112,2048]{1,0:T(8,128)(2,1)}, bf16[112,2048]{1,0:T(8,128)(2,1)S(1)}, u32[]{:S(2)}, u32[]{:S(2)}) %collective-permute-start.51) | collective-permute-done | bytes 458784 | tf_op jit(solution)/shard_map/ppermute | solution.py:23
  311.6 12.5 %shard_map.154 = (bf16[592,2048]{1,0:T(8,128)(2,1)}, f32[1,1024]{1,0:T(1,128)S(1)}, f32[1,2048]{1,0:T(1,128)S(1)}, bf16[256,2048]{1,0:T(8,128)(2,1)}, bf16[256,2...) custom-call(f32[592,1024]{1,0:T(8,128)} %get-tuple-element.369.refs_0_, ...), custom_call_target="tpu_custom_call" | custom-call | flops 1 | bytes 1 | tf_op jit(solution)/shard_map/pallas_call | solution.py:186
  327.8 6.8 %shard_map.156.refs_0_ = bf16[592,1024]{1,0:T(8,128)(2,1)} custom-call(bf16[592,2048]{1,0:T(8,128)(2,1)} %get-tuple-element.383.refs_0_.low_ref, bf16[112,2048]{1,0:T(8,128)(2,1)} %get-tuple-element.585.refs_5_.refs_1_, bf16[112,2048]{1,0:T(8,128)(2,1)S(1)} %copy-done.10, bf16[112,2048]{1,0:T(8,128)(2,1)} %get-tuple-element.359.refs_7_.refs_3_, ...), custom_call_target="tpu_custom_call" | custom-call | flops 1 | bytes 1 | tf_op jit(solution)/shard_map/pallas_call | solution.py:186
  334.6 6.5 shard_map.157
  360.2 21.5 %shard_map.159 = (f32[592,1024]{1,0:T(8,128)}, bf16[592,1024]{1,0:T(8,128)(2,1)}, bf16[592,512]{1,0:T(8,128)(2,1)}, bf16[592,512]{1,0:T(8,128)(2,1)}, bf16[592,5...) custom-call(f32[592,1024]{1,0:T(8,128)} %get-tuple-element.369.refs_, ...), custom_call_target="tpu_custom_call" | custom-call | flops 1 | bytes 1 | tf_op jit(solution)/shard_map/pallas_call | solution.py:186
  397.8 6.7 %shard_map.162.refs_1_ = bf16[592,1024]{1,0:T(8,128)(2,1)} custom-call(bf16[592,2048]{1,0:T(8,128)(2,1)} %get-tuple-element.370.refs_1_.refs_0_, bf16[112,2048]{1,0:T(8,128)(2,1)} %get-tuple-element.583.refs_3_.refs_1_, bf16[112,2048]{1,0:T(8,128)(2,1)} %get-tuple-element.372.refs_4_.refs_2_, bf16[112,2048]{1,0:T(8,128)(2,1)} %get-tuple-element.373.refs_5_.refs_3_, ...), custom_call_target="tpu_custom_call" | custom-call | flops 1 | bytes 1 | tf_op jit(solution)/shard_map/pallas_call | solution.py:186
  404.5 8.0 %shard_map.163 = (bf16[256,2048]{1,0:T(8,128)(2,1)S(1)}, bf16[256,2048]{1,0:T(8,128)(2,1)}, bf16[256,2048]{1,0:T(8,128)(2,1)}, bf16[256,2048]{1,0:T(8,128)(2,1)}) custom-call(bf16[592,1024]{1,0:T(8,128)(2,1)} %get-tuple-element.408.n_ref, bf16[592,1024]{1,0:T(8,128)(2,1)} %get-tuple-element.409.dz_ref, bf16[592,512]{1,0:T(8,128)(2,1)S(1)} %copy-done.127, ...), custom_call_target="tpu_custom_call" | custom-call | flops 1 | bytes 1 | tf_op jit(solution)/shard_map/pallas_call | solution.py:186
  432.8 12.1 %shard_map.165 = (bf16[592,2048]{1,0:T(8,128)(2,1)}, f32[1,1024]{1,0:T(1,128)S(1)}, f32[1,2048]{1,0:T(1,128)S(1)}, bf16[256,2048]{1,0:T(8,128)(2,1)}, bf16[256,2...) custom-call(f32[592,1024]{1,0:T(8,128)} %get-tuple-element.425.refs_0_, ...), custom_call_target="tpu_custom_call" | custom-call | flops 1 | bytes 1 | tf_op jit(solution)/shard_map/pallas_call | solution.py:186
  480.6 10.9 %collective-permute-done.70.refs_11_ = bf16[128,2048]{1,0:T(8,128)(2,1)} collective-permute-done((bf16[128,2048]{1,0:T(8,128)(2,1)}, bf16[128,2048]{1,0:T(8,128)(2,1)}, u32[]{:S(2)}, u32[]{:S(2)}) %collective-permute-start.70) | collective-permute-done | bytes 524320 | tf_op jit(solution)/shard_map/ppermute | solution.py:28
  510.0 21.7 %shard_map.171 = (f32[592,1024]{1,0:T(8,128)}, bf16[592,1024]{1,0:T(8,128)(2,1)}, bf16[592,512]{1,0:T(8,128)(2,1)}, bf16[592,512]{1,0:T(8,128)(2,1)}, bf16[592,5...) custom-call(f32[592,1024]{1,0:T(8,128)} %get-tuple-element.425.refs_, ...), custom_call_target="tpu_custom_call" | custom-call | flops 1 | bytes 1 | tf_op jit(solution)/shard_map/pallas_call | solution.py:186
  535.0 8.3 %shard_map.172 = (bf16[256,2048]{1,0:T(8,128)(2,1)}, bf16[256,2048]{1,0:T(8,128)(2,1)}, bf16[256,2048]{1,0:T(8,128)(2,1)}, bf16[256,2048]{1,0:T(8,128)(2,1)}) custom-call(bf16[592,1024]{1,0:T(8,128)(2,1)} %get-tuple-element.467.n_ref, bf16[592,1024]{1,0:T(8,128)(2,1)} %get-tuple-element.468.dz_ref, bf16[592,512]{1,0:T(8,128)(2,1)S(1)} %copy-done.130, ...), custom_call_target="tpu_custom_call" | custom-call | flops 1 | bytes 1 | tf_op jit(solution)/shard_map/pallas_call | solution.py:186
  597.8 10.2 %collective-permute-done.91 = bf16[16,2048]{1,0:T(8,128)(2,1)S(1)} collective-permute-done((bf16[16,2048]{1,0:T(8,128)(2,1)S(1)}, bf16[16,2048]{1,0:T(8,128)(2,1)S(1)}, u32[]{:S(2)}, u32[]{:S(2)}) %collective-permute-start.91) | collective-permute-done | bytes 65568 | tf_op jit(solution)/shard_map/ppermute | solution.py:28
  633.7 13.8 %reduce-scatter.15.cloned.1.call-done = bf16[272,512]{1,0:T(8,128)(2,1)} async-done(((bf16[272,2048]{1,0:T(8,128)(2,1)}), bf16[272,512]{1,0:T(8,128)(2,1)}) %reduce-scatter.15.cloned.1.call-update) | async-done | bytes 278544 | tf_op jit(solution)/shard_map/reduce_scatter | solution.py:122
  (933 shorter events, 360.6 us)
Async XLA Ops:
  7.2 102.7 %all-gather.6.cloned.1.call-start = ((), (), s32[]{:S(2)}) async-start(), calls=%async_computation.6 | async-start | bytes 2457600 | tf_op jit(solution)/shard_map/all_gather | solution.py:49
  51.4 49.2 %collective-permute-start.9 = (bf16[112,2048]{1,0:T(8,128)(2,1)S(1)}, bf16[112,2048]{1,0:T(8,128)(2,1)S(1)}, u32[]{:S(2)}, u32[]{:S(2)}) collective-permute-start(bf16[112,2048]{1,0:T(8,128)(2,1)S(1)} %get-tuple-element.594.refs_9_.refs_14_), channel_id=1, source_target_pairs={{0,8},{4,12},{8,0},{12,4},{1,9},{5,13},{9,1},{13,5},{2,10},{6,14},... | collective-permute-start | bytes 1376264 | tf_op jit(solution)/shard_map/ppermute | solution.py:28
  53.9 98.6 %all-gather.8.cloned.1.call-start = ((), (), s32[]{:S(2)}) async-start(), calls=%async_computation.7 | async-start | bytes 1802240 | tf_op jit(solution)/shard_map/all_gather | solution.py:49
  54.7 45.9 %collective-permute-start.7 = (bf16[112,2048]{1,0:T(8,128)(2,1)}, bf16[112,2048]{1,0:T(8,128)(2,1)S(1)}, u32[]{:S(2)}, u32[]{:S(2)}) collective-permute-start(bf16[112,2048]{1,0:T(8,128)(2,1)} %get-tuple-element.595.refs_5_.refs_10_), channel_id=1, source_target_pairs={{0,4},{4,0},{8,12},{12,8},{1,5},{5,1},{9,13},{13,9},{2,6},{6,2},{1... | collective-permute-start | bytes 1376264 | tf_op jit(solution)/shard_map/ppermute | solution.py:23
  63.0 37.6 %collective-permute-start.10 = (bf16[112,2048]{1,0:T(8,128)(2,1)S(1)}, bf16[112,2048]{1,0:T(8,128)(2,1)S(1)}, u32[]{:S(2)}, u32[]{:S(2)}) collective-permute-start(bf16[112,2048]{1,0:T(8,128)(2,1)S(1)} %collective-permute-done.6.refs_2_), channel_id=1, source_target_pairs={{0,8},{4,12},{8,0},{12,4},{1,9},{5,13},{9,1},{13,5},{2,10},{6,14},... | collective-permute-start | bytes 1376264 | tf_op jit(solution)/shard_map/ppermute | solution.py:28
  110.1 84.2 %all-gather.10.cloned.1.call-start = ((), (), s32[]{:S(2)}) async-start(), calls=%async_computation.8 | async-start | bytes 1802240 | tf_op jit(solution)/shard_map/all_gather | solution.py:49
  153.3 78.8 %all-gather.12.cloned.1.call-start = ((), (), s32[]{:S(2)}) async-start(), calls=%async_computation.9 | async-start | bytes 1802240 | tf_op jit(solution)/shard_map/all_gather | solution.py:49
  159.2 35.0 %collective-permute-start.30 = (bf16[112,2048]{1,0:T(8,128)(2,1)S(1)}, bf16[112,2048]{1,0:T(8,128)(2,1)}, u32[]{:S(2)}, u32[]{:S(2)}) collective-permute-start(bf16[112,2048]{1,0:T(8,128)(2,1)S(1)} %get-tuple-element.588.refs_5_.refs_7_), channel_id=1, source_target_pairs={{0,8},{4,12},{8,0},{12,4},{1,9},{5,13},{9,1},{13,5},{2,10},{6,14},... | collective-permute-start | bytes 1376264 | tf_op jit(solution)/shard_map/ppermute | solution.py:28
  159.6 34.6 %collective-permute-start.28 = (bf16[112,2048]{1,0:T(8,128)(2,1)}, bf16[112,2048]{1,0:T(8,128)(2,1)}, u32[]{:S(2)}, u32[]{:S(2)}) collective-permute-start(bf16[112,2048]{1,0:T(8,128)(2,1)} %get-tuple-element.589.refs_1_.refs_3_), channel_id=1, source_target_pairs={{0,4},{4,0},{8,12},{12,8},{1,5},{5,1},{9,13},{13,9},{2,6},{6,2},{1... | collective-permute-start | bytes 1376264 | tf_op jit(solution)/shard_map/ppermute | solution.py:23
  195.2 76.8 %all-gather.14.cloned.1.call-start = ((), (), s32[]{:S(2)}) async-start(), calls=%async_computation.10 | async-start | bytes 1802240 | tf_op jit(solution)/shard_map/all_gather | solution.py:49
  232.3 187.4 %reduce-scatter.7.cloned.1.call-start = ((), (), s32[]{:S(2)}) async-start(), calls=%async_computation.11 | async-start | bytes 1310720 | tf_op jit(solution)/shard_map/reduce_scatter | solution.py:122
  347.6 34.4 %collective-permute-start.60 = (bf16[256,2048]{1,0:T(8,128)(2,1)}, bf16[256,2048]{1,0:T(8,128)(2,1)}, u32[]{:S(2)}, u32[]{:S(2)}) collective-permute-start(bf16[256,2048]{1,0:T(8,128)(2,1)} %get-tuple-element.404), channel_id=1, source_target_pairs={{0,4},{4,0},{8,12},{12,8},{1,5},{5,1},{9,13},{13,9},{2,6},{6,2},{1... | collective-permute-start | bytes 3145736 | tf_op jit(solution)/shard_map/ppermute | solution.py:23
  386.6 64.9 %reduce-scatter.9.cloned.1.call-start = ((), (), s32[]{:S(2)}) async-start(), calls=%async_computation.12 | async-start | bytes 1310720 | tf_op jit(solution)/shard_map/reduce_scatter | solution.py:122
  423.2 121.6 %reduce-scatter.11.cloned.1.call-start = ((), (), s32[]{:S(2)}) async-start(), calls=%async_computation.13 | async-start | bytes 1310720 | tf_op jit(solution)/shard_map/reduce_scatter | solution.py:122
  456.5 35.0 %collective-permute-start.72 = (bf16[256,2048]{1,0:T(8,128)(2,1)}, bf16[256,2048]{1,0:T(8,128)(2,1)}, u32[]{:S(2)}, u32[]{:S(2)}) collective-permute-start(bf16[256,2048]{1,0:T(8,128)(2,1)} %get-tuple-element.453), channel_id=1, source_target_pairs={{0,4},{4,0},{8,12},{12,8},{1,5},{5,1},{9,13},{13,9},{2,6},{6,2},{1... | collective-permute-start | bytes 3145736 | tf_op jit(solution)/shard_map/ppermute | solution.py:23
  456.9 34.5 %collective-permute-start.73 = (bf16[256,2048]{1,0:T(8,128)(2,1)}, bf16[256,2048]{1,0:T(8,128)(2,1)}, u32[]{:S(2)}, u32[]{:S(2)}) collective-permute-start(bf16[256,2048]{1,0:T(8,128)(2,1)} %get-tuple-element.454), channel_id=1, source_target_pairs={{0,8},{4,12},{8,0},{12,4},{1,9},{5,13},{9,1},{13,5},{2,10},{6,14},... | collective-permute-start | bytes 3145736 | tf_op jit(solution)/shard_map/ppermute | solution.py:28
  495.3 93.5 %reduce-scatter.13.cloned.1.call-start = ((), (), s32[]{:S(2)}) async-start(), calls=%async_computation.14 | async-start | bytes 1310720 | tf_op jit(solution)/shard_map/reduce_scatter | solution.py:122
  500.0 44.7 %collective-permute-start.75 = (bf16[296,256]{1,0:T(8,128)(2,1)S(1)}, bf16[296,256]{1,0:T(8,128)(2,1)}, u32[]{:S(2)}, u32[]{:S(2)}) collective-permute-start(bf16[296,256]{1,0:T(8,128)(2,1)S(1)} %copy-done.171), channel_id=1, source_target_pairs={{0,3},{1,0},{2,1},{3,2},{4,7},{5,4},{6,5},{7,6},{8,11},{9,8},{10,9... | collective-permute-start | bytes 454664 | tf_op jit(solution)/shard_map/ppermute | solution.py:525
  504.4 40.3 %collective-permute-start.77 = (bf16[128,2048]{1,0:T(8,128)(2,1)}, bf16[128,2048]{1,0:T(8,128)(2,1)}, u32[]{:S(2)}, u32[]{:S(2)}) collective-permute-start(bf16[128,2048]{1,0:T(8,128)(2,1)} %get-tuple-element.556), channel_id=1, source_target_pairs={{0,4},{4,0},{8,12},{12,8},{1,5},{5,1},{9,13},{13,9},{2,6},{6,2},{1... | collective-permute-start | bytes 1572872 | tf_op jit(solution)/shard_map/ppermute | solution.py:23
  504.8 39.9 %collective-permute-start.78 = (bf16[256,2048]{1,0:T(8,128)(2,1)S(1)}, bf16[256,2048]{1,0:T(8,128)(2,1)}, u32[]{:S(2)}, u32[]{:S(2)}) collective-permute-start(bf16[256,2048]{1,0:T(8,128)(2,1)S(1)} %copy-done.113), channel_id=1, source_target_pairs={{0,4},{4,0},{8,12},{12,8},{1,5},{5,1},{9,13},{13,9},{2,6},{6,2},{1... | collective-permute-start | bytes 3145736 | tf_op jit(solution)/shard_map/ppermute | solution.py:23
  505.9 38.8 %collective-permute-start.79 = (bf16[256,2048]{1,0:T(8,128)(2,1)S(1)}, bf16[256,2048]{1,0:T(8,128)(2,1)}, u32[]{:S(2)}, u32[]{:S(2)}) collective-permute-start(bf16[256,2048]{1,0:T(8,128)(2,1)S(1)} %copy-done.115), channel_id=1, source_target_pairs={{0,8},{4,12},{8,0},{12,4},{1,9},{5,13},{9,1},{13,5},{2,10},{6,14},... | collective-permute-start | bytes 3145736 | tf_op jit(solution)/shard_map/ppermute | solution.py:28
  508.9 35.9 %collective-permute-start.76 = (bf16[128,2048]{1,0:T(8,128)(2,1)}, bf16[128,2048]{1,0:T(8,128)(2,1)S(1)}, u32[]{:S(2)}, u32[]{:S(2)}) collective-permute-start(bf16[128,2048]{1,0:T(8,128)(2,1)} %get-tuple-element.558), channel_id=1, source_target_pairs={{0,8},{4,12},{8,0},{12,4},{1,9},{5,13},{9,1},{13,5},{2,10},{6,14},... | collective-permute-start | bytes 1572872 | tf_op jit(solution)/shard_map/ppermute | solution.py:28
  549.2 73.8 %reduce-scatter.17.cloned.1.call-start = ((), (), s32[]{:S(2)}) async-start(), calls=%async_computation.16 | async-start | bytes 1310720 | tf_op jit(solution)/shard_map/reduce_scatter | solution.py:122
  568.6 78.9 %reduce-scatter.15.cloned.1.call-start = ((), (), s32[]{:S(2)}) async-start(), calls=%async_computation.15 | async-start | bytes 1392640 | tf_op jit(solution)/shard_map/reduce_scatter | solution.py:122
  (316 other events, 2859.8 us)
Sparse Core Ops, SparseCore 0:
  54.0 55.8 all-gather.5
  111.4 32.7 all-gather.7
  153.5 40.1 all-gather.9
  195.3 36.8 all-gather.11
  233.6 33.8 all-gather.13
  386.7 28.1 reduce-scatter.6
  423.4 28.1 reduce-scatter.8
  495.4 28.3 reduce-scatter.10
  549.4 26.5 reduce-scatter.12
  578.7 34.2 reduce-scatter.16
  618.1 29.3 reduce-scatter.14

commit v11 on v9

--- a/solution.py
+++ b/solution.py
@@ -770,98 +770,111 @@
         return little
 
     grads, got, moved, settled = [None] * number, [None] * number, [None] * number, [None] * number
-    made = [0, 1, 3, 4, 5, 6]
     grad = cotangent
     last_down = weights_of(number - 1)
     params[1]["down"] = last_down
     last_bias = params[1]["small"][0][7:8]
-    for r in range(8):
-        layer, stage = 1 - r // 4, r % 4
-        one, total = params[layer], sums[layer]
-        rows = one["small"][0]
+    rounds = [[(1, 0)], [(1, 1)], [(1, 2)], [(1, 3), (0, 0)], [(0, 1)], [(0, 2)], [(0, 3)]]
+    first_at = [1, 2, 3, 4, 5, 6]
+    late = [2, 5]
+    for r, stages in enumerate(rounds):
         tied, slots = [], []
+
+        def await_all(store, at, arrays):
+            slots.append((store, at, len(arrays)))
+            tied.extend(arrays)
+
         for c in range(number):
-            if r == made[c] + 1:
+            if r == first_at[c] and c not in late:
                 got[c] = scatter_one(*grads[c][:2])
-                slots.append((got, c, len(got[c])))
-                tied += got[c]
-            elif r == made[c] + 2:
+                await_all(got, c, got[c])
+            elif r == first_at[c] + 1:
                 stay, come = scatter_two(*grads[c][2:], got[c])
                 moved[c] = [*stay, *come]
-                if r < 7:
-                    slots.append((moved, c, len(moved[c])))
-                    tied += moved[c]
-            elif r == made[c] + 3:
-                settled[c] = scatter_column(moved[c][:2], moved[c][2:])
-                slots.append((settled, c, 0))
-                tied.append(settled[c])
-        new = None
-        if stage == 0:
-            low, total["out"], total["up_bias"], new = down_backward(
-                grad, one["hidden"], one["slope"], one["down"]
+                if r < len(rounds) - 1:
+                    await_all(moved, c, moved[c])
+            elif r == first_at[c] + 2:
+                settled[c] = [scatter_column(moved[c][:2], moved[c][2:])]
+                await_all(settled, c, settled[c])
+        for layer, stage in stages:
+            one, total = params[layer], sums[layer]
+            rows = one["small"][0]
+            if stage == 0:
+                low, total["out"], total["up_bias"], new = down_backward(
+                    grad, one["hidden"], one["slope"], one["down"]
+                )
+                grads[3 * (1 - layer)] = new
+                keep = [low]
+            elif stage == 1:
+                part = contract_wide(low, one["up"])
+                grads[3 * (1 - layer) + 1] = up_grad(one["n2"], low)
+                keep = [part]
+            elif stage == 2:
+                done = attention_backward(
+                    grad, part, swap(part), one["mid"], rows, one["saved"], one["qkvo"]
+                )
+                dmid, dz, dq, dk, dv, part, total["mid"], total["q"], total["v"] = done
+                keep = [part, dz]
+            else:
+                c = 3 * (1 - layer) + 2
+                grads[c] = attention_grad(one["n1"], dz, dq, dk, dv, one["saved"][4])
+                got[c] = scatter_one(*grads[c][:2])
+                await_all(got, c, got[c])
+                grad, total["one"] = value_backward(
+                    dmid, part, swap(part), one["u"], rows, layer == 1
+                )
+                keep = []
+        if r == 4:
+            last_part = contract_wide(params[1]["hidden"], last_down)
+            keep.append(last_part)
+        elif r == 3:
+            keep.append(params[1]["hidden"])
+        elif r == 5:
+            out_blocks = shifts(
+                image_rows(live, [params[1]["mid"], last_part, swap(last_part)], last_bias)
             )
-            carry = [low]
-        elif stage == 1:
-            part = contract_wide(low, one["up"])
-            new = up_grad(one["n2"], low)
-            carry = [part]
-        elif stage == 2:
-            done = attention_backward(
-                grad, part, swap(part), one["mid"], rows, one["saved"], one["qkvo"]
-            )
-            dmid, dz, dq, dk, dv, part, total["mid"], total["q"], total["v"] = done
-            if layer == 0:
-                new = attention_grad(one["n1"], dz, dq, dk, dv, one["saved"][4])
-            carry = [part]
-        else:
-            if layer == 1:
-                new = attention_grad(one["n1"], dz, dq, dk, dv, one["saved"][4])
-            grad, total["one"] = value_backward(dmid, part, swap(part), one["u"], rows, layer == 1)
-            carry = [grad]
-            if r == 7:
-                one_scale = jnp.ones((), jnp.float32)
-                no_bias = jnp.zeros((1, grad.shape[1]), jnp.float32)
-                carry = [small_grads()]
-                grad_blocks = shifts(image_rows(one_scale, [grad], no_bias))
-        if new is not None:
-            c = made.index(r)
-            grads[c] = new
-            fresh = [g for g in new if g is not None]
-        else:
-            fresh = []
-        if r == 3:
-            last_part = contract_wide(params[1]["hidden"], last_down)
-            carry.append(last_part)
+            keep += out_blocks
+        elif r == 6:
+            one_scale = jnp.ones((), jnp.float32)
+            no_bias = jnp.zeros((1, grad.shape[1]), jnp.float32)
+            little = small_grads()
+            keep.append(little)
+            grad_blocks = shifts(image_rows(one_scale, [grad], no_bias))
+        waiting = []
+        for c in range(number):
+            if grads[c] is None or r > first_at[c]:
+                continue
+            fresh = [g for g in grads[c] if g is not None]
+            if r == first_at[c]:
+                if c not in late:
+                    continue
+                fresh = [g for g in grads[c][2:] if g is not None]
+            waiting.append((c, len(fresh)))
+            keep += fresh
+        done = tie(keep + tied, [])
+        if r == 0:
+            low, done = done[0], done[1:]
+        elif r == 3:
+            low, params[1]["hidden"], done = done[0], done[1], done[2:]
+        elif r == 1:
+            part, done = done[0], done[1:]
+        elif r == 2 or r == 5:
+            part, dz, done = done[0], done[1], done[2:]
         elif r == 4:
-            out_blocks = image_rows(
-                live, [params[1]["mid"], last_part, swap(last_part)], last_bias
-            )
-        if 4 <= r < 4 + n_tensor - 1:
-            out_blocks[r - 3] = shift(out_blocks[r - 3], r - 3)
-            carry += out_blocks
-        if r < 8:
-            done = tie(carry + fresh + tied, [])
-            if stage == 0:
-                low = done[0]
-            elif stage == 1:
-                part = done[0]
-            elif stage == 2:
-                part = done[0]
-            elif r < 7:
-                grad = done[0]
+            part, last_part, done = done[0], done[1], done[2:]
+        if r == 5:
+            out_blocks, done = done[:n_tensor], done[n_tensor:]
+        elif r == 6:
+            little, done = done[0], done[1:]
+        for c, count in waiting:
+            if r == first_at[c]:
+                grads[c][2 : 2 + count] = done[:count]
             else:
-                little = done[0]
-            if r == 3:
-                last_part = done[1]
-            elif 4 <= r < 4 + n_tensor - 1:
-                out_blocks = done[1 : 1 + n_tensor]
-            done = done[len(carry) :]
-            if fresh:
-                grads[c] = fill(done[: len(fresh)])
-                done = done[len(fresh) :]
-            for store, at, count in slots:
-                store[at] = done[:count] if count else done[0]
-                done = done[max(count, 1) :]
+                grads[c] = fill(done[:count])
+            done = done[count:]
+        for store, at, count in slots:
+            store[at] = done[:count]
+            done = done[count:]
 
     room = jnp.zeros((n_dp, n_tensor, extra * wide - small_size), little.dtype)
     little = jnp.concatenate([little, room], -1).reshape(n_dp, n_tensor, extra, wide)
@@ -873,6 +886,7 @@
         little = add(little[0], swap_y(little[1])).astype(jnp.bfloat16)
 
     last = number - 1
+    settled = [value[0] if value else None for value in settled]
     settled[last - 1] = scatter_column(moved[last - 1][:2], moved[last - 1][2:])
     stay, come = scatter_two(*grads[last][2:], got[last])
     done = tie([*grad_blocks, *stay, *come], [])

time: 658 us -> 681 us (1.035)
  waiting for transfers between devices: 192 us -> 218 us
    ppermute x32, waiting for transfers between devices: 61.9 us -> 76.1 us  [swap_x(): return lax.ppermute(value, 'dp', [(i, i ^ 1) for i in range(n)])]
    ppermute x32, waiting for transfers between devices: 43 us -> 55.1 us  [swap_y(): return lax.ppermute(value, 'dp', [(i, i ^ 2) for i in range(n)])]
    unnamed x318 -> x292, local copies, waits for them, and re-layouts: 44.1 us -> 41 us
  transfers between devices with their start and end apart: 106 -> 106, of which waited for: 35 -> 33; matrix products, arithmetic and copies ran while one was open for 15% -> 14% of each run, Pallas kernels for 28% -> 27%
where the time goes in v11:
time: 681 us; the launch traced here: 674 us
  waiting for transfers between devices  218 us (32%)
  Pallas kernels  193 us (28%)
  starting transfers between devices  94.1 us (14%)
  local copies, waits for them, and re-layouts  75.4 us (11%)
  other arithmetic  75.1 us (11%)
  between operations  17.4 us (3%)
    pallas_call x18, Pallas kernels, run(): pl.pallas_call(kernel, out_shape=list(outs), in_specs=[block] * len(ins),...  188 us
    ppermute x32, waiting for transfers between devices, swap_x(): return lax.ppermute(value, 'dp', [(i, i ^ 1) for i in range(n)])  76.1 us
    ppermute x32, waiting for transfers between devices, swap_y(): return lax.ppermute(value, 'dp', [(i, i ^ 2) for i in range(n)])  55.1 us
    ppermute x12, waiting for transfers between devices, shift(): return lax.ppermute(block, 'tensor', [(i, (i + d) % n) for i in range(n)])  43.4 us
    unnamed x292, local copies, waits for them, and re-layouts  41 us
    convert_element_type x12, other arithmetic, scatter_two(): send.append(add(keep[half:], new[half:]).astype(jnp.bfloat16))  26.4 us
    ppermute x17, starting transfers between devices, swap(): return lax.ppermute(value, 'section', [(0, 1), (1, 0)])  25.9 us
    ppermute x32, starting transfers between devices, swap_y(): return lax.ppermute(value, 'dp', [(i, i ^ 2) for i in range(n)])  25.2 us
  transfers between devices with their start and end apart: 106, of which 33 were waited for; matrix products, arithmetic and copies ran while one was open for 14% of the time, Pallas kernels for 27%

profile of v11, /device:TPU:1, one launch (start us, length us, event | category | flops | bytes accessed | tf_op | source)
XLA Modules:
  0.0 673.7 jit_solution(13526981688737486551)
XLA Ops:
  22.5 22.7 %all-gather.7.cloned.1.call-done.refs_0_ = bf16[272,2048]{1,0:T(8,128)(2,1)} async-done(((bf16[272,512]{1,0:T(8,128)(2,1)}), bf16[272,2048]{1,0:T(8,128)(2,1)}) %all-gather.7.cloned.1.call-update) | async-done | bytes 1114128 | tf_op jit(solution)/shard_map/all_gather | solution.py:49
  103.8 15.5 %shard_map.138 = (f32[592,1024]{1,0:T(8,128)}, bf16[592,1024]{1,0:T(8,128)(2,1)}, bf16[592,512]{1,0:T(8,128)(2,1)}, bf16[592,512]{1,0:T(8,128)(2,1)}, bf16[592,5...) custom-call(f32[592,1024]{1,0:T(8,128)} %maximum_convert_fusion.refs_0_, ...), custom_call_target="tpu_custom_call" | custom-call | flops 1 | bytes 1 | tf_op jit(solution)/shard_map/pallas_call | solution.py:173
  142.3 10.6 %shard_map.141 = (f32[592,1024]{1,0:T(8,128)}, bf16[592,1024]{1,0:T(8,128)(2,1)}, bf16[592,2048]{1,0:T(8,128)(2,1)}, bf16[592,2048]{1,0:T(8,128)(2,1)}) custom-call(f32[592,1024]{1,0:T(8,128)} %get-tuple-element.290.refs_0_.u_ref, bf16[592,1024]{1,0:T(8,128)(2,1)} %get-tuple-element.291.refs_1_, bf16[592,1024]{1,0:T(8,128)(2,1)} %collective-permute-done.24.refs_2_, ...), custom_call_target="tpu_custom_call" | custom-call | flops 1 | bytes 1 | tf_op jit(solution)/shard_map/pallas_call | solution.py:173
  156.3 14.2 %collective-permute-done.29.refs_10_ = bf16[296,256]{1,0:T(8,128)(2,1)S(1)} collective-permute-done((bf16[296,256]{1,0:T(8,128)(2,1)S(1)}, bf16[296,256]{1,0:T(8,128)(2,1)S(1)}, u32[]{:S(2)}, u32[]{:S(2)}) %collective-permute-start.29) | collective-permute-done | bytes 151584 | tf_op jit(solution)/shard_map/ppermute | solution.py:517
  197.9 8.7 %collective-permute-done.36.refs_11_ = bf16[296,256]{1,0:T(8,128)(2,1)S(1)} collective-permute-done((bf16[296,256]{1,0:T(8,128)(2,1)S(1)}, bf16[296,256]{1,0:T(8,128)(2,1)S(1)}, u32[]{:S(2)}, u32[]{:S(2)}) %collective-permute-start.36) | collective-permute-done | bytes 151584 | tf_op jit(solution)/shard_map/ppermute | solution.py:517
  206.6 8.5 %collective-permute-done.33.refs_4_ = bf16[128,2048]{1,0:T(8,128)(2,1)S(1)} collective-permute-done((bf16[128,2048]{1,0:T(8,128)(2,1)}, bf16[128,2048]{1,0:T(8,128)(2,1)S(1)}, u32[]{:S(2)}, u32[]{:S(2)}) %collective-permute-start.33) | collective-permute-done | bytes 524320 | tf_op jit(solution)/shard_map/ppermute | solution.py:23
  223.9 16.9 %shard_map.147 = (f32[592,1024]{1,0:T(8,128)}, bf16[592,1024]{1,0:T(8,128)(2,1)}, bf16[592,512]{1,0:T(8,128)(2,1)}, bf16[592,512]{1,0:T(8,128)(2,1)}, bf16[592,5...) custom-call(f32[592,1024]{1,0:T(8,128)} %get-tuple-element.325.refs_0_.refs, ...), custom_call_target="tpu_custom_call" | custom-call | flops 1 | bytes 1 | tf_op jit(solution)/shard_map/pallas_call | solution.py:173
  246.8 11.2 %collective-permute-done.41.refs_4_ = bf16[128,2048]{1,0:T(8,128)(2,1)} collective-permute-done((bf16[128,2048]{1,0:T(8,128)(2,1)}, bf16[128,2048]{1,0:T(8,128)(2,1)}, u32[]{:S(2)}, u32[]{:S(2)}) %collective-permute-start.41) | collective-permute-done | bytes 524320 | tf_op jit(solution)/shard_map/ppermute | solution.py:23
  264.4 11.0 %shard_map.151 = (f32[592,1024]{1,0:T(8,128)}, bf16[592,1024]{1,0:T(8,128)(2,1)}, bf16[592,2048]{1,0:T(8,128)(2,1)}, bf16[592,2048]{1,0:T(8,128)(2,1)}) custom-call(f32[592,1024]{1,0:T(8,128)} %get-tuple-element.345.refs_0_.u_ref, bf16[592,1024]{1,0:T(8,128)(2,1)} %get-tuple-element.346.refs_1_, bf16[592,1024]{1,0:T(8,128)(2,1)} %copy-done.115, ...), custom_call_target="tpu_custom_call" | custom-call | flops 1 | bytes 1 | tf_op jit(solution)/shard_map/pallas_call | solution.py:173
  286.2 11.2 %collective-permute-done.48.refs_3_ = bf16[128,2048]{1,0:T(8,128)(2,1)} collective-permute-done((bf16[128,2048]{1,0:T(8,128)(2,1)}, bf16[128,2048]{1,0:T(8,128)(2,1)}, u32[]{:S(2)}, u32[]{:S(2)}) %collective-permute-start.48) | collective-permute-done | bytes 524320 | tf_op jit(solution)/shard_map/ppermute | solution.py:23
  297.4 11.8 %shard_map.154 = (bf16[592,2048]{1,0:T(8,128)(2,1)}, f32[1,1024]{1,0:T(1,128)S(1)}, f32[1,2048]{1,0:T(1,128)S(1)}, bf16[256,2048]{1,0:T(8,128)(2,1)}, bf16[256,2...) custom-call(f32[592,1024]{1,0:T(8,128)} %get-tuple-element.359.refs_0_, ...), custom_call_target="tpu_custom_call" | custom-call | flops 1 | bytes 1 | tf_op jit(solution)/shard_map/pallas_call | solution.py:173
  317.2 6.9 %shard_map.157 = (bf16[256,2048]{1,0:T(8,128)(2,1)S(1)}, bf16[256,2048]{1,0:T(8,128)(2,1)S(1)}, bf16[256,2048]{1,0:T(8,128)(2,1)S(1)}, bf16[256,2048]{1,0:T(8,128)(2,1)}) custom-call(bf16[592,1024]{1,0:T(8,128)(2,1)} %get-tuple-element.374.n_ref, bf16[592,2048]{1,0:T(8,128)(2,1)} %get-tuple-element.373.refs_0_.low_ref), custom_call_target="tpu_custom_call" | custom-call | flops 1 | bytes 1 | tf_op jit(solution)/shard_map/pallas_call | solution.py:173
  345.1 21.9 %shard_map.159 = (f32[592,1024]{1,0:T(8,128)}, bf16[592,1024]{1,0:T(8,128)(2,1)}, bf16[592,512]{1,0:T(8,128)(2,1)}, bf16[592,512]{1,0:T(8,128)(2,1)}, bf16[592,5...) custom-call(f32[592,1024]{1,0:T(8,128)} %get-tuple-element.359.refs_, ...), custom_call_target="tpu_custom_call" | custom-call | flops 1 | bytes 1 | tf_op jit(solution)/shard_map/pallas_call | solution.py:173
  381.8 8.2 %shard_map.163 = (bf16[256,2048]{1,0:T(8,128)(2,1)}, bf16[256,2048]{1,0:T(8,128)(2,1)}, bf16[256,2048]{1,0:T(8,128)(2,1)}, bf16[256,2048]{1,0:T(8,128)(2,1)}) custom-call(bf16[592,1024]{1,0:T(8,128)(2,1)} %get-tuple-element.401.n_ref, bf16[592,1024]{1,0:T(8,128)(2,1)} %get-tuple-element.402.dz_ref, bf16[592,512]{1,0:T(8,128)(2,1)S(1)} %copy-done.68, ...), custom_call_target="tpu_custom_call" | custom-call | flops 1 | bytes 1 | tf_op jit(solution)/shard_map/pallas_call | solution.py:173
  401.2 12.2 %shard_map.162 = (bf16[592,2048]{1,0:T(8,128)(2,1)}, f32[1,1024]{1,0:T(1,128)S(1)}, f32[1,2048]{1,0:T(1,128)S(1)}, bf16[256,2048]{1,0:T(8,128)(2,1)}, bf16[256,2...) custom-call(f32[592,1024]{1,0:T(8,128)} %get-tuple-element.398.refs_0_, ...), custom_call_target="tpu_custom_call" | custom-call | flops 1 | bytes 1 | tf_op jit(solution)/shard_map/pallas_call | solution.py:173
  413.5 12.4 %collective-permute-done.60.refs_11_ = bf16[128,2048]{1,0:T(8,128)(2,1)} collective-permute-done((bf16[128,2048]{1,0:T(8,128)(2,1)}, bf16[128,2048]{1,0:T(8,128)(2,1)}, u32[]{:S(2)}, u32[]{:S(2)}) %collective-permute-start.60) | collective-permute-done | bytes 524320 | tf_op jit(solution)/shard_map/ppermute | solution.py:28
  452.3 6.7 shard_map.166.refs_1_
  458.9 9.3 %collective-permute-done.64.refs_9_ = bf16[128,2048]{1,0:T(8,128)(2,1)} collective-permute-done((bf16[128,2048]{1,0:T(8,128)(2,1)}, bf16[128,2048]{1,0:T(8,128)(2,1)}, u32[]{:S(2)}, u32[]{:S(2)}) %collective-permute-start.64) | collective-permute-done | bytes 524320 | tf_op jit(solution)/shard_map/ppermute | solution.py:28
  488.1 21.0 %shard_map.169 = (f32[592,1024]{1,0:T(8,128)}, bf16[592,1024]{1,0:T(8,128)(2,1)}, bf16[592,512]{1,0:T(8,128)(2,1)}, bf16[592,512]{1,0:T(8,128)(2,1)}, bf16[592,5...) custom-call(f32[592,1024]{1,0:T(8,128)} %get-tuple-element.398.refs_, ...), custom_call_target="tpu_custom_call" | custom-call | flops 1 | bytes 1 | tf_op jit(solution)/shard_map/pallas_call | solution.py:173
  527.3 8.2 %shard_map.174 = (bf16[256,2048]{1,0:T(8,128)(2,1)}, bf16[256,2048]{1,0:T(8,128)(2,1)}, bf16[256,2048]{1,0:T(8,128)(2,1)}, bf16[256,2048]{1,0:T(8,128)(2,1)}) custom-call(bf16[592,1024]{1,0:T(8,128)(2,1)} %get-tuple-element.473.n_ref, bf16[592,1024]{1,0:T(8,128)(2,1)} %get-tuple-element.474.dz_ref, bf16[592,512]{1,0:T(8,128)(2,1)S(1)} %copy-done.71, ...), custom_call_target="tpu_custom_call" | custom-call | flops 1 | bytes 1 | tf_op jit(solution)/shard_map/pallas_call | solution.py:173
  545.3 24.4 %collective-permute-done.90 = bf16[128,2048]{1,0:T(8,128)(2,1)S(1)} collective-permute-done((bf16[128,2048]{1,0:T(8,128)(2,1)S(1)}, bf16[128,2048]{1,0:T(8,128)(2,1)S(1)}, u32[]{:S(2)}, u32[]{:S(2)}) %collective-permute-start.90) | collective-permute-done | bytes 524320 | tf_op jit(solution)/shard_map/ppermute | solution.py:28
  596.4 13.1 %collective-permute-done.87 = bf16[2,16,2048]{2,1,0:T(8,128)(2,1)S(1)} collective-permute-done((bf16[2,16,2048]{2,1,0:T(8,128)(2,1)S(1)}, bf16[2,16,2048]{2,1,0:T(8,128)(2,1)S(1)}, u32[]{:S(2)}, u32[]{:S(2)}) %collective-permute-start.87) | collective-permute-done | bytes 131104 | tf_op jit(solution)/shard_map/ppermute | solution.py:23
  617.8 7.5 %collective-permute-done.79.refs_2_ = bf16[296,256]{1,0:T(8,128)(2,1)S(1)} collective-permute-done((bf16[296,256]{1,0:T(8,128)(2,1)S(1)}, bf16[296,256]{1,0:T(8,128)(2,1)S(1)}, u32[]{:S(2)}, u32[]{:S(2)}) %collective-permute-start.79) | collective-permute-done | bytes 151584 | tf_op jit(solution)/shard_map/ppermute | solution.py:517
  642.0 16.4 %reduce-scatter.15.cloned.1.call-done = bf16[272,512]{1,0:T(8,128)(2,1)} async-done(((bf16[272,2048]{1,0:T(8,128)(2,1)}), bf16[272,512]{1,0:T(8,128)(2,1)}) %reduce-scatter.15.cloned.1.call-update) | async-done | bytes 278544 | tf_op jit(solution)/shard_map/reduce_scatter | solution.py:105
  (717 shorter events, 345.9 us)
Async XLA Ops:
  7.2 38.0 %all-gather.7.cloned.1.call-start = ((), (), s32[]{:S(2)}) async-start(), calls=%async_computation.6 | async-start | bytes 1392640 | tf_op jit(solution)/shard_map/all_gather | solution.py:49
  14.2 72.7 %all-gather.9.cloned.1.call-start = ((), (), s32[]{:S(2)}) async-start(), calls=%async_computation.7 | async-start | bytes 1310720 | tf_op jit(solution)/shard_map/all_gather | solution.py:49
  51.3 35.5 %collective-permute-start.4 = (bf16[128,2048]{1,0:T(8,128)(2,1)S(1)}, bf16[128,2048]{1,0:T(8,128)(2,1)S(1)}, u32[]{:S(2)}, u32[]{:S(2)}) collective-permute-start(bf16[128,2048]{1,0:T(8,128)(2,1)S(1)} %get-tuple-element.562.refs_5_.refs_10_), channel_id=1, source_target_pairs={{0,4},{4,0},{8,12},{12,8},{1,5},{5,1},{9,13},{13,9},{2,6},{6,2},{1... | collective-permute-start | bytes 1572872 | tf_op jit(solution)/shard_map/ppermute | solution.py:23
  52.5 81.6 %all-gather.11.cloned.1.call-start = ((), (), s32[]{:S(2)}) async-start(), calls=%async_computation.8 | async-start | bytes 1310720 | tf_op jit(solution)/shard_map/all_gather | solution.py:49
  96.1 74.5 %all-gather.13.cloned.1.call-start = ((), (), s32[]{:S(2)}) async-start(), calls=%async_computation.9 | async-start | bytes 1310720 | tf_op jit(solution)/shard_map/all_gather | solution.py:49
  136.7 78.4 %all-gather.15.cloned.1.call-start = ((), (), s32[]{:S(2)}) async-start(), calls=%async_computation.10 | async-start | bytes 1310720 | tf_op jit(solution)/shard_map/all_gather | solution.py:49
  177.3 69.5 %all-gather.17.cloned.1.call-start = ((), (), s32[]{:S(2)}) async-start(), calls=%async_computation.11 | async-start | bytes 1310720 | tf_op jit(solution)/shard_map/all_gather | solution.py:49
  218.1 207.8 %reduce-scatter.7.cloned.1.call-start = ((), (), s32[]{:S(2)}) async-start(), calls=%async_computation.12 | async-start | bytes 1310720 | tf_op jit(solution)/shard_map/reduce_scatter | solution.py:105
  336.0 36.6 %collective-permute-start.57 = (bf16[256,2048]{1,0:T(8,128)(2,1)}, bf16[256,2048]{1,0:T(8,128)(2,1)}, u32[]{:S(2)}, u32[]{:S(2)}) collective-permute-start(bf16[256,2048]{1,0:T(8,128)(2,1)} %get-tuple-element.395), channel_id=1, source_target_pairs={{0,4},{4,0},{8,12},{12,8},{1,5},{5,1},{9,13},{13,9},{2,6},{6,2},{1... | collective-permute-start | bytes 3145736 | tf_op jit(solution)/shard_map/ppermute | solution.py:23
  336.5 36.0 %collective-permute-start.58 = (bf16[256,2048]{1,0:T(8,128)(2,1)}, bf16[256,2048]{1,0:T(8,128)(2,1)}, u32[]{:S(2)}, u32[]{:S(2)}) collective-permute-start(bf16[256,2048]{1,0:T(8,128)(2,1)} %get-tuple-element.396), channel_id=1, source_target_pairs={{0,8},{4,12},{8,0},{12,4},{1,9},{5,13},{9,1},{13,5},{2,10},{6,14},... | collective-permute-start | bytes 3145736 | tf_op jit(solution)/shard_map/ppermute | solution.py:28
  376.3 91.9 %reduce-scatter.9.cloned.1.call-start = ((), (), s32[]{:S(2)}) async-start(), calls=%async_computation.13 | async-start | bytes 1310720 | tf_op jit(solution)/shard_map/reduce_scatter | solution.py:105
  390.0 35.9 %collective-permute-start.62 = (bf16[256,2048]{1,0:T(8,128)(2,1)}, bf16[256,2048]{1,0:T(8,128)(2,1)}, u32[]{:S(2)}, u32[]{:S(2)}) collective-permute-start(bf16[256,2048]{1,0:T(8,128)(2,1)} %get-tuple-element.420), channel_id=1, source_target_pairs={{0,4},{4,0},{8,12},{12,8},{1,5},{5,1},{9,13},{13,9},{2,6},{6,2},{1... | collective-permute-start | bytes 3145736 | tf_op jit(solution)/shard_map/ppermute | solution.py:23
  390.3 35.5 %collective-permute-start.63 = (bf16[256,2048]{1,0:T(8,128)(2,1)}, bf16[256,2048]{1,0:T(8,128)(2,1)}, u32[]{:S(2)}, u32[]{:S(2)}) collective-permute-start(bf16[256,2048]{1,0:T(8,128)(2,1)} %get-tuple-element.421), channel_id=1, source_target_pairs={{0,8},{4,12},{8,0},{12,4},{1,9},{5,13},{9,1},{13,5},{2,10},{6,14},... | collective-permute-start | bytes 3145736 | tf_op jit(solution)/shard_map/ppermute | solution.py:28
  429.7 91.5 %reduce-scatter.11.cloned.1.call-start = ((), (), s32[]{:S(2)}) async-start(), calls=%async_computation.14 | async-start | bytes 1310720 | tf_op jit(solution)/shard_map/reduce_scatter | solution.py:105
  433.9 34.3 %collective-permute-start.66 = (bf16[256,2048]{1,0:T(8,128)(2,1)}, bf16[256,2048]{1,0:T(8,128)(2,1)S(1)}, u32[]{:S(2)}, u32[]{:S(2)}) collective-permute-start(bf16[256,2048]{1,0:T(8,128)(2,1)} %get-tuple-element.437), channel_id=1, source_target_pairs={{0,4},{4,0},{8,12},{12,8},{1,5},{5,1},{9,13},{13,9},{2,6},{6,2},{1... | collective-permute-start | bytes 3145736 | tf_op jit(solution)/shard_map/ppermute | solution.py:23
  434.2 34.0 %collective-permute-start.67 = (bf16[256,2048]{1,0:T(8,128)(2,1)}, bf16[256,2048]{1,0:T(8,128)(2,1)}, u32[]{:S(2)}, u32[]{:S(2)}) collective-permute-start(bf16[256,2048]{1,0:T(8,128)(2,1)} %get-tuple-element.438), channel_id=1, source_target_pairs={{0,8},{4,12},{8,0},{12,4},{1,9},{5,13},{9,1},{13,5},{2,10},{6,14},... | collective-permute-start | bytes 3145736 | tf_op jit(solution)/shard_map/ppermute | solution.py:28
  472.9 116.0 %reduce-scatter.13.cloned.1.call-start = ((), (), s32[]{:S(2)}) async-start(), calls=%async_computation.15 | async-start | bytes 1310720 | tf_op jit(solution)/shard_map/reduce_scatter | solution.py:105
  480.9 38.4 %collective-permute-start.75 = (bf16[256,2048]{1,0:T(8,128)(2,1)}, bf16[256,2048]{1,0:T(8,128)(2,1)}, u32[]{:S(2)}, u32[]{:S(2)}) collective-permute-start(bf16[256,2048]{1,0:T(8,128)(2,1)} %get-tuple-element.457), channel_id=1, source_target_pairs={{0,4},{4,0},{8,12},{12,8},{1,5},{5,1},{9,13},{13,9},{2,6},{6,2},{1... | collective-permute-start | bytes 3145736 | tf_op jit(solution)/shard_map/ppermute | solution.py:23
  481.1 38.1 %collective-permute-start.76 = (bf16[256,2048]{1,0:T(8,128)(2,1)}, bf16[256,2048]{1,0:T(8,128)(2,1)}, u32[]{:S(2)}, u32[]{:S(2)}) collective-permute-start(bf16[256,2048]{1,0:T(8,128)(2,1)} %get-tuple-element.458), channel_id=1, source_target_pairs={{0,8},{4,12},{8,0},{12,4},{1,9},{5,13},{9,1},{13,5},{2,10},{6,14},... | collective-permute-start | bytes 3145736 | tf_op jit(solution)/shard_map/ppermute | solution.py:28
  525.6 106.8 %reduce-scatter.17.cloned.1.call-start = ((), (), s32[]{:S(2)}) async-start(), calls=%async_computation.17 | async-start | bytes 1310720 | tf_op jit(solution)/shard_map/reduce_scatter | solution.py:105
  535.5 53.4 %collective-permute-start.82 = (bf16[256,2048]{1,0:T(8,128)(2,1)}, bf16[256,2048]{1,0:T(8,128)(2,1)S(1)}, u32[]{:S(2)}, u32[]{:S(2)}) collective-permute-start(bf16[256,2048]{1,0:T(8,128)(2,1)} %get-tuple-element.484), channel_id=1, source_target_pairs={{0,4},{4,0},{8,12},{12,8},{1,5},{5,1},{9,13},{13,9},{2,6},{6,2},{1... | collective-permute-start | bytes 3145736 | tf_op jit(solution)/shard_map/ppermute | solution.py:23
  536.6 52.3 %collective-permute-start.83 = (bf16[256,2048]{1,0:T(8,128)(2,1)}, bf16[256,2048]{1,0:T(8,128)(2,1)}, u32[]{:S(2)}, u32[]{:S(2)}) collective-permute-start(bf16[256,2048]{1,0:T(8,128)(2,1)} %get-tuple-element.485), channel_id=1, source_target_pairs={{0,8},{4,12},{8,0},{12,4},{1,9},{5,13},{9,1},{13,5},{2,10},{6,14},... | collective-permute-start | bytes 3145736 | tf_op jit(solution)/shard_map/ppermute | solution.py:28
  537.0 36.1 %collective-permute-start.77 = (bf16[592,1024]{1,0:T(8,128)(2,1)S(1)}, bf16[592,1024]{1,0:T(8,128)(2,1)S(1)}, u32[]{:S(2)}, u32[]{:S(2)}) collective-permute-start(bf16[592,1024]{1,0:T(8,128)(2,1)S(1)} %copy-done.17), channel_id=1, source_target_pairs={{0,16},{16,0},{1,17},{17,1},{2,18},{18,2},{3,19},{19,3},{4,20},{20... | collective-permute-start | bytes 3637256 | tf_op jit(solution)/shard_map/ppermute | solution.py:13
  585.8 72.6 %reduce-scatter.15.cloned.1.call-start = ((), (), s32[]{:S(2)}) async-start(), calls=%async_computation.16 | async-start | bytes 1392640 | tf_op jit(solution)/shard_map/reduce_scatter | solution.py:105
  (219 other events, 2328.1 us)
Sparse Core Ops, SparseCore 0:
  14.3 30.8 all-gather.6
  52.6 29.9 all-gather.8
  96.2 27.5 all-gather.10
  136.8 32.3 all-gather.12
  177.4 29.9 all-gather.14
  218.2 26.8 all-gather.16
  376.4 26.9 reduce-scatter.6
  429.8 27.4 reduce-scatter.8
  473.0 32.1 reduce-scatter.10
  525.7 29.9 reduce-scatter.12
  585.9 27.1 reduce-scatter.16
  630.1 28.2 reduce-scatter.14

commit v12 on v9

--- a/solution.py
+++ b/solution.py
@@ -324,20 +324,29 @@
     return (list(grads) + [None, None])[:4]
 
 
-def down_backward(grad_out, hidden, slope, weights):
+def down_grad(grad_out, hidden):
+    size, depth = grad_out.shape
+    cuts, outs = weight_outs(depth, hidden.shape[1])
+
+    def kernel(g_ref, hidden_ref, sum_ref, *refs):
+        sum_ref[...] = column_sum(g_ref[...])
+        branch = g_ref[...].astype(BF)
+        for cut, ref in zip(cuts, refs):
+            ref[...] = tn(branch[:, cut[0] : cut[1]], hidden_ref[...]).astype(BF)
+
+    done = run(kernel, [shape((1, depth), F32)] + outs, [grad_out, hidden])
+    return done[0], fill(done[1:])
+
+
+def down_backward(grad_out, slope, weights):
     pieces, counts = weights
     size, depth = grad_out.shape
-    wide = hidden.shape[1]
-    cuts, grad_outs = weight_outs(depth, wide)
+    wide = slope.shape[1]
 
     def kernel(*refs):
-        g_ref, hidden_ref, slope_ref = refs[:3]
-        piece_refs, refs = refs[3 : 3 + len(pieces)], refs[3 + len(pieces) :]
-        low_ref, sum_ref, bias_ref = refs[:3]
-        sum_ref[...] = column_sum(g_ref[...])
+        g_ref, slope_ref, piece_refs = refs[0], refs[1], refs[2:-2]
+        low_ref, bias_ref = refs[-2:]
         branch = g_ref[...].astype(BF)
-        for cut, ref in zip(cuts, refs[3:]):
-            ref[...] = tn(branch[:, cut[0] : cut[1]], hidden_ref[...]).astype(BF)
         step = 512
         for at in range(0, wide, step):
             cols = slice(at, at + step)
@@ -345,9 +354,8 @@
             bias_ref[:, cols] = column_sum(back)
             low_ref[:, cols] = back.astype(BF)
 
-    outs = [shape((size, wide)), shape((1, depth), F32), shape((1, wide), F32)] + grad_outs
-    done = run(kernel, outs, [grad_out, hidden, slope, *pieces])
-    return done[0], done[1], done[2], fill(done[3:])
+    outs = [shape((size, wide)), shape((1, wide), F32)]
+    return run(kernel, outs, [grad_out, slope, *pieces])
 
 
 def up_grad(normed, low):
@@ -709,6 +717,10 @@
                     near[r - 1], extras = done[: len(near[r - 1])], done[len(near[r - 1]) :]
                 far[r - 1] = exchange_two(*halves[r - 1], *near[r - 1])
                 tied += near[r - 1] + far[r - 1]
+            if r == number:
+                last_sum, first_grads = down_grad(cotangent, extras[0])
+                first_grads = [g for g in first_grads if g is not None]
+                extras += first_grads
             if r <= 1:
                 extras += blocks_in
             if r == 1:
@@ -730,6 +742,7 @@
                 cot_half = done.pop()
             elif r == number:
                 cotangent = done.pop()
+                done, first_grads = done[: -len(first_grads)], done[-len(first_grads) :]
             if r == 1:
                 done, smalls = done[:-8], done[-8:]
                 params[0]["small"], params[1]["small"] = smalls[:4], smalls[4:]
@@ -775,7 +788,9 @@
     last_down = weights_of(number - 1)
     params[1]["down"] = last_down
     last_bias = params[1]["small"][0][7:8]
-    for r in range(8):
+    grads[0] = fill(first_grads)
+    sums[1]["out"] = last_sum
+    for r in range(1, 8):
         layer, stage = 1 - r // 4, r % 4
         one, total = params[layer], sums[layer]
         rows = one["small"][0]
@@ -797,15 +812,15 @@
                 tied.append(settled[c])
         new = None
         if stage == 0:
-            low, total["out"], total["up_bias"], new = down_backward(
-                grad, one["hidden"], one["slope"], one["down"]
-            )
+            total["out"], new = down_grad(grad, one["hidden"])
+        if stage == 0 or r == 1:
+            low, total["up_bias"] = down_backward(grad, one["slope"], one["down"])
             carry = [low]
-        elif stage == 1:
+        if stage == 1:
             part = contract_wide(low, one["up"])
             new = up_grad(one["n2"], low)
             carry = [part]
-        elif stage == 2:
+        if stage == 2:
             done = attention_backward(
                 grad, part, swap(part), one["mid"], rows, one["saved"], one["qkvo"]
             )
@@ -813,7 +828,7 @@
             if layer == 0:
                 new = attention_grad(one["n1"], dz, dq, dk, dv, one["saved"][4])
             carry = [part]
-        else:
+        if stage == 3:
             if layer == 1:
                 new = attention_grad(one["n1"], dz, dq, dk, dv, one["saved"][4])
             grad, total["one"] = value_backward(dmid, part, swap(part), one["u"], rows, layer == 1)
@@ -869,8 +884,9 @@
     if n_dp != 4:
         little = lax.psum_scatter(little, "dp", scatter_dimension=0, tiled=True)[0]
     else:
-        little = add(little[:2], swap_x(little[2:])).astype(jnp.bfloat16)
-        little = add(little[0], swap_y(little[1])).astype(jnp.bfloat16)
+        over = lax.ppermute(little[3], "dp", [(i, i ^ 3) for i in range(n_dp)])
+        little = add(little[0], swap_y(little[1])) + add(swap_x(little[2]), over)
+        little = little.astype(jnp.bfloat16)
 
     last = number - 1
     settled[last - 1] = scatter_column(moved[last - 1][:2], moved[last - 1][2:])

time: 658 us -> 677 us (1.029)
  local copies, waits for them, and re-layouts: 82.2 us -> 96 us
    unnamed x318 -> x394, local copies, waits for them, and re-layouts: 44.1 us -> 61.2 us
    ppermute x32, waiting for transfers between devices: 43 us -> 59.8 us  [swap_y(): return lax.ppermute(value, 'dp', [(i, i ^ 2) for i in range(n)])]
    ppermute x32, waiting for transfers between devices: 61.9 us -> 48.7 us  [swap_x(): return lax.ppermute(value, 'dp', [(i, i ^ 1) for i in range(n)])]
    pallas_call x18 -> x20, Pallas kernels: 187 us -> 191 us  [run(): pl.pallas_call(kernel, out_shape=list(outs), in_specs=[block] * len(ins),...]
  transfers between devices with their start and end apart: 106 -> 107, of which waited for: 35 -> 29; matrix products, arithmetic and copies ran while one was open for 15% -> 14% of each run, Pallas kernels for 28% -> 29%
where the time goes in v12:
time: 677 us; the launch traced here: 669 us
  waiting for transfers between devices  198 us (29%)
  Pallas kernels  197 us (29%)
  local copies, waits for them, and re-layouts  96 us (14%)
  starting transfers between devices  87.4 us (13%)
  other arithmetic  73.7 us (11%)
  between operations  17.5 us (3%)
    pallas_call x20, Pallas kernels, run(): pl.pallas_call(kernel, out_shape=list(outs), in_specs=[block] * len(ins),...  191 us
    unnamed x394, local copies, waits for them, and re-layouts  61.2 us
    ppermute x32, waiting for transfers between devices, swap_y(): return lax.ppermute(value, 'dp', [(i, i ^ 2) for i in range(n)])  59.8 us
    ppermute x32, waiting for transfers between devices, swap_x(): return lax.ppermute(value, 'dp', [(i, i ^ 1) for i in range(n)])  48.7 us
    ppermute x12, waiting for transfers between devices, shift(): return lax.ppermute(block, 'tensor', [(i, (i + d) % n) for i in range(n)])  41.1 us
    convert_element_type x12, other arithmetic, scatter_two(): send.append(add(keep[half:], new[half:]).astype(jnp.bfloat16))  27.1 us
    ppermute x32, starting transfers between devices, swap_y(): return lax.ppermute(value, 'dp', [(i, i ^ 2) for i in range(n)])  24.9 us
    ppermute x32, starting transfers between devices, swap_x(): return lax.ppermute(value, 'dp', [(i, i ^ 1) for i in range(n)])  24.9 us
  transfers between devices with their start and end apart: 107, of which 29 were waited for; matrix products, arithmetic and copies ran while one was open for 14% of the time, Pallas kernels for 29%

profile of v12, /device:TPU:1, one launch (start us, length us, event | category | flops | bytes accessed | tf_op | source)
XLA Modules:
  0.0 669.0 jit_solution(3395478351741714782)
XLA Ops:
  23.3 22.7 %all-gather.7.cloned.1.call-done.refs_0_ = bf16[272,2048]{1,0:T(8,128)(2,1)} async-done(((bf16[272,512]{1,0:T(8,128)(2,1)}), bf16[272,2048]{1,0:T(8,128)(2,1)}) %all-gather.7.cloned.1.call-update) | async-done | bytes 1114128 | tf_op jit(solution)/shard_map/all_gather | solution.py:49
  105.4 15.5 %shard_map.138 = (f32[592,1024]{1,0:T(8,128)}, bf16[592,1024]{1,0:T(8,128)(2,1)}, bf16[592,512]{1,0:T(8,128)(2,1)}, bf16[592,512]{1,0:T(8,128)(2,1)}, bf16[592,5...) custom-call(f32[592,1024]{1,0:T(8,128)} %maximum_convert_fusion.refs_0_, ...), custom_call_target="tpu_custom_call" | custom-call | flops 1 | bytes 1 | tf_op jit(solution)/shard_map/pallas_call | solution.py:173
  144.9 10.2 %shard_map.141 = (f32[592,1024]{1,0:T(8,128)}, bf16[592,1024]{1,0:T(8,128)(2,1)}, bf16[592,2048]{1,0:T(8,128)(2,1)}, bf16[592,2048]{1,0:T(8,128)(2,1)}) custom-call(f32[592,1024]{1,0:T(8,128)} %get-tuple-element.299.refs_0_.u_ref, bf16[592,1024]{1,0:T(8,128)(2,1)} %get-tuple-element.300.refs_1_, bf16[592,1024]{1,0:T(8,128)(2,1)} %collective-permute-done.24.refs_2_, ...), custom_call_target="tpu_custom_call" | custom-call | flops 1 | bytes 1 | tf_op jit(solution)/shard_map/pallas_call | solution.py:173
  157.8 14.3 %collective-permute-done.29.refs_10_ = bf16[296,256]{1,0:T(8,128)(2,1)S(1)} collective-permute-done((bf16[296,256]{1,0:T(8,128)(2,1)S(1)}, bf16[296,256]{1,0:T(8,128)(2,1)S(1)}, u32[]{:S(2)}, u32[]{:S(2)}) %collective-permute-start.29) | collective-permute-done | bytes 151584 | tf_op jit(solution)/shard_map/ppermute | solution.py:525
  199.5 8.7 %collective-permute-done.36.refs_11_ = bf16[296,256]{1,0:T(8,128)(2,1)S(1)} collective-permute-done((bf16[296,256]{1,0:T(8,128)(2,1)S(1)}, bf16[296,256]{1,0:T(8,128)(2,1)S(1)}, u32[]{:S(2)}, u32[]{:S(2)}) %collective-permute-start.36) | collective-permute-done | bytes 151584 | tf_op jit(solution)/shard_map/ppermute | solution.py:525
  208.2 8.3 %collective-permute-done.33.refs_4_ = bf16[128,2048]{1,0:T(8,128)(2,1)S(1)} collective-permute-done((bf16[128,2048]{1,0:T(8,128)(2,1)}, bf16[128,2048]{1,0:T(8,128)(2,1)S(1)}, u32[]{:S(2)}, u32[]{:S(2)}) %collective-permute-start.33) | collective-permute-done | bytes 524320 | tf_op jit(solution)/shard_map/ppermute | solution.py:23
  225.8 16.9 %shard_map.147 = (f32[592,1024]{1,0:T(8,128)}, bf16[592,1024]{1,0:T(8,128)(2,1)}, bf16[592,512]{1,0:T(8,128)(2,1)}, bf16[592,512]{1,0:T(8,128)(2,1)}, bf16[592,5...) custom-call(f32[592,1024]{1,0:T(8,128)} %get-tuple-element.334.refs_0_.refs, ...), custom_call_target="tpu_custom_call" | custom-call | flops 1 | bytes 1 | tf_op jit(solution)/shard_map/pallas_call | solution.py:173
  248.8 11.2 %collective-permute-done.41.refs_4_ = bf16[128,2048]{1,0:T(8,128)(2,1)} collective-permute-done((bf16[128,2048]{1,0:T(8,128)(2,1)}, bf16[128,2048]{1,0:T(8,128)(2,1)}, u32[]{:S(2)}, u32[]{:S(2)}) %collective-permute-start.41) | collective-permute-done | bytes 524320 | tf_op jit(solution)/shard_map/ppermute | solution.py:23
  266.6 10.6 %shard_map.151 = (f32[592,1024]{1,0:T(8,128)}, bf16[592,1024]{1,0:T(8,128)(2,1)}, bf16[592,2048]{1,0:T(8,128)(2,1)}, bf16[592,2048]{1,0:T(8,128)(2,1)}) custom-call(f32[592,1024]{1,0:T(8,128)} %get-tuple-element.354.refs_0_.u_ref, bf16[592,1024]{1,0:T(8,128)(2,1)} %get-tuple-element.355.refs_1_, bf16[592,1024]{1,0:T(8,128)(2,1)} %copy-done.169, ...), custom_call_target="tpu_custom_call" | custom-call | flops 1 | bytes 1 | tf_op jit(solution)/shard_map/pallas_call | solution.py:173
  283.8 6.9 %shard_map.153 = (f32[1,1024]{1,0:T(1,128)S(1)}, bf16[256,2048]{1,0:T(8,128)(2,1)S(1)}, bf16[256,2048]{1,0:T(8,128)(2,1)S(1)}, bf16[256,2048]{1,0:T(8,128)(2,1)S(1)}, bf16[256,2048]{1,0:T(8,128)(2,1)}) custom-call(f32[592,1024]{1,0:T(8,128)} %convert_multiply_fusion.g_ref.refs_11_, bf16[592,2048]{1,0:T(8,128)(2,1)} %get-tuple-element.366.hidden_ref.refs_6_), custom_call_target="tpu_custom_call" | custom-call | flops 1 | bytes 1 | tf_op jit(solution)/shard_map/pallas_call | solution.py:173
  304.9 7.3 %shard_map.155 = (bf16[592,2048]{1,0:T(8,128)(2,1)}, f32[1,2048]{1,0:T(1,128)S(1)}) custom-call(f32[592,1024]{1,0:T(8,128)} %get-tuple-element.372.refs_0_, bf16[592,2048]{1,0:T(8,128)(2,1)} %get-tuple-element.373.refs_1_, bf16[128,2048]{1,0:T(8,128)(2,1)} %get-tuple-element.582.refs_2_.refs_1_, bf16[128,2048]{1,0:T(8,128)(2,1)S(1)} %copy-done.12, ...), custom_call_target="tpu_custom_call" | custom-call | flops 1 | bytes 1 | tf_op jit(solution)/shard_map/pallas_call | solution.py:173
  312.2 6.7 %shard_map.156.refs_0_ = bf16[592,1024]{1,0:T(8,128)(2,1)} custom-call(bf16[592,2048]{1,0:T(8,128)(2,1)} %get-tuple-element.380.refs_0_.low_ref, bf16[128,2048]{1,0:T(8,128)(2,1)} %get-tuple-element.584.refs_5_.refs_1_, bf16[128,2048]{1,0:T(8,128)(2,1)S(1)} %copy-done.25, bf16[128,2048]{1,0:T(8,128)(2,1)} %get-tuple-element.358.refs_7_.refs_3_, ...), custom_call_target="tpu_custom_call" | custom-call | flops 1 | bytes 1 | tf_op jit(solution)/shard_map/pallas_call | solution.py:173
  319.0 6.5 shard_map.157
  339.5 22.0 %shard_map.159 = (f32[592,1024]{1,0:T(8,128)}, bf16[592,1024]{1,0:T(8,128)(2,1)}, bf16[592,512]{1,0:T(8,128)(2,1)}, bf16[592,512]{1,0:T(8,128)(2,1)}, bf16[592,5...) custom-call(f32[592,1024]{1,0:T(8,128)} %get-tuple-element.372.refs_, ...), custom_call_target="tpu_custom_call" | custom-call | flops 1 | bytes 1 | tf_op jit(solution)/shard_map/pallas_call | solution.py:173
  387.6 7.8 %shard_map.163 = (bf16[256,2048]{1,0:T(8,128)(2,1)S(1)}, bf16[256,2048]{1,0:T(8,128)(2,1)}, bf16[256,2048]{1,0:T(8,128)(2,1)}, bf16[256,2048]{1,0:T(8,128)(2,1)}) custom-call(bf16[592,1024]{1,0:T(8,128)(2,1)} %get-tuple-element.406.n_ref, bf16[592,1024]{1,0:T(8,128)(2,1)} %get-tuple-element.407.dz_ref, bf16[592,512]{1,0:T(8,128)(2,1)S(1)} %copy-done.107, ...), custom_call_target="tpu_custom_call" | custom-call | flops 1 | bytes 1 | tf_op jit(solution)/shard_map/pallas_call | solution.py:173
  413.7 7.0 %shard_map.167 = (f32[1,1024]{1,0:T(1,128)S(1)}, bf16[256,2048]{1,0:T(8,128)(2,1)S(1)}, bf16[256,2048]{1,0:T(8,128)(2,1)S(1)}, bf16[256,2048]{1,0:T(8,128)(2,1)S(1)}, bf16[256,2048]{1,0:T(8,128)(2,1)}) custom-call(f32[592,1024]{1,0:T(8,128)} %get-tuple-element.423.refs_0_.g_ref, bf16[592,2048]{1,0:T(8,128)(2,1)} %get-tuple-element.318.refs_0_.hidden_ref), custom_call_target="tpu_custom_call" | custom-call | flops 1 | bytes 1 | tf_op jit(solution)/shard_map/pallas_call | solution.py:173
  422.7 7.4 %shard_map.165 = (bf16[592,2048]{1,0:T(8,128)(2,1)}, f32[1,2048]{1,0:T(1,128)S(1)}) custom-call(f32[592,1024]{1,0:T(8,128)} %get-tuple-element.423.refs_0_.g_ref, bf16[592,2048]{1,0:T(8,128)(2,1)} %get-tuple-element.424.refs_1_, bf16[128,2048]{1,0:T(8,128)(2,1)} %get-tuple-element.588.refs_1_.refs_2_, bf16[128,2048]{1,0:T(8,128)(2,1)S(1)} %copy-done.4, ...), custom_call_target="tpu_custom_call" | custom-call | flops 1 | bytes 1 | tf_op jit(solution)/shard_map/pallas_call | solution.py:173
  461.9 14.1 %collective-permute-done.67.refs_11_ = bf16[128,2048]{1,0:T(8,128)(2,1)S(1)} collective-permute-done((bf16[128,2048]{1,0:T(8,128)(2,1)S(1)}, bf16[128,2048]{1,0:T(8,128)(2,1)S(1)}, u32[]{:S(2)}, u32[]{:S(2)}) %collective-permute-start.67) | collective-permute-done | bytes 524320 | tf_op jit(solution)/shard_map/ppermute | solution.py:28
  493.1 21.0 %shard_map.172 = (f32[592,1024]{1,0:T(8,128)}, bf16[592,1024]{1,0:T(8,128)(2,1)}, bf16[592,512]{1,0:T(8,128)(2,1)}, bf16[592,512]{1,0:T(8,128)(2,1)}, bf16[592,5...) custom-call(f32[592,1024]{1,0:T(8,128)} %get-tuple-element.423.refs_, ...), custom_call_target="tpu_custom_call" | custom-call | flops 1 | bytes 1 | tf_op jit(solution)/shard_map/pallas_call | solution.py:173
  517.4 8.0 %shard_map.173 = (bf16[256,2048]{1,0:T(8,128)(2,1)}, bf16[256,2048]{1,0:T(8,128)(2,1)}, bf16[256,2048]{1,0:T(8,128)(2,1)}, bf16[256,2048]{1,0:T(8,128)(2,1)}) custom-call(bf16[592,1024]{1,0:T(8,128)(2,1)} %get-tuple-element.465.n_ref, bf16[592,1024]{1,0:T(8,128)(2,1)} %get-tuple-element.466.dz_ref, bf16[592,512]{1,0:T(8,128)(2,1)S(1)} %copy-done.110, ...), custom_call_target="tpu_custom_call" | custom-call | flops 1 | bytes 1 | tf_op jit(solution)/shard_map/pallas_call | solution.py:173
  538.9 30.1 %collective-permute-done.91 = bf16[128,2048]{1,0:T(8,128)(2,1)S(1)} collective-permute-done((bf16[128,2048]{1,0:T(8,128)(2,1)S(1)}, bf16[128,2048]{1,0:T(8,128)(2,1)S(1)}, u32[]{:S(2)}, u32[]{:S(2)}) %collective-permute-start.91) | collective-permute-done | bytes 524320 | tf_op jit(solution)/shard_map/ppermute | solution.py:28
  595.3 11.6 %collective-permute-done.87 = bf16[16,2048]{1,0:T(8,128)(2,1)S(1)} collective-permute-done((bf16[16,2048]{1,0:T(8,128)(2,1)S(1)}, bf16[16,2048]{1,0:T(8,128)(2,1)S(1)}, u32[]{:S(2)}, u32[]{:S(2)}) %collective-permute-start.87) | collective-permute-done | bytes 65568 | tf_op jit(solution)/shard_map/ppermute | solution.py:28
  612.9 6.9 %collective-permute-done.79.refs_2_ = bf16[296,256]{1,0:T(8,128)(2,1)S(1)} collective-permute-done((bf16[296,256]{1,0:T(8,128)(2,1)S(1)}, bf16[296,256]{1,0:T(8,128)(2,1)S(1)}, u32[]{:S(2)}, u32[]{:S(2)}) %collective-permute-start.79) | collective-permute-done | bytes 151584 | tf_op jit(solution)/shard_map/ppermute | solution.py:525
  636.4 17.2 %reduce-scatter.15.cloned.1.call-done = bf16[272,512]{1,0:T(8,128)(2,1)} async-done(((bf16[272,2048]{1,0:T(8,128)(2,1)}), bf16[272,512]{1,0:T(8,128)(2,1)}) %reduce-scatter.15.cloned.1.call-update) | async-done | bytes 278544 | tf_op jit(solution)/shard_map/reduce_scatter | solution.py:105
  (821 shorter events, 352.3 us)
Async XLA Ops:
  7.2 38.8 %all-gather.7.cloned.1.call-start = ((), (), s32[]{:S(2)}) async-start(), calls=%async_computation.6 | async-start | bytes 1392640 | tf_op jit(solution)/shard_map/all_gather | solution.py:49
  14.9 72.7 %all-gather.9.cloned.1.call-start = ((), (), s32[]{:S(2)}) async-start(), calls=%async_computation.7 | async-start | bytes 1310720 | tf_op jit(solution)/shard_map/all_gather | solution.py:49
  52.0 35.5 %collective-permute-start.4 = (bf16[128,2048]{1,0:T(8,128)(2,1)S(1)}, bf16[128,2048]{1,0:T(8,128)(2,1)S(1)}, u32[]{:S(2)}, u32[]{:S(2)}) collective-permute-start(bf16[128,2048]{1,0:T(8,128)(2,1)S(1)} %get-tuple-element.580.refs_5_.refs_10_), channel_id=1, source_target_pairs={{0,4},{4,0},{8,12},{12,8},{1,5},{5,1},{9,13},{13,9},{2,6},{6,2},{1... | collective-permute-start | bytes 1572872 | tf_op jit(solution)/shard_map/ppermute | solution.py:23
  53.2 82.1 %all-gather.11.cloned.1.call-start = ((), (), s32[]{:S(2)}) async-start(), calls=%async_computation.8 | async-start | bytes 1310720 | tf_op jit(solution)/shard_map/all_gather | solution.py:49
  97.6 74.6 %all-gather.13.cloned.1.call-start = ((), (), s32[]{:S(2)}) async-start(), calls=%async_computation.9 | async-start | bytes 1310720 | tf_op jit(solution)/shard_map/all_gather | solution.py:49
  138.3 78.3 %all-gather.15.cloned.1.call-start = ((), (), s32[]{:S(2)}) async-start(), calls=%async_computation.10 | async-start | bytes 1310720 | tf_op jit(solution)/shard_map/all_gather | solution.py:49
  179.1 69.7 %all-gather.17.cloned.1.call-start = ((), (), s32[]{:S(2)}) async-start(), calls=%async_computation.11 | async-start | bytes 1310720 | tf_op jit(solution)/shard_map/all_gather | solution.py:49
  220.0 182.6 %reduce-scatter.7.cloned.1.call-start = ((), (), s32[]{:S(2)}) async-start(), calls=%async_computation.12 | async-start | bytes 1310720 | tf_op jit(solution)/shard_map/reduce_scatter | solution.py:105
  331.6 37.0 %collective-permute-start.57 = (bf16[256,2048]{1,0:T(8,128)(2,1)}, bf16[256,2048]{1,0:T(8,128)(2,1)}, u32[]{:S(2)}, u32[]{:S(2)}) collective-permute-start(bf16[256,2048]{1,0:T(8,128)(2,1)} %get-tuple-element.401), channel_id=1, source_target_pairs={{0,4},{4,0},{8,12},{12,8},{1,5},{5,1},{9,13},{13,9},{2,6},{6,2},{1... | collective-permute-start | bytes 3145736 | tf_op jit(solution)/shard_map/ppermute | solution.py:23
  332.8 35.8 %collective-permute-start.58 = (bf16[256,2048]{1,0:T(8,128)(2,1)}, bf16[256,2048]{1,0:T(8,128)(2,1)}, u32[]{:S(2)}, u32[]{:S(2)}) collective-permute-start(bf16[256,2048]{1,0:T(8,128)(2,1)} %get-tuple-element.402), channel_id=1, source_target_pairs={{0,8},{4,12},{8,0},{12,4},{1,9},{5,13},{9,1},{13,5},{2,10},{6,14},... | collective-permute-start | bytes 3145736 | tf_op jit(solution)/shard_map/ppermute | solution.py:28
  373.2 63.1 %reduce-scatter.9.cloned.1.call-start = ((), (), s32[]{:S(2)}) async-start(), calls=%async_computation.13 | async-start | bytes 1310720 | tf_op jit(solution)/shard_map/reduce_scatter | solution.py:105
  406.2 119.5 %reduce-scatter.11.cloned.1.call-start = ((), (), s32[]{:S(2)}) async-start(), calls=%async_computation.14 | async-start | bytes 1310720 | tf_op jit(solution)/shard_map/reduce_scatter | solution.py:105
  441.2 34.8 %collective-permute-start.69 = (bf16[256,2048]{1,0:T(8,128)(2,1)S(1)}, bf16[256,2048]{1,0:T(8,128)(2,1)S(1)}, u32[]{:S(2)}, u32[]{:S(2)}) collective-permute-start(bf16[256,2048]{1,0:T(8,128)(2,1)S(1)} %copy-done.92), channel_id=1, source_target_pairs={{0,4},{4,0},{8,12},{12,8},{1,5},{5,1},{9,13},{13,9},{2,6},{6,2},{1... | collective-permute-start | bytes 3145736 | tf_op jit(solution)/shard_map/ppermute | solution.py:23
  441.5 34.5 %collective-permute-start.70 = (bf16[256,2048]{1,0:T(8,128)(2,1)S(1)}, bf16[256,2048]{1,0:T(8,128)(2,1)S(1)}, u32[]{:S(2)}, u32[]{:S(2)}) collective-permute-start(bf16[256,2048]{1,0:T(8,128)(2,1)S(1)} %copy-done.94), channel_id=1, source_target_pairs={{0,8},{4,12},{8,0},{12,4},{1,9},{5,13},{9,1},{13,5},{2,10},{6,14},... | collective-permute-start | bytes 3145736 | tf_op jit(solution)/shard_map/ppermute | solution.py:28
  480.3 104.1 %reduce-scatter.13.cloned.1.call-start = ((), (), s32[]{:S(2)}) async-start(), calls=%async_computation.15 | async-start | bytes 1310720 | tf_op jit(solution)/shard_map/reduce_scatter | solution.py:105
  486.2 39.3 %collective-permute-start.74 = (bf16[128,2048]{1,0:T(8,128)(2,1)}, bf16[128,2048]{1,0:T(8,128)(2,1)}, u32[]{:S(2)}, u32[]{:S(2)}) collective-permute-start(bf16[128,2048]{1,0:T(8,128)(2,1)} %get-tuple-element.551), channel_id=1, source_target_pairs={{0,4},{4,0},{8,12},{12,8},{1,5},{5,1},{9,13},{13,9},{2,6},{6,2},{1... | collective-permute-start | bytes 1572872 | tf_op jit(solution)/shard_map/ppermute | solution.py:23
  487.5 38.1 %collective-permute-start.75 = (bf16[256,2048]{1,0:T(8,128)(2,1)S(1)}, bf16[256,2048]{1,0:T(8,128)(2,1)}, u32[]{:S(2)}, u32[]{:S(2)}) collective-permute-start(bf16[256,2048]{1,0:T(8,128)(2,1)S(1)} %copy-done.96), channel_id=1, source_target_pairs={{0,4},{4,0},{8,12},{12,8},{1,5},{5,1},{9,13},{13,9},{2,6},{6,2},{1... | collective-permute-start | bytes 3145736 | tf_op jit(solution)/shard_map/ppermute | solution.py:23
  487.8 37.8 %collective-permute-start.76 = (bf16[256,2048]{1,0:T(8,128)(2,1)S(1)}, bf16[256,2048]{1,0:T(8,128)(2,1)}, u32[]{:S(2)}, u32[]{:S(2)}) collective-permute-start(bf16[256,2048]{1,0:T(8,128)(2,1)S(1)} %copy-done.98), channel_id=1, source_target_pairs={{0,8},{4,12},{8,0},{12,4},{1,9},{5,13},{9,1},{13,5},{2,10},{6,14},... | collective-permute-start | bytes 3145736 | tf_op jit(solution)/shard_map/ppermute | solution.py:28
  491.6 34.0 %collective-permute-start.73 = (bf16[128,2048]{1,0:T(8,128)(2,1)}, bf16[128,2048]{1,0:T(8,128)(2,1)S(1)}, u32[]{:S(2)}, u32[]{:S(2)}) collective-permute-start(bf16[128,2048]{1,0:T(8,128)(2,1)} %get-tuple-element.553), channel_id=1, source_target_pairs={{0,8},{4,12},{8,0},{12,4},{1,9},{5,13},{9,1},{13,5},{2,10},{6,14},... | collective-permute-start | bytes 1572872 | tf_op jit(solution)/shard_map/ppermute | solution.py:28
  530.2 96.5 %reduce-scatter.17.cloned.1.call-start = ((), (), s32[]{:S(2)}) async-start(), calls=%async_computation.17 | async-start | bytes 1310720 | tf_op jit(solution)/shard_map/reduce_scatter | solution.py:105
  530.7 42.5 %collective-permute-start.77 = (bf16[592,1024]{1,0:T(8,128)(2,1)S(1)}, bf16[592,1024]{1,0:T(8,128)(2,1)S(1)}, u32[]{:S(2)}, u32[]{:S(2)}) collective-permute-start(bf16[592,1024]{1,0:T(8,128)(2,1)S(1)} %copy-done.31), channel_id=1, source_target_pairs={{0,16},{16,0},{1,17},{17,1},{2,18},{18,2},{3,19},{19,3},{4,20},{20... | collective-permute-start | bytes 3637256 | tf_op jit(solution)/shard_map/ppermute | solution.py:13
  532.3 52.1 %collective-permute-start.82 = (bf16[256,2048]{1,0:T(8,128)(2,1)}, bf16[256,2048]{1,0:T(8,128)(2,1)}, u32[]{:S(2)}, u32[]{:S(2)}) collective-permute-start(bf16[256,2048]{1,0:T(8,128)(2,1)} %get-tuple-element.503), channel_id=1, source_target_pairs={{0,4},{4,0},{8,12},{12,8},{1,5},{5,1},{9,13},{13,9},{2,6},{6,2},{1... | collective-permute-start | bytes 3145736 | tf_op jit(solution)/shard_map/ppermute | solution.py:23
  533.0 51.4 %collective-permute-start.83 = (bf16[256,2048]{1,0:T(8,128)(2,1)}, bf16[256,2048]{1,0:T(8,128)(2,1)}, u32[]{:S(2)}, u32[]{:S(2)}) collective-permute-start(bf16[256,2048]{1,0:T(8,128)(2,1)} %get-tuple-element.504), channel_id=1, source_target_pairs={{0,8},{4,12},{8,0},{12,4},{1,9},{5,13},{9,1},{13,5},{2,10},{6,14},... | collective-permute-start | bytes 3145736 | tf_op jit(solution)/shard_map/ppermute | solution.py:28
  583.0 70.6 %reduce-scatter.15.cloned.1.call-start = ((), (), s32[]{:S(2)}) async-start(), calls=%async_computation.16 | async-start | bytes 1392640 | tf_op jit(solution)/shard_map/reduce_scatter | solution.py:105
  (271 other events, 2618.8 us)
Sparse Core Ops, SparseCore 0:
  15.0 30.8 all-gather.6
  53.4 29.9 all-gather.8
  97.7 27.5 all-gather.10
  138.4 32.3 all-gather.12
  179.2 29.8 all-gather.14
  220.1 26.8 all-gather.16
  373.3 26.7 reduce-scatter.6
  406.3 29.9 reduce-scatter.8
  480.4 30.7 reduce-scatter.10
  530.3 26.8 reduce-scatter.12
  583.1 24.9 reduce-scatter.16
  623.8 29.7 reduce-scatter.14

commit v13 on v12

--- a/solution.py
+++ b/solution.py
@@ -803,9 +803,8 @@
             elif r == made[c] + 2:
                 stay, come = scatter_two(*grads[c][2:], got[c])
                 moved[c] = [*stay, *come]
-                if r < 7:
-                    slots.append((moved, c, len(moved[c])))
-                    tied += moved[c]
+                slots.append((moved, c, len(moved[c])))
+                tied += moved[c]
             elif r == made[c] + 3:
                 settled[c] = scatter_column(moved[c][:2], moved[c][2:])
                 slots.append((settled, c, 0))
@@ -836,8 +835,7 @@
             if r == 7:
                 one_scale = jnp.ones((), jnp.float32)
                 no_bias = jnp.zeros((1, grad.shape[1]), jnp.float32)
-                carry = [small_grads()]
-                grad_blocks = shifts(image_rows(one_scale, [grad], no_bias))
+                carry = [small_grads(), *shifts(image_rows(one_scale, [grad], no_bias))]
         if new is not None:
             c = made.index(r)
             grads[c] = new
@@ -865,7 +863,7 @@
             elif r < 7:
                 grad = done[0]
             else:
-                little = done[0]
+                little, grad_blocks = done[0], done[1 : 1 + n_tensor]
             if r == 3:
                 last_part = done[1]
             elif 4 <= r < 4 + n_tensor - 1:
@@ -891,10 +889,7 @@
     last = number - 1
     settled[last - 1] = scatter_column(moved[last - 1][:2], moved[last - 1][2:])
     stay, come = scatter_two(*grads[last][2:], got[last])
-    done = tie([*grad_blocks, *stay, *come], [])
-    grad_blocks, done = done[:n_tensor], done[n_tensor:]
     grad_rows, out_rows = by_image(grad_blocks), by_image(out_blocks)
-    stay, come = done[:2], done[2:]
     if come:
         stay = [add(s, c).astype(jnp.bfloat16) for s, c in zip(stay, come)]
     settled[last] = scatter_column([*stay, little], [])

time: 677 us -> 658 us (0.972)
  waiting for transfers between devices: 198 us -> 180 us
    ppermute x32, waiting for transfers between devices: 59.8 us -> 38 us  [swap_y(): return lax.ppermute(value, 'dp', [(i, i ^ 2) for i in range(n)])]
    ppermute x32, waiting for transfers between devices: 48.7 us -> 58.5 us  [swap_x(): return lax.ppermute(value, 'dp', [(i, i ^ 1) for i in range(n)])]
    ppermute x12, waiting for transfers between devices: 41.1 us -> 31.8 us  [shift(): return lax.ppermute(block, 'tensor', [(i, (i + d) % n) for i in range(n)])]
  transfers between devices with their start and end apart: 107 -> 107, of which waited for: 29 -> 30; matrix products, arithmetic and copies ran while one was open for 14% -> 14% of each run, Pallas kernels for 29% -> 30%
where the time goes in v13:
time: 658 us; the launch traced here: 650 us
  Pallas kernels  197 us (30%)
  waiting for transfers between devices  180 us (27%)
  local copies, waits for them, and re-layouts  99 us (15%)
  starting transfers between devices  87.8 us (13%)
  other arithmetic  69.2 us (11%)
  between operations  17.5 us (3%)
    pallas_call x20, Pallas kernels, run(): pl.pallas_call(kernel, out_shape=list(outs), in_specs=[block] * len(ins),...  191 us
    unnamed x394, local copies, waits for them, and re-layouts  64.2 us
    ppermute x32, waiting for transfers between devices, swap_x(): return lax.ppermute(value, 'dp', [(i, i ^ 1) for i in range(n)])  58.5 us
    ppermute x32, waiting for transfers between devices, swap_y(): return lax.ppermute(value, 'dp', [(i, i ^ 2) for i in range(n)])  38 us
    ppermute x12, waiting for transfers between devices, shift(): return lax.ppermute(block, 'tensor', [(i, (i + d) % n) for i in range(n)])  31.8 us
    convert_element_type x12, other arithmetic, scatter_two(): send.append(add(keep[half:], new[half:]).astype(jnp.bfloat16))  28 us
    ppermute x32, starting transfers between devices, swap_y(): return lax.ppermute(value, 'dp', [(i, i ^ 2) for i in range(n)])  25.3 us
    reduce_scatter x6, waiting for transfers between devices, scatter_column(): lax.psum_scatter(jnp.concatenate(stay, 0), 'tensor', scatter_dimension=1,...  24.3 us
  transfers between devices with their start and end apart: 107, of which 30 were waited for; matrix products, arithmetic and copies ran while one was open for 14% of the time, Pallas kernels for 30%

profile of v13, /device:TPU:1, one launch (start us, length us, event | category | flops | bytes accessed | tf_op | source)
XLA Modules:
  0.0 650.4 jit_solution(4347671566522942989)
XLA Ops:
  23.3 22.7 %all-gather.7.cloned.1.call-done.refs_0_ = bf16[272,2048]{1,0:T(8,128)(2,1)} async-done(((bf16[272,512]{1,0:T(8,128)(2,1)}), bf16[272,2048]{1,0:T(8,128)(2,1)}) %all-gather.7.cloned.1.call-update) | async-done | bytes 1114128 | tf_op jit(solution)/shard_map/all_gather | solution.py:49
  105.4 15.5 %shard_map.138 = (f32[592,1024]{1,0:T(8,128)}, bf16[592,1024]{1,0:T(8,128)(2,1)}, bf16[592,512]{1,0:T(8,128)(2,1)}, bf16[592,512]{1,0:T(8,128)(2,1)}, bf16[592,5...) custom-call(f32[592,1024]{1,0:T(8,128)} %maximum_convert_fusion.refs_0_, ...), custom_call_target="tpu_custom_call" | custom-call | flops 1 | bytes 1 | tf_op jit(solution)/shard_map/pallas_call | solution.py:173
  145.0 10.2 %shard_map.141 = (f32[592,1024]{1,0:T(8,128)}, bf16[592,1024]{1,0:T(8,128)(2,1)}, bf16[592,2048]{1,0:T(8,128)(2,1)}, bf16[592,2048]{1,0:T(8,128)(2,1)}) custom-call(f32[592,1024]{1,0:T(8,128)} %get-tuple-element.299.refs_0_.u_ref, bf16[592,1024]{1,0:T(8,128)(2,1)} %get-tuple-element.300.refs_1_, bf16[592,1024]{1,0:T(8,128)(2,1)} %collective-permute-done.24.refs_2_, ...), custom_call_target="tpu_custom_call" | custom-call | flops 1 | bytes 1 | tf_op jit(solution)/shard_map/pallas_call | solution.py:173
  157.8 14.3 %collective-permute-done.29.refs_10_ = bf16[296,256]{1,0:T(8,128)(2,1)S(1)} collective-permute-done((bf16[296,256]{1,0:T(8,128)(2,1)S(1)}, bf16[296,256]{1,0:T(8,128)(2,1)S(1)}, u32[]{:S(2)}, u32[]{:S(2)}) %collective-permute-start.29) | collective-permute-done | bytes 151584 | tf_op jit(solution)/shard_map/ppermute | solution.py:525
  199.5 8.7 %collective-permute-done.36.refs_11_ = bf16[296,256]{1,0:T(8,128)(2,1)S(1)} collective-permute-done((bf16[296,256]{1,0:T(8,128)(2,1)S(1)}, bf16[296,256]{1,0:T(8,128)(2,1)S(1)}, u32[]{:S(2)}, u32[]{:S(2)}) %collective-permute-start.36) | collective-permute-done | bytes 151584 | tf_op jit(solution)/shard_map/ppermute | solution.py:525
  208.2 8.3 %collective-permute-done.33.refs_4_ = bf16[128,2048]{1,0:T(8,128)(2,1)S(1)} collective-permute-done((bf16[128,2048]{1,0:T(8,128)(2,1)}, bf16[128,2048]{1,0:T(8,128)(2,1)S(1)}, u32[]{:S(2)}, u32[]{:S(2)}) %collective-permute-start.33) | collective-permute-done | bytes 524320 | tf_op jit(solution)/shard_map/ppermute | solution.py:23
  225.8 16.9 %shard_map.147 = (f32[592,1024]{1,0:T(8,128)}, bf16[592,1024]{1,0:T(8,128)(2,1)}, bf16[592,512]{1,0:T(8,128)(2,1)}, bf16[592,512]{1,0:T(8,128)(2,1)}, bf16[592,5...) custom-call(f32[592,1024]{1,0:T(8,128)} %get-tuple-element.334.refs_0_.refs, ...), custom_call_target="tpu_custom_call" | custom-call | flops 1 | bytes 1 | tf_op jit(solution)/shard_map/pallas_call | solution.py:173
  248.8 11.2 %collective-permute-done.41.refs_4_ = bf16[128,2048]{1,0:T(8,128)(2,1)} collective-permute-done((bf16[128,2048]{1,0:T(8,128)(2,1)}, bf16[128,2048]{1,0:T(8,128)(2,1)}, u32[]{:S(2)}, u32[]{:S(2)}) %collective-permute-start.41) | collective-permute-done | bytes 524320 | tf_op jit(solution)/shard_map/ppermute | solution.py:23
  266.6 10.6 %shard_map.151 = (f32[592,1024]{1,0:T(8,128)}, bf16[592,1024]{1,0:T(8,128)(2,1)}, bf16[592,2048]{1,0:T(8,128)(2,1)}, bf16[592,2048]{1,0:T(8,128)(2,1)}) custom-call(f32[592,1024]{1,0:T(8,128)} %get-tuple-element.354.refs_0_.u_ref, bf16[592,1024]{1,0:T(8,128)(2,1)} %get-tuple-element.355.refs_1_, bf16[592,1024]{1,0:T(8,128)(2,1)} %copy-done.169, ...), custom_call_target="tpu_custom_call" | custom-call | flops 1 | bytes 1 | tf_op jit(solution)/shard_map/pallas_call | solution.py:173
  283.8 6.9 %shard_map.153 = (f32[1,1024]{1,0:T(1,128)S(1)}, bf16[256,2048]{1,0:T(8,128)(2,1)S(1)}, bf16[256,2048]{1,0:T(8,128)(2,1)S(1)}, bf16[256,2048]{1,0:T(8,128)(2,1)S(1)}, bf16[256,2048]{1,0:T(8,128)(2,1)}) custom-call(f32[592,1024]{1,0:T(8,128)} %convert_multiply_fusion.g_ref.refs_11_, bf16[592,2048]{1,0:T(8,128)(2,1)} %get-tuple-element.366.hidden_ref.refs_6_), custom_call_target="tpu_custom_call" | custom-call | flops 1 | bytes 1 | tf_op jit(solution)/shard_map/pallas_call | solution.py:173
  304.9 7.3 %shard_map.155 = (bf16[592,2048]{1,0:T(8,128)(2,1)}, f32[1,2048]{1,0:T(1,128)S(1)}) custom-call(f32[592,1024]{1,0:T(8,128)} %get-tuple-element.372.refs_0_, bf16[592,2048]{1,0:T(8,128)(2,1)} %get-tuple-element.373.refs_1_, bf16[128,2048]{1,0:T(8,128)(2,1)} %get-tuple-element.582.refs_2_.refs_1_, bf16[128,2048]{1,0:T(8,128)(2,1)S(1)} %copy-done.12, ...), custom_call_target="tpu_custom_call" | custom-call | flops 1 | bytes 1 | tf_op jit(solution)/shard_map/pallas_call | solution.py:173
  312.3 6.7 %shard_map.156.refs_0_ = bf16[592,1024]{1,0:T(8,128)(2,1)} custom-call(bf16[592,2048]{1,0:T(8,128)(2,1)} %get-tuple-element.380.refs_0_.low_ref, bf16[128,2048]{1,0:T(8,128)(2,1)} %get-tuple-element.584.refs_5_.refs_1_, bf16[128,2048]{1,0:T(8,128)(2,1)S(1)} %copy-done.25, bf16[128,2048]{1,0:T(8,128)(2,1)} %get-tuple-element.358.refs_7_.refs_3_, ...), custom_call_target="tpu_custom_call" | custom-call | flops 1 | bytes 1 | tf_op jit(solution)/shard_map/pallas_call | solution.py:173
  319.0 6.5 %shard_map.157 = (bf16[256,2048]{1,0:T(8,128)(2,1)S(1)}, bf16[256,2048]{1,0:T(8,128)(2,1)S(1)}, bf16[256,2048]{1,0:T(8,128)(2,1)S(1)}, bf16[256,2048]{1,0:T(8,128)(2,1)}) custom-call(bf16[592,1024]{1,0:T(8,128)(2,1)} %get-tuple-element.381.n_ref, bf16[592,2048]{1,0:T(8,128)(2,1)} %get-tuple-element.380.refs_0_.low_ref), custom_call_target="tpu_custom_call" | custom-call | flops 1 | bytes 1 | tf_op jit(solution)/shard_map/pallas_call | solution.py:173
  339.5 22.0 %shard_map.159 = (f32[592,1024]{1,0:T(8,128)}, bf16[592,1024]{1,0:T(8,128)(2,1)}, bf16[592,512]{1,0:T(8,128)(2,1)}, bf16[592,512]{1,0:T(8,128)(2,1)}, bf16[592,5...) custom-call(f32[592,1024]{1,0:T(8,128)} %get-tuple-element.372.refs_, ...), custom_call_target="tpu_custom_call" | custom-call | flops 1 | bytes 1 | tf_op jit(solution)/shard_map/pallas_call | solution.py:173
  387.6 7.9 %shard_map.163 = (bf16[256,2048]{1,0:T(8,128)(2,1)S(1)}, bf16[256,2048]{1,0:T(8,128)(2,1)}, bf16[256,2048]{1,0:T(8,128)(2,1)}, bf16[256,2048]{1,0:T(8,128)(2,1)}) custom-call(bf16[592,1024]{1,0:T(8,128)(2,1)} %get-tuple-element.406.n_ref, bf16[592,1024]{1,0:T(8,128)(2,1)} %get-tuple-element.407.dz_ref, bf16[592,512]{1,0:T(8,128)(2,1)S(1)} %copy-done.109, ...), custom_call_target="tpu_custom_call" | custom-call | flops 1 | bytes 1 | tf_op jit(solution)/shard_map/pallas_call | solution.py:173
  413.7 7.0 %shard_map.167 = (f32[1,1024]{1,0:T(1,128)S(1)}, bf16[256,2048]{1,0:T(8,128)(2,1)S(1)}, bf16[256,2048]{1,0:T(8,128)(2,1)S(1)}, bf16[256,2048]{1,0:T(8,128)(2,1)S(1)}, bf16[256,2048]{1,0:T(8,128)(2,1)}) custom-call(f32[592,1024]{1,0:T(8,128)} %get-tuple-element.423.refs_0_.g_ref, bf16[592,2048]{1,0:T(8,128)(2,1)} %get-tuple-element.318.refs_0_.hidden_ref), custom_call_target="tpu_custom_call" | custom-call | flops 1 | bytes 1 | tf_op jit(solution)/shard_map/pallas_call | solution.py:173
  422.7 7.4 %shard_map.165 = (bf16[592,2048]{1,0:T(8,128)(2,1)}, f32[1,2048]{1,0:T(1,128)S(1)}) custom-call(f32[592,1024]{1,0:T(8,128)} %get-tuple-element.423.refs_0_.g_ref, bf16[592,2048]{1,0:T(8,128)(2,1)} %get-tuple-element.424.refs_1_, bf16[128,2048]{1,0:T(8,128)(2,1)} %get-tuple-element.588.refs_1_.refs_2_, bf16[128,2048]{1,0:T(8,128)(2,1)S(1)} %copy-done.4, ...), custom_call_target="tpu_custom_call" | custom-call | flops 1 | bytes 1 | tf_op jit(solution)/shard_map/pallas_call | solution.py:173
  462.0 14.0 %collective-permute-done.67.refs_11_ = bf16[128,2048]{1,0:T(8,128)(2,1)S(1)} collective-permute-done((bf16[128,2048]{1,0:T(8,128)(2,1)S(1)}, bf16[128,2048]{1,0:T(8,128)(2,1)S(1)}, u32[]{:S(2)}, u32[]{:S(2)}) %collective-permute-start.67) | collective-permute-done | bytes 524320 | tf_op jit(solution)/shard_map/ppermute | solution.py:28
  493.1 21.0 %shard_map.172 = (f32[592,1024]{1,0:T(8,128)}, bf16[592,1024]{1,0:T(8,128)(2,1)}, bf16[592,512]{1,0:T(8,128)(2,1)}, bf16[592,512]{1,0:T(8,128)(2,1)}, bf16[592,5...) custom-call(f32[592,1024]{1,0:T(8,128)} %get-tuple-element.423.refs_, ...), custom_call_target="tpu_custom_call" | custom-call | flops 1 | bytes 1 | tf_op jit(solution)/shard_map/pallas_call | solution.py:173
  517.4 7.8 %shard_map.173 = (bf16[256,2048]{1,0:T(8,128)(2,1)S(1)}, bf16[256,2048]{1,0:T(8,128)(2,1)}, bf16[256,2048]{1,0:T(8,128)(2,1)}, bf16[256,2048]{1,0:T(8,128)(2,1)}) custom-call(bf16[592,1024]{1,0:T(8,128)(2,1)} %get-tuple-element.465.n_ref, bf16[592,1024]{1,0:T(8,128)(2,1)} %get-tuple-element.466.dz_ref, bf16[592,512]{1,0:T(8,128)(2,1)S(1)} %copy-done.112, ...), custom_call_target="tpu_custom_call" | custom-call | flops 1 | bytes 1 | tf_op jit(solution)/shard_map/pallas_call | solution.py:173
  556.8 9.2 %collective-permute-done.84.refs_10_ = bf16[256,2048]{1,0:T(8,128)(2,1)} collective-permute-done((bf16[256,2048]{1,0:T(8,128)(2,1)S(1)}, bf16[256,2048]{1,0:T(8,128)(2,1)}, u32[]{:S(2)}, u32[]{:S(2)}) %collective-permute-start.84) | collective-permute-done | bytes 1048608 | tf_op jit(solution)/shard_map/ppermute | solution.py:23
  565.9 9.8 %collective-permute-done.85.refs_11_ = bf16[256,2048]{1,0:T(8,128)(2,1)} collective-permute-done((bf16[256,2048]{1,0:T(8,128)(2,1)}, bf16[256,2048]{1,0:T(8,128)(2,1)}, u32[]{:S(2)}, u32[]{:S(2)}) %collective-permute-start.85) | collective-permute-done | bytes 1048608 | tf_op jit(solution)/shard_map/ppermute | solution.py:28
  588.7 9.9 %collective-permute-done.89 = bf16[16,2048]{1,0:T(8,128)(2,1)S(1)} collective-permute-done((bf16[16,2048]{1,0:T(8,128)(2,1)S(1)}, bf16[16,2048]{1,0:T(8,128)(2,1)S(1)}, u32[]{:S(2)}, u32[]{:S(2)}) %collective-permute-start.89) | collective-permute-done | bytes 65568 | tf_op jit(solution)/shard_map/ppermute | solution.py:28
  614.2 20.8 %reduce-scatter.15.cloned.1.call-done = bf16[272,512]{1,0:T(8,128)(2,1)} async-done(((bf16[272,2048]{1,0:T(8,128)(2,1)}), bf16[272,512]{1,0:T(8,128)(2,1)}) %reduce-scatter.15.cloned.1.call-update) | async-done | bytes 278544 | tf_op jit(solution)/shard_map/reduce_scatter | solution.py:105
  (820 shorter events, 350.2 us)
Async XLA Ops:
  7.2 38.8 %all-gather.7.cloned.1.call-start = ((), (), s32[]{:S(2)}) async-start(), calls=%async_computation.6 | async-start | bytes 1392640 | tf_op jit(solution)/shard_map/all_gather | solution.py:49
  14.9 72.7 %all-gather.9.cloned.1.call-start = ((), (), s32[]{:S(2)}) async-start(), calls=%async_computation.7 | async-start | bytes 1310720 | tf_op jit(solution)/shard_map/all_gather | solution.py:49
  52.0 35.5 %collective-permute-start.4 = (bf16[128,2048]{1,0:T(8,128)(2,1)S(1)}, bf16[128,2048]{1,0:T(8,128)(2,1)S(1)}, u32[]{:S(2)}, u32[]{:S(2)}) collective-permute-start(bf16[128,2048]{1,0:T(8,128)(2,1)S(1)} %get-tuple-element.580.refs_5_.refs_10_), channel_id=1, source_target_pairs={{0,4},{4,0},{8,12},{12,8},{1,5},{5,1},{9,13},{13,9},{2,6},{6,2},{1... | collective-permute-start | bytes 1572872 | tf_op jit(solution)/shard_map/ppermute | solution.py:23
  53.2 82.1 %all-gather.11.cloned.1.call-start = ((), (), s32[]{:S(2)}) async-start(), calls=%async_computation.8 | async-start | bytes 1310720 | tf_op jit(solution)/shard_map/all_gather | solution.py:49
  53.7 33.9 %collective-permute-start.6 = (bf16[128,2048]{1,0:T(8,128)(2,1)S(1)}, bf16[128,2048]{1,0:T(8,128)(2,1)S(1)}, u32[]{:S(2)}, u32[]{:S(2)}) collective-permute-start(bf16[128,2048]{1,0:T(8,128)(2,1)S(1)} %get-tuple-element.579.refs_9_.refs_14_), channel_id=1, source_target_pairs={{0,8},{4,12},{8,0},{12,4},{1,9},{5,13},{9,1},{13,5},{2,10},{6,14},... | collective-permute-start | bytes 1572872 | tf_op jit(solution)/shard_map/ppermute | solution.py:28
  97.6 74.6 %all-gather.13.cloned.1.call-start = ((), (), s32[]{:S(2)}) async-start(), calls=%async_computation.9 | async-start | bytes 1310720 | tf_op jit(solution)/shard_map/all_gather | solution.py:49
  138.3 78.3 %all-gather.15.cloned.1.call-start = ((), (), s32[]{:S(2)}) async-start(), calls=%async_computation.10 | async-start | bytes 1310720 | tf_op jit(solution)/shard_map/all_gather | solution.py:49
  179.1 69.7 %all-gather.17.cloned.1.call-start = ((), (), s32[]{:S(2)}) async-start(), calls=%async_computation.11 | async-start | bytes 1310720 | tf_op jit(solution)/shard_map/all_gather | solution.py:49
  220.0 182.6 %reduce-scatter.7.cloned.1.call-start = ((), (), s32[]{:S(2)}) async-start(), calls=%async_computation.12 | async-start | bytes 1310720 | tf_op jit(solution)/shard_map/reduce_scatter | solution.py:105
  331.6 37.0 %collective-permute-start.57 = (bf16[256,2048]{1,0:T(8,128)(2,1)}, bf16[256,2048]{1,0:T(8,128)(2,1)}, u32[]{:S(2)}, u32[]{:S(2)}) collective-permute-start(bf16[256,2048]{1,0:T(8,128)(2,1)} %get-tuple-element.401), channel_id=1, source_target_pairs={{0,4},{4,0},{8,12},{12,8},{1,5},{5,1},{9,13},{13,9},{2,6},{6,2},{1... | collective-permute-start | bytes 3145736 | tf_op jit(solution)/shard_map/ppermute | solution.py:23
  332.8 35.8 %collective-permute-start.58 = (bf16[256,2048]{1,0:T(8,128)(2,1)}, bf16[256,2048]{1,0:T(8,128)(2,1)}, u32[]{:S(2)}, u32[]{:S(2)}) collective-permute-start(bf16[256,2048]{1,0:T(8,128)(2,1)} %get-tuple-element.402), channel_id=1, source_target_pairs={{0,8},{4,12},{8,0},{12,4},{1,9},{5,13},{9,1},{13,5},{2,10},{6,14},... | collective-permute-start | bytes 3145736 | tf_op jit(solution)/shard_map/ppermute | solution.py:28
  373.2 63.2 %reduce-scatter.9.cloned.1.call-start = ((), (), s32[]{:S(2)}) async-start(), calls=%async_computation.13 | async-start | bytes 1310720 | tf_op jit(solution)/shard_map/reduce_scatter | solution.py:105
  406.2 120.3 %reduce-scatter.11.cloned.1.call-start = ((), (), s32[]{:S(2)}) async-start(), calls=%async_computation.14 | async-start | bytes 1310720 | tf_op jit(solution)/shard_map/reduce_scatter | solution.py:105
  441.3 34.8 %collective-permute-start.69 = (bf16[256,2048]{1,0:T(8,128)(2,1)S(1)}, bf16[256,2048]{1,0:T(8,128)(2,1)S(1)}, u32[]{:S(2)}, u32[]{:S(2)}) collective-permute-start(bf16[256,2048]{1,0:T(8,128)(2,1)S(1)} %copy-done.94), channel_id=1, source_target_pairs={{0,4},{4,0},{8,12},{12,8},{1,5},{5,1},{9,13},{13,9},{2,6},{6,2},{1... | collective-permute-start | bytes 3145736 | tf_op jit(solution)/shard_map/ppermute | solution.py:23
  441.6 34.5 %collective-permute-start.70 = (bf16[256,2048]{1,0:T(8,128)(2,1)S(1)}, bf16[256,2048]{1,0:T(8,128)(2,1)S(1)}, u32[]{:S(2)}, u32[]{:S(2)}) collective-permute-start(bf16[256,2048]{1,0:T(8,128)(2,1)S(1)} %copy-done.96), channel_id=1, source_target_pairs={{0,8},{4,12},{8,0},{12,4},{1,9},{5,13},{9,1},{13,5},{2,10},{6,14},... | collective-permute-start | bytes 3145736 | tf_op jit(solution)/shard_map/ppermute | solution.py:28
  480.4 95.4 %reduce-scatter.13.cloned.1.call-start = ((), (), s32[]{:S(2)}) async-start(), calls=%async_computation.15 | async-start | bytes 1310720 | tf_op jit(solution)/shard_map/reduce_scatter | solution.py:105
  486.3 40.1 %collective-permute-start.74 = (bf16[128,2048]{1,0:T(8,128)(2,1)}, bf16[128,2048]{1,0:T(8,128)(2,1)}, u32[]{:S(2)}, u32[]{:S(2)}) collective-permute-start(bf16[128,2048]{1,0:T(8,128)(2,1)} %get-tuple-element.551), channel_id=1, source_target_pairs={{0,4},{4,0},{8,12},{12,8},{1,5},{5,1},{9,13},{13,9},{2,6},{6,2},{1... | collective-permute-start | bytes 1572872 | tf_op jit(solution)/shard_map/ppermute | solution.py:23
  487.5 38.9 %collective-permute-start.75 = (bf16[256,2048]{1,0:T(8,128)(2,1)S(1)}, bf16[256,2048]{1,0:T(8,128)(2,1)}, u32[]{:S(2)}, u32[]{:S(2)}) collective-permute-start(bf16[256,2048]{1,0:T(8,128)(2,1)S(1)} %copy-done.98), channel_id=1, source_target_pairs={{0,4},{4,0},{8,12},{12,8},{1,5},{5,1},{9,13},{13,9},{2,6},{6,2},{1... | collective-permute-start | bytes 3145736 | tf_op jit(solution)/shard_map/ppermute | solution.py:23
  487.8 38.6 %collective-permute-start.76 = (bf16[256,2048]{1,0:T(8,128)(2,1)S(1)}, bf16[256,2048]{1,0:T(8,128)(2,1)}, u32[]{:S(2)}, u32[]{:S(2)}) collective-permute-start(bf16[256,2048]{1,0:T(8,128)(2,1)S(1)} %copy-done.100), channel_id=1, source_target_pairs={{0,8},{4,12},{8,0},{12,4},{1,9},{5,13},{9,1},{13,5},{2,10},{6,14},... | collective-permute-start | bytes 3145736 | tf_op jit(solution)/shard_map/ppermute | solution.py:28
  491.6 34.8 %collective-permute-start.73 = (bf16[128,2048]{1,0:T(8,128)(2,1)}, bf16[128,2048]{1,0:T(8,128)(2,1)S(1)}, u32[]{:S(2)}, u32[]{:S(2)}) collective-permute-start(bf16[128,2048]{1,0:T(8,128)(2,1)} %get-tuple-element.553), channel_id=1, source_target_pairs={{0,8},{4,12},{8,0},{12,4},{1,9},{5,13},{9,1},{13,5},{2,10},{6,14},... | collective-permute-start | bytes 1572872 | tf_op jit(solution)/shard_map/ppermute | solution.py:28
  491.9 34.5 %collective-permute-start.72 = (bf16[296,256]{1,0:T(8,128)(2,1)S(1)}, bf16[296,256]{1,0:T(8,128)(2,1)S(1)}, u32[]{:S(2)}, u32[]{:S(2)}) collective-permute-start(bf16[296,256]{1,0:T(8,128)(2,1)S(1)} %copy-done.165), channel_id=1, source_target_pairs={{0,3},{1,0},{2,1},{3,2},{4,7},{5,4},{6,5},{7,6},{8,11},{9,8},{10,9... | collective-permute-start | bytes 454664 | tf_op jit(solution)/shard_map/ppermute | solution.py:525
  536.3 72.9 %reduce-scatter.17.cloned.1.call-start = ((), (), s32[]{:S(2)}) async-start(), calls=%async_computation.17 | async-start | bytes 1310720 | tf_op jit(solution)/shard_map/reduce_scatter | solution.py:105
  540.9 34.8 %collective-permute-start.85 = (bf16[256,2048]{1,0:T(8,128)(2,1)}, bf16[256,2048]{1,0:T(8,128)(2,1)}, u32[]{:S(2)}, u32[]{:S(2)}) collective-permute-start(bf16[256,2048]{1,0:T(8,128)(2,1)} %get-tuple-element.507), channel_id=1, source_target_pairs={{0,8},{4,12},{8,0},{12,4},{1,9},{5,13},{9,1},{13,5},{2,10},{6,14},... | collective-permute-start | bytes 3145736 | tf_op jit(solution)/shard_map/ppermute | solution.py:28
  580.2 54.8 %reduce-scatter.15.cloned.1.call-start = ((), (), s32[]{:S(2)}) async-start(), calls=%async_computation.16 | async-start | bytes 1392640 | tf_op jit(solution)/shard_map/reduce_scatter | solution.py:105
  (271 other events, 2517.0 us)
Sparse Core Ops, SparseCore 0:
  15.0 30.8 all-gather.6
  53.4 29.9 all-gather.8
  97.7 27.5 all-gather.10
  138.4 32.3 all-gather.12
  179.2 29.8 all-gather.14
  220.1 26.8 all-gather.16
  373.3 26.7 reduce-scatter.6
  406.3 29.9 reduce-scatter.8
  480.5 30.7 reduce-scatter.10
  536.4 28.0 reduce-scatter.12
  580.3 25.5 reduce-scatter.16
  608.2 26.7 reduce-scatter.14

commit v14 on v13

--- a/solution.py
+++ b/solution.py
@@ -784,6 +784,7 @@
 
     grads, got, moved, settled = [None] * number, [None] * number, [None] * number, [None] * number
     made = [0, 1, 3, 4, 5, 6]
+    column_at = [4, 5, 6, 7]
     grad = cotangent
     last_down = weights_of(number - 1)
     params[1]["down"] = last_down
@@ -803,9 +804,10 @@
             elif r == made[c] + 2:
                 stay, come = scatter_two(*grads[c][2:], got[c])
                 moved[c] = [*stay, *come]
-                slots.append((moved, c, len(moved[c])))
-                tied += moved[c]
-            elif r == made[c] + 3:
+                if r < 7:
+                    slots.append((moved, c, len(moved[c])))
+                    tied += moved[c]
+            elif c < len(column_at) and r == column_at[c]:
                 settled[c] = scatter_column(moved[c][:2], moved[c][2:])
                 slots.append((settled, c, 0))
                 tied.append(settled[c])
@@ -833,6 +835,9 @@
             grad, total["one"] = value_backward(dmid, part, swap(part), one["u"], rows, layer == 1)
             carry = [grad]
             if r == 7:
+                done = tie([grad, *moved[4]], [])
+                grad, moved[4] = done[0], done[1:]
+                settled[4] = scatter_column(moved[4][:2], moved[4][2:])
                 one_scale = jnp.ones((), jnp.float32)
                 no_bias = jnp.zeros((1, grad.shape[1]), jnp.float32)
                 carry = [small_grads(), *shifts(image_rows(one_scale, [grad], no_bias))]
@@ -887,7 +892,6 @@
         little = little.astype(jnp.bfloat16)
 
     last = number - 1
-    settled[last - 1] = scatter_column(moved[last - 1][:2], moved[last - 1][2:])
     stay, come = scatter_two(*grads[last][2:], got[last])
     grad_rows, out_rows = by_image(grad_blocks), by_image(out_blocks)
     if come:

time: 658 us -> 654 us (level)
  waiting for transfers between devices: 180 us -> 161 us
  other arithmetic: 69.2 us -> 76.9 us
  local copies, waits for them, and re-layouts: 99 us -> 106 us
    ppermute x32, waiting for transfers between devices: 58.5 us -> 41.8 us  [swap_x(): return lax.ppermute(value, 'dp', [(i, i ^ 1) for i in range(n)])]
    ppermute x12, waiting for transfers between devices: 31.8 us -> 42.8 us  [shift(): return lax.ppermute(block, 'tensor', [(i, (i + d) % n) for i in range(n)])]
    unnamed x394 -> x386, local copies, waits for them, and re-layouts: 64.2 us -> 61.9 us
  transfers between devices with their start and end apart: 107 -> 107, of which waited for: 30 -> 26; matrix products, arithmetic and copies ran while one was open for 14% -> 18% of each run, Pallas kernels for 30% -> 30%
where the time goes in v14:
time: 654 us; the launch traced here: 646 us
  Pallas kernels  197 us (30%)
  waiting for transfers between devices  161 us (25%)
  local copies, waits for them, and re-layouts  106 us (16%)
  starting transfers between devices  87.2 us (13%)
  other arithmetic  76.9 us (12%)
  between operations  17.4 us (3%)
    pallas_call x20, Pallas kernels, run(): pl.pallas_call(kernel, out_shape=list(outs), in_specs=[block] * len(ins),...  191 us
    unnamed x386, local copies, waits for them, and re-layouts  61.9 us
    ppermute x12, waiting for transfers between devices, shift(): return lax.ppermute(block, 'tensor', [(i, (i + d) % n) for i in range(n)])  42.8 us
    ppermute x32, waiting for transfers between devices, swap_x(): return lax.ppermute(value, 'dp', [(i, i ^ 1) for i in range(n)])  41.8 us
    ppermute x32, waiting for transfers between devices, swap_y(): return lax.ppermute(value, 'dp', [(i, i ^ 2) for i in range(n)])  31.6 us
    convert_element_type x12, other arithmetic, scatter_two(): send.append(add(keep[half:], new[half:]).astype(jnp.bfloat16))  27.9 us
    ppermute x32, starting transfers between devices, swap_y(): return lax.ppermute(value, 'dp', [(i, i ^ 2) for i in range(n)])  24.4 us
    ppermute x32, starting transfers between devices, swap_x(): return lax.ppermute(value, 'dp', [(i, i ^ 1) for i in range(n)])  24.2 us
  transfers between devices with their start and end apart: 107, of which 26 were waited for; matrix products, arithmetic and copies ran while one was open for 18% of the time, Pallas kernels for 30%

profile of v14, /device:TPU:1, one launch (start us, length us, event | category | flops | bytes accessed | tf_op | source)
XLA Modules:
  0.0 646.1 jit_solution(8232138285152876052)
XLA Ops:
  23.2 22.7 %all-gather.7.cloned.1.call-done.refs_0_ = bf16[272,2048]{1,0:T(8,128)(2,1)} async-done(((bf16[272,512]{1,0:T(8,128)(2,1)}), bf16[272,2048]{1,0:T(8,128)(2,1)}) %all-gather.7.cloned.1.call-update) | async-done | bytes 1114128 | tf_op jit(solution)/shard_map/all_gather | solution.py:49
  105.8 15.4 %shard_map.138 = (f32[592,1024]{1,0:T(8,128)}, bf16[592,1024]{1,0:T(8,128)(2,1)}, bf16[592,512]{1,0:T(8,128)(2,1)}, bf16[592,512]{1,0:T(8,128)(2,1)}, bf16[592,5...) custom-call(f32[592,1024]{1,0:T(8,128)} %maximum_convert_fusion.refs_0_, ...), custom_call_target="tpu_custom_call" | custom-call | flops 1 | bytes 1 | tf_op jit(solution)/shard_map/pallas_call | solution.py:173
  145.3 10.2 %shard_map.141 = (f32[592,1024]{1,0:T(8,128)}, bf16[592,1024]{1,0:T(8,128)(2,1)}, bf16[592,2048]{1,0:T(8,128)(2,1)}, bf16[592,2048]{1,0:T(8,128)(2,1)}) custom-call(f32[592,1024]{1,0:T(8,128)} %get-tuple-element.300.refs_0_.u_ref, bf16[592,1024]{1,0:T(8,128)(2,1)} %get-tuple-element.301.refs_1_, bf16[592,1024]{1,0:T(8,128)(2,1)} %collective-permute-done.24.refs_2_, ...), custom_call_target="tpu_custom_call" | custom-call | flops 1 | bytes 1 | tf_op jit(solution)/shard_map/pallas_call | solution.py:173
  158.1 14.4 %collective-permute-done.29.refs_10_ = bf16[296,256]{1,0:T(8,128)(2,1)S(1)} collective-permute-done((bf16[296,256]{1,0:T(8,128)(2,1)S(1)}, bf16[296,256]{1,0:T(8,128)(2,1)S(1)}, u32[]{:S(2)}, u32[]{:S(2)}) %collective-permute-start.29) | collective-permute-done | bytes 151584 | tf_op jit(solution)/shard_map/ppermute | solution.py:525
  199.8 8.7 %collective-permute-done.36.refs_11_ = bf16[296,256]{1,0:T(8,128)(2,1)S(1)} collective-permute-done((bf16[296,256]{1,0:T(8,128)(2,1)S(1)}, bf16[296,256]{1,0:T(8,128)(2,1)S(1)}, u32[]{:S(2)}, u32[]{:S(2)}) %collective-permute-start.36) | collective-permute-done | bytes 151584 | tf_op jit(solution)/shard_map/ppermute | solution.py:525
  208.4 8.4 %collective-permute-done.33.refs_4_ = bf16[128,2048]{1,0:T(8,128)(2,1)S(1)} collective-permute-done((bf16[128,2048]{1,0:T(8,128)(2,1)}, bf16[128,2048]{1,0:T(8,128)(2,1)S(1)}, u32[]{:S(2)}, u32[]{:S(2)}) %collective-permute-start.33) | collective-permute-done | bytes 524320 | tf_op jit(solution)/shard_map/ppermute | solution.py:23
  226.0 16.9 %shard_map.147 = (f32[592,1024]{1,0:T(8,128)}, bf16[592,1024]{1,0:T(8,128)(2,1)}, bf16[592,512]{1,0:T(8,128)(2,1)}, bf16[592,512]{1,0:T(8,128)(2,1)}, bf16[592,5...) custom-call(f32[592,1024]{1,0:T(8,128)} %get-tuple-element.335.refs_0_.refs, ...), custom_call_target="tpu_custom_call" | custom-call | flops 1 | bytes 1 | tf_op jit(solution)/shard_map/pallas_call | solution.py:173
  248.9 11.2 %collective-permute-done.41.refs_4_ = bf16[128,2048]{1,0:T(8,128)(2,1)} collective-permute-done((bf16[128,2048]{1,0:T(8,128)(2,1)}, bf16[128,2048]{1,0:T(8,128)(2,1)}, u32[]{:S(2)}, u32[]{:S(2)}) %collective-permute-start.41) | collective-permute-done | bytes 524320 | tf_op jit(solution)/shard_map/ppermute | solution.py:23
  266.7 10.8 %shard_map.151 = (f32[592,1024]{1,0:T(8,128)}, bf16[592,1024]{1,0:T(8,128)(2,1)}, bf16[592,2048]{1,0:T(8,128)(2,1)}, bf16[592,2048]{1,0:T(8,128)(2,1)}) custom-call(f32[592,1024]{1,0:T(8,128)} %get-tuple-element.355.refs_0_.u_ref, bf16[592,1024]{1,0:T(8,128)(2,1)} %get-tuple-element.356.refs_1_, bf16[592,1024]{1,0:T(8,128)(2,1)} %copy-done.162, ...), custom_call_target="tpu_custom_call" | custom-call | flops 1 | bytes 1 | tf_op jit(solution)/shard_map/pallas_call | solution.py:173
  284.2 6.9 %shard_map.153 = (f32[1,1024]{1,0:T(1,128)S(1)}, bf16[256,2048]{1,0:T(8,128)(2,1)S(1)}, bf16[256,2048]{1,0:T(8,128)(2,1)S(1)}, bf16[256,2048]{1,0:T(8,128)(2,1)S(1)}, bf16[256,2048]{1,0:T(8,128)(2,1)}) custom-call(f32[592,1024]{1,0:T(8,128)} %convert_multiply_fusion.g_ref.refs_11_, bf16[592,2048]{1,0:T(8,128)(2,1)} %get-tuple-element.367.hidden_ref.refs_6_), custom_call_target="tpu_custom_call" | custom-call | flops 1 | bytes 1 | tf_op jit(solution)/shard_map/pallas_call | solution.py:173
  305.1 7.3 %shard_map.155 = (bf16[592,2048]{1,0:T(8,128)(2,1)}, f32[1,2048]{1,0:T(1,128)S(1)}) custom-call(f32[592,1024]{1,0:T(8,128)} %get-tuple-element.373.refs_0_, bf16[592,2048]{1,0:T(8,128)(2,1)} %get-tuple-element.374.refs_1_, bf16[128,2048]{1,0:T(8,128)(2,1)} %get-tuple-element.584.refs_2_.refs_1_, bf16[128,2048]{1,0:T(8,128)(2,1)S(1)} %copy-done.13, ...), custom_call_target="tpu_custom_call" | custom-call | flops 1 | bytes 1 | tf_op jit(solution)/shard_map/pallas_call | solution.py:173
  312.4 6.5 %shard_map.156.refs_0_ = bf16[592,1024]{1,0:T(8,128)(2,1)} custom-call(bf16[592,2048]{1,0:T(8,128)(2,1)} %get-tuple-element.381.refs_0_.low_ref, bf16[128,2048]{1,0:T(8,128)(2,1)} %get-tuple-element.586.refs_5_.refs_1_, bf16[128,2048]{1,0:T(8,128)(2,1)S(1)} %copy-done.26, bf16[128,2048]{1,0:T(8,128)(2,1)} %get-tuple-element.359.refs_7_.refs_3_, ...), custom_call_target="tpu_custom_call" | custom-call | flops 1 | bytes 1 | tf_op jit(solution)/shard_map/pallas_call | solution.py:173
  318.9 6.5 %shard_map.157 = (bf16[256,2048]{1,0:T(8,128)(2,1)S(1)}, bf16[256,2048]{1,0:T(8,128)(2,1)S(1)}, bf16[256,2048]{1,0:T(8,128)(2,1)S(1)}, bf16[256,2048]{1,0:T(8,128)(2,1)}) custom-call(bf16[592,1024]{1,0:T(8,128)(2,1)} %get-tuple-element.382.n_ref, bf16[592,2048]{1,0:T(8,128)(2,1)} %get-tuple-element.381.refs_0_.low_ref), custom_call_target="tpu_custom_call" | custom-call | flops 1 | bytes 1 | tf_op jit(solution)/shard_map/pallas_call | solution.py:173
  347.8 22.2 %shard_map.159 = (f32[592,1024]{1,0:T(8,128)}, bf16[592,1024]{1,0:T(8,128)(2,1)}, bf16[592,512]{1,0:T(8,128)(2,1)}, bf16[592,512]{1,0:T(8,128)(2,1)}, bf16[592,5...) custom-call(f32[592,1024]{1,0:T(8,128)} %get-tuple-element.373.refs_, ...), custom_call_target="tpu_custom_call" | custom-call | flops 1 | bytes 1 | tf_op jit(solution)/shard_map/pallas_call | solution.py:173
  382.6 7.8 %shard_map.163 = (bf16[256,2048]{1,0:T(8,128)(2,1)S(1)}, bf16[256,2048]{1,0:T(8,128)(2,1)}, bf16[256,2048]{1,0:T(8,128)(2,1)}, bf16[256,2048]{1,0:T(8,128)(2,1)}) custom-call(bf16[592,1024]{1,0:T(8,128)(2,1)} %get-tuple-element.407.n_ref, bf16[592,1024]{1,0:T(8,128)(2,1)} %get-tuple-element.408.dz_ref, bf16[592,512]{1,0:T(8,128)(2,1)S(1)} %copy-done.108, ...), custom_call_target="tpu_custom_call" | custom-call | flops 1 | bytes 1 | tf_op jit(solution)/shard_map/pallas_call | solution.py:173
  405.9 7.1 %shard_map.167 = (f32[1,1024]{1,0:T(1,128)S(1)}, bf16[256,2048]{1,0:T(8,128)(2,1)S(1)}, bf16[256,2048]{1,0:T(8,128)(2,1)S(1)}, bf16[256,2048]{1,0:T(8,128)(2,1)S(1)}, bf16[256,2048]{1,0:T(8,128)(2,1)}) custom-call(f32[592,1024]{1,0:T(8,128)} %get-tuple-element.420.refs_0_.g_ref, bf16[592,2048]{1,0:T(8,128)(2,1)} %get-tuple-element.319.refs_0_.hidden_ref), custom_call_target="tpu_custom_call" | custom-call | flops 1 | bytes 1 | tf_op jit(solution)/shard_map/pallas_call | solution.py:173
  414.9 7.4 %shard_map.165 = (bf16[592,2048]{1,0:T(8,128)(2,1)}, f32[1,2048]{1,0:T(1,128)S(1)}) custom-call(f32[592,1024]{1,0:T(8,128)} %get-tuple-element.420.refs_0_.g_ref, bf16[592,2048]{1,0:T(8,128)(2,1)} %get-tuple-element.421.refs_1_, bf16[128,2048]{1,0:T(8,128)(2,1)} %get-tuple-element.590.refs_1_.refs_2_, bf16[128,2048]{1,0:T(8,128)(2,1)S(1)} %copy-done.5, ...), custom_call_target="tpu_custom_call" | custom-call | flops 1 | bytes 1 | tf_op jit(solution)/shard_map/pallas_call | solution.py:173
  425.8 8.5 %collective-permute-done.63.refs_2_ = bf16[296,256]{1,0:T(8,128)(2,1)S(1)} collective-permute-done((bf16[296,256]{1,0:T(8,128)(2,1)S(1)}, bf16[296,256]{1,0:T(8,128)(2,1)S(1)}, u32[]{:S(2)}, u32[]{:S(2)}) %collective-permute-start.63) | collective-permute-done | bytes 151584 | tf_op jit(solution)/shard_map/ppermute | solution.py:525
  450.0 6.5 %shard_map.170 = (bf16[256,2048]{1,0:T(8,128)(2,1)S(1)}, bf16[256,2048]{1,0:T(8,128)(2,1)S(1)}, bf16[256,2048]{1,0:T(8,128)(2,1)S(1)}, bf16[256,2048]{1,0:T(8,128)(2,1)}) custom-call(bf16[592,1024]{1,0:T(8,128)(2,1)} %get-tuple-element.439.n_ref, bf16[592,2048]{1,0:T(8,128)(2,1)} %get-tuple-element.434.refs_0_.low_ref), custom_call_target="tpu_custom_call" | custom-call | flops 1 | bytes 1 | tf_op jit(solution)/shard_map/pallas_call | solution.py:173
  459.5 15.3 %collective-permute-done.67.refs_12_ = bf16[128,2048]{1,0:T(8,128)(2,1)} collective-permute-done((bf16[128,2048]{1,0:T(8,128)(2,1)S(1)}, bf16[128,2048]{1,0:T(8,128)(2,1)}, u32[]{:S(2)}, u32[]{:S(2)}) %collective-permute-start.67) | collective-permute-done | bytes 524320 | tf_op jit(solution)/shard_map/ppermute | solution.py:28
  492.4 21.2 %shard_map.172 = (f32[592,1024]{1,0:T(8,128)}, bf16[592,1024]{1,0:T(8,128)(2,1)}, bf16[592,512]{1,0:T(8,128)(2,1)}, bf16[592,512]{1,0:T(8,128)(2,1)}, bf16[592,5...) custom-call(f32[592,1024]{1,0:T(8,128)} %get-tuple-element.420.refs_, ...), custom_call_target="tpu_custom_call" | custom-call | flops 1 | bytes 1 | tf_op jit(solution)/shard_map/pallas_call | solution.py:173
  516.8 7.8 %shard_map.173 = (bf16[256,2048]{1,0:T(8,128)(2,1)S(1)}, bf16[256,2048]{1,0:T(8,128)(2,1)}, bf16[256,2048]{1,0:T(8,128)(2,1)}, bf16[256,2048]{1,0:T(8,128)(2,1)}) custom-call(bf16[592,1024]{1,0:T(8,128)(2,1)} %get-tuple-element.466.n_ref, bf16[592,1024]{1,0:T(8,128)(2,1)} %get-tuple-element.467.dz_ref, bf16[592,512]{1,0:T(8,128)(2,1)S(1)} %copy-done.111, ...), custom_call_target="tpu_custom_call" | custom-call | flops 1 | bytes 1 | tf_op jit(solution)/shard_map/pallas_call | solution.py:173
  586.5 8.8 %collective-permute-done.89 = bf16[16,2048]{1,0:T(8,128)(2,1)S(1)} collective-permute-done((bf16[16,2048]{1,0:T(8,128)(2,1)S(1)}, bf16[16,2048]{1,0:T(8,128)(2,1)S(1)}, u32[]{:S(2)}, u32[]{:S(2)}) %collective-permute-start.89) | collective-permute-done | bytes 65568 | tf_op jit(solution)/shard_map/ppermute | solution.py:28
  612.9 18.0 %reduce-scatter.15.cloned.1.call-done = bf16[272,512]{1,0:T(8,128)(2,1)} async-done(((bf16[272,2048]{1,0:T(8,128)(2,1)}), bf16[272,512]{1,0:T(8,128)(2,1)}) %reduce-scatter.15.cloned.1.call-update) | async-done | bytes 278544 | tf_op jit(solution)/shard_map/reduce_scatter | solution.py:105
  (814 shorter events, 351.9 us)
Async XLA Ops:
  7.2 38.8 %all-gather.7.cloned.1.call-start = ((), (), s32[]{:S(2)}) async-start(), calls=%async_computation.6 | async-start | bytes 1392640 | tf_op jit(solution)/shard_map/all_gather | solution.py:49
  14.9 72.7 %all-gather.9.cloned.1.call-start = ((), (), s32[]{:S(2)}) async-start(), calls=%async_computation.7 | async-start | bytes 1310720 | tf_op jit(solution)/shard_map/all_gather | solution.py:49
  52.0 35.5 %collective-permute-start.4 = (bf16[128,2048]{1,0:T(8,128)(2,1)S(1)}, bf16[128,2048]{1,0:T(8,128)(2,1)S(1)}, u32[]{:S(2)}, u32[]{:S(2)}) collective-permute-start(bf16[128,2048]{1,0:T(8,128)(2,1)S(1)} %get-tuple-element.582.refs_5_.refs_10_), channel_id=1, source_target_pairs={{0,4},{4,0},{8,12},{12,8},{1,5},{5,1},{9,13},{13,9},{2,6},{6,2},{1... | collective-permute-start | bytes 1572872 | tf_op jit(solution)/shard_map/ppermute | solution.py:23
  53.2 82.5 %all-gather.11.cloned.1.call-start = ((), (), s32[]{:S(2)}) async-start(), calls=%async_computation.8 | async-start | bytes 1310720 | tf_op jit(solution)/shard_map/all_gather | solution.py:49
  97.6 75.0 %all-gather.13.cloned.1.call-start = ((), (), s32[]{:S(2)}) async-start(), calls=%async_computation.9 | async-start | bytes 1310720 | tf_op jit(solution)/shard_map/all_gather | solution.py:49
  138.7 78.2 %all-gather.15.cloned.1.call-start = ((), (), s32[]{:S(2)}) async-start(), calls=%async_computation.10 | async-start | bytes 1310720 | tf_op jit(solution)/shard_map/all_gather | solution.py:49
  179.4 69.5 %all-gather.17.cloned.1.call-start = ((), (), s32[]{:S(2)}) async-start(), calls=%async_computation.11 | async-start | bytes 1310720 | tf_op jit(solution)/shard_map/all_gather | solution.py:49
  220.3 205.4 %reduce-scatter.7.cloned.1.call-start = ((), (), s32[]{:S(2)}) async-start(), calls=%async_computation.12 | async-start | bytes 1310720 | tf_op jit(solution)/shard_map/reduce_scatter | solution.py:105
  331.5 38.5 %collective-permute-start.57 = (bf16[256,2048]{1,0:T(8,128)(2,1)}, bf16[256,2048]{1,0:T(8,128)(2,1)}, u32[]{:S(2)}, u32[]{:S(2)}) collective-permute-start(bf16[256,2048]{1,0:T(8,128)(2,1)} %get-tuple-element.402), channel_id=1, source_target_pairs={{0,4},{4,0},{8,12},{12,8},{1,5},{5,1},{9,13},{13,9},{2,6},{6,2},{1... | collective-permute-start | bytes 3145736 | tf_op jit(solution)/shard_map/ppermute | solution.py:23
  332.7 37.3 %collective-permute-start.58 = (bf16[256,2048]{1,0:T(8,128)(2,1)}, bf16[256,2048]{1,0:T(8,128)(2,1)}, u32[]{:S(2)}, u32[]{:S(2)}) collective-permute-start(bf16[256,2048]{1,0:T(8,128)(2,1)} %get-tuple-element.403), channel_id=1, source_target_pairs={{0,8},{4,12},{8,0},{12,4},{1,9},{5,13},{9,1},{13,5},{2,10},{6,14},... | collective-permute-start | bytes 3145736 | tf_op jit(solution)/shard_map/ppermute | solution.py:28
  335.9 34.1 %collective-permute-start.56 = (bf16[128,2048]{1,0:T(8,128)(2,1)}, bf16[128,2048]{1,0:T(8,128)(2,1)}, u32[]{:S(2)}, u32[]{:S(2)}) collective-permute-start(bf16[128,2048]{1,0:T(8,128)(2,1)} %get-tuple-element.565), channel_id=1, source_target_pairs={{0,4},{4,0},{8,12},{12,8},{1,5},{5,1},{9,13},{13,9},{2,6},{6,2},{1... | collective-permute-start | bytes 1572872 | tf_op jit(solution)/shard_map/ppermute | solution.py:23
  373.7 101.1 %reduce-scatter.9.cloned.1.call-start = ((), (), s32[]{:S(2)}) async-start(), calls=%async_computation.13 | async-start | bytes 1310720 | tf_op jit(solution)/shard_map/reduce_scatter | solution.py:105
  404.9 122.2 %reduce-scatter.11.cloned.1.call-start = ((), (), s32[]{:S(2)}) async-start(), calls=%async_computation.14 | async-start | bytes 1310720 | tf_op jit(solution)/shard_map/reduce_scatter | solution.py:105
  439.8 35.0 %collective-permute-start.69 = (bf16[256,2048]{1,0:T(8,128)(2,1)S(1)}, bf16[256,2048]{1,0:T(8,128)(2,1)S(1)}, u32[]{:S(2)}, u32[]{:S(2)}) collective-permute-start(bf16[256,2048]{1,0:T(8,128)(2,1)S(1)} %copy-done.92), channel_id=1, source_target_pairs={{0,4},{4,0},{8,12},{12,8},{1,5},{5,1},{9,13},{13,9},{2,6},{6,2},{1... | collective-permute-start | bytes 3145736 | tf_op jit(solution)/shard_map/ppermute | solution.py:23
  440.1 34.7 %collective-permute-start.70 = (bf16[256,2048]{1,0:T(8,128)(2,1)S(1)}, bf16[256,2048]{1,0:T(8,128)(2,1)}, u32[]{:S(2)}, u32[]{:S(2)}) collective-permute-start(bf16[256,2048]{1,0:T(8,128)(2,1)S(1)} %copy-done.94), channel_id=1, source_target_pairs={{0,8},{4,12},{8,0},{12,4},{1,9},{5,13},{9,1},{13,5},{2,10},{6,14},... | collective-permute-start | bytes 3145736 | tf_op jit(solution)/shard_map/ppermute | solution.py:28
  479.5 98.9 %reduce-scatter.13.cloned.1.call-start = ((), (), s32[]{:S(2)}) async-start(), calls=%async_computation.15 | async-start | bytes 1310720 | tf_op jit(solution)/shard_map/reduce_scatter | solution.py:105
  486.4 40.6 %collective-permute-start.74 = (bf16[128,2048]{1,0:T(8,128)(2,1)}, bf16[128,2048]{1,0:T(8,128)(2,1)}, u32[]{:S(2)}, u32[]{:S(2)}) collective-permute-start(bf16[128,2048]{1,0:T(8,128)(2,1)} %get-tuple-element.553), channel_id=1, source_target_pairs={{0,4},{4,0},{8,12},{12,8},{1,5},{5,1},{9,13},{13,9},{2,6},{6,2},{1... | collective-permute-start | bytes 1572872 | tf_op jit(solution)/shard_map/ppermute | solution.py:23
  487.7 39.4 %collective-permute-start.75 = (bf16[256,2048]{1,0:T(8,128)(2,1)S(1)}, bf16[256,2048]{1,0:T(8,128)(2,1)}, u32[]{:S(2)}, u32[]{:S(2)}) collective-permute-start(bf16[256,2048]{1,0:T(8,128)(2,1)S(1)} %copy-done.99), channel_id=1, source_target_pairs={{0,4},{4,0},{8,12},{12,8},{1,5},{5,1},{9,13},{13,9},{2,6},{6,2},{1... | collective-permute-start | bytes 3145736 | tf_op jit(solution)/shard_map/ppermute | solution.py:23
  488.0 39.1 %collective-permute-start.76 = (bf16[256,2048]{1,0:T(8,128)(2,1)S(1)}, bf16[256,2048]{1,0:T(8,128)(2,1)}, u32[]{:S(2)}, u32[]{:S(2)}) collective-permute-start(bf16[256,2048]{1,0:T(8,128)(2,1)S(1)} %copy-done.101), channel_id=1, source_target_pairs={{0,8},{4,12},{8,0},{12,4},{1,9},{5,13},{9,1},{13,5},{2,10},{6,14},... | collective-permute-start | bytes 3145736 | tf_op jit(solution)/shard_map/ppermute | solution.py:28
  491.8 35.3 %collective-permute-start.73 = (bf16[128,2048]{1,0:T(8,128)(2,1)}, bf16[128,2048]{1,0:T(8,128)(2,1)S(1)}, u32[]{:S(2)}, u32[]{:S(2)}) collective-permute-start(bf16[128,2048]{1,0:T(8,128)(2,1)} %get-tuple-element.555), channel_id=1, source_target_pairs={{0,8},{4,12},{8,0},{12,4},{1,9},{5,13},{9,1},{13,5},{2,10},{6,14},... | collective-permute-start | bytes 1572872 | tf_op jit(solution)/shard_map/ppermute | solution.py:28
  492.1 35.0 %collective-permute-start.72 = (bf16[296,256]{1,0:T(8,128)(2,1)S(1)}, bf16[296,256]{1,0:T(8,128)(2,1)S(1)}, u32[]{:S(2)}, u32[]{:S(2)}) collective-permute-start(bf16[296,256]{1,0:T(8,128)(2,1)S(1)} %copy-done.159), channel_id=1, source_target_pairs={{0,3},{1,0},{2,1},{3,2},{4,7},{5,4},{6,5},{7,6},{8,11},{9,8},{10,9... | collective-permute-start | bytes 454664 | tf_op jit(solution)/shard_map/ppermute | solution.py:525
  532.9 75.1 %reduce-scatter.17.cloned.1.call-start = ((), (), s32[]{:S(2)}) async-start(), calls=%async_computation.17 | async-start | bytes 1310720 | tf_op jit(solution)/shard_map/reduce_scatter | solution.py:105
  541.6 34.5 %collective-permute-start.85 = (bf16[256,2048]{1,0:T(8,128)(2,1)}, bf16[256,2048]{1,0:T(8,128)(2,1)}, u32[]{:S(2)}, u32[]{:S(2)}) collective-permute-start(bf16[256,2048]{1,0:T(8,128)(2,1)} %get-tuple-element.509), channel_id=1, source_target_pairs={{0,8},{4,12},{8,0},{12,4},{1,9},{5,13},{9,1},{13,5},{2,10},{6,14},... | collective-permute-start | bytes 3145736 | tf_op jit(solution)/shard_map/ppermute | solution.py:28
  571.3 59.6 %reduce-scatter.15.cloned.1.call-start = ((), (), s32[]{:S(2)}) async-start(), calls=%async_computation.16 | async-start | bytes 1392640 | tf_op jit(solution)/shard_map/reduce_scatter | solution.py:105
  (268 other events, 2528.2 us)
Sparse Core Ops, SparseCore 0:
  15.0 30.8 all-gather.6
  53.4 29.9 all-gather.8
  97.7 27.5 all-gather.10
  138.8 32.3 all-gather.12
  179.5 29.7 all-gather.14
  220.4 26.8 all-gather.16
  373.8 27.0 reduce-scatter.6
  405.0 26.3 reduce-scatter.8
  479.7 29.8 reduce-scatter.10
  533.0 25.8 reduce-scatter.12
  571.4 26.0 reduce-scatter.16
  600.7 30.1 reduce-scatter.14

commit v15 on v14

--- a/solution.py
+++ b/solution.py
@@ -854,8 +854,9 @@
             out_blocks = image_rows(
                 live, [params[1]["mid"], last_part, swap(last_part)], last_bias
             )
-        if 4 <= r < 4 + n_tensor - 1:
-            out_blocks[r - 3] = shift(out_blocks[r - 3], r - 3)
+        if 4 <= r < 7:
+            for d in ((), (1,), range(2, n_tensor))[r - 4]:
+                out_blocks[d] = shift(out_blocks[d], d)
             carry += out_blocks
         if r < 8:
             done = tie(carry + fresh + tied, [])
@@ -871,7 +872,7 @@
                 little, grad_blocks = done[0], done[1 : 1 + n_tensor]
             if r == 3:
                 last_part = done[1]
-            elif 4 <= r < 4 + n_tensor - 1:
+            elif 4 <= r < 7:
                 out_blocks = done[1 : 1 + n_tensor]
             done = done[len(carry) :]
             if fresh:

time: 654 us -> 647 us (0.989)
    ppermute x12, waiting for transfers between devices: 42.8 us -> 35.6 us  [shift(): return lax.ppermute(block, 'tensor', [(i, (i + d) % n) for i in range(n)])]
    unnamed x386 -> x392, local copies, waits for them, and re-layouts: 61.9 us -> 59.8 us
  transfers between devices with their start and end apart: 107 -> 107, of which waited for: 26 -> 25; matrix products, arithmetic and copies ran while one was open for 18% -> 18% of each run, Pallas kernels for 30% -> 30%
where the time goes in v15:
time: 647 us; the launch traced here: 639 us
  Pallas kernels  197 us (30%)
  waiting for transfers between devices  157 us (24%)
  local copies, waits for them, and re-layouts  105 us (16%)
  starting transfers between devices  88.4 us (14%)
  other arithmetic  75 us (12%)
  between operations  17.7 us (3%)
    pallas_call x20, Pallas kernels, run(): pl.pallas_call(kernel, out_shape=list(outs), in_specs=[block] * len(ins),...  191 us
    unnamed x392, local copies, waits for them, and re-layouts  59.8 us
    ppermute x32, waiting for transfers between devices, swap_x(): return lax.ppermute(value, 'dp', [(i, i ^ 1) for i in range(n)])  45 us
    ppermute x12, waiting for transfers between devices, shift(): return lax.ppermute(block, 'tensor', [(i, (i + d) % n) for i in range(n)])  35.6 us
    ppermute x32, waiting for transfers between devices, swap_y(): return lax.ppermute(value, 'dp', [(i, i ^ 2) for i in range(n)])  30.9 us
    convert_element_type x12, other arithmetic, scatter_two(): send.append(add(keep[half:], new[half:]).astype(jnp.bfloat16))  25.8 us
    ppermute x32, starting transfers between devices, swap_x(): return lax.ppermute(value, 'dp', [(i, i ^ 1) for i in range(n)])  24.8 us
    ppermute x32, starting transfers between devices, swap_y(): return lax.ppermute(value, 'dp', [(i, i ^ 2) for i in range(n)])  23.6 us
  transfers between devices with their start and end apart: 107, of which 25 were waited for; matrix products, arithmetic and copies ran while one was open for 18% of the time, Pallas kernels for 30%

profile of v15, /device:TPU:1, one launch (start us, length us, event | category | flops | bytes accessed | tf_op | source)
XLA Modules:
  0.0 639.2 jit_solution(13450508576089709019)
XLA Ops:
  22.5 22.7 %all-gather.7.cloned.1.call-done.refs_0_ = bf16[272,2048]{1,0:T(8,128)(2,1)} async-done(((bf16[272,512]{1,0:T(8,128)(2,1)}), bf16[272,2048]{1,0:T(8,128)(2,1)}) %all-gather.7.cloned.1.call-update) | async-done | bytes 1114128 | tf_op jit(solution)/shard_map/all_gather | solution.py:49
  104.7 15.5 %shard_map.138 = (f32[592,1024]{1,0:T(8,128)}, bf16[592,1024]{1,0:T(8,128)(2,1)}, bf16[592,512]{1,0:T(8,128)(2,1)}, bf16[592,512]{1,0:T(8,128)(2,1)}, bf16[592,5...) custom-call(f32[592,1024]{1,0:T(8,128)} %maximum_convert_fusion.refs_0_, ...), custom_call_target="tpu_custom_call" | custom-call | flops 1 | bytes 1 | tf_op jit(solution)/shard_map/pallas_call | solution.py:173
  144.5 10.2 %shard_map.141 = (f32[592,1024]{1,0:T(8,128)}, bf16[592,1024]{1,0:T(8,128)(2,1)}, bf16[592,2048]{1,0:T(8,128)(2,1)}, bf16[592,2048]{1,0:T(8,128)(2,1)}) custom-call(f32[592,1024]{1,0:T(8,128)} %get-tuple-element.300.refs_0_.u_ref, bf16[592,1024]{1,0:T(8,128)(2,1)} %get-tuple-element.301.refs_1_, bf16[592,1024]{1,0:T(8,128)(2,1)} %collective-permute-done.24.refs_2_, ...), custom_call_target="tpu_custom_call" | custom-call | flops 1 | bytes 1 | tf_op jit(solution)/shard_map/pallas_call | solution.py:173
  157.3 14.2 %collective-permute-done.29.refs_10_ = bf16[296,256]{1,0:T(8,128)(2,1)S(1)} collective-permute-done((bf16[296,256]{1,0:T(8,128)(2,1)S(1)}, bf16[296,256]{1,0:T(8,128)(2,1)S(1)}, u32[]{:S(2)}, u32[]{:S(2)}) %collective-permute-start.29) | collective-permute-done | bytes 151584 | tf_op jit(solution)/shard_map/ppermute | solution.py:525
  199.0 8.6 %collective-permute-done.36.refs_11_ = bf16[296,256]{1,0:T(8,128)(2,1)S(1)} collective-permute-done((bf16[296,256]{1,0:T(8,128)(2,1)S(1)}, bf16[296,256]{1,0:T(8,128)(2,1)S(1)}, u32[]{:S(2)}, u32[]{:S(2)}) %collective-permute-start.36) | collective-permute-done | bytes 151584 | tf_op jit(solution)/shard_map/ppermute | solution.py:525
  207.6 8.4 %collective-permute-done.33.refs_4_ = bf16[128,2048]{1,0:T(8,128)(2,1)S(1)} collective-permute-done((bf16[128,2048]{1,0:T(8,128)(2,1)}, bf16[128,2048]{1,0:T(8,128)(2,1)S(1)}, u32[]{:S(2)}, u32[]{:S(2)}) %collective-permute-start.33) | collective-permute-done | bytes 524320 | tf_op jit(solution)/shard_map/ppermute | solution.py:23
  225.1 16.9 %shard_map.147 = (f32[592,1024]{1,0:T(8,128)}, bf16[592,1024]{1,0:T(8,128)(2,1)}, bf16[592,512]{1,0:T(8,128)(2,1)}, bf16[592,512]{1,0:T(8,128)(2,1)}, bf16[592,5...) custom-call(f32[592,1024]{1,0:T(8,128)} %get-tuple-element.335.refs_0_.refs, ...), custom_call_target="tpu_custom_call" | custom-call | flops 1 | bytes 1 | tf_op jit(solution)/shard_map/pallas_call | solution.py:173
  248.1 11.2 %collective-permute-done.41.refs_4_ = bf16[128,2048]{1,0:T(8,128)(2,1)} collective-permute-done((bf16[128,2048]{1,0:T(8,128)(2,1)}, bf16[128,2048]{1,0:T(8,128)(2,1)}, u32[]{:S(2)}, u32[]{:S(2)}) %collective-permute-start.41) | collective-permute-done | bytes 524320 | tf_op jit(solution)/shard_map/ppermute | solution.py:23
  265.9 10.6 %shard_map.151 = (f32[592,1024]{1,0:T(8,128)}, bf16[592,1024]{1,0:T(8,128)(2,1)}, bf16[592,2048]{1,0:T(8,128)(2,1)}, bf16[592,2048]{1,0:T(8,128)(2,1)}) custom-call(f32[592,1024]{1,0:T(8,128)} %get-tuple-element.355.refs_0_.u_ref, bf16[592,1024]{1,0:T(8,128)(2,1)} %get-tuple-element.356.refs_1_, bf16[592,1024]{1,0:T(8,128)(2,1)} %copy-done.163, ...), custom_call_target="tpu_custom_call" | custom-call | flops 1 | bytes 1 | tf_op jit(solution)/shard_map/pallas_call | solution.py:173
  283.2 6.9 %shard_map.153 = (f32[1,1024]{1,0:T(1,128)S(1)}, bf16[256,2048]{1,0:T(8,128)(2,1)S(1)}, bf16[256,2048]{1,0:T(8,128)(2,1)S(1)}, bf16[256,2048]{1,0:T(8,128)(2,1)S(1)}, bf16[256,2048]{1,0:T(8,128)(2,1)}) custom-call(f32[592,1024]{1,0:T(8,128)} %convert_multiply_fusion.g_ref.refs_11_, bf16[592,2048]{1,0:T(8,128)(2,1)} %get-tuple-element.367.hidden_ref.refs_6_), custom_call_target="tpu_custom_call" | custom-call | flops 1 | bytes 1 | tf_op jit(solution)/shard_map/pallas_call | solution.py:173
  304.2 7.3 %shard_map.155 = (bf16[592,2048]{1,0:T(8,128)(2,1)}, f32[1,2048]{1,0:T(1,128)S(1)}) custom-call(f32[592,1024]{1,0:T(8,128)} %get-tuple-element.373.refs_0_, bf16[592,2048]{1,0:T(8,128)(2,1)} %get-tuple-element.374.refs_1_, bf16[128,2048]{1,0:T(8,128)(2,1)} %get-tuple-element.584.refs_2_.refs_1_, bf16[128,2048]{1,0:T(8,128)(2,1)S(1)} %copy-done.13, ...), custom_call_target="tpu_custom_call" | custom-call | flops 1 | bytes 1 | tf_op jit(solution)/shard_map/pallas_call | solution.py:173
  311.6 6.7 %shard_map.156.refs_0_ = bf16[592,1024]{1,0:T(8,128)(2,1)} custom-call(bf16[592,2048]{1,0:T(8,128)(2,1)} %get-tuple-element.381.refs_0_.low_ref, bf16[128,2048]{1,0:T(8,128)(2,1)} %get-tuple-element.586.refs_5_.refs_1_, bf16[128,2048]{1,0:T(8,128)(2,1)S(1)} %copy-done.26, bf16[128,2048]{1,0:T(8,128)(2,1)} %get-tuple-element.359.refs_7_.refs_3_, ...), custom_call_target="tpu_custom_call" | custom-call | flops 1 | bytes 1 | tf_op jit(solution)/shard_map/pallas_call | solution.py:173
  318.3 6.5 %shard_map.157 = (bf16[256,2048]{1,0:T(8,128)(2,1)S(1)}, bf16[256,2048]{1,0:T(8,128)(2,1)S(1)}, bf16[256,2048]{1,0:T(8,128)(2,1)S(1)}, bf16[256,2048]{1,0:T(8,128)(2,1)}) custom-call(bf16[592,1024]{1,0:T(8,128)(2,1)} %get-tuple-element.382.n_ref, bf16[592,2048]{1,0:T(8,128)(2,1)} %get-tuple-element.381.refs_0_.low_ref), custom_call_target="tpu_custom_call" | custom-call | flops 1 | bytes 1 | tf_op jit(solution)/shard_map/pallas_call | solution.py:173
  347.2 22.1 %shard_map.159 = (f32[592,1024]{1,0:T(8,128)}, bf16[592,1024]{1,0:T(8,128)(2,1)}, bf16[592,512]{1,0:T(8,128)(2,1)}, bf16[592,512]{1,0:T(8,128)(2,1)}, bf16[592,5...) custom-call(f32[592,1024]{1,0:T(8,128)} %get-tuple-element.373.refs_, ...), custom_call_target="tpu_custom_call" | custom-call | flops 1 | bytes 1 | tf_op jit(solution)/shard_map/pallas_call | solution.py:173
  381.9 7.9 %shard_map.163 = (bf16[256,2048]{1,0:T(8,128)(2,1)S(1)}, bf16[256,2048]{1,0:T(8,128)(2,1)}, bf16[256,2048]{1,0:T(8,128)(2,1)}, bf16[256,2048]{1,0:T(8,128)(2,1)}) custom-call(bf16[592,1024]{1,0:T(8,128)(2,1)} %get-tuple-element.407.n_ref, bf16[592,1024]{1,0:T(8,128)(2,1)} %get-tuple-element.408.dz_ref, bf16[592,512]{1,0:T(8,128)(2,1)S(1)} %copy-done.106, ...), custom_call_target="tpu_custom_call" | custom-call | flops 1 | bytes 1 | tf_op jit(solution)/shard_map/pallas_call | solution.py:173
  391.4 6.3 shard_map.161
  405.5 7.0 %shard_map.167 = (f32[1,1024]{1,0:T(1,128)S(1)}, bf16[256,2048]{1,0:T(8,128)(2,1)S(1)}, bf16[256,2048]{1,0:T(8,128)(2,1)S(1)}, bf16[256,2048]{1,0:T(8,128)(2,1)S(1)}, bf16[256,2048]{1,0:T(8,128)(2,1)}) custom-call(f32[592,1024]{1,0:T(8,128)} %get-tuple-element.420.refs_0_.g_ref, bf16[592,2048]{1,0:T(8,128)(2,1)} %get-tuple-element.319.refs_0_.hidden_ref), custom_call_target="tpu_custom_call" | custom-call | flops 1 | bytes 1 | tf_op jit(solution)/shard_map/pallas_call | solution.py:173
  414.5 7.4 %shard_map.165 = (bf16[592,2048]{1,0:T(8,128)(2,1)}, f32[1,2048]{1,0:T(1,128)S(1)}) custom-call(f32[592,1024]{1,0:T(8,128)} %get-tuple-element.420.refs_0_.g_ref, bf16[592,2048]{1,0:T(8,128)(2,1)} %get-tuple-element.421.refs_1_, bf16[128,2048]{1,0:T(8,128)(2,1)} %get-tuple-element.590.refs_1_.refs_2_, bf16[128,2048]{1,0:T(8,128)(2,1)S(1)} %copy-done.5, ...), custom_call_target="tpu_custom_call" | custom-call | flops 1 | bytes 1 | tf_op jit(solution)/shard_map/pallas_call | solution.py:173
  440.5 6.5 %shard_map.170 = (bf16[256,2048]{1,0:T(8,128)(2,1)S(1)}, bf16[256,2048]{1,0:T(8,128)(2,1)}, bf16[256,2048]{1,0:T(8,128)(2,1)S(1)}, bf16[256,2048]{1,0:T(8,128)(2,1)}) custom-call(bf16[592,1024]{1,0:T(8,128)(2,1)} %get-tuple-element.439.n_ref, bf16[592,2048]{1,0:T(8,128)(2,1)} %get-tuple-element.434.refs_0_.low_ref), custom_call_target="tpu_custom_call" | custom-call | flops 1 | bytes 1 | tf_op jit(solution)/shard_map/pallas_call | solution.py:173
  449.0 16.3 %collective-permute-done.66.refs_12_ = bf16[128,2048]{1,0:T(8,128)(2,1)} collective-permute-done((bf16[128,2048]{1,0:T(8,128)(2,1)S(1)}, bf16[128,2048]{1,0:T(8,128)(2,1)}, u32[]{:S(2)}, u32[]{:S(2)}) %collective-permute-start.66) | collective-permute-done | bytes 524320 | tf_op jit(solution)/shard_map/ppermute | solution.py:28
  481.4 21.1 %shard_map.172 = (f32[592,1024]{1,0:T(8,128)}, bf16[592,1024]{1,0:T(8,128)(2,1)}, bf16[592,512]{1,0:T(8,128)(2,1)}, bf16[592,512]{1,0:T(8,128)(2,1)}, bf16[592,5...) custom-call(f32[592,1024]{1,0:T(8,128)} %get-tuple-element.420.refs_, ...), custom_call_target="tpu_custom_call" | custom-call | flops 1 | bytes 1 | tf_op jit(solution)/shard_map/pallas_call | solution.py:173
  508.2 7.9 %shard_map.173 = (bf16[256,2048]{1,0:T(8,128)(2,1)S(1)}, bf16[256,2048]{1,0:T(8,128)(2,1)}, bf16[256,2048]{1,0:T(8,128)(2,1)}, bf16[256,2048]{1,0:T(8,128)(2,1)}) custom-call(bf16[592,1024]{1,0:T(8,128)(2,1)} %get-tuple-element.466.n_ref, bf16[592,1024]{1,0:T(8,128)(2,1)} %get-tuple-element.467.dz_ref, bf16[592,512]{1,0:T(8,128)(2,1)S(1)} %copy-done.109, ...), custom_call_target="tpu_custom_call" | custom-call | flops 1 | bytes 1 | tf_op jit(solution)/shard_map/pallas_call | solution.py:173
  577.9 9.5 %collective-permute-done.89 = bf16[16,2048]{1,0:T(8,128)(2,1)S(1)} collective-permute-done((bf16[16,2048]{1,0:T(8,128)(2,1)S(1)}, bf16[16,2048]{1,0:T(8,128)(2,1)S(1)}, u32[]{:S(2)}, u32[]{:S(2)}) %collective-permute-start.89) | collective-permute-done | bytes 65568 | tf_op jit(solution)/shard_map/ppermute | solution.py:28
  605.6 18.1 %reduce-scatter.15.cloned.1.call-done = bf16[272,512]{1,0:T(8,128)(2,1)} async-done(((bf16[272,2048]{1,0:T(8,128)(2,1)}), bf16[272,512]{1,0:T(8,128)(2,1)}) %reduce-scatter.15.cloned.1.call-update) | async-done | bytes 278544 | tf_op jit(solution)/shard_map/reduce_scatter | solution.py:105
  (820 shorter events, 345.3 us)
Async XLA Ops:
  7.2 38.0 %all-gather.7.cloned.1.call-start = ((), (), s32[]{:S(2)}) async-start(), calls=%async_computation.6 | async-start | bytes 1392640 | tf_op jit(solution)/shard_map/all_gather | solution.py:49
  14.2 72.7 %all-gather.9.cloned.1.call-start = ((), (), s32[]{:S(2)}) async-start(), calls=%async_computation.7 | async-start | bytes 1310720 | tf_op jit(solution)/shard_map/all_gather | solution.py:49
  51.3 35.5 %collective-permute-start.4 = (bf16[128,2048]{1,0:T(8,128)(2,1)S(1)}, bf16[128,2048]{1,0:T(8,128)(2,1)S(1)}, u32[]{:S(2)}, u32[]{:S(2)}) collective-permute-start(bf16[128,2048]{1,0:T(8,128)(2,1)S(1)} %get-tuple-element.582.refs_5_.refs_10_), channel_id=1, source_target_pairs={{0,4},{4,0},{8,12},{12,8},{1,5},{5,1},{9,13},{13,9},{2,6},{6,2},{1... | collective-permute-start | bytes 1572872 | tf_op jit(solution)/shard_map/ppermute | solution.py:23
  52.5 82.1 %all-gather.11.cloned.1.call-start = ((), (), s32[]{:S(2)}) async-start(), calls=%async_computation.8 | async-start | bytes 1310720 | tf_op jit(solution)/shard_map/all_gather | solution.py:49
  96.9 74.6 %all-gather.13.cloned.1.call-start = ((), (), s32[]{:S(2)}) async-start(), calls=%async_computation.9 | async-start | bytes 1310720 | tf_op jit(solution)/shard_map/all_gather | solution.py:49
  137.6 78.4 %all-gather.15.cloned.1.call-start = ((), (), s32[]{:S(2)}) async-start(), calls=%async_computation.10 | async-start | bytes 1310720 | tf_op jit(solution)/shard_map/all_gather | solution.py:49
  178.6 69.5 %all-gather.17.cloned.1.call-start = ((), (), s32[]{:S(2)}) async-start(), calls=%async_computation.11 | async-start | bytes 1310720 | tf_op jit(solution)/shard_map/all_gather | solution.py:49
  219.5 205.9 %reduce-scatter.7.cloned.1.call-start = ((), (), s32[]{:S(2)}) async-start(), calls=%async_computation.12 | async-start | bytes 1310720 | tf_op jit(solution)/shard_map/reduce_scatter | solution.py:105
  330.9 38.4 %collective-permute-start.57 = (bf16[256,2048]{1,0:T(8,128)(2,1)}, bf16[256,2048]{1,0:T(8,128)(2,1)}, u32[]{:S(2)}, u32[]{:S(2)}) collective-permute-start(bf16[256,2048]{1,0:T(8,128)(2,1)} %get-tuple-element.402), channel_id=1, source_target_pairs={{0,4},{4,0},{8,12},{12,8},{1,5},{5,1},{9,13},{13,9},{2,6},{6,2},{1... | collective-permute-start | bytes 3145736 | tf_op jit(solution)/shard_map/ppermute | solution.py:23
  332.1 37.2 %collective-permute-start.58 = (bf16[256,2048]{1,0:T(8,128)(2,1)}, bf16[256,2048]{1,0:T(8,128)(2,1)}, u32[]{:S(2)}, u32[]{:S(2)}) collective-permute-start(bf16[256,2048]{1,0:T(8,128)(2,1)} %get-tuple-element.403), channel_id=1, source_target_pairs={{0,8},{4,12},{8,0},{12,4},{1,9},{5,13},{9,1},{13,5},{2,10},{6,14},... | collective-permute-start | bytes 3145736 | tf_op jit(solution)/shard_map/ppermute | solution.py:28
  335.3 34.1 %collective-permute-start.56 = (bf16[128,2048]{1,0:T(8,128)(2,1)}, bf16[128,2048]{1,0:T(8,128)(2,1)}, u32[]{:S(2)}, u32[]{:S(2)}) collective-permute-start(bf16[128,2048]{1,0:T(8,128)(2,1)} %get-tuple-element.565), channel_id=1, source_target_pairs={{0,4},{4,0},{8,12},{12,8},{1,5},{5,1},{9,13},{13,9},{2,6},{6,2},{1... | collective-permute-start | bytes 1572872 | tf_op jit(solution)/shard_map/ppermute | solution.py:23
  373.1 92.3 %reduce-scatter.9.cloned.1.call-start = ((), (), s32[]{:S(2)}) async-start(), calls=%async_computation.13 | async-start | bytes 1310720 | tf_op jit(solution)/shard_map/reduce_scatter | solution.py:105
  404.3 114.2 %reduce-scatter.11.cloned.1.call-start = ((), (), s32[]{:S(2)}) async-start(), calls=%async_computation.14 | async-start | bytes 1310720 | tf_op jit(solution)/shard_map/reduce_scatter | solution.py:105
  430.3 35.1 %collective-permute-start.68 = (bf16[256,2048]{1,0:T(8,128)(2,1)S(1)}, bf16[256,2048]{1,0:T(8,128)(2,1)S(1)}, u32[]{:S(2)}, u32[]{:S(2)}) collective-permute-start(bf16[256,2048]{1,0:T(8,128)(2,1)S(1)} %copy-done.94), channel_id=1, source_target_pairs={{0,4},{4,0},{8,12},{12,8},{1,5},{5,1},{9,13},{13,9},{2,6},{6,2},{1... | collective-permute-start | bytes 3145736 | tf_op jit(solution)/shard_map/ppermute | solution.py:23
  430.5 34.8 %collective-permute-start.69 = (bf16[256,2048]{1,0:T(8,128)(2,1)S(1)}, bf16[256,2048]{1,0:T(8,128)(2,1)}, u32[]{:S(2)}, u32[]{:S(2)}) collective-permute-start(bf16[256,2048]{1,0:T(8,128)(2,1)S(1)} %copy-done.96), channel_id=1, source_target_pairs={{0,8},{4,12},{8,0},{12,4},{1,9},{5,13},{9,1},{13,5},{2,10},{6,14},... | collective-permute-start | bytes 3145736 | tf_op jit(solution)/shard_map/ppermute | solution.py:28
  470.1 100.2 %reduce-scatter.13.cloned.1.call-start = ((), (), s32[]{:S(2)}) async-start(), calls=%async_computation.15 | async-start | bytes 1310720 | tf_op jit(solution)/shard_map/reduce_scatter | solution.py:105
  476.7 41.8 %collective-permute-start.74 = (bf16[128,2048]{1,0:T(8,128)(2,1)}, bf16[128,2048]{1,0:T(8,128)(2,1)}, u32[]{:S(2)}, u32[]{:S(2)}) collective-permute-start(bf16[128,2048]{1,0:T(8,128)(2,1)} %get-tuple-element.553), channel_id=1, source_target_pairs={{0,4},{4,0},{8,12},{12,8},{1,5},{5,1},{9,13},{13,9},{2,6},{6,2},{1... | collective-permute-start | bytes 1572872 | tf_op jit(solution)/shard_map/ppermute | solution.py:23
  477.9 40.5 %collective-permute-start.75 = (bf16[256,2048]{1,0:T(8,128)(2,1)S(1)}, bf16[256,2048]{1,0:T(8,128)(2,1)S(1)}, u32[]{:S(2)}, u32[]{:S(2)}) collective-permute-start(bf16[256,2048]{1,0:T(8,128)(2,1)S(1)} %copy-done.99), channel_id=1, source_target_pairs={{0,4},{4,0},{8,12},{12,8},{1,5},{5,1},{9,13},{13,9},{2,6},{6,2},{1... | collective-permute-start | bytes 3145736 | tf_op jit(solution)/shard_map/ppermute | solution.py:23
  478.2 40.3 %collective-permute-start.76 = (bf16[256,2048]{1,0:T(8,128)(2,1)}, bf16[256,2048]{1,0:T(8,128)(2,1)}, u32[]{:S(2)}, u32[]{:S(2)}) collective-permute-start(bf16[256,2048]{1,0:T(8,128)(2,1)} %get-tuple-element.484), channel_id=1, source_target_pairs={{0,8},{4,12},{8,0},{12,4},{1,9},{5,13},{9,1},{13,5},{2,10},{6,14},... | collective-permute-start | bytes 3145736 | tf_op jit(solution)/shard_map/ppermute | solution.py:28
  480.3 38.1 %collective-permute-start.73 = (bf16[128,2048]{1,0:T(8,128)(2,1)}, bf16[128,2048]{1,0:T(8,128)(2,1)S(1)}, u32[]{:S(2)}, u32[]{:S(2)}) collective-permute-start(bf16[128,2048]{1,0:T(8,128)(2,1)} %get-tuple-element.555), channel_id=1, source_target_pairs={{0,8},{4,12},{8,0},{12,4},{1,9},{5,13},{9,1},{13,5},{2,10},{6,14},... | collective-permute-start | bytes 1572872 | tf_op jit(solution)/shard_map/ppermute | solution.py:28
  524.7 75.9 %reduce-scatter.17.cloned.1.call-start = ((), (), s32[]{:S(2)}) async-start(), calls=%async_computation.17 | async-start | bytes 1310720 | tf_op jit(solution)/shard_map/reduce_scatter | solution.py:105
  530.8 35.5 %collective-permute-start.84 = (bf16[256,2048]{1,0:T(8,128)(2,1)S(1)}, bf16[256,2048]{1,0:T(8,128)(2,1)S(1)}, u32[]{:S(2)}, u32[]{:S(2)}) collective-permute-start(bf16[256,2048]{1,0:T(8,128)(2,1)S(1)} %copy-done.92), channel_id=1, source_target_pairs={{0,4},{4,0},{8,12},{12,8},{1,5},{5,1},{9,13},{13,9},{2,6},{6,2},{1... | collective-permute-start | bytes 3145736 | tf_op jit(solution)/shard_map/ppermute | solution.py:23
  531.6 34.9 %collective-permute-start.85 = (bf16[256,2048]{1,0:T(8,128)(2,1)}, bf16[256,2048]{1,0:T(8,128)(2,1)}, u32[]{:S(2)}, u32[]{:S(2)}) collective-permute-start(bf16[256,2048]{1,0:T(8,128)(2,1)} %get-tuple-element.509), channel_id=1, source_target_pairs={{0,8},{4,12},{8,0},{12,4},{1,9},{5,13},{9,1},{13,5},{2,10},{6,14},... | collective-permute-start | bytes 3145736 | tf_op jit(solution)/shard_map/ppermute | solution.py:28
  562.0 61.7 %reduce-scatter.15.cloned.1.call-start = ((), (), s32[]{:S(2)}) async-start(), calls=%async_computation.16 | async-start | bytes 1392640 | tf_op jit(solution)/shard_map/reduce_scatter | solution.py:105
  (271 other events, 2553.8 us)
Sparse Core Ops, SparseCore 0:
  14.3 30.8 all-gather.6
  52.6 29.9 all-gather.8
  97.0 27.5 all-gather.10
  137.8 32.3 all-gather.12
  178.7 29.7 all-gather.14
  219.6 26.8 all-gather.16
  373.2 27.0 reduce-scatter.6
  404.4 26.3 reduce-scatter.8
  470.3 32.3 reduce-scatter.10
  524.8 25.0 reduce-scatter.12
  562.1 25.5 reduce-scatter.16
  594.1 29.5 reduce-scatter.14
